TPU v7x, 32 devices: a whole 2x2x4 slice. The times are simulated.
32 devices in a mesh: tok: 4 (over x, core), feat: 4 (over z), row: 2 (over y).
Axes of the slice: x: 2, y: 2, z: 4, core: 2. Of those that a mesh axis runs over, the one named last changes fastest.
Arguments:
- quantized: bfloat16 [16384, 28672], P('tok', 'feat'), may hold values from -8 to 8
- exponents: int32 [16384, 224], P('tok', 'feat'), may hold values from -3 to 3
- weights: bfloat16 [8192, 28672], P(('tok', 'row'), 'feat'), may hold values from -6 to 6
- keep_mask: int32 [8192, 256], P(('tok', 'row')), may hold values from 0 to 1, as said below
Outputs:
- pruned: bfloat16 [8192, 28672], P(('tok', 'row'), 'feat')
Inputs may be any that keep to these rules, and one draw needn't show every extreme that they name: `keep_mask`: in every row each group of four consecutive columns holds exactly two ones.
All inputs are finite; a program needn't handle non-finite values.
Results may differ from a plain program's by a relative error of at most 0.0012.
Values may be sent and summed in bfloat16 or wider, within the bound.
No kernel may reach another device: no remote copies, remote signals or barrier semaphores. Data moves between devices by JAX's collectives and lax.ppermute only.
A program may use at most 256 MiB of HBM per device.

v0:
```python
import jax
import jax.numpy as jnp
from jax import lax
from jax.sharding import PartitionSpec as P

PANEL = 256
QBLOCK = 128


def from_root(x, axis, root):
    mine = lax.axis_index(axis) == root
    return lax.psum(jnp.where(mine, x, jnp.zeros_like(x)), axis)


def matmul_high(left, right):
    return jnp.dot(left, right, precision=lax.Precision.HIGHEST)


def factor_small(block):
    size = block.shape[0]
    lower = jnp.zeros_like(block)
    for j in range(size):
        head = lower[j, :j]
        diag_value = jnp.sqrt(block[j, j] - jnp.sum(head * head))
        column = (block[j:, j] - matmul_high(lower[j:, :j], head)) / diag_value
        lower = lower.at[j:, j].set(column)
    ident = jnp.eye(size, dtype=block.dtype)
    inverse = jnp.zeros_like(block)
    for i in range(size):
        row_value = (ident[i] - matmul_high(lower[i, :i], inverse[:i, :])) / lower[i, i]
        inverse = inverse.at[i].set(row_value)
    return (lower, inverse)


def factor_with_inverse(block):
    size = block.shape[0]
    if size <= 16:
        return factor_small(block)
    half = size // 2
    upper_lower, upper_inverse = factor_with_inverse(block[:half, :half])
    below = matmul_high(block[half:, :half], upper_inverse.T)
    rest = block[half:, half:] - matmul_high(below, below.T)
    rest_lower, rest_inverse = factor_with_inverse(rest)
    zeros_top = jnp.zeros((half, size - half), block.dtype)
    lower = jnp.concatenate(
        [
            jnp.concatenate([upper_lower, zeros_top], axis=1),
            jnp.concatenate([below, rest_lower], axis=1),
        ],
        axis=0,
    )
    cross = -matmul_high(rest_inverse, matmul_high(below, upper_inverse))
    inverse = jnp.concatenate(
        [
            jnp.concatenate([upper_inverse, zeros_top], axis=1),
            jnp.concatenate([cross, rest_inverse], axis=1),
        ],
        axis=0,
    )
    return (lower, inverse)


def solve_coeffs(diag_block, panel_weights, keep_mask):
    factor, factor_inv = factor_with_inverse(diag_block)
    pruned_error = panel_weights * (1.0 - keep_mask.astype(jnp.float32))
    return matmul_high(matmul_high(pruned_error, factor_inv.T), factor_inv)


def shards(quantized, exponents, weights, keep_mask):
    feat_cols = quantized.shape[1]
    panel_weights = weights[:, :PANEL]
    row_share = quantized.shape[0] // lax.axis_size("row")
    row_start = lax.axis_index("row") * row_share
    tok_quant = lax.dynamic_slice_in_dim(quantized, row_start, row_share, 0)
    tok_exps = lax.dynamic_slice_in_dim(exponents, row_start, row_share, 0)
    tok_rows = tok_quant.shape[0]
    scales = jnp.exp2(tok_exps.astype(jnp.float32)).astype(jnp.bfloat16)
    activations = (
        tok_quant.reshape(tok_rows, feat_cols // QBLOCK, QBLOCK) * scales[:, :, None]
    ).reshape(tok_rows, feat_cols)
    panel_acts = from_root(activations[:, :PANEL], "feat", 0)
    partial_gram = lax.dot_general(
        activations, panel_acts, (((0,), (0,)), ((), ())), preferred_element_type=jnp.float32
    )
    hessian_panel = lax.psum(partial_gram, ("tok", "row"))
    head_block = hessian_panel[:PANEL]
    damping = 0.01 * jnp.mean(jnp.diagonal(head_block))
    diag_block = head_block + damping * jnp.eye(PANEL, dtype=jnp.float32)
    own_coeffs = solve_coeffs(diag_block, panel_weights.astype(jnp.float32), keep_mask)
    coefficients = from_root(own_coeffs, "feat", 0)
    update = jnp.dot(coefficients, hessian_panel.T, precision=lax.Precision.HIGHEST)
    columns = lax.axis_index("feat") * feat_cols + jnp.arange(feat_cols, dtype=jnp.int32)[None, :]
    weights_float = weights.astype(jnp.float32)
    mask_padded = (
        jnp.ones((weights.shape[0], feat_cols), jnp.float32)
        .at[:, :PANEL]
        .set(keep_mask.astype(jnp.float32))
    )
    result = jnp.where(columns < PANEL, weights_float * mask_padded, weights_float + update)
    return result.astype(jnp.bfloat16)


def solution(mesh):
    placed = (
        P("tok", "feat"),
        P("tok", "feat"),
        P(("tok", "row"), "feat"),
        P(("tok", "row"), None),
    )
    return jax.shard_map(
        shards, mesh=mesh, in_specs=placed, out_specs=P(("tok", "row"), "feat"), check_vma=False
    )
```

profile of v0, /device:TPU:9, one launch (start us, length us, event | category | flops | bytes accessed | tf_op | source)
XLA Modules:
  0.0 1401.8 jit_solution(7257698037239752491)
XLA Ops:
  7.9 18.7 %mul.769 = bf16[2048,56,128]{2,1,0:T(8,128)(2,1)} broadcast(bf16[2048,56]{1,0:T(8,128)(2,1)S(1)} %copy.230), dimensions={0,1} | broadcast | bytes 29589504 | tf_op jit(solution)/shard_map/mul | solution.py:79
  26.6 29.9 %bitcast_multiply_fusion = bf16[2048,7168]{1,0:T(8,128)(2,1)} fusion(bf16[256,8,56,128]{3,2,1,0:T(8,128)(2,1)} %bitcast.7895, bf16[4096,7168]{1,0:T(8,128)(2,1)} %param.1030, s32[]{:T(128)S(6)} %select_n.29), kind=kLoop, calls=%fused_computation.5 | loop fusion | flops 58720256 | bytes 88080384 | tf_op jit(solution)/shard_map/mul | solution.py:79
  56.5 2.3 slice_select_fusion
  58.8 52.7 %all-reduce.52.cloned.1.call-done = bf16[2048,256]{1,0:T(8,128)(2,1)} async-done(((bf16[2048,256]{1,0:T(8,128)(2,1)}), bf16[2048,256]{1,0:T(8,128)(2,1)}) %all-reduce.52.cloned.1.call-update) | async-done | bytes 1048592 | tf_op jit(solution)/shard_map/psum | solution.py:12
  111.5 15.5 %fusion.2579 = f32[7168,256]{1,0:T(8,128)} fusion(bf16[2048,7168]{1,0:T(8,128)(2,1)} %bitcast_multiply_fusion, bf16[2048,256]{1,0:T(8,128)(2,1)} %all-reduce.52.cloned.1.call-done), kind=kOutput, calls=%fused_computation.3786 | convolution fusion | flops 7516192768 | bytes 37748736 | tf_op jit(solution)/shard_map/dot_general | solution.py:82
  127.9 114.6 %all-reduce.54.cloned.1.call-done = f32[7168,256]{1,0:T(8,128)} async-done(((f32[7168,256]{1,0:T(8,128)}), f32[7168,256]{1,0:T(8,128)}) %all-reduce.54.cloned.1.call-update) | async-done | bytes 7340048 | tf_op jit(solution)/shard_map/psum | solution.py:85
  243.6 2.3 gather_fusion
  290.2 1.9 subtract_divide_fusion.15
  295.1 1.5 fusion.649
  301.1 1.5 fusion.661
  304.0 1.5 fusion.225
  355.6 2.6 subtract_divide_fusion.14
  422.0 2.6 subtract_divide_fusion.13
  487.9 2.6 subtract_divide_fusion.12
  493.5 1.5 fusion.757
  499.5 1.5 fusion.769
  502.5 1.5 fusion.303
  555.0 2.6 subtract_divide_fusion.11
  560.6 1.5 fusion.793
  566.6 1.5 fusion.805
  621.1 2.6 subtract_divide_fusion.10
  687.5 2.6 subtract_divide_fusion.9
  753.4 2.6 subtract_divide_fusion.8
  759.0 1.5 fusion.901
  765.0 1.5 fusion.913
  768.0 1.5 fusion.407
  820.8 2.6 subtract_divide_fusion.7
  826.4 1.5 fusion.937
  832.4 1.5 fusion.949
  835.3 1.5 fusion.433
  886.9 2.6 subtract_divide_fusion.6
  953.5 2.6 subtract_divide_fusion.5
  1019.4 2.6 subtract_divide_fusion.4
  1025.0 1.5 fusion.1045
  1031.0 1.5 fusion.1057
  1033.9 1.5 fusion.511
  1086.3 2.6 subtract_divide_fusion.3
  1091.9 1.5 fusion.1081
  1097.9 1.5 fusion.1093
  1100.8 1.5 fusion.537
  1152.4 2.6 subtract_divide_fusion.2
  1218.8 2.6 subtract_divide_fusion.1
  1283.4 2.7 subtract_divide_fusion
  1287.5 1.5 fusion.1186
  1308.0 2.1 fusion.1282
  1310.1 2.0 convolution_select_fusion
  1313.5 50.6 %all-reduce.56.cloned.1.call-done = f32[1024,256]{1,0:T(8,128)} async-done(((f32[1024,256]{1,0:T(8,128)}), f32[1024,256]{1,0:T(8,128)}) %all-reduce.56.cloned.1.call-update) | async-done | bytes 1048592 | tf_op jit(solution)/shard_map/psum | solution.py:12
  1364.0 30.8 %fusion.1 = bf16[1024,7168]{1,0:T(8,128)(2,1)} fusion(bf16[1024,7168]{1,0:T(8,128)(2,1)} %param.1032, f32[1024,256]{1,0:T(8,128)S(1)} %convert_select_fusion, pred[7168]{0:T(1024)(128)(4,1)S(1)} %add_compare_fusion, f32[1024,256]{1,0:T(8,128)} %all-reduce.56.cloned.1.call-done, f32[7168,256]{1,0:T(8,128)} %all-reduce.54.cloned.1.call-done), kind=kOutput, calls=%fused_computation.4 | convolution fusion | flops 22585278464 | bytes 38804480 | tf_op jit(solution)/shard_map/dot_general | solution.py:91
  (1738 shorter events, 634.1 us)
Async XLA Ops:
  6.5 105.0 %all-reduce.52.cloned.1.call-start = ((), (), s32[]{:S(2)}) async-start(), calls=%async_computation | async-start | bytes 2097152 | tf_op jit(solution)/shard_map/psum | solution.py:12
  58.7 183.8 %all-reduce.54.cloned.1.call-start = ((), (), s32[]{:S(2)}) async-start(), calls=%async_computation.1 | async-start | bytes 14680064 | tf_op jit(solution)/shard_map/psum | solution.py:85
  127.0 1181.0 %copy-start = (s32[1024,256]{1,0:T(8,128)S(1)}, s32[1024,256]{1,0:T(8,128)}, u32[]{:S(2)}) copy-start(s32[1024,256]{1,0:T(8,128)} %param.1033) | copy-start | bytes 3145732
  127.1 1237.0 %all-reduce.56.cloned.1.call-start = ((), (), s32[]{:S(2)}) async-start(), calls=%async_computation.2 | async-start | bytes 2097152 | tf_op jit(solution)/shard_map/psum | solution.py:12
  127.9 164.2 %copy-start.1 = (f32[16,16]{1,0:T(8,128)}, f32[16,16]{1,0:T(8,128)S(1)}, u32[]{:S(2)}) copy-start(f32[16,16]{1,0:T(8,128)S(1)} %fusion.1626) | copy-start | bytes 3076
  287.6 4.6 copy-start.6
  485.3 5.3 copy-start.2
  552.4 5.3 copy-start.7
  750.7 5.3 copy-start.3
  818.1 5.3 copy-start.8
  1016.7 5.3 copy-start.4
  1083.6 5.3 copy-start.9
  1280.6 5.5 copy-start.5
Sparse Core Ops, SparseCore 0:
  58.9 52.5 all-reduce.51
  127.2 115.3 all-reduce.53
  1312.3 51.6 all-reduce.55
where the time goes:
time: 1430 us; the launch traced here: 1400 us
  matrix products  394 us (28%)
  between operations  373 us (26%)
  other arithmetic  243 us (17%)
  waiting for transfers between devices  218 us (15%)
  local copies, waits for them, and re-layouts  174 us (12%)
    dot_general x494, matrix products, matmul_high(): return jnp.dot(left, right, precision=lax.Precision.HIGHEST)  347 us
    reduce_sum x224, other arithmetic, factor_small(): diag_value = jnp.sqrt(block[j, j] - jnp.sum(head * head))  143 us
    psum x1, waiting for transfers between devices, shards(): hessian_panel = lax.psum(partial_gram, ('tok', 'row'))  115 us
    psum x2, waiting for transfers between devices, from_root(): return lax.psum(jnp.where(mine, x, jnp.zeros_like(x)), axis)  103 us
    scatter x240, local copies, waits for them, and re-layouts, factor_small(): lower = lower.at[j:, j].set(column)  53.6 us
    slice x224, local copies, waits for them, and re-layouts, factor_small(): column = (block[j:, j] - matmul_high(lower[j:, :j], head)) / diag_value  49.7 us
    div x16, other arithmetic, factor_small(): (ident[i] - matmul_high(lower[i, :i], inverse[:i, :])) / lower[i, i]  41.2 us
    dot_general x1, matrix products, shards(): jnp.dot(coefficients, hessian_panel.T, precision=lax.Precision.HIGHEST)  30.8 us
  transfers between devices with their start and end apart: 3, of which 3 were waited for; matrix products, arithmetic and copies ran while one was open for 0% of the time, Pallas kernels for 0%

commit v1 on v0

v1 whole, which is shorter than its diff:
```python
import functools

import jax
import jax.numpy as jnp
from jax import lax
from jax.experimental import pallas as pl
from jax.experimental.pallas import tpu as pltpu
from jax.sharding import PartitionSpec as P

PANEL = 256
QBLOCK = 128
CHUNKS = 4
F32 = jnp.float32
BF16 = jnp.bfloat16


def dot_high(left, right):
    return jnp.dot(left, right, precision=lax.Precision.HIGHEST, preferred_element_type=F32)


def gram_kernel(blocks, place_ref, quant_ref, scale_ref, panel_ref, out_ref, acts_ref):
    col = place_ref[0]
    shift = lax.rem(QBLOCK - lax.rem(col * blocks, QBLOCK), QBLOCK)
    scale = pltpu.roll(scale_ref[...], shift, 1)
    rows = scale.shape[0]
    for c in range(blocks):
        span = slice(c * QBLOCK, (c + 1) * QBLOCK)
        wide = jnp.broadcast_to(scale[:, c : c + 1], (rows, QBLOCK)).astype(BF16)
        acts_ref[:, span] = quant_ref[:, span] * wide
    part = jnp.dot(panel_ref[...], acts_ref[...], preferred_element_type=F32)

    @pl.when(pl.program_id(0) == 0)
    def _():
        out_ref[...] = part

    @pl.when(pl.program_id(0) > 0)
    def _():
        out_ref[...] += part


def gram_block(quantized, scale_pad, panel_t, col, width):
    tokens, cols = quantized.shape
    if width % QBLOCK or cols // QBLOCK > QBLOCK:
        quant = lax.dynamic_slice_in_dim(quantized, col * width, width, 1)
        index = (col * width + jnp.arange(width)) // QBLOCK
        acts = quant * jnp.take(scale_pad, index, axis=1).astype(BF16)
        return jnp.dot(panel_t, acts, preferred_element_type=F32)
    step = min(tokens, 1024)
    return pl.pallas_call(
        functools.partial(gram_kernel, width // QBLOCK),
        out_shape=jax.ShapeDtypeStruct((PANEL, width), F32),
        grid_spec=pltpu.PrefetchScalarGridSpec(
            num_scalar_prefetch=1,
            grid=(tokens // step,),
            in_specs=[
                pl.BlockSpec((step, width), lambda k, place: (k, place[0])),
                pl.BlockSpec((step, QBLOCK), lambda k, place: (k, 0)),
                pl.BlockSpec((PANEL, step), lambda k, place: (0, k)),
            ],
            out_specs=pl.BlockSpec((PANEL, width), lambda k, place: (0, 0)),
            scratch_shapes=[pltpu.VMEM((step, width), BF16)],
        ),
        compiler_params=pltpu.CompilerParams(vmem_limit_bytes=40 << 20),
        cost_estimate=pl.CostEstimate(
            flops=2 * tokens * width * PANEL,
            bytes_accessed=2 * tokens * width + 4 * PANEL * width,
            transcendentals=0,
        ),
    )(col.reshape(1).astype(jnp.int32), quantized, scale_pad, panel_t)


def inverse_kernel(head_ref, out_ref, pair_ref):
    size = PANEL
    rows = lax.broadcasted_iota(jnp.int32, (size, size), 0)
    cols = lax.broadcasted_iota(jnp.int32, (size, size), 1)
    eye = jnp.where(rows == cols, 1.0, 0.0).astype(F32)
    head = head_ref[...]
    damping = 0.01 * (jnp.sum(head * eye) / size)
    block = head + damping * eye
    high = jnp.max(jnp.sum(jnp.abs(block), axis=0))
    start = 2.0 / (high + damping)
    spread = (high - damping) / (high + damping)
    pair_ref[:size] = start * eye
    pair_ref[size:] = start * block

    def more(spread):
        return spread > 1e-3

    def step(spread):
        square = spread * spread
        gain = 2.0 / (2.0 - square)
        turn = gain * (2.0 * eye - pair_ref[size:])
        pair_ref[...] = dot_high(pair_ref[...], turn)
        return square / (2.0 - square)

    lax.while_loop(more, step, spread)
    out = pair_ref[:size]
    for _ in range(2):
        out = out + dot_high(out, eye - dot_high(block, out))
    out_ref[...] = out


def invert(head):
    return pl.pallas_call(
        inverse_kernel,
        out_shape=jax.ShapeDtypeStruct((PANEL, PANEL), F32),
        scratch_shapes=[pltpu.VMEM((2 * PANEL, PANEL), F32)],
        compiler_params=pltpu.CompilerParams(vmem_limit_bytes=32 << 20),
        cost_estimate=pl.CostEstimate(
            flops=28 * 12 * PANEL**3, bytes_accessed=8 * PANEL * PANEL, transcendentals=0
        ),
    )(head)


def gains_kernel(inverse_ref, first_ref, second_ref, third_ref, high_ref, low_ref):
    total = first_ref[...] + second_ref[...] + third_ref[...]
    gains = dot_high(inverse_ref[...], total)
    high = gains.astype(BF16)
    high_ref[...] = high
    low_ref[...] = (gains - high.astype(F32)).astype(BF16)


def make_gains(inverse, parts):
    width = parts[0].shape[1]
    shape = jax.ShapeDtypeStruct((PANEL, width), BF16)
    return pl.pallas_call(
        gains_kernel,
        out_shape=(shape, shape),
        compiler_params=pltpu.CompilerParams(vmem_limit_bytes=32 << 20),
        cost_estimate=pl.CostEstimate(
            flops=12 * PANEL * PANEL * width, bytes_accessed=16 * PANEL * width, transcendentals=0
        ),
    )(inverse, *parts)


def update_kernel(count, aliased, place_ref, weights_ref, error_ref, *refs):
    gains = refs[:count]
    out_ref = refs[-1]
    error = error_ref[...]
    total = weights_ref[...].astype(F32)
    for gain in gains:
        total = total + jnp.dot(error, gain[...], preferred_element_type=F32)
    out_ref[...] = total.astype(BF16)

    @pl.when(place_ref[1] == 1)
    def _():
        out_ref[:, :PANEL] = weights_ref[:, :PANEL] - error


def update_block(out, weights, error, gains, col, first):
    rows, cols = weights.shape
    width = gains[0].shape[1]
    if width % QBLOCK or width < PANEL:
        start = col * width
        total = lax.dynamic_slice_in_dim(weights, start, width, 1).astype(F32)
        for gain in gains:
            total = total + jnp.dot(error, gain, preferred_element_type=F32)
        if out is None:
            out = jnp.zeros_like(weights)
        return lax.dynamic_update_slice_in_dim(out, total.astype(BF16), start, 1)
    step = min(rows, 256)
    place = jnp.stack([col, (first & (col == 0)).astype(jnp.int32)]).astype(jnp.int32)
    specs = [
        pl.BlockSpec((step, width), lambda i, place: (i, place[0])),
        pl.BlockSpec((step, PANEL), lambda i, place: (i, 0)),
    ] + [pl.BlockSpec((PANEL, width), lambda i, place: (0, 0))] * len(gains)
    args = [place, weights, error, *gains]
    aliases = {}
    if out is not None:
        specs.append(pl.BlockSpec(memory_space=pl.ANY))
        aliases = {len(args): 0}
        args.append(out)
    return pl.pallas_call(
        functools.partial(update_kernel, len(gains), out is not None),
        out_shape=jax.ShapeDtypeStruct((rows, cols), BF16),
        grid_spec=pltpu.PrefetchScalarGridSpec(
            num_scalar_prefetch=1,
            grid=(rows // step,),
            in_specs=specs,
            out_specs=pl.BlockSpec((step, width), lambda i, place: (i, place[0])),
        ),
        input_output_aliases=aliases,
        compiler_params=pltpu.CompilerParams(vmem_limit_bytes=32 << 20),
        cost_estimate=pl.CostEstimate(
            flops=2 * rows * width * PANEL * len(gains),
            bytes_accessed=4 * rows * width,
            transcendentals=0,
        ),
    )(*args)


def swap(x, axis, bit):
    size = lax.axis_size(axis)
    return lax.ppermute(x, axis, [(i, i ^ bit) for i in range(size)])


def from_first(x, axis):
    size = lax.axis_size(axis)
    index = lax.axis_index(axis)
    held, result = x, x
    for hop in range(size - 1):
        held = lax.ppermute(held, axis, [(hop, hop + 1)])
        result = jnp.where(index == hop + 1, held, result)
    return result


def shards(quantized, exponents, weights, keep_mask):
    tokens, cols = quantized.shape
    toks, rows = lax.axis_size("tok"), lax.axis_size("row")
    tok, row, feat = lax.axis_index("tok"), lax.axis_index("row"), lax.axis_index("feat")
    width = cols // (toks * rows)

    share = tokens // rows
    scale = jnp.exp2(exponents.astype(F32))
    scale_pad = jnp.pad(scale, ((0, 0), (0, -scale.shape[1] % QBLOCK)))
    piece = share // CHUNKS
    own, other = [], []
    for c in range(CHUNKS):
        at = row * share + c * piece
        raw = lax.dynamic_slice(quantized, (at, 0), (piece, PANEL))
        exps = lax.dynamic_slice(scale, (at, 0), (piece, PANEL // QBLOCK)).astype(BF16)
        acts = (raw.reshape(piece, PANEL // QBLOCK, QBLOCK) * exps[:, :, None]).reshape(piece, PANEL)
        mine = from_first(acts.T, "feat")
        own.append(mine)
        other.append(swap(mine, "row", 1))
    mine, theirs = jnp.concatenate(own, axis=1), jnp.concatenate(other, axis=1)
    panel_t = jnp.concatenate(
        [jnp.where(row == 0, mine, theirs), jnp.where(row == 0, theirs, mine)], axis=1
    )

    error = from_first(
        jnp.where(keep_mask == 0, weights[:, :PANEL], jnp.zeros((), BF16)), "feat"
    )

    head = lax.dot_general(
        panel_t, panel_t, (((1,), (1,)), ((), ())), preferred_element_type=F32
    )
    head = head + swap(head, "tok", 1)
    head = head + swap(head, "tok", 2)

    def gram(k):
        return gram_block(quantized, scale_pad, panel_t, row * toks + (tok ^ k), width)

    block3 = gram(3)
    from3 = swap(block3, "tok", 1)
    block2 = gram(2)
    fromx = swap(block2 + from3, "tok", 2)
    block1 = gram(1)
    from1 = swap(block1, "tok", 1)
    block0 = gram(0)
    inverse = invert(head)
    high, low = make_gains(inverse, (block0, from1, fromx))

    half = PANEL // 2
    near_high, near_low = swap(high, "tok", 1), swap(low, "tok", 1)
    in_x, in_y = swap(high, "tok", 2), swap(high, "row", 1)
    far = jnp.concatenate([swap(in_y[:half], "tok", 2), swap(in_x[half:], "row", 1)], axis=0)
    near_x, near_y, near_far = swap(in_x, "tok", 1), swap(in_y, "tok", 1), swap(far, "tok", 1)

    out = None
    plan = [
        ((high, low), 0, 0),
        ((near_high, near_low), 1, 0),
        ((in_x,), 2, 0),
        ((in_y,), 0, 1),
        ((near_x,), 3, 0),
        ((near_y,), 1, 1),
        ((far,), 2, 1),
        ((near_far,), 3, 1),
    ]
    for gains, tok_bits, row_bit in plan:
        col = (row ^ row_bit) * toks + (tok ^ tok_bits)
        out = update_block(out, weights, error, gains, col, feat == 0)
    if width % QBLOCK or width < PANEL:
        panel = jnp.where(feat == 0, weights[:, :PANEL] - error, out[:, :PANEL])
        out = lax.dynamic_update_slice_in_dim(out, panel, 0, 1)
    return out


def solution(mesh):
    placed = (
        P("tok", "feat"),
        P("tok", "feat"),
        P(("tok", "row"), "feat"),
        P(("tok", "row"), None),
    )
    return jax.shard_map(
        shards, mesh=mesh, in_specs=placed, out_specs=P(("tok", "row"), "feat"), check_vma=False
    )
```

time: 1430 us -> 205 us (0.14)
  the two profiles are of different devices: /device:TPU:9 before, /device:TPU:0 now
where the time goes in v1:
time: 205 us; the launch traced here: 204 us
  Pallas kernels  70.2 us (34%)
  waiting for transfers between devices  56.7 us (28%)
  starting transfers between devices  43.1 us (21%)
  local copies, waits for them, and re-layouts  22.9 us (11%)
  other arithmetic  9.8 us (5%)
    ppermute x18, waiting for transfers between devices, swap(): return lax.ppermute(x, axis, [(i, i ^ bit) for i in range(size)])  45.7 us
    pallas_call x8, Pallas kernels, update_block(): pl.pallas_call(functools.partial(update_kernel, len(gains), out is not No...  30.5 us
    ppermute x15, starting transfers between devices, from_first(): held = lax.ppermute(held, axis, [(hop, hop + 1)])  28.9 us
    pallas_call x4, Pallas kernels, gram_block(): pl.pallas_call(functools.partial(gram_kernel, width // QBLOCK), out_shape...  28.4 us
    unnamed x47, local copies, waits for them, and re-layouts  16 us
    ppermute x18, starting transfers between devices, swap(): return lax.ppermute(x, axis, [(i, i ^ bit) for i in range(size)])  14.2 us
    ppermute x15, waiting for transfers between devices, from_first(): held = lax.ppermute(held, axis, [(hop, hop + 1)])  11 us
    pallas_call x1, Pallas kernels, invert(): pl.pallas_call(inverse_kernel, out_shape=jax.ShapeDtypeStruct((PANEL, PAN...  7.82 us
  transfers between devices with their start and end apart: 33, of which 10 were waited for; matrix products, arithmetic and copies ran while one was open for 7% of the time, Pallas kernels for 28%

profile of v1, /device:TPU:0, one launch (start us, length us, event | category | flops | bytes accessed | tf_op | source)
XLA Modules:
  0.0 203.8 jit_solution(75700745559071650)
XLA Ops:
  0.0 3.1 %copy.22 = s32[4096,56]{1,0:T(8,128)} copy(s32[4096,56]{0,1:T(8,128)} %param.5) | data formatting | bytes 1835008 | tf_op args[1]
  3.1 1.9 multiply_exponential_fusion
  7.5 4.9 %collective-permute-start.9 = (bf16[256,512]{1,0:T(8,128)(2,1)S(1)}, bf16[256,512]{1,0:T(8,128)(2,1)S(1)}, u32[]{:S(2)}, u32[]{:S(2)}) collective-permute-start(bf16[256,512]{1,0:T(8,128)(2,1)S(1)} %bitcast.36), channel_id=1, source_target_pairs={{0,2},{1,3},{8,10},{9,11},{16,18},{17,19},{24,26},{25,27}} | collective-permute-start | bytes 786440 | tf_op jit(solution)/shard_map/ppermute | solution.py:202
  17.7 2.0 collective-permute-start.6
  19.7 1.3 collective-permute-start.10
  21.1 3.6 %collective-permute-done.3 = bf16[256,512]{1,0:T(8,128)(2,1)S(1)} collective-permute-done((bf16[256,512]{1,0:T(8,128)(2,1)S(1)}, bf16[256,512]{1,0:T(8,128)(2,1)S(1)}, u32[]{:S(2)}, u32[]{:S(2)}) %collective-permute-start.3) | collective-permute-done | bytes 262176 | tf_op jit(solution)/shard_map/ppermute | solution.py:202
  24.7 1.4 collective-permute-start.4
  26.1 4.2 %collective-permute-done.12 = bf16[256,512]{1,0:T(8,128)(2,1)S(1)} collective-permute-done((bf16[256,512]{1,0:T(8,128)(2,1)S(1)}, bf16[256,512]{1,0:T(8,128)(2,1)S(1)}, u32[]{:S(2)}, u32[]{:S(2)}) %collective-permute-start.12) | collective-permute-done | bytes 262176 | tf_op jit(solution)/shard_map/ppermute | solution.py:202
  30.3 1.4 collective-permute-start.13
  31.7 3.1 %collective-permute-done.6 = bf16[256,512]{1,0:T(8,128)(2,1)} collective-permute-done((bf16[256,512]{1,0:T(8,128)(2,1)S(1)}, bf16[256,512]{1,0:T(8,128)(2,1)}, u32[]{:S(2)}, u32[]{:S(2)}) %collective-permute-start.6) | collective-permute-done | bytes 262176 | tf_op jit(solution)/shard_map/ppermute | solution.py:202
  34.8 1.4 collective-permute-start.7
  36.2 1.4 collective-permute-start.11
  37.6 1.4 collective-permute-start.5
  38.9 1.7 pad.4.scale_ref
  42.2 1.6 collective-permute-start.17
  44.5 1.6 collective-permute-start.16
  46.7 10.4 %collective-permute-done.15 = bf16[256,512]{1,0:T(8,128)(2,1)S(1)} collective-permute-done((bf16[256,512]{1,0:T(8,128)(2,1)S(1)}, bf16[256,512]{1,0:T(8,128)(2,1)S(1)}, u32[]{:S(2)}, u32[]{:S(2)}) %collective-permute-start.15) | collective-permute-done | bytes 262176 | tf_op jit(solution)/shard_map/ppermute | solution.py:194
  57.1 5.6 %collective-permute-done.16 = bf16[256,512]{1,0:T(8,128)(2,1)S(1)} collective-permute-done((bf16[256,512]{1,0:T(8,128)(2,1)S(1)}, bf16[256,512]{1,0:T(8,128)(2,1)S(1)}, u32[]{:S(2)}, u32[]{:S(2)}) %collective-permute-start.16) | collective-permute-done | bytes 262176 | tf_op jit(solution)/shard_map/ppermute | solution.py:194
  62.8 3.5 %collective-permute-done.18 = bf16[256,512]{1,0:T(8,128)(2,1)S(1)} collective-permute-done((bf16[256,512]{1,0:T(8,128)(2,1)S(1)}, bf16[256,512]{1,0:T(8,128)(2,1)S(1)}, u32[]{:S(2)}, u32[]{:S(2)}) %collective-permute-start.18) | collective-permute-done | bytes 262176 | tf_op jit(solution)/shard_map/ppermute | solution.py:194
  68.1 8.4 %shard_map.50 = f32[256,896]{1,0:T(8,128)} custom-call(s32[1]{0:T(128)} %bitcast.13.place_ref, bf16[4096,7168]{1,0:T(8,128)(2,1)} %quant_ref.7, f32[4096,128]{1,0:T(8,128)S(1)} %pad.4.scale_ref, bf16[256,4096]{1,0:T(8,128)(2,1)S(1)} %pad_maximum_fusion.panel_ref), custom_call_target="tpu_custom_call" | custom-call | flops 1879048192 | bytes 8257536 | tf_op jit(solution)/shard_map/pallas_call | solution.py:49
  77.7 6.9 %collective-permute-start = (bf16[1024,256]{1,0:T(8,128)(2,1)S(1)}, bf16[1024,256]{1,0:T(8,128)(2,1)}, u32[]{:S(2)}, u32[]{:S(2)}) collective-permute-start(bf16[1024,256]{1,0:T(8,128)(2,1)S(1)} %compare_select_fusion), channel_id=1, source_target_pairs={{0,2},{1,3},{8,10},{9,11},{16,18},{17,19},{24,26},{25,27}} | collective-permute-start | bytes 1572872 | tf_op jit(solution)/shard_map/ppermute | solution.py:202
  84.5 1.6 copy-done.2
  86.1 6.8 %shard_map.48 = f32[256,896]{1,0:T(8,128)S(1)} custom-call(s32[1]{0:T(128)} %bitcast.11.place_ref, bf16[4096,7168]{1,0:T(8,128)(2,1)} %quant_ref.7, f32[4096,128]{1,0:T(8,128)S(1)} %pad.4.scale_ref, bf16[256,4096]{1,0:T(8,128)(2,1)S(1)} %copy-done.2), custom_call_target="tpu_custom_call" | custom-call | flops 1879048192 | bytes 8257536 | tf_op jit(solution)/shard_map/pallas_call | solution.py:49
  94.3 6.6 %shard_map.49 = f32[256,896]{1,0:T(8,128)S(1)} custom-call(s32[1]{0:T(128)} %bitcast.12.place_ref, bf16[4096,7168]{1,0:T(8,128)(2,1)} %quant_ref.7, f32[4096,128]{1,0:T(8,128)S(1)} %pad.4.scale_ref, bf16[256,4096]{1,0:T(8,128)(2,1)S(1)} %copy-done.2), custom_call_target="tpu_custom_call" | custom-call | flops 1879048192 | bytes 8257536 | tf_op jit(solution)/shard_map/pallas_call | solution.py:49
  100.9 2.2 %add.84 = f32[256,896]{1,0:T(8,128)} add(f32[256,896]{1,0:T(8,128)S(1)} %shard_map.49, f32[256,896]{1,0:T(8,128)} %collective-permute-done.22) | non-fusion elementwise | flops 229376 | bytes 2752512 | tf_op jit(solution)/shard_map/add | solution.py:247
  103.2 1.5 collective-permute-start.23
  105.9 1.4 collective-permute-start.1
  107.4 1.6 copy-done.3
  109.0 6.6 %shard_map.47.first_ref = f32[256,896]{1,0:T(8,128)S(1)} custom-call(s32[1]{0:T(128)} %bitcast.10.place_ref, bf16[4096,7168]{1,0:T(8,128)(2,1)} %quant_ref.7, f32[4096,128]{1,0:T(8,128)S(1)} %pad.4.scale_ref, bf16[256,4096]{1,0:T(8,128)(2,1)S(1)} %copy-done.3), custom_call_target="tpu_custom_call" | custom-call | flops 1879048192 | bytes 8257536 | tf_op jit(solution)/shard_map/pallas_call | solution.py:49
  115.6 16.0 %collective-permute-done.20 = f32[256,256]{1,0:T(8,128)} collective-permute-done((f32[256,256]{1,0:T(8,128)}, f32[256,256]{1,0:T(8,128)}, u32[]{:S(2)}, u32[]{:S(2)}) %collective-permute-start.20) | collective-permute-done | bytes 262176 | tf_op jit(solution)/shard_map/ppermute | solution.py:194
  132.6 7.8 %shard_map.46.inverse_ref = f32[256,256]{1,0:T(8,128)S(1)} custom-call(f32[256,256]{1,0:T(8,128)S(1)} %add.79.head_ref), custom_call_target="tpu_custom_call" | custom-call | flops 5637144576 | bytes 524288 | tf_op jit(solution)/shard_map/pallas_call | solution.py:104
  140.5 3.5 %shard_map.51 = (bf16[256,896]{1,0:T(8,128)(2,1)}, bf16[256,896]{1,0:T(8,128)(2,1)S(1)}) custom-call(f32[256,256]{1,0:T(8,128)S(1)} %shard_map.46.inverse_ref, f32[256,896]{1,0:T(8,128)S(1)} %shard_map.47.first_ref, f32[256,896]{1,0:T(8,128)} %collective-permute-done.21.second_ref, f32[256,896]{1,0:T(8,128)} %collective-permute-done.23.third_ref), custom_call_target="tpu_custom_call" | custom-call | flops 704643072 | bytes 3670016 | tf_op jit(solution)/shard_map/pallas_call | solution.py:126
  144.0 1.5 collective-permute-start.24
  145.6 1.5 collective-permute-start.26
  147.3 1.5 collective-permute-start.2
  148.7 7.3 %collective-permute-done.24.refs_0_ = bf16[256,896]{1,0:T(8,128)(2,1)S(1)} collective-permute-done((bf16[256,896]{1,0:T(8,128)(2,1)}, bf16[256,896]{1,0:T(8,128)(2,1)S(1)}, u32[]{:S(2)}, u32[]{:S(2)}) %collective-permute-start.24) | collective-permute-done | bytes 458784 | tf_op jit(solution)/shard_map/ppermute | solution.py:194
  156.7 1.5 collective-permute-start.25
  158.4 1.6 collective-permute-start.27
  160.6 2.5 %collective-permute-done.25 = bf16[128,896]{1,0:T(8,128)(2,1)} collective-permute-done((bf16[128,896]{1,0:T(8,128)(2,1)}, bf16[128,896]{1,0:T(8,128)(2,1)}, u32[]{:S(2)}, u32[]{:S(2)}) %collective-permute-start.25) | collective-permute-done | bytes 229408 | tf_op jit(solution)/shard_map/ppermute | solution.py:194
  166.3 5.2 %copy-done = bf16[1024,7168]{1,0:T(8,128)(2,1)S(1)} copy-done((bf16[1024,7168]{1,0:T(8,128)(2,1)S(1)}, bf16[1024,7168]{1,0:T(8,128)(2,1)}, u32[]{:S(2)}) %copy-start) | copy-done | bytes 14680088
  171.4 4.9 %shard_map.52.refs_2_ = bf16[1024,7168]{1,0:T(8,128)(2,1)} custom-call(s32[2]{0:T(128)S(1)} %pad_add_fusion.7.place_ref, bf16[1024,7168]{1,0:T(8,128)(2,1)S(1)} %copy-done, bf16[1024,256]{1,0:T(8,128)(2,1)S(1)} %select_select_fusion.error_ref, bf16[256,896]{1,0:T(8,128)(2,1)} %get-tuple-element.7.refs_0_, bf16[256,896]{1,0:T(8,128)(2,1)S(1)} %get-tuple-element.8.refs_1_), custom_call_target="tpu_custom_call" | custom-call | flops 939524096 | bytes 3670016 | tf_op jit(solution)/shard_map/pallas_call | solution.py:173
  178.2 4.6 %shard_map.53.refs_1_ = bf16[1024,7168]{1,0:T(8,128)(2,1)} custom-call(s32[2]{0:T(128)S(1)} %pad_add_fusion.6.place_ref, bf16[1024,7168]{1,0:T(8,128)(2,1)S(1)} %bitcast.33, bf16[1024,256]{1,0:T(8,128)(2,1)S(1)} %select_select_fusion.error_ref, bf16[256,896]{1,0:T(8,128)(2,1)S(1)} %copy-done.5, ...), custom_call_target="tpu_custom_call", output_to_operand_aliasing={{}: (5, {})} | custom-call | flops 939524096 | bytes 3670016 | tf_op jit(solution)/shard_map/pallas_call | solution.py:173
  182.7 3.2 %shard_map.54.refs_1_ = bf16[1024,7168]{1,0:T(8,128)(2,1)} custom-call(s32[2]{0:T(128)S(1)} %pad_add_fusion.5.place_ref, bf16[1024,7168]{1,0:T(8,128)(2,1)S(1)} %bitcast.33, bf16[1024,256]{1,0:T(8,128)(2,1)S(1)} %select_select_fusion.error_ref, bf16[256,896]{1,0:T(8,128)(2,1)S(1)} %collective-permute-done.26.refs_0_, ...), custom_call_target="tpu_custom_call", output_to_operand_aliasing={{}: (4, {})} | custom-call | flops 469762048 | bytes 3670016 | tf_op jit(solution)/shard_map/pallas_call | solution.py:173
  185.9 3.2 %shard_map.55.refs_1_ = bf16[1024,7168]{1,0:T(8,128)(2,1)} custom-call(s32[2]{0:T(128)S(1)} %pad_add_fusion.4.place_ref, bf16[1024,7168]{1,0:T(8,128)(2,1)S(1)} %bitcast.33, bf16[1024,256]{1,0:T(8,128)(2,1)S(1)} %select_select_fusion.error_ref, bf16[256,896]{1,0:T(8,128)(2,1)S(1)} %collective-permute-done.24.refs_0_, ...), custom_call_target="tpu_custom_call", output_to_operand_aliasing={{}: (4, {})} | custom-call | flops 469762048 | bytes 3670016 | tf_op jit(solution)/shard_map/pallas_call | solution.py:173
  189.1 3.2 %shard_map.56.refs_1_ = bf16[1024,7168]{1,0:T(8,128)(2,1)} custom-call(s32[2]{0:T(128)S(1)} %pad_add_fusion.3.place_ref, bf16[1024,7168]{1,0:T(8,128)(2,1)S(1)} %bitcast.33, bf16[1024,256]{1,0:T(8,128)(2,1)S(1)} %select_select_fusion.error_ref, bf16[256,896]{1,0:T(8,128)(2,1)S(1)} %collective-permute-done.30.refs_0_, ...), custom_call_target="tpu_custom_call", output_to_operand_aliasing={{}: (4, {})} | custom-call | flops 469762048 | bytes 3670016 | tf_op jit(solution)/shard_map/pallas_call | solution.py:173
  192.3 4.2 %shard_map.57.refs_1_ = bf16[1024,7168]{1,0:T(8,128)(2,1)} custom-call(s32[2]{0:T(128)S(1)} %pad_add_fusion.2.place_ref, bf16[1024,7168]{1,0:T(8,128)(2,1)S(1)} %bitcast.33, bf16[1024,256]{1,0:T(8,128)(2,1)S(1)} %select_select_fusion.error_ref, bf16[256,896]{1,0:T(8,128)(2,1)} %collective-permute-done.29.refs_0_, ...), custom_call_target="tpu_custom_call", output_to_operand_aliasing={{}: (4, {})} | custom-call | flops 469762048 | bytes 3670016 | tf_op jit(solution)/shard_map/pallas_call | solution.py:173
  196.5 3.2 %shard_map.58.refs_1_ = bf16[1024,7168]{1,0:T(8,128)(2,1)} custom-call(s32[2]{0:T(128)S(1)} %get-tuple-element.20.place_ref, bf16[1024,7168]{1,0:T(8,128)(2,1)S(1)} %bitcast.33, bf16[1024,256]{1,0:T(8,128)(2,1)S(1)} %select_select_fusion.error_ref, bf16[256,896]{1,0:T(8,128)(2,1)S(1)} %constant_dynamic-update-slice_fusion.4.refs_0_, ...), custom_call_target="tpu_custom_call", output_to_operand_aliasing={{}: (4, {})} | custom-call | flops 469762048 | bytes 3670016 | tf_op jit(solution)/shard_map/pallas_call | solution.py:173
  199.6 4.2 %shard_map.59 = bf16[1024,7168]{1,0:T(8,128)(2,1)} custom-call(s32[2]{0:T(128)S(1)} %get-tuple-element.19.place_ref, bf16[1024,7168]{1,0:T(8,128)(2,1)S(1)} %bitcast.33, bf16[1024,256]{1,0:T(8,128)(2,1)S(1)} %select_select_fusion.error_ref, bf16[256,896]{1,0:T(8,128)(2,1)} %collective-permute-done.28.refs_0_, ...), custom_call_target="tpu_custom_call", output_to_operand_aliasing={{}: (4, {})} | custom-call | flops 469762048 | bytes 3670016 | tf_op jit(solution)/shard_map/pallas_call | solution.py:173
  (115 shorter events, 24.1 us)
Async XLA Ops:
  5.0 2.5 %copy-start.6 = (f32[4096,56]{1,0:T(8,128)}, f32[4096,56]{1,0:T(8,128)S(1)}, u32[]{:S(2)}) copy-start(f32[4096,56]{1,0:T(8,128)S(1)} %multiply_exponential_fusion) | copy-start | bytes 2752516
  7.5 12.3 %collective-permute-start.9 = (bf16[256,512]{1,0:T(8,128)(2,1)S(1)}, bf16[256,512]{1,0:T(8,128)(2,1)S(1)}, u32[]{:S(2)}, u32[]{:S(2)}) collective-permute-start(bf16[256,512]{1,0:T(8,128)(2,1)S(1)} %bitcast.36), channel_id=1, source_target_pairs={{0,2},{1,3},{8,10},{9,11},{16,18},{17,19},{24,26},{25,27}} | collective-permute-start | bytes 786440 | tf_op jit(solution)/shard_map/ppermute | solution.py:202
  13.6 11.1 %collective-permute-start.3 = (bf16[256,512]{1,0:T(8,128)(2,1)S(1)}, bf16[256,512]{1,0:T(8,128)(2,1)S(1)}, u32[]{:S(2)}, u32[]{:S(2)}) collective-permute-start(bf16[256,512]{1,0:T(8,128)(2,1)S(1)} %bitcast.35), channel_id=1, source_target_pairs={{0,2},{1,3},{8,10},{9,11},{16,18},{17,19},{24,26},{25,27}} | collective-permute-start | bytes 786440 | tf_op jit(solution)/shard_map/ppermute | solution.py:202
  16.1 14.2 %collective-permute-start.12 = (bf16[256,512]{1,0:T(8,128)(2,1)S(1)}, bf16[256,512]{1,0:T(8,128)(2,1)S(1)}, u32[]{:S(2)}, u32[]{:S(2)}) collective-permute-start(bf16[256,512]{1,0:T(8,128)(2,1)S(1)} %bitcast.34), channel_id=1, source_target_pairs={{0,2},{1,3},{8,10},{9,11},{16,18},{17,19},{24,26},{25,27}} | collective-permute-start | bytes 786440 | tf_op jit(solution)/shard_map/ppermute | solution.py:202
  17.7 17.1 %collective-permute-start.6 = (bf16[256,512]{1,0:T(8,128)(2,1)S(1)}, bf16[256,512]{1,0:T(8,128)(2,1)}, u32[]{:S(2)}, u32[]{:S(2)}) collective-permute-start(bf16[256,512]{1,0:T(8,128)(2,1)S(1)} %bitcast.37), channel_id=1, source_target_pairs={{0,2},{1,3},{8,10},{9,11},{16,18},{17,19},{24,26},{25,27}} | collective-permute-start | bytes 786440 | tf_op jit(solution)/shard_map/ppermute | solution.py:202
  19.7 19.2 %copy-start.14 = (bf16[256,512]{1,0:T(8,128)(2,1)}, bf16[256,512]{1,0:T(8,128)(2,1)S(1)}, u32[]{:S(2)}) copy-start(bf16[256,512]{1,0:T(8,128)(2,1)S(1)} %collective-permute-done.9) | copy-start | bytes 786436
  19.7 16.4 %collective-permute-start.10 = (bf16[256,512]{1,0:T(8,128)(2,1)S(1)}, bf16[256,512]{1,0:T(8,128)(2,1)}, u32[]{:S(2)}, u32[]{:S(2)}) collective-permute-start(bf16[256,512]{1,0:T(8,128)(2,1)S(1)} %collective-permute-done.9), channel_id=1, source_target_pairs={{2,4},{3,5},{10,12},{11,13},{18,20},{19,21},{26,28},{27,29}} | collective-permute-start | bytes 786440 | tf_op jit(solution)/shard_map/ppermute | solution.py:202
  24.7 14.2 %copy-start.13 = (bf16[256,512]{1,0:T(8,128)(2,1)}, bf16[256,512]{1,0:T(8,128)(2,1)S(1)}, u32[]{:S(2)}) copy-start(bf16[256,512]{1,0:T(8,128)(2,1)S(1)} %collective-permute-done.3) | copy-start | bytes 786436
  24.7 12.8 %collective-permute-start.4 = (bf16[256,512]{1,0:T(8,128)(2,1)S(1)}, bf16[256,512]{1,0:T(8,128)(2,1)}, u32[]{:S(2)}, u32[]{:S(2)}) collective-permute-start(bf16[256,512]{1,0:T(8,128)(2,1)S(1)} %collective-permute-done.3), channel_id=1, source_target_pairs={{2,4},{3,5},{10,12},{11,13},{18,20},{19,21},{26,28},{27,29}} | collective-permute-start | bytes 786440 | tf_op jit(solution)/shard_map/ppermute | solution.py:202
  30.3 10.3 %collective-permute-start.13 = (bf16[256,512]{1,0:T(8,128)(2,1)S(1)}, bf16[256,512]{1,0:T(8,128)(2,1)}, u32[]{:S(2)}, u32[]{:S(2)}) collective-permute-start(bf16[256,512]{1,0:T(8,128)(2,1)S(1)} %collective-permute-done.12), channel_id=1, source_target_pairs={{2,4},{3,5},{10,12},{11,13},{18,20},{19,21},{26,28},{27,29}} | collective-permute-start | bytes 786440 | tf_op jit(solution)/shard_map/ppermute | solution.py:202
  34.8 6.6 %collective-permute-start.7 = (bf16[256,512]{1,0:T(8,128)(2,1)}, bf16[256,512]{1,0:T(8,128)(2,1)}, u32[]{:S(2)}, u32[]{:S(2)}) collective-permute-start(bf16[256,512]{1,0:T(8,128)(2,1)} %collective-permute-done.6), channel_id=1, source_target_pairs={{2,4},{3,5},{10,12},{11,13},{18,20},{19,21},{26,28},{27,29}} | collective-permute-start | bytes 786440 | tf_op jit(solution)/shard_map/ppermute | solution.py:202
  36.2 5.9 %collective-permute-start.11 = (bf16[256,512]{1,0:T(8,128)(2,1)}, bf16[256,512]{1,0:T(8,128)(2,1)}, u32[]{:S(2)}, u32[]{:S(2)}) collective-permute-start(bf16[256,512]{1,0:T(8,128)(2,1)} %collective-permute-done.10), channel_id=1, source_target_pairs={{4,6},{5,7},{12,14},{13,15},{20,22},{21,23},{28,30},{29,31}} | collective-permute-start | bytes 786440 | tf_op jit(solution)/shard_map/ppermute | solution.py:202
  37.6 6.2 %collective-permute-start.5 = (bf16[256,512]{1,0:T(8,128)(2,1)}, bf16[256,512]{1,0:T(8,128)(2,1)}, u32[]{:S(2)}, u32[]{:S(2)}) collective-permute-start(bf16[256,512]{1,0:T(8,128)(2,1)} %collective-permute-done.4), channel_id=1, source_target_pairs={{4,6},{5,7},{12,14},{13,15},{20,22},{21,23},{28,30},{29,31}} | collective-permute-start | bytes 786440 | tf_op jit(solution)/shard_map/ppermute | solution.py:202
  40.7 5.4 %collective-permute-start.14 = (bf16[256,512]{1,0:T(8,128)(2,1)}, bf16[256,512]{1,0:T(8,128)(2,1)S(1)}, u32[]{:S(2)}, u32[]{:S(2)}) collective-permute-start(bf16[256,512]{1,0:T(8,128)(2,1)} %collective-permute-done.13), channel_id=1, source_target_pairs={{4,6},{5,7},{12,14},{13,15},{20,22},{21,23},{28,30},{29,31}} | collective-permute-start | bytes 786440 | tf_op jit(solution)/shard_map/ppermute | solution.py:202
  41.4 3.0 %collective-permute-start.8 = (bf16[256,512]{1,0:T(8,128)(2,1)}, bf16[256,512]{1,0:T(8,128)(2,1)S(1)}, u32[]{:S(2)}, u32[]{:S(2)}) collective-permute-start(bf16[256,512]{1,0:T(8,128)(2,1)} %collective-permute-done.7), channel_id=1, source_target_pairs={{4,6},{5,7},{12,14},{13,15},{20,22},{21,23},{28,30},{29,31}} | collective-permute-start | bytes 786440 | tf_op jit(solution)/shard_map/ppermute | solution.py:202
  42.2 20.6 %collective-permute-start.17 = (bf16[256,512]{1,0:T(8,128)(2,1)S(1)}, bf16[256,512]{1,0:T(8,128)(2,1)S(1)}, u32[]{:S(2)}, u32[]{:S(2)}) collective-permute-start(bf16[256,512]{1,0:T(8,128)(2,1)S(1)} %select_select_fusion.2), channel_id=1, source_target_pairs={{0,1},{1,0},{2,3},{3,2},{4,5},{5,4},{6,7},{7,6},{8,9},{9,8},{10,11... | collective-permute-start | bytes 786440 | tf_op jit(solution)/shard_map/ppermute | solution.py:194
  43.8 13.3 %collective-permute-start.15 = (bf16[256,512]{1,0:T(8,128)(2,1)S(1)}, bf16[256,512]{1,0:T(8,128)(2,1)S(1)}, u32[]{:S(2)}, u32[]{:S(2)}) collective-permute-start(bf16[256,512]{1,0:T(8,128)(2,1)S(1)} %select_select_fusion.4), channel_id=1, source_target_pairs={{0,1},{1,0},{2,3},{3,2},{4,5},{5,4},{6,7},{7,6},{8,9},{9,8},{10,11... | collective-permute-start | bytes 786440 | tf_op jit(solution)/shard_map/ppermute | solution.py:194
  44.5 18.2 %collective-permute-start.16 = (bf16[256,512]{1,0:T(8,128)(2,1)S(1)}, bf16[256,512]{1,0:T(8,128)(2,1)S(1)}, u32[]{:S(2)}, u32[]{:S(2)}) collective-permute-start(bf16[256,512]{1,0:T(8,128)(2,1)S(1)} %select_select_fusion.3), channel_id=1, source_target_pairs={{0,1},{1,0},{2,3},{3,2},{4,5},{5,4},{6,7},{7,6},{8,9},{9,8},{10,11... | collective-permute-start | bytes 786440 | tf_op jit(solution)/shard_map/ppermute | solution.py:194
  46.1 20.1 %collective-permute-start.18 = (bf16[256,512]{1,0:T(8,128)(2,1)S(1)}, bf16[256,512]{1,0:T(8,128)(2,1)S(1)}, u32[]{:S(2)}, u32[]{:S(2)}) collective-permute-start(bf16[256,512]{1,0:T(8,128)(2,1)S(1)} %select_select_fusion.1), channel_id=1, source_target_pairs={{0,1},{1,0},{2,3},{3,2},{4,5},{5,4},{6,7},{7,6},{8,9},{9,8},{10,11... | collective-permute-start | bytes 786440 | tf_op jit(solution)/shard_map/ppermute | solution.py:194
  68.1 8.4 %copy-start.1 = (bf16[256,4096]{1,0:T(8,128)(2,1)}, bf16[256,4096]{1,0:T(8,128)(2,1)S(1)}, u32[]{:S(2)}) copy-start(bf16[256,4096]{1,0:T(8,128)(2,1)S(1)} %pad_maximum_fusion.panel_ref) | copy-start | bytes 6291460
  68.1 8.4 %copy-start.12 = (s32[1024,256]{1,0:T(8,128)S(1)}, s32[1024,256]{1,0:T(8,128)}, u32[]{:S(2)}) copy-start(s32[1024,256]{1,0:T(8,128)} %param.7) | copy-start | bytes 3145732
  76.5 24.5 %collective-permute-start.22 = (f32[256,896]{1,0:T(8,128)}, f32[256,896]{1,0:T(8,128)}, u32[]{:S(2)}, u32[]{:S(2)}) collective-permute-start(f32[256,896]{1,0:T(8,128)} %shard_map.50), channel_id=1, source_target_pairs={{0,8},{8,0},{16,24},{24,16},{1,9},{9,1},{17,25},{25,17},{2,10},{10... | collective-permute-start | bytes 2752520 | tf_op jit(solution)/shard_map/ppermute | solution.py:194
  77.7 15.3 %copy-start.11 = (bf16[1024,256]{1,0:T(8,128)(2,1)}, bf16[1024,256]{1,0:T(8,128)(2,1)S(1)}, u32[]{:S(2)}) copy-start(bf16[1024,256]{1,0:T(8,128)(2,1)S(1)} %compare_select_fusion) | copy-start | bytes 1572868
  77.7 28.3 %collective-permute-start = (bf16[1024,256]{1,0:T(8,128)(2,1)S(1)}, bf16[1024,256]{1,0:T(8,128)(2,1)}, u32[]{:S(2)}, u32[]{:S(2)}) collective-permute-start(bf16[1024,256]{1,0:T(8,128)(2,1)S(1)} %compare_select_fusion), channel_id=1, source_target_pairs={{0,2},{1,3},{8,10},{9,11},{16,18},{17,19},{24,26},{25,27}} | collective-permute-start | bytes 1572872 | tf_op jit(solution)/shard_map/ppermute | solution.py:202
  84.5 1.6 copy-start.2
  86.1 7.1 %copy-start.8 = (bf16[256,2048]{1,0:T(8,128)(2,1)S(1)}, bf16[256,2048]{1,0:T(8,128)(2,1)}, u32[]{:S(2)}) copy-start(bf16[256,2048]{1,0:T(8,128)(2,1)} %copy-done.7) | copy-start | bytes 3145732
  86.1 7.1 %copy-start.10 = (bf16[256,2048]{1,0:T(8,128)(2,1)S(1)}, bf16[256,2048]{1,0:T(8,128)(2,1)}, u32[]{:S(2)}) copy-start(bf16[256,2048]{1,0:T(8,128)(2,1)} %copy-done.9) | copy-start | bytes 3145732
  92.9 47.6 %collective-permute-start.21 = (f32[256,896]{1,0:T(8,128)S(1)}, f32[256,896]{1,0:T(8,128)}, u32[]{:S(2)}, u32[]{:S(2)}) collective-permute-start(f32[256,896]{1,0:T(8,128)S(1)} %shard_map.48), channel_id=1, source_target_pairs={{0,8},{8,0},{16,24},{24,16},{1,9},{9,1},{17,25},{25,17},{2,10},{10... | collective-permute-start | bytes 2752520 | tf_op jit(solution)/shard_map/ppermute | solution.py:194
  94.0 10.7 %collective-permute-start.19 = (f32[256,256]{1,0:T(8,128)S(1)}, f32[256,256]{1,0:T(8,128)S(1)}, u32[]{:S(2)}, u32[]{:S(2)}) collective-permute-start(f32[256,256]{1,0:T(8,128)S(1)} %fusion), channel_id=1, source_target_pairs={{0,8},{8,0},{16,24},{24,16},{1,9},{9,1},{17,25},{25,17},{2,10},{10... | collective-permute-start | bytes 786440 | tf_op jit(solution)/shard_map/ppermute | solution.py:194
  103.2 37.3 %collective-permute-start.23 = (f32[256,896]{1,0:T(8,128)}, f32[256,896]{1,0:T(8,128)}, u32[]{:S(2)}, u32[]{:S(2)}) collective-permute-start(f32[256,896]{1,0:T(8,128)} %add.84), channel_id=1, source_target_pairs={{0,16},{8,24},{16,0},{24,8},{1,17},{9,25},{17,1},{25,9},{2,18},{10... | collective-permute-start | bytes 2752520 | tf_op jit(solution)/shard_map/ppermute | solution.py:194
  105.4 26.2 %collective-permute-start.20 = (f32[256,256]{1,0:T(8,128)}, f32[256,256]{1,0:T(8,128)}, u32[]{:S(2)}, u32[]{:S(2)}) collective-permute-start(f32[256,256]{1,0:T(8,128)} %add.78), channel_id=1, source_target_pairs={{0,16},{8,24},{16,0},{24,8},{1,17},{9,25},{17,1},{25,9},{2,18},{10... | collective-permute-start | bytes 786440 | tf_op jit(solution)/shard_map/ppermute | solution.py:194
  105.9 41.3 %collective-permute-start.1 = (bf16[1024,256]{1,0:T(8,128)(2,1)}, bf16[1024,256]{1,0:T(8,128)(2,1)}, u32[]{:S(2)}, u32[]{:S(2)}) collective-permute-start(bf16[1024,256]{1,0:T(8,128)(2,1)} %collective-permute-done), channel_id=1, source_target_pairs={{2,4},{3,5},{10,12},{11,13},{18,20},{19,21},{26,28},{27,29}} | collective-permute-start | bytes 1572872 | tf_op jit(solution)/shard_map/ppermute | solution.py:202
  107.4 1.6 copy-start.3
  140.5 36.6 %slice-start = ((s8[14680064]{0:T(1024)(128)(4,1)}), s8[2097152]{0:T(1024)(128)(4,1)S(1)}, s32[]{:S(2)}) async-start(s8[14680064]{0:T(1024)(128)(4,1)} %bitcast.32), calls=%async_computation | async-start | bytes 4194304
  144.0 12.0 %collective-permute-start.24 = (bf16[256,896]{1,0:T(8,128)(2,1)}, bf16[256,896]{1,0:T(8,128)(2,1)S(1)}, u32[]{:S(2)}, u32[]{:S(2)}) collective-permute-start(bf16[256,896]{1,0:T(8,128)(2,1)} %get-tuple-element.7.refs_0_), channel_id=1, source_target_pairs={{0,1},{1,0},{2,3},{3,2},{4,5},{5,4},{6,7},{7,6},{8,9},{9,8},{10,11... | collective-permute-start | bytes 1376264 | tf_op jit(solution)/shard_map/ppermute | solution.py:194
  145.6 12.8 %collective-permute-start.26 = (bf16[256,896]{1,0:T(8,128)(2,1)}, bf16[256,896]{1,0:T(8,128)(2,1)S(1)}, u32[]{:S(2)}, u32[]{:S(2)}) collective-permute-start(bf16[256,896]{1,0:T(8,128)(2,1)} %get-tuple-element.7.refs_0_), channel_id=1, source_target_pairs={{0,16},{8,24},{16,0},{24,8},{1,17},{9,25},{17,1},{25,9},{2,18},{10... | collective-permute-start | bytes 1376264 | tf_op jit(solution)/shard_map/ppermute | solution.py:194
  147.3 17.3 %collective-permute-start.2 = (bf16[1024,256]{1,0:T(8,128)(2,1)}, bf16[1024,256]{1,0:T(8,128)(2,1)}, u32[]{:S(2)}, u32[]{:S(2)}) collective-permute-start(bf16[1024,256]{1,0:T(8,128)(2,1)} %collective-permute-done.1), channel_id=1, source_target_pairs={{4,6},{5,7},{12,14},{13,15},{20,22},{21,23},{28,30},{29,31}} | collective-permute-start | bytes 1572872 | tf_op jit(solution)/shard_map/ppermute | solution.py:202
  156.7 6.3 %collective-permute-start.25 = (bf16[128,896]{1,0:T(8,128)(2,1)}, bf16[128,896]{1,0:T(8,128)(2,1)}, u32[]{:S(2)}, u32[]{:S(2)}) collective-permute-start(bf16[128,896]{1,0:T(8,128)(2,1)} %slice.12), channel_id=1, source_target_pairs={{0,16},{8,24},{16,0},{24,8},{1,17},{9,25},{17,1},{25,9},{2,18},{10... | collective-permute-start | bytes 688136 | tf_op jit(solution)/shard_map/ppermute | solution.py:194
  158.4 6.1 %collective-permute-start.27 = (bf16[128,896]{1,0:T(8,128)(2,1)S(1)}, bf16[128,896]{1,0:T(8,128)(2,1)S(1)}, u32[]{:S(2)}, u32[]{:S(2)}) collective-permute-start(bf16[128,896]{1,0:T(8,128)(2,1)S(1)} %slice.13), channel_id=1, source_target_pairs={{0,1},{1,0},{2,3},{3,2},{4,5},{5,4},{6,7},{7,6},{8,9},{9,8},{10,11... | collective-permute-start | bytes 688136 | tf_op jit(solution)/shard_map/ppermute | solution.py:194
  160.0 16.3 %collective-permute-start.31 = (bf16[256,896]{1,0:T(8,128)(2,1)}, bf16[256,896]{1,0:T(8,128)(2,1)S(1)}, u32[]{:S(2)}, u32[]{:S(2)}) collective-permute-start(bf16[256,896]{1,0:T(8,128)(2,1)} %get-tuple-element.7.refs_0_), channel_id=1, source_target_pairs={{0,8},{8,0},{16,24},{24,16},{1,9},{9,1},{17,25},{25,17},{2,10},{10... | collective-permute-start | bytes 1376264 | tf_op jit(solution)/shard_map/ppermute | solution.py:194
  160.0 17.1 %collective-permute-start.32 = (bf16[256,896]{1,0:T(8,128)(2,1)S(1)}, bf16[256,896]{1,0:T(8,128)(2,1)}, u32[]{:S(2)}, u32[]{:S(2)}) collective-permute-start(bf16[256,896]{1,0:T(8,128)(2,1)S(1)} %get-tuple-element.8.refs_1_), channel_id=1, source_target_pairs={{0,8},{8,0},{16,24},{24,16},{1,9},{9,1},{17,25},{25,17},{2,10},{10... | collective-permute-start | bytes 1376264 | tf_op jit(solution)/shard_map/ppermute | solution.py:194
  163.1 26.1 %collective-permute-start.30 = (bf16[256,896]{1,0:T(8,128)(2,1)S(1)}, bf16[256,896]{1,0:T(8,128)(2,1)S(1)}, u32[]{:S(2)}, u32[]{:S(2)}) collective-permute-start(bf16[256,896]{1,0:T(8,128)(2,1)S(1)} %collective-permute-done.26.refs_0_), channel_id=1, source_target_pairs={{0,8},{8,0},{16,24},{24,16},{1,9},{9,1},{17,25},{25,17},{2,10},{10... | collective-permute-start | bytes 1376264 | tf_op jit(solution)/shard_map/ppermute | solution.py:194
  164.5 27.8 %collective-permute-start.29 = (bf16[256,896]{1,0:T(8,128)(2,1)S(1)}, bf16[256,896]{1,0:T(8,128)(2,1)}, u32[]{:S(2)}, u32[]{:S(2)}) collective-permute-start(bf16[256,896]{1,0:T(8,128)(2,1)S(1)} %collective-permute-done.24.refs_0_), channel_id=1, source_target_pairs={{0,8},{8,0},{16,24},{24,16},{1,9},{9,1},{17,25},{25,17},{2,10},{10... | collective-permute-start | bytes 1376264 | tf_op jit(solution)/shard_map/ppermute | solution.py:194
  164.6 35.0 %collective-permute-start.28 = (bf16[256,896]{1,0:T(8,128)(2,1)S(1)}, bf16[256,896]{1,0:T(8,128)(2,1)}, u32[]{:S(2)}, u32[]{:S(2)}) collective-permute-start(bf16[256,896]{1,0:T(8,128)(2,1)S(1)} %constant_dynamic-update-slice_fusion.4.refs_0_), channel_id=1, source_target_pairs={{0,8},{8,0},{16,24},{24,16},{1,9},{9,1},{17,25},{25,17},{2,10},{10... | collective-permute-start | bytes 1376264 | tf_op jit(solution)/shard_map/ppermute | solution.py:194
  166.2 5.2 %copy-start = (bf16[1024,7168]{1,0:T(8,128)(2,1)S(1)}, bf16[1024,7168]{1,0:T(8,128)(2,1)}, u32[]{:S(2)}) copy-start(bf16[1024,7168]{1,0:T(8,128)(2,1)} %weights_ref.15) | copy-start | bytes 44040196
  171.4 5.7 %slice-start.1 = ((s8[14680064]{0:T(1024)(128)(4,1)}), s8[4194304]{0:T(1024)(128)(4,1)S(1)}, s32[]{:S(2)}) async-start(s8[14680064]{0:T(1024)(128)(4,1)} %bitcast.32), calls=%async_computation.1 | async-start | bytes 8388608
  171.4 5.7 %slice-start.2 = ((s8[14680064]{0:T(1024)(128)(4,1)}), s8[4194304]{0:T(1024)(128)(4,1)S(1)}, s32[]{:S(2)}) async-start(s8[14680064]{0:T(1024)(128)(4,1)} %bitcast.32), calls=%async_computation.2 | async-start | bytes 8388608
  171.4 5.7 %slice-start.3 = ((s8[14680064]{0:T(1024)(128)(4,1)}), s8[4194304]{0:T(1024)(128)(4,1)S(1)}, s32[]{:S(2)}) async-start(s8[14680064]{0:T(1024)(128)(4,1)} %bitcast.32), calls=%async_computation.3 | async-start | bytes 8388608
  (4 other events, 4.1 us)

commit v2 on v1

v2 whole, which is shorter than its diff:
```python
import functools

import jax
import jax.numpy as jnp
from jax import lax
from jax.experimental import pallas as pl
from jax.experimental.pallas import tpu as pltpu
from jax.sharding import PartitionSpec as P

PANEL = 256
QBLOCK = 128
ROUNDS = 4
F32 = jnp.float32
BF16 = jnp.bfloat16
MIB = 1 << 20


def dot_high(left, right):
    return jnp.dot(left, right, precision=lax.Precision.HIGHEST, preferred_element_type=F32)


def panel_kernel(place_ref, quant_ref, exps_ref, first_ref, second_ref):
    scale = jnp.exp2(exps_ref[:, : PANEL // QBLOCK].astype(F32))
    rows = scale.shape[0]
    wide = [
        jnp.broadcast_to(scale[:, c : c + 1], (rows, QBLOCK)) for c in range(PANEL // QBLOCK)
    ]
    acts = quant_ref[...].astype(F32) * jnp.concatenate(wide, axis=1)
    turned = acts.T.astype(BF16)
    half = rows // 2
    first_ref[...] = turned[:, :half]
    second_ref[...] = turned[:, half:]


def panel_piece(quantized, exponents, at, piece):
    blocks = exponents.shape[1]
    shape = jax.ShapeDtypeStruct((PANEL, piece // 2), BF16)
    return pl.pallas_call(
        panel_kernel,
        out_shape=(shape, shape),
        grid_spec=pltpu.PrefetchScalarGridSpec(
            num_scalar_prefetch=1,
            grid=(1,),
            in_specs=[
                pl.BlockSpec((piece, PANEL), lambda i, place: (place[0], 0)),
                pl.BlockSpec((piece, blocks), lambda i, place: (place[0], 0)),
            ],
            out_specs=[pl.BlockSpec((PANEL, piece // 2), lambda i, place: (0, 0))] * 2,
        ),
        compiler_params=pltpu.CompilerParams(vmem_limit_bytes=48 * MIB),
        cost_estimate=pl.CostEstimate(
            flops=piece * PANEL, bytes_accessed=4 * piece * PANEL, transcendentals=0
        ),
    )(at.reshape(1).astype(jnp.int32), quantized, exponents)


def head_kernel(place_ref, panel_ref, out_ref):
    @pl.when(pl.program_id(0) == 0)
    def _():
        out_ref[...] = jnp.zeros_like(out_ref)

    panel = panel_ref[...]
    out_ref[...] += lax.dot_general(
        panel, panel, (((1,), (1,)), ((), ())), preferred_element_type=F32
    )


def slot(step, start, slots):
    return jnp.where(step < ROUNDS, start + step, slots // 2 + start + step - ROUNDS)


def head_block(stack, start):
    slots, _, piece = stack.shape
    return pl.pallas_call(
        head_kernel,
        out_shape=jax.ShapeDtypeStruct((PANEL, PANEL), F32),
        grid_spec=pltpu.PrefetchScalarGridSpec(
            num_scalar_prefetch=1,
            grid=(2 * ROUNDS,),
            in_specs=[
                pl.BlockSpec(
                    (None, PANEL, piece), lambda k, place: (slot(k, place[0], slots), 0, 0)
                )
            ],
            out_specs=pl.BlockSpec((PANEL, PANEL), lambda k, place: (0, 0)),
        ),
        compiler_params=pltpu.CompilerParams(vmem_limit_bytes=32 * MIB),
        cost_estimate=pl.CostEstimate(
            flops=4 * ROUNDS * piece * PANEL * PANEL,
            bytes_accessed=4 * ROUNDS * piece * PANEL,
            transcendentals=0,
        ),
    )(start.reshape(1).astype(jnp.int32), stack)


def gram_kernel(blocks, place_ref, quant_ref, rows_ref, left_ref, right_ref, *refs):
    out_ref = refs[-1]

    @pl.when(pl.program_id(0) == 0)
    def _():
        out_ref[...] = refs[0][...] if len(refs) > 1 else jnp.zeros_like(out_ref)

    rows = rows_ref[...]
    turned = rows.T
    step = quant_ref.shape[0]
    panel = jnp.concatenate([left_ref[...], right_ref[...]], axis=1)
    for c in range(0, blocks, 2):
        left = panel * jnp.broadcast_to(rows[c : c + 1].astype(BF16), (PANEL, step))
        right = quant_ref[:, c * QBLOCK : (c + 1) * QBLOCK]
        if c + 1 < blocks:
            ratio = jnp.broadcast_to(turned[:, c + 1 : c + 2], (step, QBLOCK)).astype(BF16)
            second = quant_ref[:, (c + 1) * QBLOCK : (c + 2) * QBLOCK] * ratio
            right = jnp.concatenate([right, second], axis=1)
        span = slice(c * QBLOCK, c * QBLOCK + right.shape[1])
        out_ref[:, span] += jnp.dot(left, right, preferred_element_type=F32)


def gram_block(quantized, exponents, scale_rows, stack, row, start, col, width, extra=None):
    tokens, _ = quantized.shape
    slots, _, piece = stack.shape
    blocks = width // QBLOCK
    if scale_rows is None:
        half = slots // 2
        held = [lax.dynamic_slice_in_dim(stack, start + i * half, ROUNDS, 0) for i in range(2)]
        panel = jnp.concatenate(held, axis=0).transpose(1, 0, 2).reshape(PANEL, tokens)
        quant = lax.dynamic_slice_in_dim(quantized, col * width, width, 1)
        scale = jnp.exp2(exponents.astype(F32)).astype(BF16)
        acts = quant * jnp.take(scale, (col * width + jnp.arange(width)) // QBLOCK, axis=1)
        acts = jnp.roll(acts, -row * (tokens // 2), axis=0)
        total = jnp.dot(panel, acts, preferred_element_type=F32)
        return total if extra is None else total + extra
    step = 2 * piece
    steps = tokens // step
    place = jnp.stack([row, start, col]).astype(jnp.int32)

    def tokens_at(k, place):
        return lax.rem(k + place[0] * (steps // 2), steps)

    specs = [
        pl.BlockSpec((step, width), lambda k, place: (tokens_at(k, place), place[2])),
        pl.BlockSpec((8, step), lambda k, place: (place[2], tokens_at(k, place))),
        pl.BlockSpec((None, PANEL, piece), lambda k, place: (slot(2 * k, place[1], slots), 0, 0)),
        pl.BlockSpec(
            (None, PANEL, piece), lambda k, place: (slot(2 * k + 1, place[1], slots), 0, 0)
        ),
    ]
    args = [place, quantized, scale_rows, stack, stack]
    if extra is not None:
        specs.append(pl.BlockSpec((PANEL, width), lambda k, place: (0, 0)))
        args.append(extra)
    return pl.pallas_call(
        functools.partial(gram_kernel, blocks),
        out_shape=jax.ShapeDtypeStruct((PANEL, width), F32),
        grid_spec=pltpu.PrefetchScalarGridSpec(
            num_scalar_prefetch=1,
            grid=(steps,),
            in_specs=specs,
            out_specs=pl.BlockSpec((PANEL, width), lambda k, place: (0, 0)),
        ),
        compiler_params=pltpu.CompilerParams(vmem_limit_bytes=32 * MIB),
        cost_estimate=pl.CostEstimate(
            flops=2 * tokens * width * PANEL,
            bytes_accessed=2 * tokens * width + 4 * PANEL * width,
            transcendentals=0,
        ),
    )(*args)


def inverse_kernel(head_ref, out_ref, pair_ref):
    size = PANEL
    rows = lax.broadcasted_iota(jnp.int32, (size, size), 0)
    cols = lax.broadcasted_iota(jnp.int32, (size, size), 1)
    eye = jnp.where(rows == cols, 1.0, 0.0).astype(F32)
    head = head_ref[...]
    damping = 0.01 * (jnp.sum(head * eye) / size)
    block = head + damping * eye
    high = jnp.max(jnp.sum(jnp.abs(block), axis=0))
    start = 2.0 / (high + damping)
    spread = (high - damping) / (high + damping)
    pair_ref[:size] = start * eye
    pair_ref[size:] = start * block

    def more(spread):
        return spread > 1e-3

    def step(spread):
        square = spread * spread
        gain = 2.0 / (2.0 - square)
        turn = gain * (2.0 * eye - pair_ref[size:])
        pair_ref[...] = dot_high(pair_ref[...], turn)
        return square / (2.0 - square)

    lax.while_loop(more, step, spread)
    out = pair_ref[:size]
    for _ in range(2):
        out = out + dot_high(out, eye - dot_high(block, out))
    out_ref[...] = out


def invert(head):
    return pl.pallas_call(
        inverse_kernel,
        out_shape=jax.ShapeDtypeStruct((PANEL, PANEL), F32),
        scratch_shapes=[pltpu.VMEM((2 * PANEL, PANEL), F32)],
        compiler_params=pltpu.CompilerParams(vmem_limit_bytes=32 * MIB),
        cost_estimate=pl.CostEstimate(
            flops=28 * 12 * PANEL**3, bytes_accessed=8 * PANEL * PANEL, transcendentals=0
        ),
    )(head)


def gains_kernel(inverse_ref, first_ref, second_ref, third_ref, high_ref, pair_ref):
    total = first_ref[...] + second_ref[...] + third_ref[...]
    gains = dot_high(inverse_ref[...], total)
    high = gains.astype(BF16)
    high_ref[...] = high
    pair_ref[:PANEL] = high
    pair_ref[PANEL:] = (gains - high.astype(F32)).astype(BF16)


def make_gains(inverse, parts):
    width = parts[0].shape[1]
    return pl.pallas_call(
        gains_kernel,
        out_shape=(
            jax.ShapeDtypeStruct((PANEL, width), BF16),
            jax.ShapeDtypeStruct((2 * PANEL, width), BF16),
        ),
        compiler_params=pltpu.CompilerParams(vmem_limit_bytes=32 * MIB),
        cost_estimate=pl.CostEstimate(
            flops=12 * PANEL * PANEL * width, bytes_accessed=16 * PANEL * width, transcendentals=0
        ),
    )(inverse, *parts)


def update_kernel(count, place_ref, weights_ref, error_ref, *refs):
    gains, out_ref = refs[:count], refs[-1]
    for j in range(count):

        @pl.when(pl.program_id(0) == j)
        def _():
            total = weights_ref[...].astype(F32)
            for at in range(0, gains[j].shape[0], PANEL):
                total += jnp.dot(
                    error_ref[...], gains[j][at : at + PANEL], preferred_element_type=F32
                )
            out_ref[...] = total.astype(BF16)

    @pl.when(place_ref[count + pl.program_id(0)] == 1)
    def _():
        out_ref[:, :PANEL] = weights_ref[:, :PANEL] - error_ref[...]


def update_blocks(out, weights, error, gains, spots, first):
    rows, cols = weights.shape
    width = gains[0].shape[1]
    count = len(gains)
    if width % QBLOCK or width < PANEL:
        out = jnp.zeros_like(weights) if out is None else out
        for gain, col in zip(gains, spots):
            total = lax.dynamic_slice_in_dim(weights, col * width, width, 1).astype(F32)
            for at in range(0, gain.shape[0], PANEL):
                total += jnp.dot(error, gain[at : at + PANEL], preferred_element_type=F32)
            out = lax.dynamic_update_slice_in_dim(out, total.astype(BF16), col * width, 1)
        return out
    step = min(rows, 512)
    place = jnp.stack(list(spots) + [first & (col == 0) for col in spots]).astype(jnp.int32)
    specs = [
        pl.BlockSpec((step, width), lambda j, i, place: (i, place[j])),
        pl.BlockSpec((step, PANEL), lambda j, i, place: (i, 0)),
    ] + [pl.BlockSpec(gain.shape, lambda j, i, place: (0, 0)) for gain in gains]
    args = [place, weights, error, *gains]
    aliases = {}
    if out is not None:
        specs.append(pl.BlockSpec(memory_space=pl.ANY))
        aliases = {len(args): 0}
        args.append(out)
    return pl.pallas_call(
        functools.partial(update_kernel, count),
        out_shape=jax.ShapeDtypeStruct((rows, cols), BF16),
        grid_spec=pltpu.PrefetchScalarGridSpec(
            num_scalar_prefetch=1,
            grid=(count, rows // step),
            in_specs=specs,
            out_specs=pl.BlockSpec((step, width), lambda j, i, place: (i, place[j])),
        ),
        input_output_aliases=aliases,
        compiler_params=pltpu.CompilerParams(vmem_limit_bytes=56 * MIB),
        cost_estimate=pl.CostEstimate(
            flops=2 * rows * width * PANEL * count,
            bytes_accessed=4 * rows * width * count,
            transcendentals=0,
        ),
    )(*args)


def swap(x, axis, bit):
    size = lax.axis_size(axis)
    return lax.ppermute(x, axis, [(i, i ^ bit) for i in range(size)])


def forward(x, axis):
    size = lax.axis_size(axis)
    return lax.ppermute(x, axis, [(i, i + 1) for i in range(size - 1)])


def shards(quantized, exponents, weights, keep_mask):
    tokens, cols = quantized.shape
    toks, rows, feats = lax.axis_size("tok"), lax.axis_size("row"), lax.axis_size("feat")
    tok, row, feat = lax.axis_index("tok"), lax.axis_index("row"), lax.axis_index("feat")
    width = cols // (toks * rows)
    root = feat == 0

    piece = tokens // rows // ROUNDS
    sources = [
        panel_piece(quantized, exponents, row * ROUNDS + c, piece) for c in range(ROUNDS)
    ]
    none = jnp.zeros((PANEL, piece // 2), BF16)
    held = [jnp.where(root, x, none) for x in sources[0]]
    own, other = [], []
    for r in range(ROUNDS + feats - 1):
        both = jnp.concatenate(held, axis=1)
        own.append(both)
        other.append(swap(both, "row", 1))
        if r < ROUNDS + feats - 2:
            held = [forward(x, "feat") for x in held]
            if r + 1 < ROUNDS:
                held = [jnp.where(root, x, y) for x, y in zip(sources[r + 1], held)]
    stack = jnp.stack(own + other)

    scale_rows = None
    if width % QBLOCK == 0 and width // QBLOCK <= 8:
        blocks = width // QBLOCK
        exps = exponents.T.reshape(toks * rows, blocks, tokens)
        before = jnp.pad(exps[:, :-1], ((0, 0), (1, 0), (0, 0)))
        odd = (jnp.arange(blocks) % 2 == 1)[None, :, None]
        exps = jnp.where(odd, exps - before, exps)
        exps = jnp.pad(exps, ((0, 0), (0, 8 - blocks), (0, 0)))
        scale_rows = jnp.exp2(exps.astype(F32)).reshape(-1, tokens)

    error = jnp.where(keep_mask == 0, weights[:, :PANEL], jnp.zeros((), BF16))
    error, stack = lax.optimization_barrier((error, stack))
    errors = [error, forward(error, "feat")]

    def gram(k, extra=None):
        col = row * toks + (tok ^ k)
        return gram_block(
            quantized, exponents, scale_rows, stack, row, feat, col, width, extra
        )

    head = head_block(stack, feat)
    from_core = swap(head, "tok", 1)
    from3 = swap(gram(3), "tok", 1)
    head = head + from_core
    head = head + swap(head, "tok", 2)
    block2 = gram(2, from3)
    fromx = swap(block2, "tok", 2)
    from1 = swap(gram(1), "tok", 1)
    block0 = gram(0)
    inverse = invert(head)
    for _ in range(feats - 2):
        if len(errors) == 2:
            block0, last = lax.optimization_barrier((block0, errors[-1]))
        elif len(errors) == 3:
            inverse, last = lax.optimization_barrier((inverse, errors[-1]))
        else:
            last = errors[-1]
        errors[-1] = last
        errors.append(forward(last, "feat"))
    for hop in range(1, feats):
        error = jnp.where(feat == hop, errors[hop], error)
    high, pair = make_gains(inverse, (block0, from1, fromx))

    half = PANEL // 2
    in_x, in_y = swap(high, "tok", 2), swap(high, "row", 1)
    near = swap(pair, "tok", 1)
    far = jnp.concatenate([swap(in_y[:half], "tok", 2), swap(in_x[half:], "row", 1)], axis=0)
    near_x, near_y, near_far = swap(in_x, "tok", 1), swap(in_y, "tok", 1), swap(far, "tok", 1)

    out = None
    plan = [
        [(pair, 0, 0), (near, 1, 0)],
        [(in_x, 2, 0), (in_y, 0, 1), (near_x, 3, 0), (near_y, 1, 1)],
        [(far, 2, 1), (near_far, 3, 1)],
    ]
    for group in plan:
        spots = [(row ^ row_bit) * toks + (tok ^ tok_bits) for _, tok_bits, row_bit in group]
        out = update_blocks(out, weights, error, [gain for gain, _, _ in group], spots, root)
    if width % QBLOCK or width < PANEL:
        panel = jnp.where(root, weights[:, :PANEL] - error, out[:, :PANEL])
        out = lax.dynamic_update_slice_in_dim(out, panel, 0, 1)
    return out


def solution(mesh):
    placed = (
        P("tok", "feat"),
        P("tok", "feat"),
        P(("tok", "row"), "feat"),
        P(("tok", "row"), None),
    )
    return jax.shard_map(
        shards, mesh=mesh, in_specs=placed, out_specs=P(("tok", "row"), "feat"), check_vma=False
    )
```

time: 205 us -> 202 us (0.985)
  the two profiles are of different devices: /device:TPU:0 before, /device:TPU:9 now
where the time goes in v2:
time: 202 us; the launch traced here: 198 us
  Pallas kernels  69 us (34%)
  starting transfers between devices  58.7 us (29%)
  waiting for transfers between devices  46.4 us (23%)
  local copies, waits for them, and re-layouts  12.5 us (6%)
  other arithmetic  10.8 us (5%)
    ppermute x20, waiting for transfers between devices, swap(): return lax.ppermute(x, axis, [(i, i ^ bit) for i in range(size)])  34.9 us
    ppermute x15, starting transfers between devices, forward(): return lax.ppermute(x, axis, [(i, i + 1) for i in range(size - 1)])  33.8 us
    pallas_call x4, Pallas kernels, gram_block(): pl.pallas_call(functools.partial(gram_kernel, blocks), out_shape=jax.Shap...  27.4 us
    pallas_call x3, Pallas kernels, update_blocks(): pl.pallas_call(functools.partial(update_kernel, count), out_shape=jax.Sha...  25.4 us
    ppermute x20, starting transfers between devices, swap(): return lax.ppermute(x, axis, [(i, i ^ bit) for i in range(size)])  25 us
    ppermute x15, waiting for transfers between devices, forward(): return lax.ppermute(x, axis, [(i, i + 1) for i in range(size - 1)])  11.5 us
    unnamed x46, local copies, waits for them, and re-layouts  9.72 us
    pallas_call x1, Pallas kernels, invert(): pl.pallas_call(inverse_kernel, out_shape=jax.ShapeDtypeStruct((PANEL, PAN...  7.82 us
  transfers between devices with their start and end apart: 35, of which 14 were waited for; matrix products, arithmetic and copies ran while one was open for 8% of the time, Pallas kernels for 27%

profile of v2, /device:TPU:9, one launch (start us, length us, event | category | flops | bytes accessed | tf_op | source)
XLA Modules:
  0.0 198.1 jit_solution(3569732178058143933)
XLA Ops:
  0.0 1.8 copy.11.exps_ref
  1.8 1.2 shard_map.46
  3.7 3.2 %collective-permute-start = (bf16[256,256]{1,0:T(8,128)(2,1)}, bf16[256,256]{1,0:T(8,128)(2,1)}, u32[]{:S(2)}, u32[]{:S(2)}) collective-permute-start(bf16[256,256]{1,0:T(8,128)(2,1)} %broadcast_select_fusion.7), channel_id=1, source_target_pairs={{0,2},{2,4},{4,6},{1,3},{3,5},{5,7},{8,10},{10,12},{12,14},{9,11},... | collective-permute-start | bytes 393224 | tf_op jit(solution)/shard_map/ppermute | solution.py:304
  7.6 3.2 %collective-permute-start.1 = (bf16[256,256]{1,0:T(8,128)(2,1)}, bf16[256,256]{1,0:T(8,128)(2,1)}, u32[]{:S(2)}, u32[]{:S(2)}) collective-permute-start(bf16[256,256]{1,0:T(8,128)(2,1)} %broadcast_select_fusion.6), channel_id=1, source_target_pairs={{0,2},{2,4},{4,6},{1,3},{3,5},{5,7},{8,10},{10,12},{12,14},{9,11},... | collective-permute-start | bytes 393224 | tf_op jit(solution)/shard_map/ppermute | solution.py:304
  10.8 1.7 pad_maximum_fusion
  13.7 1.3 reshape.36
  16.3 2.0 compare_select_fusion
  18.3 1.2 shard_map.47
  21.5 1.3 shard_map.49
  24.7 1.9 collective-permute-start.2
  27.6 1.9 collective-permute-start.3
  30.4 1.9 collective-permute-start.4
  32.4 1.4 collective-permute-done.3
  33.8 1.9 collective-permute-start.5
  37.0 1.9 collective-permute-start.6
  38.9 2.0 %collective-permute-done.5 = bf16[256,256]{1,0:T(8,128)(2,1)S(1)} collective-permute-done((bf16[256,256]{1,0:T(8,128)(2,1)S(1)}, bf16[256,256]{1,0:T(8,128)(2,1)S(1)}, u32[]{:S(2)}, u32[]{:S(2)}) %collective-permute-start.5) | collective-permute-done | bytes 131104 | tf_op jit(solution)/shard_map/ppermute | solution.py:304
  41.0 2.2 %collective-permute-start.7 = (bf16[256,256]{1,0:T(8,128)(2,1)S(1)}, bf16[256,256]{1,0:T(8,128)(2,1)S(1)}, u32[]{:S(2)}, u32[]{:S(2)}) collective-permute-start(bf16[256,256]{1,0:T(8,128)(2,1)S(1)} %broadcast_select_fusion), channel_id=1, source_target_pairs={{0,2},{2,4},{4,6},{1,3},{3,5},{5,7},{8,10},{10,12},{12,14},{9,11},... | collective-permute-start | bytes 393224 | tf_op jit(solution)/shard_map/ppermute | solution.py:304
  44.4 1.9 collective-permute-start.8
  47.2 2.5 %collective-permute-start.9 = (bf16[256,256]{1,0:T(8,128)(2,1)S(1)}, bf16[256,256]{1,0:T(8,128)(2,1)S(1)}, u32[]{:S(2)}, u32[]{:S(2)}) collective-permute-start(bf16[256,256]{1,0:T(8,128)(2,1)S(1)} %collective-permute-done.7), channel_id=1, source_target_pairs={{0,2},{2,4},{4,6},{1,3},{3,5},{5,7},{8,10},{10,12},{12,14},{9,11},... | collective-permute-start | bytes 393224 | tf_op jit(solution)/shard_map/ppermute | solution.py:304
  50.9 2.2 %collective-permute-start.10 = (bf16[256,256]{1,0:T(8,128)(2,1)S(1)}, bf16[256,256]{1,0:T(8,128)(2,1)S(1)}, u32[]{:S(2)}, u32[]{:S(2)}) collective-permute-start(bf16[256,256]{1,0:T(8,128)(2,1)S(1)} %collective-permute-done.8), channel_id=1, source_target_pairs={{0,2},{2,4},{4,6},{1,3},{3,5},{5,7},{8,10},{10,12},{12,14},{9,11},... | collective-permute-start | bytes 393224 | tf_op jit(solution)/shard_map/ppermute | solution.py:304
  53.2 2.2 %collective-permute-start.11 = (bf16[256,256]{1,0:T(8,128)(2,1)S(1)}, bf16[256,256]{1,0:T(8,128)(2,1)S(1)}, u32[]{:S(2)}, u32[]{:S(2)}) collective-permute-start(bf16[256,256]{1,0:T(8,128)(2,1)S(1)} %collective-permute-done.9), channel_id=1, source_target_pairs={{0,2},{2,4},{4,6},{1,3},{3,5},{5,7},{8,10},{10,12},{12,14},{9,11},... | collective-permute-start | bytes 393224 | tf_op jit(solution)/shard_map/ppermute | solution.py:304
  57.6 2.2 %collective-permute-done.11 = bf16[256,256]{1,0:T(8,128)(2,1)S(1)} collective-permute-done((bf16[256,256]{1,0:T(8,128)(2,1)S(1)}, bf16[256,256]{1,0:T(8,128)(2,1)S(1)}, u32[]{:S(2)}, u32[]{:S(2)}) %collective-permute-start.11) | collective-permute-done | bytes 131104 | tf_op jit(solution)/shard_map/ppermute | solution.py:304
  59.9 1.4 collective-permute-start.17
  62.6 2.7 %collective-permute-done.16 = bf16[256,512]{1,0:T(8,128)(2,1)S(1)} collective-permute-done((bf16[256,512]{1,0:T(8,128)(2,1)S(1)}, bf16[256,512]{1,0:T(8,128)(2,1)S(1)}, u32[]{:S(2)}, u32[]{:S(2)}) %collective-permute-start.16) | collective-permute-done | bytes 262176 | tf_op jit(solution)/shard_map/ppermute | solution.py:299
  65.3 5.1 %collective-permute-done.17 = bf16[256,512]{1,0:T(8,128)(2,1)S(1)} collective-permute-done((bf16[256,512]{1,0:T(8,128)(2,1)S(1)}, bf16[256,512]{1,0:T(8,128)(2,1)S(1)}, u32[]{:S(2)}, u32[]{:S(2)}) %collective-permute-start.17) | collective-permute-done | bytes 262176 | tf_op jit(solution)/shard_map/ppermute | solution.py:299
  70.4 5.6 %collective-permute-done.18 = bf16[256,512]{1,0:T(8,128)(2,1)S(1)} collective-permute-done((bf16[256,512]{1,0:T(8,128)(2,1)S(1)}, bf16[256,512]{1,0:T(8,128)(2,1)S(1)}, u32[]{:S(2)}, u32[]{:S(2)}) %collective-permute-start.18) | collective-permute-done | bytes 262176 | tf_op jit(solution)/shard_map/ppermute | solution.py:299
  76.0 7.5 %shard_map.54 = f32[256,896]{1,0:T(8,128)S(1)} custom-call(s32[3]{0:T(128)S(1)} %get-tuple-element.37.place_ref, bf16[4096,7168]{1,0:T(8,128)(2,1)} %quant_ref.15, f32[64,4096]{1,0:T(8,128)S(1)} %exponential_bitcast_fusion.rows_ref, bf16[14,256,512]{2,1,0:T(8,128)(2,1)S(1)} %bitcast_dynamic-update-slice_fusion.panel_ref.left_ref.right_ref, ...), custom_call_target="tpu_custom_call" | custom-call | flops 1879048192 | bytes 8257536 | tf_op jit(solution)/shard_map/pallas_call | solution.py:151
  83.5 6.6 %collective-permute-start.25 = (f32[256,896]{1,0:T(8,128)S(1)}, f32[256,896]{1,0:T(8,128)S(1)}, u32[]{:S(2)}, u32[]{:S(2)}) collective-permute-start(f32[256,896]{1,0:T(8,128)S(1)} %shard_map.54), channel_id=1, source_target_pairs={{0,8},{8,0},{16,24},{24,16},{1,9},{9,1},{17,25},{25,17},{2,10},{10... | collective-permute-start | bytes 2752520 | tf_op jit(solution)/shard_map/ppermute | solution.py:299
  90.2 1.9 collective-permute-start.21
  92.1 2.0 %copy-done.1 = bf16[14,256,512]{2,1,0:T(8,128)(2,1)S(1)} copy-done((bf16[14,256,512]{2,1,0:T(8,128)(2,1)S(1)}, bf16[14,256,512]{2,1,0:T(8,128)(2,1)}, u32[]{:S(2)}) %copy-start.1) | copy-done | bytes 3670040
  94.2 2.2 %shard_map.50 = f32[256,256]{1,0:T(8,128)S(1)} custom-call(s32[1]{0:T(128)} %bitcast.4.place_ref, bf16[14,256,512]{2,1,0:T(8,128)(2,1)S(1)} %copy-done.1), custom_call_target="tpu_custom_call" | custom-call | flops 536870912 | bytes 2097152 | tf_op jit(solution)/shard_map/pallas_call | solution.py:74
  96.8 6.6 %shard_map.53 = f32[256,896]{1,0:T(8,128)S(1)} custom-call(s32[3]{0:T(128)S(1)} %get-tuple-element.40.place_ref, bf16[4096,7168]{1,0:T(8,128)(2,1)} %quant_ref.15, f32[64,4096]{1,0:T(8,128)S(1)} %exponential_bitcast_fusion.rows_ref, bf16[14,256,512]{2,1,0:T(8,128)(2,1)S(1)} %copy-done.2, bf16[14,256,512]{2,1,0:T(8,128)(2,1)S(1)} %copy-done.2), custom_call_target="tpu_custom_call" | custom-call | flops 1879048192 | bytes 8257536 | tf_op jit(solution)/shard_map/pallas_call | solution.py:151
  103.7 6.6 %shard_map.55 = f32[256,896]{1,0:T(8,128)S(1)} custom-call(s32[3]{0:T(128)S(1)} %get-tuple-element.39.place_ref, bf16[4096,7168]{1,0:T(8,128)(2,1)} %quant_ref.15, f32[64,4096]{1,0:T(8,128)S(1)} %exponential_bitcast_fusion.rows_ref, bf16[14,256,512]{2,1,0:T(8,128)(2,1)S(1)} %copy-done.2, bf16[14,256,512]{2,1,0:T(8,128)(2,1)S(1)} %copy-done.2, ...), custom_call_target="tpu_custom_call" | custom-call | flops 1879048192 | bytes 8257536 | tf_op jit(solution)/shard_map/pallas_call | solution.py:151
  110.3 1.2 collective-permute-start.26
  112.0 6.6 %shard_map.52.first_ref = f32[256,896]{1,0:T(8,128)S(1)} custom-call(s32[3]{0:T(128)S(1)} %get-tuple-element.41.place_ref, bf16[4096,7168]{1,0:T(8,128)(2,1)} %quant_ref.15, f32[64,4096]{1,0:T(8,128)S(1)} %exponential_bitcast_fusion.rows_ref, bf16[14,256,512]{2,1,0:T(8,128)(2,1)S(1)} %copy-done.2, bf16[14,256,512]{2,1,0:T(8,128)(2,1)S(1)} %copy-done.2), custom_call_target="tpu_custom_call" | custom-call | flops 1879048192 | bytes 8257536 | tf_op jit(solution)/shard_map/pallas_call | solution.py:151
  118.6 2.5 %collective-permute-start.22 = (bf16[1024,256]{1,0:T(8,128)(2,1)S(1)}, bf16[1024,256]{1,0:T(8,128)(2,1)}, u32[]{:S(2)}, u32[]{:S(2)}) collective-permute-start(bf16[1024,256]{1,0:T(8,128)(2,1)S(1)} %collective-permute-done.21), channel_id=1, source_target_pairs={{0,2},{2,4},{4,6},{1,3},{3,5},{5,7},{8,10},{10,12},{12,14},{9,11},... | collective-permute-start | bytes 1572872 | tf_op jit(solution)/shard_map/ppermute | solution.py:304
  121.1 16.5 %collective-permute-done.20 = f32[256,256]{1,0:T(8,128)S(1)} collective-permute-done((f32[256,256]{1,0:T(8,128)S(1)}, f32[256,256]{1,0:T(8,128)S(1)}, u32[]{:S(2)}, u32[]{:S(2)}) %collective-permute-start.20) | collective-permute-done | bytes 262176 | tf_op jit(solution)/shard_map/ppermute | solution.py:299
  137.7 7.8 %shard_map.51.inverse_ref = f32[256,256]{1,0:T(8,128)S(1)} custom-call(f32[256,256]{1,0:T(8,128)S(1)} %add.63.head_ref), custom_call_target="tpu_custom_call" | custom-call | flops 5637144576 | bytes 524288 | tf_op jit(solution)/shard_map/pallas_call | solution.py:201
  147.5 1.3 collective-permute-start.29
  148.8 1.7 collective-permute-start.34
  150.5 2.3 %collective-permute-start.23 = (bf16[1024,256]{1,0:T(8,128)(2,1)}, bf16[1024,256]{1,0:T(8,128)(2,1)}, u32[]{:S(2)}, u32[]{:S(2)}) collective-permute-start(bf16[1024,256]{1,0:T(8,128)(2,1)} %collective-permute-done.22), channel_id=1, source_target_pairs={{0,2},{2,4},{4,6},{1,3},{3,5},{5,7},{8,10},{10,12},{12,14},{9,11},... | collective-permute-start | bytes 1572872 | tf_op jit(solution)/shard_map/ppermute | solution.py:304
  152.8 5.0 %collective-permute-done.27.refs_1_ = bf16[256,896]{1,0:T(8,128)(2,1)S(1)} collective-permute-done((bf16[256,896]{1,0:T(8,128)(2,1)S(1)}, bf16[256,896]{1,0:T(8,128)(2,1)S(1)}, u32[]{:S(2)}, u32[]{:S(2)}) %collective-permute-start.27) | collective-permute-done | bytes 458784 | tf_op jit(solution)/shard_map/ppermute | solution.py:299
  162.6 2.5 %collective-permute-start.32 = (bf16[256,896]{1,0:T(8,128)(2,1)S(1)}, bf16[256,896]{1,0:T(8,128)(2,1)S(1)}, u32[]{:S(2)}, u32[]{:S(2)}) collective-permute-start(bf16[256,896]{1,0:T(8,128)(2,1)S(1)} %collective-permute-done.29.refs_0_), channel_id=1, source_target_pairs={{0,8},{8,0},{16,24},{24,16},{1,9},{9,1},{17,25},{25,17},{2,10},{10... | collective-permute-start | bytes 1376264 | tf_op jit(solution)/shard_map/ppermute | solution.py:299
  165.0 1.8 collective-permute-start.33
  167.9 1.5 collective-permute-start.31
  170.3 7.4 %shard_map.57.refs_4_ = bf16[1024,7168]{1,0:T(8,128)(2,1)} custom-call(s32[4]{0:T(128)} %pad_add_fusion.6.place_ref, bf16[1024,7168]{1,0:T(8,128)(2,1)} %weights_ref.5, bf16[1024,256]{1,0:T(8,128)(2,1)} %select_select_fusion.error_ref, bf16[512,896]{1,0:T(8,128)(2,1)} %copy-done.3, bf16[512,896]{1,0:T(8,128)(2,1)} %collective-permute-done.34.refs_1_), custom_call_target="tpu_custom_call" | custom-call | flops 939524096 | bytes 7340032 | tf_op jit(solution)/shard_map/pallas_call | solution.py:278
  179.2 11.6 %shard_map.58.refs_2_ = bf16[1024,7168]{1,0:T(8,128)(2,1)} custom-call(s32[8]{0:T(128)} %stack.193.place_ref, bf16[1024,7168]{1,0:T(8,128)(2,1)} %weights_ref.5, bf16[1024,256]{1,0:T(8,128)(2,1)} %select_select_fusion.error_ref, bf16[256,896]{1,0:T(8,128)(2,1)} %copy-done.9, bf16[256,896]{1,0:T(8,128)(2,1)} %copy-done.8, ...), custom_call_target="tpu_custom_call", output_to_operand_aliasing={{}: (7, {})} | custom-call | flops 1879048192 | bytes 14680064 | tf_op jit(solution)/shard_map/pallas_call | solution.py:278
  191.6 6.5 %shard_map.59 = bf16[1024,7168]{1,0:T(8,128)(2,1)} custom-call(s32[4]{0:T(128)} %pad_add_fusion.place_ref, bf16[1024,7168]{1,0:T(8,128)(2,1)} %weights_ref.5, bf16[1024,256]{1,0:T(8,128)(2,1)} %select_select_fusion.error_ref, bf16[256,896]{1,0:T(8,128)(2,1)} %copy-done.10, bf16[256,896]{1,0:T(8,128)(2,1)} %copy-done.15, ...), custom_call_target="tpu_custom_call", output_to_operand_aliasing={{}: (5, {})} | custom-call | flops 939524096 | bytes 7340032 | tf_op jit(solution)/shard_map/pallas_call | solution.py:278
  (118 shorter events, 29.7 us)
Async XLA Ops:
  3.7 20.0 %collective-permute-start = (bf16[256,256]{1,0:T(8,128)(2,1)}, bf16[256,256]{1,0:T(8,128)(2,1)}, u32[]{:S(2)}, u32[]{:S(2)}) collective-permute-start(bf16[256,256]{1,0:T(8,128)(2,1)} %broadcast_select_fusion.7), channel_id=1, source_target_pairs={{0,2},{2,4},{4,6},{1,3},{3,5},{5,7},{8,10},{10,12},{12,14},{9,11},... | collective-permute-start | bytes 393224 | tf_op jit(solution)/shard_map/ppermute | solution.py:304
  7.6 19.0 %collective-permute-start.1 = (bf16[256,256]{1,0:T(8,128)(2,1)}, bf16[256,256]{1,0:T(8,128)(2,1)}, u32[]{:S(2)}, u32[]{:S(2)}) collective-permute-start(bf16[256,256]{1,0:T(8,128)(2,1)} %broadcast_select_fusion.6), channel_id=1, source_target_pairs={{0,2},{2,4},{4,6},{1,3},{3,5},{5,7},{8,10},{10,12},{12,14},{9,11},... | collective-permute-start | bytes 393224 | tf_op jit(solution)/shard_map/ppermute | solution.py:304
  12.5 47.4 %collective-permute-start.12 = (bf16[256,512]{1,0:T(8,128)(2,1)}, bf16[256,512]{1,0:T(8,128)(2,1)}, u32[]{:S(2)}, u32[]{:S(2)}) collective-permute-start(bf16[256,512]{1,0:T(8,128)(2,1)} %pad_maximum_fusion), channel_id=1, source_target_pairs={{0,1},{1,0},{2,3},{3,2},{4,5},{5,4},{6,7},{7,6},{8,9},{9,8},{10,11... | collective-permute-start | bytes 786440 | tf_op jit(solution)/shard_map/ppermute | solution.py:299
  15.0 1.2 copy-start.7
  21.5 2.3 %copy-start.5 = (bf16[256,256]{1,0:T(8,128)(2,1)S(1)}, bf16[256,256]{1,0:T(8,128)(2,1)}, u32[]{:S(2)}) copy-start(bf16[256,256]{1,0:T(8,128)(2,1)} %copy-done.4) | copy-start | bytes 393220
  24.7 5.7 %collective-permute-start.2 = (bf16[256,256]{1,0:T(8,128)(2,1)S(1)}, bf16[256,256]{1,0:T(8,128)(2,1)S(1)}, u32[]{:S(2)}, u32[]{:S(2)}) collective-permute-start(bf16[256,256]{1,0:T(8,128)(2,1)S(1)} %broadcast_select_fusion.5), channel_id=1, source_target_pairs={{0,2},{2,4},{4,6},{1,3},{3,5},{5,7},{8,10},{10,12},{12,14},{9,11},... | collective-permute-start | bytes 393224 | tf_op jit(solution)/shard_map/ppermute | solution.py:304
  27.6 6.2 %collective-permute-start.3 = (bf16[256,256]{1,0:T(8,128)(2,1)S(1)}, bf16[256,256]{1,0:T(8,128)(2,1)S(1)}, u32[]{:S(2)}, u32[]{:S(2)}) collective-permute-start(bf16[256,256]{1,0:T(8,128)(2,1)S(1)} %broadcast_select_fusion.4), channel_id=1, source_target_pairs={{0,2},{2,4},{4,6},{1,3},{3,5},{5,7},{8,10},{10,12},{12,14},{9,11},... | collective-permute-start | bytes 393224 | tf_op jit(solution)/shard_map/ppermute | solution.py:304
  29.5 32.8 %collective-permute-start.13 = (bf16[256,512]{1,0:T(8,128)(2,1)S(1)}, bf16[256,512]{1,0:T(8,128)(2,1)S(1)}, u32[]{:S(2)}, u32[]{:S(2)}) collective-permute-start(bf16[256,512]{1,0:T(8,128)(2,1)S(1)} %pad_maximum_fusion.1), channel_id=1, source_target_pairs={{0,1},{1,0},{2,3},{3,2},{4,5},{5,4},{6,7},{7,6},{8,9},{9,8},{10,11... | collective-permute-start | bytes 786440 | tf_op jit(solution)/shard_map/ppermute | solution.py:299
  30.4 6.5 %collective-permute-start.4 = (bf16[256,256]{1,0:T(8,128)(2,1)S(1)}, bf16[256,256]{1,0:T(8,128)(2,1)S(1)}, u32[]{:S(2)}, u32[]{:S(2)}) collective-permute-start(bf16[256,256]{1,0:T(8,128)(2,1)S(1)} %broadcast_select_fusion.3), channel_id=1, source_target_pairs={{0,2},{2,4},{4,6},{1,3},{3,5},{5,7},{8,10},{10,12},{12,14},{9,11},... | collective-permute-start | bytes 393224 | tf_op jit(solution)/shard_map/ppermute | solution.py:304
  33.8 7.1 %collective-permute-start.5 = (bf16[256,256]{1,0:T(8,128)(2,1)S(1)}, bf16[256,256]{1,0:T(8,128)(2,1)S(1)}, u32[]{:S(2)}, u32[]{:S(2)}) collective-permute-start(bf16[256,256]{1,0:T(8,128)(2,1)S(1)} %broadcast_select_fusion.2), channel_id=1, source_target_pairs={{0,2},{2,4},{4,6},{1,3},{3,5},{5,7},{8,10},{10,12},{12,14},{9,11},... | collective-permute-start | bytes 393224 | tf_op jit(solution)/shard_map/ppermute | solution.py:304
  35.8 26.7 %collective-permute-start.14 = (bf16[256,512]{1,0:T(8,128)(2,1)S(1)}, bf16[256,512]{1,0:T(8,128)(2,1)S(1)}, u32[]{:S(2)}, u32[]{:S(2)}) collective-permute-start(bf16[256,512]{1,0:T(8,128)(2,1)S(1)} %pad_maximum_fusion.2), channel_id=1, source_target_pairs={{0,1},{1,0},{2,3},{3,2},{4,5},{5,4},{6,7},{7,6},{8,9},{9,8},{10,11... | collective-permute-start | bytes 786440 | tf_op jit(solution)/shard_map/ppermute | solution.py:299
  37.0 7.4 %collective-permute-start.6 = (bf16[256,256]{1,0:T(8,128)(2,1)S(1)}, bf16[256,256]{1,0:T(8,128)(2,1)S(1)}, u32[]{:S(2)}, u32[]{:S(2)}) collective-permute-start(bf16[256,256]{1,0:T(8,128)(2,1)S(1)} %broadcast_select_fusion.1), channel_id=1, source_target_pairs={{0,2},{2,4},{4,6},{1,3},{3,5},{5,7},{8,10},{10,12},{12,14},{9,11},... | collective-permute-start | bytes 393224 | tf_op jit(solution)/shard_map/ppermute | solution.py:304
  41.0 6.3 %collective-permute-start.7 = (bf16[256,256]{1,0:T(8,128)(2,1)S(1)}, bf16[256,256]{1,0:T(8,128)(2,1)S(1)}, u32[]{:S(2)}, u32[]{:S(2)}) collective-permute-start(bf16[256,256]{1,0:T(8,128)(2,1)S(1)} %broadcast_select_fusion), channel_id=1, source_target_pairs={{0,2},{2,4},{4,6},{1,3},{3,5},{5,7},{8,10},{10,12},{12,14},{9,11},... | collective-permute-start | bytes 393224 | tf_op jit(solution)/shard_map/ppermute | solution.py:304
  44.4 6.6 %collective-permute-start.8 = (bf16[256,256]{1,0:T(8,128)(2,1)S(1)}, bf16[256,256]{1,0:T(8,128)(2,1)S(1)}, u32[]{:S(2)}, u32[]{:S(2)}) collective-permute-start(bf16[256,256]{1,0:T(8,128)(2,1)S(1)} %collective-permute-done.6), channel_id=1, source_target_pairs={{0,2},{2,4},{4,6},{1,3},{3,5},{5,7},{8,10},{10,12},{12,14},{9,11},... | collective-permute-start | bytes 393224 | tf_op jit(solution)/shard_map/ppermute | solution.py:304
  47.2 5.9 %collective-permute-start.9 = (bf16[256,256]{1,0:T(8,128)(2,1)S(1)}, bf16[256,256]{1,0:T(8,128)(2,1)S(1)}, u32[]{:S(2)}, u32[]{:S(2)}) collective-permute-start(bf16[256,256]{1,0:T(8,128)(2,1)S(1)} %collective-permute-done.7), channel_id=1, source_target_pairs={{0,2},{2,4},{4,6},{1,3},{3,5},{5,7},{8,10},{10,12},{12,14},{9,11},... | collective-permute-start | bytes 393224 | tf_op jit(solution)/shard_map/ppermute | solution.py:304
  50.9 5.7 %collective-permute-start.10 = (bf16[256,256]{1,0:T(8,128)(2,1)S(1)}, bf16[256,256]{1,0:T(8,128)(2,1)S(1)}, u32[]{:S(2)}, u32[]{:S(2)}) collective-permute-start(bf16[256,256]{1,0:T(8,128)(2,1)S(1)} %collective-permute-done.8), channel_id=1, source_target_pairs={{0,2},{2,4},{4,6},{1,3},{3,5},{5,7},{8,10},{10,12},{12,14},{9,11},... | collective-permute-start | bytes 393224 | tf_op jit(solution)/shard_map/ppermute | solution.py:304
  53.2 6.5 %collective-permute-start.11 = (bf16[256,256]{1,0:T(8,128)(2,1)S(1)}, bf16[256,256]{1,0:T(8,128)(2,1)S(1)}, u32[]{:S(2)}, u32[]{:S(2)}) collective-permute-start(bf16[256,256]{1,0:T(8,128)(2,1)S(1)} %collective-permute-done.9), channel_id=1, source_target_pairs={{0,2},{2,4},{4,6},{1,3},{3,5},{5,7},{8,10},{10,12},{12,14},{9,11},... | collective-permute-start | bytes 393224 | tf_op jit(solution)/shard_map/ppermute | solution.py:304
  56.6 5.9 %collective-permute-start.15 = (bf16[256,512]{1,0:T(8,128)(2,1)S(1)}, bf16[256,512]{1,0:T(8,128)(2,1)S(1)}, u32[]{:S(2)}, u32[]{:S(2)}) collective-permute-start(bf16[256,512]{1,0:T(8,128)(2,1)S(1)} %pad_maximum_fusion.3), channel_id=1, source_target_pairs={{0,1},{1,0},{2,3},{3,2},{4,5},{5,4},{6,7},{7,6},{8,9},{9,8},{10,11... | collective-permute-start | bytes 786440 | tf_op jit(solution)/shard_map/ppermute | solution.py:299
  59.7 5.5 %collective-permute-start.16 = (bf16[256,512]{1,0:T(8,128)(2,1)S(1)}, bf16[256,512]{1,0:T(8,128)(2,1)S(1)}, u32[]{:S(2)}, u32[]{:S(2)}) collective-permute-start(bf16[256,512]{1,0:T(8,128)(2,1)S(1)} %constant_dynamic-update-slice_fusion), channel_id=1, source_target_pairs={{0,1},{1,0},{2,3},{3,2},{4,5},{5,4},{6,7},{7,6},{8,9},{9,8},{10,11... | collective-permute-start | bytes 786440 | tf_op jit(solution)/shard_map/ppermute | solution.py:299
  59.9 10.5 %collective-permute-start.17 = (bf16[256,512]{1,0:T(8,128)(2,1)S(1)}, bf16[256,512]{1,0:T(8,128)(2,1)S(1)}, u32[]{:S(2)}, u32[]{:S(2)}) collective-permute-start(bf16[256,512]{1,0:T(8,128)(2,1)S(1)} %constant_dynamic-update-slice_fusion.2), channel_id=1, source_target_pairs={{0,1},{1,0},{2,3},{3,2},{4,5},{5,4},{6,7},{7,6},{8,9},{9,8},{10,11... | collective-permute-start | bytes 786440 | tf_op jit(solution)/shard_map/ppermute | solution.py:299
  62.3 13.7 %collective-permute-start.18 = (bf16[256,512]{1,0:T(8,128)(2,1)S(1)}, bf16[256,512]{1,0:T(8,128)(2,1)S(1)}, u32[]{:S(2)}, u32[]{:S(2)}) collective-permute-start(bf16[256,512]{1,0:T(8,128)(2,1)S(1)} %constant_dynamic-update-slice_fusion.4), channel_id=1, source_target_pairs={{0,1},{1,0},{2,3},{3,2},{4,5},{5,4},{6,7},{7,6},{8,9},{9,8},{10,11... | collective-permute-start | bytes 786440 | tf_op jit(solution)/shard_map/ppermute | solution.py:299
  76.0 7.5 %copy-start = (bf16[14,256,512]{2,1,0:T(8,128)(2,1)}, bf16[14,256,512]{2,1,0:T(8,128)(2,1)S(1)}, u32[]{:S(2)}) copy-start(bf16[14,256,512]{2,1,0:T(8,128)(2,1)S(1)} %bitcast_dynamic-update-slice_fusion.panel_ref.left_ref.right_ref) | copy-start | bytes 11010052
  76.0 14.2 %copy-start.6 = (bf16[1024,256]{1,0:T(8,128)(2,1)S(1)}, bf16[1024,256]{1,0:T(8,128)(2,1)}, u32[]{:S(2)}) copy-start(bf16[1024,256]{1,0:T(8,128)(2,1)} %compare_select_fusion) | copy-start | bytes 1572868
  83.5 20.2 %collective-permute-start.25 = (f32[256,896]{1,0:T(8,128)S(1)}, f32[256,896]{1,0:T(8,128)S(1)}, u32[]{:S(2)}, u32[]{:S(2)}) collective-permute-start(f32[256,896]{1,0:T(8,128)S(1)} %shard_map.54), channel_id=1, source_target_pairs={{0,8},{8,0},{16,24},{24,16},{1,9},{9,1},{17,25},{25,17},{2,10},{10... | collective-permute-start | bytes 2752520 | tf_op jit(solution)/shard_map/ppermute | solution.py:299
  90.2 28.4 %collective-permute-start.21 = (bf16[1024,256]{1,0:T(8,128)(2,1)S(1)}, bf16[1024,256]{1,0:T(8,128)(2,1)S(1)}, u32[]{:S(2)}, u32[]{:S(2)}) collective-permute-start(bf16[1024,256]{1,0:T(8,128)(2,1)S(1)} %copy-done.6), channel_id=1, source_target_pairs={{0,2},{2,4},{4,6},{1,3},{3,5},{5,7},{8,10},{10,12},{12,14},{9,11},... | collective-permute-start | bytes 1572872 | tf_op jit(solution)/shard_map/ppermute | solution.py:304
  92.1 2.0 %copy-start.1 = (bf16[14,256,512]{2,1,0:T(8,128)(2,1)S(1)}, bf16[14,256,512]{2,1,0:T(8,128)(2,1)}, u32[]{:S(2)}) copy-start(bf16[14,256,512]{2,1,0:T(8,128)(2,1)} %copy-done) | copy-start | bytes 11010052
  94.2 2.6 %copy-start.2 = (bf16[14,256,512]{2,1,0:T(8,128)(2,1)S(1)}, bf16[14,256,512]{2,1,0:T(8,128)(2,1)}, u32[]{:S(2)}) copy-start(bf16[14,256,512]{2,1,0:T(8,128)(2,1)} %copy-done) | copy-start | bytes 11010052
  96.4 15.2 %collective-permute-start.19 = (f32[256,256]{1,0:T(8,128)S(1)}, f32[256,256]{1,0:T(8,128)S(1)}, u32[]{:S(2)}, u32[]{:S(2)}) collective-permute-start(f32[256,256]{1,0:T(8,128)S(1)} %shard_map.50), channel_id=1, source_target_pairs={{0,8},{8,0},{16,24},{24,16},{1,9},{9,1},{17,25},{25,17},{2,10},{10... | collective-permute-start | bytes 786440 | tf_op jit(solution)/shard_map/ppermute | solution.py:299
  103.4 42.1 %collective-permute-start.24 = (f32[256,896]{1,0:T(8,128)S(1)}, f32[256,896]{1,0:T(8,128)S(1)}, u32[]{:S(2)}, u32[]{:S(2)}) collective-permute-start(f32[256,896]{1,0:T(8,128)S(1)} %shard_map.53), channel_id=1, source_target_pairs={{0,8},{8,0},{16,24},{24,16},{1,9},{9,1},{17,25},{25,17},{2,10},{10... | collective-permute-start | bytes 2752520 | tf_op jit(solution)/shard_map/ppermute | solution.py:299
  110.3 35.2 %collective-permute-start.26 = (f32[256,896]{1,0:T(8,128)S(1)}, f32[256,896]{1,0:T(8,128)S(1)}, u32[]{:S(2)}, u32[]{:S(2)}) collective-permute-start(f32[256,896]{1,0:T(8,128)S(1)} %shard_map.55), channel_id=1, source_target_pairs={{0,16},{8,24},{16,0},{24,8},{1,17},{9,25},{17,1},{25,9},{2,18},{10... | collective-permute-start | bytes 2752520 | tf_op jit(solution)/shard_map/ppermute | solution.py:299
  111.6 26.0 %collective-permute-start.20 = (f32[256,256]{1,0:T(8,128)S(1)}, f32[256,256]{1,0:T(8,128)S(1)}, u32[]{:S(2)}, u32[]{:S(2)}) collective-permute-start(f32[256,256]{1,0:T(8,128)S(1)} %add.62), channel_id=1, source_target_pairs={{0,16},{8,24},{16,0},{24,8},{1,17},{9,25},{17,1},{25,9},{2,18},{10... | collective-permute-start | bytes 786440 | tf_op jit(solution)/shard_map/ppermute | solution.py:299
  118.6 26.9 %copy-start.11 = (bf16[1024,256]{1,0:T(8,128)(2,1)}, bf16[1024,256]{1,0:T(8,128)(2,1)S(1)}, u32[]{:S(2)}) copy-start(bf16[1024,256]{1,0:T(8,128)(2,1)S(1)} %collective-permute-done.21) | copy-start | bytes 1572868
  118.6 26.9 %collective-permute-start.22 = (bf16[1024,256]{1,0:T(8,128)(2,1)S(1)}, bf16[1024,256]{1,0:T(8,128)(2,1)}, u32[]{:S(2)}, u32[]{:S(2)}) collective-permute-start(bf16[1024,256]{1,0:T(8,128)(2,1)S(1)} %collective-permute-done.21), channel_id=1, source_target_pairs={{0,2},{2,4},{4,6},{1,3},{3,5},{5,7},{8,10},{10,12},{12,14},{9,11},... | collective-permute-start | bytes 1572872 | tf_op jit(solution)/shard_map/ppermute | solution.py:304
  145.6 23.9 %copy-start.12 = (bf16[1024,256]{1,0:T(8,128)(2,1)S(1)}, bf16[1024,256]{1,0:T(8,128)(2,1)}, u32[]{:S(2)}) copy-start(bf16[1024,256]{1,0:T(8,128)(2,1)} %copy-done.11) | copy-start | bytes 1572868
  146.7 23.6 %copy-start.3 = (bf16[512,896]{1,0:T(8,128)(2,1)}, bf16[512,896]{1,0:T(8,128)(2,1)S(1)}, u32[]{:S(2)}) copy-start(bf16[512,896]{1,0:T(8,128)(2,1)S(1)} %get-tuple-element.36.refs_0_) | copy-start | bytes 2752516
  146.7 11.0 %collective-permute-start.27 = (bf16[256,896]{1,0:T(8,128)(2,1)S(1)}, bf16[256,896]{1,0:T(8,128)(2,1)S(1)}, u32[]{:S(2)}, u32[]{:S(2)}) collective-permute-start(bf16[256,896]{1,0:T(8,128)(2,1)S(1)} %get-tuple-element.35), channel_id=1, source_target_pairs={{0,1},{1,0},{2,3},{3,2},{4,5},{5,4},{6,7},{7,6},{8,9},{9,8},{10,11... | collective-permute-start | bytes 1376264 | tf_op jit(solution)/shard_map/ppermute | solution.py:299
  147.5 13.4 %collective-permute-start.29 = (bf16[256,896]{1,0:T(8,128)(2,1)S(1)}, bf16[256,896]{1,0:T(8,128)(2,1)S(1)}, u32[]{:S(2)}, u32[]{:S(2)}) collective-permute-start(bf16[256,896]{1,0:T(8,128)(2,1)S(1)} %get-tuple-element.35), channel_id=1, source_target_pairs={{0,16},{8,24},{16,0},{24,8},{1,17},{9,25},{17,1},{25,9},{2,18},{10... | collective-permute-start | bytes 1376264 | tf_op jit(solution)/shard_map/ppermute | solution.py:299
  148.8 21.5 %collective-permute-start.34 = (bf16[512,896]{1,0:T(8,128)(2,1)S(1)}, bf16[512,896]{1,0:T(8,128)(2,1)}, u32[]{:S(2)}, u32[]{:S(2)}) collective-permute-start(bf16[512,896]{1,0:T(8,128)(2,1)S(1)} %get-tuple-element.36.refs_0_), channel_id=1, source_target_pairs={{0,8},{8,0},{16,24},{24,16},{1,9},{9,1},{17,25},{25,17},{2,10},{10... | collective-permute-start | bytes 2752520 | tf_op jit(solution)/shard_map/ppermute | solution.py:299
  150.5 18.9 %collective-permute-start.23 = (bf16[1024,256]{1,0:T(8,128)(2,1)}, bf16[1024,256]{1,0:T(8,128)(2,1)}, u32[]{:S(2)}, u32[]{:S(2)}) collective-permute-start(bf16[1024,256]{1,0:T(8,128)(2,1)} %collective-permute-done.22), channel_id=1, source_target_pairs={{0,2},{2,4},{4,6},{1,3},{3,5},{5,7},{8,10},{10,12},{12,14},{9,11},... | collective-permute-start | bytes 1572872 | tf_op jit(solution)/shard_map/ppermute | solution.py:304
  157.8 19.9 %copy-start.8 = (bf16[256,896]{1,0:T(8,128)(2,1)}, bf16[256,896]{1,0:T(8,128)(2,1)S(1)}, u32[]{:S(2)}) copy-start(bf16[256,896]{1,0:T(8,128)(2,1)S(1)} %collective-permute-done.27.refs_1_) | copy-start | bytes 1376260
  158.5 6.5 %collective-permute-start.28 = (bf16[128,896]{1,0:T(8,128)(2,1)}, bf16[128,896]{1,0:T(8,128)(2,1)}, u32[]{:S(2)}, u32[]{:S(2)}) collective-permute-start(bf16[128,896]{1,0:T(8,128)(2,1)} %slice.17), channel_id=1, source_target_pairs={{0,16},{8,24},{16,0},{24,8},{1,17},{9,25},{17,1},{25,9},{2,18},{10... | collective-permute-start | bytes 688136 | tf_op jit(solution)/shard_map/ppermute | solution.py:299
  160.9 16.7 %copy-start.9 = (bf16[256,896]{1,0:T(8,128)(2,1)}, bf16[256,896]{1,0:T(8,128)(2,1)S(1)}, u32[]{:S(2)}) copy-start(bf16[256,896]{1,0:T(8,128)(2,1)S(1)} %collective-permute-done.29.refs_0_) | copy-start | bytes 1376260
  161.0 6.9 %collective-permute-start.30 = (bf16[128,896]{1,0:T(8,128)(2,1)S(1)}, bf16[128,896]{1,0:T(8,128)(2,1)S(1)}, u32[]{:S(2)}, u32[]{:S(2)}) collective-permute-start(bf16[128,896]{1,0:T(8,128)(2,1)S(1)} %slice.18), channel_id=1, source_target_pairs={{0,1},{1,0},{2,3},{3,2},{4,5},{5,4},{6,7},{7,6},{8,9},{9,8},{10,11... | collective-permute-start | bytes 688136 | tf_op jit(solution)/shard_map/ppermute | solution.py:299
  162.6 15.1 %collective-permute-start.32 = (bf16[256,896]{1,0:T(8,128)(2,1)S(1)}, bf16[256,896]{1,0:T(8,128)(2,1)S(1)}, u32[]{:S(2)}, u32[]{:S(2)}) collective-permute-start(bf16[256,896]{1,0:T(8,128)(2,1)S(1)} %collective-permute-done.29.refs_0_), channel_id=1, source_target_pairs={{0,8},{8,0},{16,24},{24,16},{1,9},{9,1},{17,25},{25,17},{2,10},{10... | collective-permute-start | bytes 1376264 | tf_op jit(solution)/shard_map/ppermute | solution.py:299
  165.0 12.7 %collective-permute-start.33 = (bf16[256,896]{1,0:T(8,128)(2,1)S(1)}, bf16[256,896]{1,0:T(8,128)(2,1)S(1)}, u32[]{:S(2)}, u32[]{:S(2)}) collective-permute-start(bf16[256,896]{1,0:T(8,128)(2,1)S(1)} %collective-permute-done.27.refs_1_), channel_id=1, source_target_pairs={{0,8},{8,0},{16,24},{24,16},{1,9},{9,1},{17,25},{25,17},{2,10},{10... | collective-permute-start | bytes 1376264 | tf_op jit(solution)/shard_map/ppermute | solution.py:299
  167.9 9.8 %copy-start.10 = (bf16[256,896]{1,0:T(8,128)(2,1)}, bf16[256,896]{1,0:T(8,128)(2,1)S(1)}, u32[]{:S(2)}) copy-start(bf16[256,896]{1,0:T(8,128)(2,1)S(1)} %constant_dynamic-update-slice_fusion.6.refs_0_) | copy-start | bytes 1376260
  167.9 22.9 %collective-permute-start.31 = (bf16[256,896]{1,0:T(8,128)(2,1)S(1)}, bf16[256,896]{1,0:T(8,128)(2,1)S(1)}, u32[]{:S(2)}, u32[]{:S(2)}) collective-permute-start(bf16[256,896]{1,0:T(8,128)(2,1)S(1)} %constant_dynamic-update-slice_fusion.6.refs_0_), channel_id=1, source_target_pairs={{0,8},{8,0},{16,24},{24,16},{1,9},{9,1},{17,25},{25,17},{2,10},{10... | collective-permute-start | bytes 1376264 | tf_op jit(solution)/shard_map/ppermute | solution.py:299
  190.8 0.8 copy-start.15
  (3 other events, 2.2 us)

commit v3 on v2

--- a/solution.py
+++ b/solution.py
@@ -10,6 +10,7 @@
 PANEL = 256
 QBLOCK = 128
 ROUNDS = 4
+SPLIT = 4
 F32 = jnp.float32
 BF16 = jnp.bfloat16
 MIB = 1 << 20
@@ -19,25 +20,21 @@
     return jnp.dot(left, right, precision=lax.Precision.HIGHEST, preferred_element_type=F32)
 
 
-def panel_kernel(place_ref, quant_ref, exps_ref, first_ref, second_ref):
+def panel_kernel(place_ref, quant_ref, exps_ref, out_ref):
     scale = jnp.exp2(exps_ref[:, : PANEL // QBLOCK].astype(F32))
     rows = scale.shape[0]
     wide = [
         jnp.broadcast_to(scale[:, c : c + 1], (rows, QBLOCK)) for c in range(PANEL // QBLOCK)
     ]
     acts = quant_ref[...].astype(F32) * jnp.concatenate(wide, axis=1)
-    turned = acts.T.astype(BF16)
-    half = rows // 2
-    first_ref[...] = turned[:, :half]
-    second_ref[...] = turned[:, half:]
+    out_ref[...] = acts.T.astype(BF16)
 
 
 def panel_piece(quantized, exponents, at, piece):
     blocks = exponents.shape[1]
-    shape = jax.ShapeDtypeStruct((PANEL, piece // 2), BF16)
     return pl.pallas_call(
         panel_kernel,
-        out_shape=(shape, shape),
+        out_shape=jax.ShapeDtypeStruct((PANEL, piece), BF16),
         grid_spec=pltpu.PrefetchScalarGridSpec(
             num_scalar_prefetch=1,
             grid=(1,),
@@ -45,7 +42,7 @@
                 pl.BlockSpec((piece, PANEL), lambda i, place: (place[0], 0)),
                 pl.BlockSpec((piece, blocks), lambda i, place: (place[0], 0)),
             ],
-            out_specs=[pl.BlockSpec((PANEL, piece // 2), lambda i, place: (0, 0))] * 2,
+            out_specs=pl.BlockSpec((PANEL, piece), lambda i, place: (0, 0)),
         ),
         compiler_params=pltpu.CompilerParams(vmem_limit_bytes=48 * MIB),
         cost_estimate=pl.CostEstimate(
@@ -93,8 +90,8 @@
     )(start.reshape(1).astype(jnp.int32), stack)
 
 
-def gram_kernel(blocks, place_ref, quant_ref, rows_ref, left_ref, right_ref, *refs):
-    out_ref = refs[-1]
+def gram_kernel(blocks, place_ref, rows_ref, left_ref, right_ref, *refs):
+    quants, refs, out_ref = refs[:SPLIT], refs[SPLIT:], refs[-1]
 
     @pl.when(pl.program_id(0) == 0)
     def _():
@@ -102,15 +99,18 @@
 
     rows = rows_ref[...]
     turned = rows.T
-    step = quant_ref.shape[0]
+    step = rows.shape[1]
+
+    def quant(c):
+        return jnp.concatenate([q[:, c * QBLOCK : (c + 1) * QBLOCK] for q in quants], axis=0)
+
     panel = jnp.concatenate([left_ref[...], right_ref[...]], axis=1)
     for c in range(0, blocks, 2):
         left = panel * jnp.broadcast_to(rows[c : c + 1].astype(BF16), (PANEL, step))
-        right = quant_ref[:, c * QBLOCK : (c + 1) * QBLOCK]
+        right = quant(c)
         if c + 1 < blocks:
             ratio = jnp.broadcast_to(turned[:, c + 1 : c + 2], (step, QBLOCK)).astype(BF16)
-            second = quant_ref[:, (c + 1) * QBLOCK : (c + 2) * QBLOCK] * ratio
-            right = jnp.concatenate([right, second], axis=1)
+            right = jnp.concatenate([right, quant(c + 1) * ratio], axis=1)
         span = slice(c * QBLOCK, c * QBLOCK + right.shape[1])
         out_ref[:, span] += jnp.dot(left, right, preferred_element_type=F32)
 
@@ -137,14 +137,22 @@
         return lax.rem(k + place[0] * (steps // 2), steps)
 
     specs = [
-        pl.BlockSpec((step, width), lambda k, place: (tokens_at(k, place), place[2])),
         pl.BlockSpec((8, step), lambda k, place: (place[2], tokens_at(k, place))),
         pl.BlockSpec((None, PANEL, piece), lambda k, place: (slot(2 * k, place[1], slots), 0, 0)),
         pl.BlockSpec(
             (None, PANEL, piece), lambda k, place: (slot(2 * k + 1, place[1], slots), 0, 0)
         ),
     ]
-    args = [place, quantized, scale_rows, stack, stack]
+    specs += [
+        pl.BlockSpec(
+            (step // SPLIT, width),
+            functools.partial(
+                lambda i, k, place: (SPLIT * tokens_at(k, place) + i, place[2]), i
+            ),
+        )
+        for i in range(SPLIT)
+    ]
+    args = [place, scale_rows, stack, stack] + [quantized] * SPLIT
     if extra is not None:
         specs.append(pl.BlockSpec((PANEL, width), lambda k, place: (0, 0)))
         args.append(extra)
@@ -233,59 +241,87 @@
     )(inverse, *parts)
 
 
-def update_kernel(count, place_ref, weights_ref, error_ref, *refs):
-    gains, out_ref = refs[:count], refs[-1]
-    for j in range(count):
-
-        @pl.when(pl.program_id(0) == j)
+def update_kernel(shapes, place_ref, error_ref, weights_ref, *refs):
+    count = len(shapes)
+    groups, at = [], 0
+    for pieces in shapes:
+        groups.append(refs[at : at + len(pieces)])
+        at += len(pieces)
+    out_ref, read_ref, made_ref, read_sems, made_sems = refs[-5:]
+    _, parts, step, width = read_ref.shape
+
+    def window(ref, j, i):
+        col = pl.multiple_of(place_ref[j] * width, QBLOCK)
+        return ref.at[pl.ds(i * step, step), pl.ds(col, width)]
+
+    def read(j, i):
+        return pltpu.make_async_copy(window(weights_ref, j, i), read_ref.at[j, i], read_sems.at[j, i])
+
+    def made(j, i):
+        return pltpu.make_async_copy(made_ref.at[j, i], window(out_ref, j, i), made_sems.at[j, i])
+
+    spots = [(j, i) for j in range(count) for i in range(parts)]
+    for j, i in spots:
+        read(j, i).start()
+    for j, i in spots:
+        read(j, i).wait()
+        error = error_ref[i * step : (i + 1) * step, :]
+        total = read_ref[j, i].astype(F32)
+        row = 0
+        for gain in groups[j]:
+            for top in range(0, gain.shape[0], PANEL):
+                size = min(PANEL, gain.shape[0])
+                total += jnp.dot(
+                    error[:, row : row + size],
+                    gain[top : top + size, :],
+                    preferred_element_type=F32,
+                )
+                row = (row + size) % PANEL
+        made_ref[j, i] = total.astype(BF16)
+
+        @pl.when(place_ref[count + j] == 1)
         def _():
-            total = weights_ref[...].astype(F32)
-            for at in range(0, gains[j].shape[0], PANEL):
-                total += jnp.dot(
-                    error_ref[...], gains[j][at : at + PANEL], preferred_element_type=F32
-                )
-            out_ref[...] = total.astype(BF16)
-
-    @pl.when(place_ref[count + pl.program_id(0)] == 1)
-    def _():
-        out_ref[:, :PANEL] = weights_ref[:, :PANEL] - error_ref[...]
+            made_ref[j, i, :, :PANEL] = read_ref[j, i, :, :PANEL] - error
+
+        made(j, i).start()
+    for j, i in spots:
+        made(j, i).wait()
 
 
 def update_blocks(out, weights, error, gains, spots, first):
     rows, cols = weights.shape
-    width = gains[0].shape[1]
+    width = gains[0][0].shape[1]
     count = len(gains)
     if width % QBLOCK or width < PANEL:
         out = jnp.zeros_like(weights) if out is None else out
-        for gain, col in zip(gains, spots):
+        for pieces, col in zip(gains, spots):
             total = lax.dynamic_slice_in_dim(weights, col * width, width, 1).astype(F32)
+            gain = jnp.concatenate(pieces, axis=0)
             for at in range(0, gain.shape[0], PANEL):
                 total += jnp.dot(error, gain[at : at + PANEL], preferred_element_type=F32)
             out = lax.dynamic_update_slice_in_dim(out, total.astype(BF16), col * width, 1)
         return out
-    step = min(rows, 512)
+    parts = 4 if rows % 64 == 0 else 1
     place = jnp.stack(list(spots) + [first & (col == 0) for col in spots]).astype(jnp.int32)
-    specs = [
-        pl.BlockSpec((step, width), lambda j, i, place: (i, place[j])),
-        pl.BlockSpec((step, PANEL), lambda j, i, place: (i, 0)),
-    ] + [pl.BlockSpec(gain.shape, lambda j, i, place: (0, 0)) for gain in gains]
-    args = [place, weights, error, *gains]
+    flat = [piece for pieces in gains for piece in pieces]
+    vmem, anywhere = pl.BlockSpec(memory_space=pltpu.VMEM), pl.BlockSpec(memory_space=pl.ANY)
+    specs = [pl.BlockSpec(memory_space=pltpu.SMEM), vmem, anywhere] + [vmem] * len(flat)
+    args = [place, error, weights, *flat]
     aliases = {}
     if out is not None:
-        specs.append(pl.BlockSpec(memory_space=pl.ANY))
+        specs.append(anywhere)
         aliases = {len(args): 0}
         args.append(out)
-    return pl.pallas_call(
-        functools.partial(update_kernel, count),
+    buffer = pltpu.VMEM((count, parts, rows // parts, width), BF16)
+    sems = pltpu.SemaphoreType.DMA((count, parts))
+    return pl.pallas_call(
+        functools.partial(update_kernel, [[p.shape for p in pieces] for pieces in gains]),
         out_shape=jax.ShapeDtypeStruct((rows, cols), BF16),
-        grid_spec=pltpu.PrefetchScalarGridSpec(
-            num_scalar_prefetch=1,
-            grid=(count, rows // step),
-            in_specs=specs,
-            out_specs=pl.BlockSpec((step, width), lambda j, i, place: (i, place[j])),
-        ),
+        in_specs=specs,
+        out_specs=anywhere,
+        scratch_shapes=[buffer, buffer, sems, sems],
         input_output_aliases=aliases,
-        compiler_params=pltpu.CompilerParams(vmem_limit_bytes=56 * MIB),
+        compiler_params=pltpu.CompilerParams(vmem_limit_bytes=48 * MIB),
         cost_estimate=pl.CostEstimate(
             flops=2 * rows * width * PANEL * count,
             bytes_accessed=4 * rows * width * count,
@@ -301,7 +337,7 @@
 
 def forward(x, axis):
     size = lax.axis_size(axis)
-    return lax.ppermute(x, axis, [(i, i + 1) for i in range(size - 1)])
+    return lax.ppermute(x, axis, [(i, (i + 1) % size) for i in range(size)])
 
 
 def shards(quantized, exponents, weights, keep_mask):
@@ -315,17 +351,21 @@
     sources = [
         panel_piece(quantized, exponents, row * ROUNDS + c, piece) for c in range(ROUNDS)
     ]
-    none = jnp.zeros((PANEL, piece // 2), BF16)
-    held = [jnp.where(root, x, none) for x in sources[0]]
-    own, other = [], []
-    for r in range(ROUNDS + feats - 1):
-        both = jnp.concatenate(held, axis=1)
-        own.append(both)
-        other.append(swap(both, "row", 1))
-        if r < ROUNDS + feats - 2:
-            held = [forward(x, "feat") for x in held]
-            if r + 1 < ROUNDS:
-                held = [jnp.where(root, x, y) for x, y in zip(sources[r + 1], held)]
+    error = jnp.where(keep_mask == 0, weights[:, :PANEL], jnp.zeros((), BF16)).T
+    extras = -(-error.shape[1] // piece)
+    error = jnp.pad(error, ((0, 0), (0, extras * piece - error.shape[1])))
+    sources += [error[:, i * piece : (i + 1) * piece] for i in range(extras)]
+    held, own, other, late = sources[0], [], [], []
+    for r in range(len(sources) + feats - 1):
+        if r:
+            held = forward(held, "feat")
+            if r < len(sources):
+                held = jnp.where(root, sources[r], held)
+        if r < ROUNDS + feats - 1:
+            own.append(held)
+            other.append(swap(held, "row", 1))
+        if r >= ROUNDS:
+            late.append(held)
     stack = jnp.stack(own + other)
 
     scale_rows = None
@@ -338,10 +378,6 @@
         exps = jnp.pad(exps, ((0, 0), (0, 8 - blocks), (0, 0)))
         scale_rows = jnp.exp2(exps.astype(F32)).reshape(-1, tokens)
 
-    error = jnp.where(keep_mask == 0, weights[:, :PANEL], jnp.zeros((), BF16))
-    error, stack = lax.optimization_barrier((error, stack))
-    errors = [error, forward(error, "feat")]
-
     def gram(k, extra=None):
         col = row * toks + (tok ^ k)
         return gram_block(
@@ -349,38 +385,33 @@
         )
 
     head = head_block(stack, feat)
-    from_core = swap(head, "tok", 1)
+    head = head + swap(head, "tok", 1)
     from3 = swap(gram(3), "tok", 1)
-    head = head + from_core
     head = head + swap(head, "tok", 2)
-    block2 = gram(2, from3)
+    from1 = swap(gram(1), "tok", 1)
+    from3, late[-2] = lax.optimization_barrier((from3, late[-2]))
+    block2, head = lax.optimization_barrier((gram(2, from3), head))
     fromx = swap(block2, "tok", 2)
-    from1 = swap(gram(1), "tok", 1)
     block0 = gram(0)
+    head, late[-1] = lax.optimization_barrier((head, late[-1]))
     inverse = invert(head)
-    for _ in range(feats - 2):
-        if len(errors) == 2:
-            block0, last = lax.optimization_barrier((block0, errors[-1]))
-        elif len(errors) == 3:
-            inverse, last = lax.optimization_barrier((inverse, errors[-1]))
-        else:
-            last = errors[-1]
-        errors[-1] = last
-        errors.append(forward(last, "feat"))
-    for hop in range(1, feats):
-        error = jnp.where(feat == hop, errors[hop], error)
+    error = jnp.concatenate(
+        list(lax.dynamic_slice_in_dim(jnp.stack(late), feat, extras, 0)), axis=1
+    )[:, : weights.shape[0]].T
+    inverse, error = lax.optimization_barrier((inverse, error))
     high, pair = make_gains(inverse, (block0, from1, fromx))
 
     half = PANEL // 2
     in_x, in_y = swap(high, "tok", 2), swap(high, "row", 1)
     near = swap(pair, "tok", 1)
-    far = jnp.concatenate([swap(in_y[:half], "tok", 2), swap(in_x[half:], "row", 1)], axis=0)
-    near_x, near_y, near_far = swap(in_x, "tok", 1), swap(in_y, "tok", 1), swap(far, "tok", 1)
+    far = (swap(in_y[:half], "tok", 2), swap(in_x[half:], "row", 1))
+    near_x, near_y = swap(in_x, "tok", 1), swap(in_y, "tok", 1)
+    near_far = tuple(swap(x, "tok", 1) for x in far)
 
     out = None
     plan = [
-        [(pair, 0, 0), (near, 1, 0)],
-        [(in_x, 2, 0), (in_y, 0, 1), (near_x, 3, 0), (near_y, 1, 1)],
+        [((pair,), 0, 0), ((near,), 1, 0)],
+        [((in_x,), 2, 0), ((in_y,), 0, 1), ((near_x,), 3, 0), ((near_y,), 1, 1)],
         [(far, 2, 1), (near_far, 3, 1)],
     ]
     for group in plan:

time: 202 us -> 192 us (0.950); the launches traced: 198 us -> 191 us
  starting transfers between devices: 58.7 us -> 29.5 us
  local copies, waits for them, and re-layouts: 12.5 us -> 26.6 us
  waiting for transfers between devices: 46.4 us -> 59.3 us
  Pallas kernels: 69 us -> 62.9 us
    ppermute x15 -> x8, starting transfers between devices: 33.8 us -> 8.31 us  [forward(): return lax.ppermute(x, axis, [(i, (i + 1) % size) for i in range(size)])]
    ppermute x15 -> x8, waiting for transfers between devices: 11.5 us -> 24.2 us  [forward(): return lax.ppermute(x, axis, [(i, (i + 1) % size) for i in range(size)])]
    another operation x1 -> x2, local copies, waits for them, and re-layouts: 0.02 us -> 6.66 us  [shards(): stack = jnp.stack(own + other)]
    select_n x10 -> x0, other arithmetic: 6.12 us -> none  [the longest x1 1.96 us: shards(): error = jnp.where(keep_mask == 0, weights[:, :PANEL], jnp.zeros((), BF16))]
    unnamed x46 -> x26, local copies, waits for them, and re-layouts: 9.72 us -> 15.8 us
    unnamed x4 -> x5, other arithmetic: 1.04 us -> 6.93 us
    pallas_call x7, Pallas kernels: 30.4 us -> 25.5 us  [the longest x3 20.5 us: update_blocks(): pl.pallas_call(functools.partial(update_kernel, [[p.shape for p in pieces...]
    ppermute x20 -> x21, starting transfers between devices: 25 us -> 21.2 us  [swap(): return lax.ppermute(x, axis, [(i, i ^ bit) for i in range(size)])]
  transfers between devices with their start and end apart: 35 -> 29, of which waited for: 14 -> 12; matrix products, arithmetic and copies ran while one was open for 8% -> 13% of each run, Pallas kernels for 27% -> 25%
where the time goes in v3:
time: 192 us; the launch traced here: 191 us
  Pallas kernels  62.9 us (33%)
  waiting for transfers between devices  59.3 us (31%)
  starting transfers between devices  29.5 us (15%)
  local copies, waits for them, and re-layouts  26.6 us (14%)
  other arithmetic  12.4 us (6%)
    ppermute x21, waiting for transfers between devices, swap(): return lax.ppermute(x, axis, [(i, i ^ bit) for i in range(size)])  35.2 us
    pallas_call x4, Pallas kernels, gram_block(): pl.pallas_call(functools.partial(gram_kernel, blocks), out_shape=jax.Shap...  26.3 us
    ppermute x8, waiting for transfers between devices, forward(): return lax.ppermute(x, axis, [(i, (i + 1) % size) for i in range(size)])  24.2 us
    ppermute x21, starting transfers between devices, swap(): return lax.ppermute(x, axis, [(i, i ^ bit) for i in range(size)])  21.2 us
    pallas_call x3, Pallas kernels, update_blocks(): pl.pallas_call(functools.partial(update_kernel, [[p.shape for p in pieces...  20.5 us
    unnamed x26, local copies, waits for them, and re-layouts  15.8 us
    ppermute x8, starting transfers between devices, forward(): return lax.ppermute(x, axis, [(i, (i + 1) % size) for i in range(size)])  8.31 us
    pallas_call x1, Pallas kernels, invert(): pl.pallas_call(inverse_kernel, out_shape=jax.ShapeDtypeStruct((PANEL, PAN...  7.83 us
  transfers between devices with their start and end apart: 29, of which 12 were waited for; matrix products, arithmetic and copies ran while one was open for 13% of the time, Pallas kernels for 25%

profile of v3, /device:TPU:9, one launch (start us, length us, event | category | flops | bytes accessed | tf_op | source)
XLA Modules:
  0.0 191.2 jit_solution(671850376899636102)
XLA Ops:
  0.0 1.8 copy.26.exps_ref
  1.8 1.2 shard_map.46
  3.2 1.3 collective-permute-start
  4.5 1.2 collective-permute-start.6
  5.8 1.2 shard_map.47
  7.9 1.3 reshape.29
  10.5 1.8 bitcast_dynamic-update-slice_fusion.17
  12.3 1.3 collective-permute-start.1
  13.6 1.2 subtract_select_fusion
  14.8 1.2 shard_map.48
  16.1 1.2 shard_map.49
  17.6 2.8 %collective-permute-done.1 = bf16[256,512]{0,1:T(8,128)(2,1)} collective-permute-done((bf16[256,512]{0,1:T(8,128)(2,1)}, bf16[256,512]{0,1:T(8,128)(2,1)}, u32[]{:S(2)}, u32[]{:S(2)}) %collective-permute-start.1) | collective-permute-done | bytes 262176 | tf_op jit(solution)/shard_map/ppermute | solution.py:340
  20.4 1.8 bitcast_dynamic-update-slice_fusion.16
  22.2 1.4 exponential_bitcast_fusion.rows_ref
  23.6 5.3 %collective-permute-done.2 = bf16[256,512]{0,1:T(8,128)(2,1)S(1)} collective-permute-done((bf16[256,512]{0,1:T(8,128)(2,1)}, bf16[256,512]{0,1:T(8,128)(2,1)S(1)}, u32[]{:S(2)}, u32[]{:S(2)}) %collective-permute-start.2) | collective-permute-done | bytes 262176 | tf_op jit(solution)/shard_map/ppermute | solution.py:340
  29.7 1.5 fusion
  31.2 5.5 %collective-permute-done.3 = bf16[256,512]{0,1:T(8,128)(2,1)S(1)} collective-permute-done((bf16[256,512]{0,1:T(8,128)(2,1)}, bf16[256,512]{0,1:T(8,128)(2,1)S(1)}, u32[]{:S(2)}, u32[]{:S(2)}) %collective-permute-start.3) | collective-permute-done | bytes 262176 | tf_op jit(solution)/shard_map/ppermute | solution.py:340
  37.9 1.1 collective-permute-start.8
  39.4 5.1 %collective-permute-done.4 = bf16[256,512]{0,1:T(8,128)(2,1)S(1)} collective-permute-done((bf16[256,512]{0,1:T(8,128)(2,1)S(1)}, bf16[256,512]{0,1:T(8,128)(2,1)S(1)}, u32[]{:S(2)}, u32[]{:S(2)}) %collective-permute-start.4) | collective-permute-done | bytes 262176 | tf_op jit(solution)/shard_map/ppermute | solution.py:340
  45.2 1.7 bitcast_dynamic-update-slice_fusion.11
  48.3 4.9 %collective-permute-done.5 = bf16[256,512]{0,1:T(8,128)(2,1)S(1)} collective-permute-done((bf16[256,512]{0,1:T(8,128)(2,1)S(1)}, bf16[256,512]{0,1:T(8,128)(2,1)S(1)}, u32[]{:S(2)}, u32[]{:S(2)}) %collective-permute-start.5) | collective-permute-done | bytes 262176 | tf_op jit(solution)/shard_map/ppermute | solution.py:340
  54.4 1.1 collective-permute-start.11
  55.6 1.7 bitcast_dynamic-update-slice_fusion.8
  60.6 2.9 %collective-permute-done.11 = bf16[256,512]{0,1:T(8,128)(2,1)S(1)} collective-permute-done((bf16[256,512]{0,1:T(8,128)(2,1)S(1)}, bf16[256,512]{0,1:T(8,128)(2,1)S(1)}, u32[]{:S(2)}, u32[]{:S(2)}) %collective-permute-start.11) | collective-permute-done | bytes 262176 | tf_op jit(solution)/shard_map/ppermute | solution.py:335
  64.3 4.9 %collective-permute-done.12 = bf16[256,512]{0,1:T(8,128)(2,1)S(1)} collective-permute-done((bf16[256,512]{0,1:T(8,128)(2,1)S(1)}, bf16[256,512]{0,1:T(8,128)(2,1)S(1)}, u32[]{:S(2)}, u32[]{:S(2)}) %collective-permute-start.12) | collective-permute-done | bytes 262176 | tf_op jit(solution)/shard_map/ppermute | solution.py:335
  69.9 5.9 %copy.38.left_ref.right_ref.panel_ref = bf16[14,256,512]{2,1,0:T(8,128)(2,1)} copy(bf16[14,256,512]{1,2,0:T(8,128)(2,1)} %bitcast_dynamic-update-slice_fusion.2) | data formatting | bytes 7340032 | tf_op jit(solution)/shard_map/stack | solution.py:369
  75.8 2.0 %copy-done = bf16[14,256,512]{2,1,0:T(8,128)(2,1)S(1)} copy-done((bf16[14,256,512]{2,1,0:T(8,128)(2,1)S(1)}, bf16[14,256,512]{2,1,0:T(8,128)(2,1)}, u32[]{:S(2)}) %copy-start) | copy-done | bytes 3670040
  77.9 6.8 %shard_map.50 = f32[256,896]{1,0:T(8,128)S(1)} custom-call(s32[3]{0:T(128)S(1)} %get-tuple-element.42.place_ref, f32[64,4096]{1,0:T(8,128)S(1)} %exponential_bitcast_fusion.rows_ref, bf16[14,256,512]{2,1,0:T(8,128)(2,1)S(1)} %copy-done, bf16[14,256,512]{2,1,0:T(8,128)(2,1)S(1)} %copy-done, bf16[4096,7168]{1,0:T(8,128)(2,1)} %refs_3_.7, ...), custom_call_target="tpu_custom_call" | custom-call | flops 1879048192 | bytes 8257536 | tf_op jit(solution)/shard_map/pallas_call | solution.py:159
  84.7 5.5 %collective-permute-start.13 = (f32[256,896]{1,0:T(8,128)S(1)}, f32[256,896]{1,0:T(8,128)S(1)}, u32[]{:S(2)}, u32[]{:S(2)}) collective-permute-start(f32[256,896]{1,0:T(8,128)S(1)} %shard_map.50), channel_id=1, source_target_pairs={{0,8},{8,0},{16,24},{24,16},{1,9},{9,1},{17,25},{25,17},{2,10},{10... | collective-permute-start | bytes 2752520 | tf_op jit(solution)/shard_map/ppermute | solution.py:335
  90.2 2.2 %shard_map.52 = f32[256,256]{1,0:T(8,128)S(1)} custom-call(s32[1]{0:T(128)} %bitcast.5.place_ref, bf16[14,256,512]{2,1,0:T(8,128)(2,1)S(1)} %copy-done.1), custom_call_target="tpu_custom_call" | custom-call | flops 536870912 | bytes 2097152 | tf_op jit(solution)/shard_map/pallas_call | solution.py:71
  92.6 2.0 %collective-permute-start.14 = (bf16[256,512]{0,1:T(8,128)(2,1)S(1)}, bf16[256,512]{0,1:T(8,128)(2,1)}, u32[]{:S(2)}, u32[]{:S(2)}) collective-permute-start(bf16[256,512]{0,1:T(8,128)(2,1)S(1)} %copy-done.5), channel_id=1, source_target_pairs={{0,2},{2,4},{4,6},{6,0},{1,3},{3,5},{5,7},{7,1},{8,10},{10,12},{12... | collective-permute-start | bytes 786440 | tf_op jit(solution)/shard_map/ppermute | solution.py:340
  96.0 2.0 %copy-done.2 = bf16[14,256,512]{2,1,0:T(8,128)(2,1)S(1)} copy-done((bf16[14,256,512]{2,1,0:T(8,128)(2,1)S(1)}, bf16[14,256,512]{2,1,0:T(8,128)(2,1)}, u32[]{:S(2)}) %copy-start.2) | copy-done | bytes 3670040
  98.0 6.5 %shard_map.55 = f32[256,896]{1,0:T(8,128)S(1)} custom-call(s32[3]{0:T(128)S(1)} %get-tuple-element.25.place_ref, f32[64,4096]{1,0:T(8,128)S(1)} %exponential_bitcast_fusion.rows_ref, bf16[14,256,512]{2,1,0:T(8,128)(2,1)S(1)} %copy-done.2, bf16[14,256,512]{2,1,0:T(8,128)(2,1)S(1)} %copy-done.2, bf16[4096,7168]{1,0:T(8,128)(2,1)} %refs_3_.7, ...), custom_call_target="tpu_custom_call" | custom-call | flops 1879048192 | bytes 8257536 | tf_op jit(solution)/shard_map/pallas_call | solution.py:159
  105.6 3.6 %collective-permute-start.17 = (bf16[256,512]{0,1:T(8,128)(2,1)}, bf16[256,512]{0,1:T(8,128)(2,1)S(1)}, u32[]{:S(2)}, u32[]{:S(2)}) collective-permute-start(bf16[256,512]{0,1:T(8,128)(2,1)} %collective-permute-done.14), channel_id=1, source_target_pairs={{0,2},{2,4},{4,6},{6,0},{1,3},{3,5},{5,7},{7,1},{8,10},{10,12},{12... | collective-permute-start | bytes 786440 | tf_op jit(solution)/shard_map/ppermute | solution.py:340
  109.2 6.5 %shard_map.54.first_ref = f32[256,896]{1,0:T(8,128)S(1)} custom-call(s32[3]{0:T(128)S(1)} %get-tuple-element.41.place_ref, f32[64,4096]{1,0:T(8,128)S(1)} %exponential_bitcast_fusion.rows_ref, bf16[14,256,512]{2,1,0:T(8,128)(2,1)S(1)} %copy-done.2, bf16[14,256,512]{2,1,0:T(8,128)(2,1)S(1)} %copy-done.2, bf16[4096,7168]{1,0:T(8,128)(2,1)} %refs_3_.7, ...), custom_call_target="tpu_custom_call" | custom-call | flops 1879048192 | bytes 8257536 | tf_op jit(solution)/shard_map/pallas_call | solution.py:159
  115.8 6.5 %shard_map.51 = f32[256,896]{1,0:T(8,128)S(1)} custom-call(s32[3]{0:T(128)S(1)} %get-tuple-element.43.place_ref, f32[64,4096]{1,0:T(8,128)S(1)} %exponential_bitcast_fusion.rows_ref, bf16[14,256,512]{2,1,0:T(8,128)(2,1)S(1)} %copy-done.2, bf16[14,256,512]{2,1,0:T(8,128)(2,1)S(1)} %copy-done.2, bf16[4096,7168]{1,0:T(8,128)(2,1)} %refs_3_.7, ...), custom_call_target="tpu_custom_call" | custom-call | flops 1879048192 | bytes 8257536 | tf_op jit(solution)/shard_map/pallas_call | solution.py:159
  122.3 1.2 collective-permute-start.19
  124.6 7.8 %shard_map.53.inverse_ref = f32[256,256]{1,0:T(8,128)S(1)} custom-call(f32[256,256]{1,0:T(8,128)S(1)} %add.69.head_ref), custom_call_target="tpu_custom_call" | custom-call | flops 5637144576 | bytes 524288 | tf_op jit(solution)/shard_map/pallas_call | solution.py:209
  132.5 11.5 %collective-permute-done.19.third_ref = f32[256,896]{1,0:T(8,128)S(1)} collective-permute-done((f32[256,896]{1,0:T(8,128)S(1)}, f32[256,896]{1,0:T(8,128)S(1)}, u32[]{:S(2)}, u32[]{:S(2)}) %collective-permute-start.19) | collective-permute-done | bytes 917536 | tf_op jit(solution)/shard_map/ppermute | solution.py:335
  145.0 1.2 collective-permute-start.28
  146.3 1.2 collective-permute-start.22
  147.8 10.6 %collective-permute-done.22.refs_0_ = bf16[256,896]{1,0:T(8,128)(2,1)S(1)} collective-permute-done((bf16[256,896]{1,0:T(8,128)(2,1)S(1)}, bf16[256,896]{1,0:T(8,128)(2,1)S(1)}, u32[]{:S(2)}, u32[]{:S(2)}) %collective-permute-start.22) | collective-permute-done | bytes 458784 | tf_op jit(solution)/shard_map/ppermute | solution.py:335
  159.2 1.2 collective-permute-start.27
  162.1 1.2 collective-permute-start.23
  163.5 5.1 %collective-permute-done.21.refs_0_ = bf16[128,896]{1,0:T(8,128)(2,1)S(1)} collective-permute-done((bf16[128,896]{1,0:T(8,128)(2,1)}, bf16[128,896]{1,0:T(8,128)(2,1)S(1)}, u32[]{:S(2)}, u32[]{:S(2)}) %collective-permute-start.21) | collective-permute-done | bytes 229408 | tf_op jit(solution)/shard_map/ppermute | solution.py:335
  170.4 6.0 %shard_map.57.refs_4_ = bf16[1024,7168]{1,0:T(8,128)(2,1)} custom-call(s32[4]{0:T(128)S(1)} %pad_add_fusion.6.place_ref, bf16[1024,256]{1,0:T(8,128)(2,1)S(1)} %maximum_bitcast_fusion.error_ref, bf16[1024,7168]{1,0:T(8,128)(2,1)} %weights_ref.5, bf16[512,896]{1,0:T(8,128)(2,1)S(1)} %get-tuple-element.24.refs_0_, ...), custom_call_target="tpu_custom_call" | custom-call | flops 939524096 | bytes 7340032 | tf_op jit(solution)/shard_map/pallas_call | solution.py:317
  176.5 8.2 %shard_map.58.refs_4_ = bf16[1024,7168]{1,0:T(8,128)(2,1)} custom-call(s32[8]{0:T(128)S(1)} %stack.211.place_ref, bf16[1024,256]{1,0:T(8,128)(2,1)S(1)} %maximum_bitcast_fusion.error_ref, bf16[1024,7168]{1,0:T(8,128)(2,1)} %weights_ref.5, bf16[256,896]{1,0:T(8,128)(2,1)S(1)} %collective-permute-done.22.refs_0_, ...), custom_call_target="tpu_custom_call", output_to_operand_aliasing={{}: (7, {})} | custom-call | flops 1879048192 | bytes 14680064 | tf_op jit(solution)/shard_map/pallas_call | solution.py:317
  184.7 6.3 %shard_map.59 = bf16[1024,7168]{1,0:T(8,128)(2,1)} custom-call(s32[4]{0:T(128)S(1)} %pad_add_fusion.place_ref, bf16[1024,256]{1,0:T(8,128)(2,1)S(1)} %maximum_bitcast_fusion.error_ref, bf16[1024,7168]{1,0:T(8,128)(2,1)} %weights_ref.5, bf16[128,896]{1,0:T(8,128)(2,1)S(1)} %collective-permute-done.21.refs_0_, ...), custom_call_target="tpu_custom_call", output_to_operand_aliasing={{}: (7, {})} | custom-call | flops 939524096 | bytes 7340032 | tf_op jit(solution)/shard_map/pallas_call | solution.py:317
  (78 shorter events, 22.8 us)
Async XLA Ops:
  3.2 7.3 %collective-permute-start = (bf16[256,512]{0,1:T(8,128)(2,1)S(1)}, bf16[256,512]{0,1:T(8,128)(2,1)}, u32[]{:S(2)}, u32[]{:S(2)}) collective-permute-start(bf16[256,512]{0,1:T(8,128)(2,1)S(1)} %copy.27), channel_id=1, source_target_pairs={{0,2},{2,4},{4,6},{6,0},{1,3},{3,5},{5,7},{7,1},{8,10},{10,12},{12... | collective-permute-start | bytes 786440 | tf_op jit(solution)/shard_map/ppermute | solution.py:340
  4.5 49.9 %collective-permute-start.6 = (bf16[256,512]{0,1:T(8,128)(2,1)S(1)}, bf16[256,512]{0,1:T(8,128)(2,1)}, u32[]{:S(2)}, u32[]{:S(2)}) collective-permute-start(bf16[256,512]{0,1:T(8,128)(2,1)S(1)} %copy.27), channel_id=1, source_target_pairs={{0,1},{1,0},{2,3},{3,2},{4,5},{5,4},{6,7},{7,6},{8,9},{9,8},{10,11... | collective-permute-start | bytes 786440 | tf_op jit(solution)/shard_map/ppermute | solution.py:335
  12.3 8.1 %collective-permute-start.1 = (bf16[256,512]{0,1:T(8,128)(2,1)}, bf16[256,512]{0,1:T(8,128)(2,1)}, u32[]{:S(2)}, u32[]{:S(2)}) collective-permute-start(bf16[256,512]{0,1:T(8,128)(2,1)} %get-tuple-element.36), channel_id=1, source_target_pairs={{0,2},{2,4},{4,6},{6,0},{1,3},{3,5},{5,7},{7,1},{8,10},{10,12},{12... | collective-permute-start | bytes 786440 | tf_op jit(solution)/shard_map/ppermute | solution.py:340
  22.2 6.7 %collective-permute-start.2 = (bf16[256,512]{0,1:T(8,128)(2,1)}, bf16[256,512]{0,1:T(8,128)(2,1)S(1)}, u32[]{:S(2)}, u32[]{:S(2)}) collective-permute-start(bf16[256,512]{0,1:T(8,128)(2,1)} %get-tuple-element.34), channel_id=1, source_target_pairs={{0,2},{2,4},{4,6},{6,0},{1,3},{3,5},{5,7},{7,1},{8,10},{10,12},{12... | collective-permute-start | bytes 786440 | tf_op jit(solution)/shard_map/ppermute | solution.py:340
  29.7 7.0 %collective-permute-start.3 = (bf16[256,512]{0,1:T(8,128)(2,1)}, bf16[256,512]{0,1:T(8,128)(2,1)S(1)}, u32[]{:S(2)}, u32[]{:S(2)}) collective-permute-start(bf16[256,512]{0,1:T(8,128)(2,1)} %get-tuple-element.32), channel_id=1, source_target_pairs={{0,2},{2,4},{4,6},{6,0},{1,3},{3,5},{5,7},{7,1},{8,10},{10,12},{12... | collective-permute-start | bytes 786440 | tf_op jit(solution)/shard_map/ppermute | solution.py:340
  37.5 7.0 %collective-permute-start.4 = (bf16[256,512]{0,1:T(8,128)(2,1)S(1)}, bf16[256,512]{0,1:T(8,128)(2,1)S(1)}, u32[]{:S(2)}, u32[]{:S(2)}) collective-permute-start(bf16[256,512]{0,1:T(8,128)(2,1)S(1)} %get-tuple-element.30), channel_id=1, source_target_pairs={{0,2},{2,4},{4,6},{6,0},{1,3},{3,5},{5,7},{7,1},{8,10},{10,12},{12... | collective-permute-start | bytes 786440 | tf_op jit(solution)/shard_map/ppermute | solution.py:340
  37.6 19.6 %collective-permute-start.7 = (bf16[256,512]{0,1:T(8,128)(2,1)}, bf16[256,512]{0,1:T(8,128)(2,1)S(1)}, u32[]{:S(2)}, u32[]{:S(2)}) collective-permute-start(bf16[256,512]{0,1:T(8,128)(2,1)} %get-tuple-element.36), channel_id=1, source_target_pairs={{0,1},{1,0},{2,3},{3,2},{4,5},{5,4},{6,7},{7,6},{8,9},{9,8},{10,11... | collective-permute-start | bytes 786440 | tf_op jit(solution)/shard_map/ppermute | solution.py:335
  37.9 20.4 %collective-permute-start.8 = (bf16[256,512]{0,1:T(8,128)(2,1)}, bf16[256,512]{0,1:T(8,128)(2,1)S(1)}, u32[]{:S(2)}, u32[]{:S(2)}) collective-permute-start(bf16[256,512]{0,1:T(8,128)(2,1)} %get-tuple-element.34), channel_id=1, source_target_pairs={{0,1},{1,0},{2,3},{3,2},{4,5},{5,4},{6,7},{7,6},{8,9},{9,8},{10,11... | collective-permute-start | bytes 786440 | tf_op jit(solution)/shard_map/ppermute | solution.py:335
  39.1 19.9 %collective-permute-start.9 = (bf16[256,512]{0,1:T(8,128)(2,1)}, bf16[256,512]{0,1:T(8,128)(2,1)S(1)}, u32[]{:S(2)}, u32[]{:S(2)}) collective-permute-start(bf16[256,512]{0,1:T(8,128)(2,1)} %get-tuple-element.32), channel_id=1, source_target_pairs={{0,1},{1,0},{2,3},{3,2},{4,5},{5,4},{6,7},{7,6},{8,9},{9,8},{10,11... | collective-permute-start | bytes 786440 | tf_op jit(solution)/shard_map/ppermute | solution.py:335
  44.5 0.7 copy-start.6
  46.9 6.4 %collective-permute-start.5 = (bf16[256,512]{0,1:T(8,128)(2,1)S(1)}, bf16[256,512]{0,1:T(8,128)(2,1)S(1)}, u32[]{:S(2)}, u32[]{:S(2)}) collective-permute-start(bf16[256,512]{0,1:T(8,128)(2,1)S(1)} %get-tuple-element.28), channel_id=1, source_target_pairs={{0,2},{2,4},{4,6},{6,0},{1,3},{3,5},{5,7},{7,1},{8,10},{10,12},{12... | collective-permute-start | bytes 786440 | tf_op jit(solution)/shard_map/ppermute | solution.py:340
  53.3 22.6 %copy-start.4 = (bf16[256,512]{0,1:T(8,128)(2,1)}, bf16[256,512]{0,1:T(8,128)(2,1)S(1)}, u32[]{:S(2)}) copy-start(bf16[256,512]{0,1:T(8,128)(2,1)S(1)} %collective-permute-done.5) | copy-start | bytes 786436
  53.3 6.6 %collective-permute-start.10 = (bf16[256,512]{0,1:T(8,128)(2,1)S(1)}, bf16[256,512]{0,1:T(8,128)(2,1)S(1)}, u32[]{:S(2)}, u32[]{:S(2)}) collective-permute-start(bf16[256,512]{0,1:T(8,128)(2,1)S(1)} %get-tuple-element.30), channel_id=1, source_target_pairs={{0,1},{1,0},{2,3},{3,2},{4,5},{5,4},{6,7},{7,6},{8,9},{9,8},{10,11... | collective-permute-start | bytes 786440 | tf_op jit(solution)/shard_map/ppermute | solution.py:335
  54.4 9.1 %collective-permute-start.11 = (bf16[256,512]{0,1:T(8,128)(2,1)S(1)}, bf16[256,512]{0,1:T(8,128)(2,1)S(1)}, u32[]{:S(2)}, u32[]{:S(2)}) collective-permute-start(bf16[256,512]{0,1:T(8,128)(2,1)S(1)} %get-tuple-element.28), channel_id=1, source_target_pairs={{0,1},{1,0},{2,3},{3,2},{4,5},{5,4},{6,7},{7,6},{8,9},{9,8},{10,11... | collective-permute-start | bytes 786440 | tf_op jit(solution)/shard_map/ppermute | solution.py:335
  57.2 11.9 %collective-permute-start.12 = (bf16[256,512]{0,1:T(8,128)(2,1)S(1)}, bf16[256,512]{0,1:T(8,128)(2,1)S(1)}, u32[]{:S(2)}, u32[]{:S(2)}) collective-permute-start(bf16[256,512]{0,1:T(8,128)(2,1)S(1)} %collective-permute-done.5), channel_id=1, source_target_pairs={{0,1},{1,0},{2,3},{3,2},{4,5},{5,4},{6,7},{7,6},{8,9},{9,8},{10,11... | collective-permute-start | bytes 786440 | tf_op jit(solution)/shard_map/ppermute | solution.py:335
  75.8 2.0 %copy-start = (bf16[14,256,512]{2,1,0:T(8,128)(2,1)S(1)}, bf16[14,256,512]{2,1,0:T(8,128)(2,1)}, u32[]{:S(2)}) copy-start(bf16[14,256,512]{2,1,0:T(8,128)(2,1)} %copy.38.left_ref.right_ref.panel_ref) | copy-start | bytes 11010052
  77.9 12.3 %copy-start.1 = (bf16[14,256,512]{2,1,0:T(8,128)(2,1)S(1)}, bf16[14,256,512]{2,1,0:T(8,128)(2,1)}, u32[]{:S(2)}) copy-start(bf16[14,256,512]{2,1,0:T(8,128)(2,1)} %copy.38.left_ref.right_ref.panel_ref) | copy-start | bytes 11010052
  84.7 7.9 %copy-start.5 = (bf16[256,512]{0,1:T(8,128)(2,1)S(1)}, bf16[256,512]{0,1:T(8,128)(2,1)}, u32[]{:S(2)}) copy-start(bf16[256,512]{0,1:T(8,128)(2,1)} %copy-done.4) | copy-start | bytes 786436
  84.7 31.1 %collective-permute-start.13 = (f32[256,896]{1,0:T(8,128)S(1)}, f32[256,896]{1,0:T(8,128)S(1)}, u32[]{:S(2)}, u32[]{:S(2)}) collective-permute-start(f32[256,896]{1,0:T(8,128)S(1)} %shard_map.50), channel_id=1, source_target_pairs={{0,8},{8,0},{16,24},{24,16},{1,9},{9,1},{17,25},{25,17},{2,10},{10... | collective-permute-start | bytes 2752520 | tf_op jit(solution)/shard_map/ppermute | solution.py:335
  92.5 2.2 %collective-permute-start.15 = (f32[256,256]{1,0:T(8,128)S(1)}, f32[256,256]{1,0:T(8,128)}, u32[]{:S(2)}, u32[]{:S(2)}) collective-permute-start(f32[256,256]{1,0:T(8,128)S(1)} %shard_map.52), channel_id=1, source_target_pairs={{0,8},{8,0},{16,24},{24,16},{1,9},{9,1},{17,25},{25,17},{2,10},{10... | collective-permute-start | bytes 786440 | tf_op jit(solution)/shard_map/ppermute | solution.py:335
  92.6 13.0 %collective-permute-start.14 = (bf16[256,512]{0,1:T(8,128)(2,1)S(1)}, bf16[256,512]{0,1:T(8,128)(2,1)}, u32[]{:S(2)}, u32[]{:S(2)}) collective-permute-start(bf16[256,512]{0,1:T(8,128)(2,1)S(1)} %copy-done.5), channel_id=1, source_target_pairs={{0,2},{2,4},{4,6},{6,0},{1,3},{3,5},{5,7},{7,1},{8,10},{10,12},{12... | collective-permute-start | bytes 786440 | tf_op jit(solution)/shard_map/ppermute | solution.py:340
  95.6 20.1 %collective-permute-start.16 = (f32[256,256]{1,0:T(8,128)S(1)}, f32[256,256]{1,0:T(8,128)S(1)}, u32[]{:S(2)}, u32[]{:S(2)}) collective-permute-start(f32[256,256]{1,0:T(8,128)S(1)} %add.68), channel_id=1, source_target_pairs={{0,16},{8,24},{16,0},{24,8},{1,17},{9,25},{17,1},{25,9},{2,18},{10... | collective-permute-start | bytes 786440 | tf_op jit(solution)/shard_map/ppermute | solution.py:335
  96.0 2.0 %copy-start.2 = (bf16[14,256,512]{2,1,0:T(8,128)(2,1)S(1)}, bf16[14,256,512]{2,1,0:T(8,128)(2,1)}, u32[]{:S(2)}) copy-start(bf16[14,256,512]{2,1,0:T(8,128)(2,1)} %copy.38.left_ref.right_ref.panel_ref) | copy-start | bytes 11010052
  104.5 28.0 %collective-permute-start.18 = (f32[256,896]{1,0:T(8,128)S(1)}, f32[256,896]{1,0:T(8,128)S(1)}, u32[]{:S(2)}, u32[]{:S(2)}) collective-permute-start(f32[256,896]{1,0:T(8,128)S(1)} %shard_map.55), channel_id=1, source_target_pairs={{0,8},{8,0},{16,24},{24,16},{1,9},{9,1},{17,25},{25,17},{2,10},{10... | collective-permute-start | bytes 2752520 | tf_op jit(solution)/shard_map/ppermute | solution.py:335
  105.6 16.7 %collective-permute-start.17 = (bf16[256,512]{0,1:T(8,128)(2,1)}, bf16[256,512]{0,1:T(8,128)(2,1)S(1)}, u32[]{:S(2)}, u32[]{:S(2)}) collective-permute-start(bf16[256,512]{0,1:T(8,128)(2,1)} %collective-permute-done.14), channel_id=1, source_target_pairs={{0,2},{2,4},{4,6},{6,0},{1,3},{3,5},{5,7},{7,1},{8,10},{10,12},{12... | collective-permute-start | bytes 786440 | tf_op jit(solution)/shard_map/ppermute | solution.py:340
  115.8 7.8 %copy-start.3 = (bf16[5,256,512]{1,2,0:T(8,128)(2,1)S(1)}, bf16[5,256,512]{1,2,0:T(8,128)(2,1)}, u32[]{:S(2)}) copy-start(bf16[5,256,512]{1,2,0:T(8,128)(2,1)} %get-tuple-element.39) | copy-start | bytes 3932164
  122.3 21.7 %collective-permute-start.19 = (f32[256,896]{1,0:T(8,128)S(1)}, f32[256,896]{1,0:T(8,128)S(1)}, u32[]{:S(2)}, u32[]{:S(2)}) collective-permute-start(f32[256,896]{1,0:T(8,128)S(1)} %shard_map.51), channel_id=1, source_target_pairs={{0,16},{8,24},{16,0},{24,8},{1,17},{9,25},{17,1},{25,9},{2,18},{10... | collective-permute-start | bytes 2752520 | tf_op jit(solution)/shard_map/ppermute | solution.py:335
  145.0 25.4 %collective-permute-start.28 = (bf16[512,896]{1,0:T(8,128)(2,1)S(1)}, bf16[512,896]{1,0:T(8,128)(2,1)S(1)}, u32[]{:S(2)}, u32[]{:S(2)}) collective-permute-start(bf16[512,896]{1,0:T(8,128)(2,1)S(1)} %get-tuple-element.24.refs_0_), channel_id=1, source_target_pairs={{0,8},{8,0},{16,24},{24,16},{1,9},{9,1},{17,25},{25,17},{2,10},{10... | collective-permute-start | bytes 2752520 | tf_op jit(solution)/shard_map/ppermute | solution.py:335
  146.3 12.1 %collective-permute-start.22 = (bf16[256,896]{1,0:T(8,128)(2,1)S(1)}, bf16[256,896]{1,0:T(8,128)(2,1)S(1)}, u32[]{:S(2)}, u32[]{:S(2)}) collective-permute-start(bf16[256,896]{1,0:T(8,128)(2,1)S(1)} %get-tuple-element.23), channel_id=1, source_target_pairs={{0,16},{8,24},{16,0},{24,8},{1,17},{9,25},{17,1},{25,9},{2,18},{10... | collective-permute-start | bytes 1376264 | tf_op jit(solution)/shard_map/ppermute | solution.py:335
  147.5 11.8 %collective-permute-start.20 = (bf16[256,896]{1,0:T(8,128)(2,1)S(1)}, bf16[256,896]{1,0:T(8,128)(2,1)S(1)}, u32[]{:S(2)}, u32[]{:S(2)}) collective-permute-start(bf16[256,896]{1,0:T(8,128)(2,1)S(1)} %get-tuple-element.23), channel_id=1, source_target_pairs={{0,1},{1,0},{2,3},{3,2},{4,5},{5,4},{6,7},{7,6},{8,9},{9,8},{10,11... | collective-permute-start | bytes 1376264 | tf_op jit(solution)/shard_map/ppermute | solution.py:335
  158.4 18.1 %collective-permute-start.26 = (bf16[256,896]{1,0:T(8,128)(2,1)S(1)}, bf16[256,896]{1,0:T(8,128)(2,1)}, u32[]{:S(2)}, u32[]{:S(2)}) collective-permute-start(bf16[256,896]{1,0:T(8,128)(2,1)S(1)} %collective-permute-done.22.refs_0_), channel_id=1, source_target_pairs={{0,8},{8,0},{16,24},{24,16},{1,9},{9,1},{17,25},{25,17},{2,10},{10... | collective-permute-start | bytes 1376264 | tf_op jit(solution)/shard_map/ppermute | solution.py:335
  159.2 17.3 %collective-permute-start.27 = (bf16[256,896]{1,0:T(8,128)(2,1)S(1)}, bf16[256,896]{1,0:T(8,128)(2,1)}, u32[]{:S(2)}, u32[]{:S(2)}) collective-permute-start(bf16[256,896]{1,0:T(8,128)(2,1)S(1)} %collective-permute-done.20.refs_1_), channel_id=1, source_target_pairs={{0,8},{8,0},{16,24},{24,16},{1,9},{9,1},{17,25},{25,17},{2,10},{10... | collective-permute-start | bytes 1376264 | tf_op jit(solution)/shard_map/ppermute | solution.py:335
  161.1 7.6 %collective-permute-start.21 = (bf16[128,896]{1,0:T(8,128)(2,1)}, bf16[128,896]{1,0:T(8,128)(2,1)S(1)}, u32[]{:S(2)}, u32[]{:S(2)}) collective-permute-start(bf16[128,896]{1,0:T(8,128)(2,1)} %slice.27), channel_id=1, source_target_pairs={{0,16},{8,24},{16,0},{24,8},{1,17},{9,25},{17,1},{25,9},{2,18},{10... | collective-permute-start | bytes 688136 | tf_op jit(solution)/shard_map/ppermute | solution.py:335
  162.1 7.2 %collective-permute-start.23 = (bf16[128,896]{1,0:T(8,128)(2,1)}, bf16[128,896]{1,0:T(8,128)(2,1)}, u32[]{:S(2)}, u32[]{:S(2)}) collective-permute-start(bf16[128,896]{1,0:T(8,128)(2,1)} %slice.28), channel_id=1, source_target_pairs={{0,1},{1,0},{2,3},{3,2},{4,5},{5,4},{6,7},{7,6},{8,9},{9,8},{10,11... | collective-permute-start | bytes 688136 | tf_op jit(solution)/shard_map/ppermute | solution.py:335
  168.7 16.1 %collective-permute-start.24 = (bf16[128,896]{1,0:T(8,128)(2,1)S(1)}, bf16[128,896]{1,0:T(8,128)(2,1)S(1)}, u32[]{:S(2)}, u32[]{:S(2)}) collective-permute-start(bf16[128,896]{1,0:T(8,128)(2,1)S(1)} %collective-permute-done.21.refs_0_), channel_id=1, source_target_pairs={{0,8},{8,0},{16,24},{24,16},{1,9},{9,1},{17,25},{25,17},{2,10},{10... | collective-permute-start | bytes 688136 | tf_op jit(solution)/shard_map/ppermute | solution.py:335
  169.3 15.4 %collective-permute-start.25 = (bf16[128,896]{1,0:T(8,128)(2,1)}, bf16[128,896]{1,0:T(8,128)(2,1)S(1)}, u32[]{:S(2)}, u32[]{:S(2)}) collective-permute-start(bf16[128,896]{1,0:T(8,128)(2,1)} %collective-permute-done.23.refs_1_), channel_id=1, source_target_pairs={{0,8},{8,0},{16,24},{24,16},{1,9},{9,1},{17,25},{25,17},{2,10},{10... | collective-permute-start | bytes 688136 | tf_op jit(solution)/shard_map/ppermute | solution.py:335

commit v4 on v0

v4 whole, which is shorter than its diff:
```python
import functools

import jax
import jax.numpy as jnp
from jax import lax
from jax.experimental import pallas as pl
from jax.experimental.pallas import tpu as pltpu
from jax.sharding import PartitionSpec as P

PANEL = 256
QBLOCK = 128
ROUNDS = 4
F32 = jnp.float32
BF16 = jnp.bfloat16
MIB = 1 << 20


def dot_high(left, right):
    return jnp.dot(left, right, precision=lax.Precision.HIGHEST, preferred_element_type=F32)


def panel_kernel(place_ref, quant_ref, exps_ref, out_ref):
    scale = jnp.exp2(exps_ref[:, : PANEL // QBLOCK].astype(F32))
    rows = scale.shape[0]
    wide = [
        jnp.broadcast_to(scale[:, c : c + 1], (rows, QBLOCK)) for c in range(PANEL // QBLOCK)
    ]
    acts = quant_ref[...].astype(F32) * jnp.concatenate(wide, axis=1)
    out_ref[...] = acts.T.astype(BF16)


def panel_piece(quantized, exponents, at, piece):
    blocks = exponents.shape[1]
    return pl.pallas_call(
        panel_kernel,
        out_shape=jax.ShapeDtypeStruct((PANEL, piece), BF16),
        grid_spec=pltpu.PrefetchScalarGridSpec(
            num_scalar_prefetch=1,
            grid=(1,),
            in_specs=[
                pl.BlockSpec((piece, PANEL), lambda i, place: (place[0], 0)),
                pl.BlockSpec((piece, blocks), lambda i, place: (place[0], 0)),
            ],
            out_specs=pl.BlockSpec((PANEL, piece), lambda i, place: (0, 0)),
        ),
        compiler_params=pltpu.CompilerParams(vmem_limit_bytes=48 * MIB),
        cost_estimate=pl.CostEstimate(
            flops=piece * PANEL, bytes_accessed=4 * piece * PANEL, transcendentals=0
        ),
    )(at.reshape(1).astype(jnp.int32), quantized, exponents)


def inverse_kernel(head_ref, out_ref, pair_ref):
    size = PANEL
    rows = lax.broadcasted_iota(jnp.int32, (size, size), 0)
    cols = lax.broadcasted_iota(jnp.int32, (size, size), 1)
    eye = jnp.where(rows == cols, 1.0, 0.0).astype(F32)
    head = head_ref[...]
    damping = 0.01 * (jnp.sum(head * eye) / size)
    block = head + damping * eye
    high = jnp.max(jnp.sum(jnp.abs(block), axis=0))
    start = 2.0 / (high + damping)
    spread = (high - damping) / (high + damping)
    pair_ref[:size] = start * eye
    pair_ref[size:] = start * block

    def more(spread):
        return spread > 1e-3

    def step(spread):
        square = spread * spread
        gain = 2.0 / (2.0 - square)
        turn = gain * (2.0 * eye - pair_ref[size:])
        pair_ref[...] = dot_high(pair_ref[...], turn)
        return square / (2.0 - square)

    lax.while_loop(more, step, spread)
    out = pair_ref[:size]
    for _ in range(2):
        out = out + dot_high(out, eye - dot_high(block, out))
    out_ref[...] = out


def invert(head):
    return pl.pallas_call(
        inverse_kernel,
        out_shape=jax.ShapeDtypeStruct((PANEL, PANEL), F32),
        scratch_shapes=[pltpu.VMEM((2 * PANEL, PANEL), F32)],
        compiler_params=pltpu.CompilerParams(vmem_limit_bytes=32 * MIB),
        cost_estimate=pl.CostEstimate(
            flops=28 * 12 * PANEL**3, bytes_accessed=8 * PANEL * PANEL, transcendentals=0
        ),
    )(head)


def gains_kernel(place_ref, inverse_ref, first_ref, second_ref, third_ref, high_ref, pair_ref):
    total = first_ref[...] + second_ref[...] + third_ref[...]
    gains = dot_high(inverse_ref[...], total)
    rows = lax.broadcasted_iota(jnp.int32, gains.shape, 0)
    cols = lax.broadcasted_iota(jnp.int32, gains.shape, 1) + place_ref[0]
    gains = jnp.where(cols < PANEL, jnp.where(rows == cols, -1.0, 0.0), gains)
    high = gains.astype(BF16)
    high_ref[...] = high
    pair_ref[:PANEL] = high
    pair_ref[PANEL:] = (gains - high.astype(F32)).astype(BF16)


def make_gains(inverse, parts, start):
    width = parts[0].shape[1]
    vmem = pl.BlockSpec(memory_space=pltpu.VMEM)
    return pl.pallas_call(
        gains_kernel,
        out_shape=(
            jax.ShapeDtypeStruct((PANEL, width), BF16),
            jax.ShapeDtypeStruct((2 * PANEL, width), BF16),
        ),
        in_specs=[pl.BlockSpec(memory_space=pltpu.SMEM)] + [vmem] * 4,
        compiler_params=pltpu.CompilerParams(vmem_limit_bytes=32 * MIB),
        cost_estimate=pl.CostEstimate(
            flops=12 * PANEL * PANEL * width, bytes_accessed=16 * PANEL * width, transcendentals=0
        ),
    )(start.reshape(1).astype(jnp.int32), inverse, *parts)


def swap(x, axis, bit):
    size = lax.axis_size(axis)
    return lax.ppermute(x, axis, [(i, i ^ bit) for i in range(size)])


def forward(x, axis):
    size = lax.axis_size(axis)
    return lax.ppermute(x, axis, [(i, i + 1) for i in range(size - 1)])


def after(x, *others):
    return lax.optimization_barrier((x, *others))[0]


def dot(left, right):
    return jnp.dot(left, right, preferred_element_type=F32)


def shards(quantized, exponents, weights, keep_mask):
    tokens, cols = quantized.shape
    toks, rows, feats = lax.axis_size("tok"), lax.axis_size("row"), lax.axis_size("feat")
    tok, row, feat = lax.axis_index("tok"), lax.axis_index("row"), lax.axis_index("feat")
    width = cols // (toks * rows)
    root = feat == 0

    piece = tokens // rows // ROUNDS
    sources = [
        panel_piece(quantized, exponents, row * ROUNDS + c, piece) for c in range(ROUNDS)
    ]
    panel_weights = after(weights[:, :PANEL], sources[0])
    error = jnp.where(keep_mask == 0, panel_weights, jnp.zeros((), BF16)).T
    extras = -(-error.shape[1] // piece)
    error = jnp.pad(error, ((0, 0), (0, extras * piece - error.shape[1])))
    sources += [error[:, i * piece : (i + 1) * piece] for i in range(extras)]
    panel_rounds = ROUNDS + feats - 1
    held, swapped = [jnp.where(root, sources[0], jnp.zeros((), BF16))], []

    def advance(*others):
        r = len(held)
        x = forward(after(held[-1], *others) if others else held[-1], "feat")
        held.append(jnp.where(root, sources[r], x) if r < len(sources) else x)

    for r in range(1, panel_rounds):
        swapped.append(swap(held[r - 1], "row", 1))
        advance(*swapped[r - 2 : r - 1])
    swapped.append(swap(held[-1], "row", 1))

    scale = jnp.exp2(after(exponents, sources[0]).astype(F32)).astype(BF16)
    acts = []
    for k, link in zip((3, 2, 1, 0), (1, 2, 3, 4)):
        col = row * toks + (tok ^ k)
        block = (col * width + lax.broadcasted_iota(jnp.int32, (1, width), 1)) // QBLOCK
        spread = lax.broadcasted_iota(jnp.int32, (scale.shape[1], width), 0) == block
        wide = dot(after(scale, held[link]), spread.astype(BF16)).astype(BF16)
        acts.insert(0, lax.dynamic_slice_in_dim(quantized, col * width, width, 1) * wide)

    def window(rounds, first, count):
        rounds = jnp.concatenate(rounds, axis=1)
        return lax.dynamic_slice_in_dim(rounds, first * piece, count * piece, 1)

    own = window(held[:panel_rounds], feat, ROUNDS)
    other = window(swapped, feat, ROUNDS)
    panel = jnp.concatenate(
        [jnp.where(row == 0, own, other), jnp.where(row == 0, other, own)], axis=1
    )

    head = lax.dot_general(
        panel, panel, (((1,), (1,)), ((), ())), preferred_element_type=F32
    )
    head = head + swap(head, "tok", 1)
    block3 = dot(panel, acts[3])
    from3 = swap(block3, "tok", 1)
    head = head + swap(head, "tok", 2)
    advance(block3)
    block2 = dot(panel, acts[2]) + from3
    block2, head = lax.optimization_barrier((block2, head))
    fromx = swap(block2, "tok", 2)
    block1 = dot(panel, acts[1])
    from1 = swap(block1, "tok", 1)
    block0 = dot(panel, acts[0])
    while len(held) < len(sources) + feats - 1:
        advance(block1)
    inverse = invert(after(head, held[-1]))
    error = window(held[ROUNDS:], feat, extras)[:, : weights.shape[0]].T
    inverse, error = lax.optimization_barrier((inverse, error))
    start = jnp.where(root, (row * toks + tok) * width, PANEL)
    high, pair = make_gains(inverse, (block0, from1, fromx), start)

    half = PANEL // 2

    def update(out, gain, tok_bits, row_bit):
        start = ((row ^ row_bit) * toks + (tok ^ tok_bits)) * width
        total = lax.dynamic_slice_in_dim(weights, start, width, 1).astype(F32)
        for top in range(0, gain.shape[0], PANEL):
            total = total + dot(error, gain[top : top + PANEL])
        return lax.dynamic_update_slice_in_dim(out, total.astype(BF16), start, 1)

    near = swap(pair, "tok", 1)
    in_x, in_y = swap(high, "tok", 2), swap(high, "row", 1)
    out = jnp.zeros_like(weights)
    out = update(out, pair, 0, 0)
    out = update(out, near, 1, 0)
    in_x, in_y, out = lax.optimization_barrier((in_x, in_y, out))
    far = jnp.concatenate([swap(in_y[:half], "tok", 2), swap(in_x[half:], "row", 1)], axis=0)
    near_x, near_y = swap(in_x, "tok", 1), swap(in_y, "tok", 1)
    out = update(out, in_x, 2, 0)
    out = update(out, in_y, 0, 1)
    far, out = lax.optimization_barrier((far, out))
    near_far = swap(far, "tok", 1)
    out = update(out, near_x, 3, 0)
    out = update(out, near_y, 1, 1)
    out = update(out, far, 2, 1)
    return update(out, near_far, 3, 1)


def solution(mesh):
    placed = (
        P("tok", "feat"),
        P("tok", "feat"),
        P(("tok", "row"), "feat"),
        P(("tok", "row"), None),
    )
    return jax.shard_map(
        shards, mesh=mesh, in_specs=placed, out_specs=P(("tok", "row"), "feat"), check_vma=False
    )
```

time: 1430 us -> 177 us (0.12)
  the two profiles are of different devices: /device:TPU:9 before, /device:TPU:1 now
where the time goes in v4:
time: 177 us; the launch traced here: 176 us
  matrix products  62.8 us (35%)
  starting transfers between devices  53.2 us (30%)
  waiting for transfers between devices  19.9 us (11%)
  local copies, waits for them, and re-layouts  19.8 us (11%)
  Pallas kernels  14.1 us (8%)
  other arithmetic  6.01 us (3%)
    dot_general x14, matrix products, dot(): return jnp.dot(left, right, preferred_element_type=F32)  62 us
    ppermute x8, starting transfers between devices, forward(): return lax.ppermute(x, axis, [(i, i + 1) for i in range(size - 1)])  29.8 us
    ppermute x20, starting transfers between devices, swap(): return lax.ppermute(x, axis, [(i, i ^ bit) for i in range(size)])  23.4 us
    ppermute x8, waiting for transfers between devices, forward(): return lax.ppermute(x, axis, [(i, i + 1) for i in range(size - 1)])  10.4 us
    ppermute x20, waiting for transfers between devices, swap(): return lax.ppermute(x, axis, [(i, i ^ bit) for i in range(size)])  9.43 us
    pallas_call x1, Pallas kernels, invert(): pl.pallas_call(inverse_kernel, out_shape=jax.ShapeDtypeStruct((PANEL, PAN...  7.86 us
    unnamed x36, local copies, waits for them, and re-layouts  7.73 us
    broadcast_in_dim x1, local copies, waits for them, and re-layouts, shards(): out = jnp.zeros_like(weights)  7.3 us
  transfers between devices with their start and end apart: 28, of which 10 were waited for; matrix products, arithmetic and copies ran while one was open for 41% of the time, Pallas kernels for 7%

profile of v4, /device:TPU:1, one launch (start us, length us, event | category | flops | bytes accessed | tf_op | source)
XLA Modules:
  0.0 176.2 jit_solution(12850652479013265058)
XLA Ops:
  0.0 1.8 %copy.5.exps_ref = s32[4096,56]{1,0:T(8,128)S(1)} copy(s32[4096,56]{0,1:T(8,128)} %param.5) | data formatting | bytes 1835008 | tf_op args[1]
  1.8 1.2 shard_map.46
  3.8 4.0 %collective-permute-start = (bf16[256,512]{1,0:T(8,128)(2,1)S(1)}, bf16[256,512]{1,0:T(8,128)(2,1)S(1)}, u32[]{:S(2)}, u32[]{:S(2)}) collective-permute-start(bf16[256,512]{1,0:T(8,128)(2,1)S(1)} %get-tuple-element.66), channel_id=1, source_target_pairs={{0,2},{2,4},{4,6},{1,3},{3,5},{5,7},{8,10},{10,12},{12,14},{9,11},... | collective-permute-start | bytes 786440 | tf_op jit(solution)/shard_map/ppermute | solution.py:132
  7.8 1.3 collective-permute-start.1
  9.1 1.2 shard_map.47
  10.4 2.4 %collective-permute-done = bf16[256,512]{1,0:T(8,128)(2,1)S(1)} collective-permute-done((bf16[256,512]{1,0:T(8,128)(2,1)S(1)}, bf16[256,512]{1,0:T(8,128)(2,1)S(1)}, u32[]{:S(2)}, u32[]{:S(2)}) %collective-permute-start) | collective-permute-done | bytes 262176 | tf_op jit(solution)/shard_map/ppermute | solution.py:132
  13.6 1.2 collective-permute-done.1
  14.8 3.2 %collective-permute-start.2 = (bf16[256,512]{1,0:T(8,128)(2,1)S(1)}, bf16[256,512]{1,0:T(8,128)(2,1)S(1)}, u32[]{:S(2)}, u32[]{:S(2)}) collective-permute-start(bf16[256,512]{1,0:T(8,128)(2,1)S(1)} %get-tuple-element.30), channel_id=1, source_target_pairs={{0,2},{2,4},{4,6},{1,3},{3,5},{5,7},{8,10},{10,12},{12,14},{9,11},... | collective-permute-start | bytes 786440 | tf_op jit(solution)/shard_map/ppermute | solution.py:132
  18.0 1.3 collective-permute-start.3
  19.3 1.3 shard_map.48
  22.5 1.2 collective-permute-start.5
  23.8 4.8 %collective-permute-start.4 = (bf16[256,512]{1,0:T(8,128)(2,1)}, bf16[256,512]{1,0:T(8,128)(2,1)}, u32[]{:S(2)}, u32[]{:S(2)}) collective-permute-start(bf16[256,512]{1,0:T(8,128)(2,1)} %get-tuple-element.31), channel_id=1, source_target_pairs={{0,2},{2,4},{4,6},{1,3},{3,5},{5,7},{8,10},{10,12},{12,14},{9,11},... | collective-permute-start | bytes 786440 | tf_op jit(solution)/shard_map/ppermute | solution.py:132
  29.5 1.3 shard_map.49
  31.0 1.6 copy.9
  33.4 3.9 %collective-permute-start.6 = (bf16[256,512]{1,0:T(8,128)(2,1)S(1)}, bf16[256,512]{1,0:T(8,128)(2,1)S(1)}, u32[]{:S(2)}, u32[]{:S(2)}) collective-permute-start(bf16[256,512]{1,0:T(8,128)(2,1)S(1)} %get-tuple-element.33), channel_id=1, source_target_pairs={{0,2},{2,4},{4,6},{1,3},{3,5},{5,7},{8,10},{10,12},{12,14},{9,11},... | collective-permute-start | bytes 786440 | tf_op jit(solution)/shard_map/ppermute | solution.py:132
  37.8 2.8 %collective-permute-done.6 = bf16[256,512]{1,0:T(8,128)(2,1)S(1)} collective-permute-done((bf16[256,512]{1,0:T(8,128)(2,1)S(1)}, bf16[256,512]{1,0:T(8,128)(2,1)S(1)}, u32[]{:S(2)}, u32[]{:S(2)}) %collective-permute-start.6) | collective-permute-done | bytes 262176 | tf_op jit(solution)/shard_map/ppermute | solution.py:132
  40.7 2.0 %collective-permute-done.7 = bf16[256,512]{1,0:T(8,128)(2,1)S(1)} collective-permute-done((bf16[256,512]{1,0:T(8,128)(2,1)S(1)}, bf16[256,512]{1,0:T(8,128)(2,1)S(1)}, u32[]{:S(2)}, u32[]{:S(2)}) %collective-permute-start.7) | collective-permute-done | bytes 262176 | tf_op jit(solution)/shard_map/ppermute | solution.py:127
  42.7 3.2 %collective-permute-start.8 = (bf16[256,512]{1,0:T(8,128)(2,1)S(1)}, bf16[256,512]{1,0:T(8,128)(2,1)S(1)}, u32[]{:S(2)}, u32[]{:S(2)}) collective-permute-start(bf16[256,512]{1,0:T(8,128)(2,1)S(1)} %get-tuple-element.34), channel_id=1, source_target_pairs={{0,2},{2,4},{4,6},{1,3},{3,5},{5,7},{8,10},{10,12},{12,14},{9,11},... | collective-permute-start | bytes 786440 | tf_op jit(solution)/shard_map/ppermute | solution.py:132
  47.3 1.9 %collective-permute-done.8 = bf16[256,512]{1,0:T(8,128)(2,1)S(1)} collective-permute-done((bf16[256,512]{1,0:T(8,128)(2,1)S(1)}, bf16[256,512]{1,0:T(8,128)(2,1)S(1)}, u32[]{:S(2)}, u32[]{:S(2)}) %collective-permute-start.8) | collective-permute-done | bytes 262176 | tf_op jit(solution)/shard_map/ppermute | solution.py:132
  49.3 2.0 %collective-permute-done.9 = bf16[256,512]{1,0:T(8,128)(2,1)S(1)} collective-permute-done((bf16[256,512]{1,0:T(8,128)(2,1)S(1)}, bf16[256,512]{1,0:T(8,128)(2,1)S(1)}, u32[]{:S(2)}, u32[]{:S(2)}) %collective-permute-start.9) | collective-permute-done | bytes 262176 | tf_op jit(solution)/shard_map/ppermute | solution.py:127
  51.3 3.7 %collective-permute-start.10 = (bf16[256,512]{1,0:T(8,128)(2,1)S(1)}, bf16[256,512]{1,0:T(8,128)(2,1)}, u32[]{:S(2)}, u32[]{:S(2)}) collective-permute-start(bf16[256,512]{1,0:T(8,128)(2,1)S(1)} %get-tuple-element.35), channel_id=1, source_target_pairs={{0,2},{2,4},{4,6},{1,3},{3,5},{5,7},{8,10},{10,12},{12,14},{9,11},... | collective-permute-start | bytes 786440 | tf_op jit(solution)/shard_map/ppermute | solution.py:132
  55.6 2.3 %collective-permute-done.10 = bf16[256,512]{1,0:T(8,128)(2,1)} collective-permute-done((bf16[256,512]{1,0:T(8,128)(2,1)S(1)}, bf16[256,512]{1,0:T(8,128)(2,1)}, u32[]{:S(2)}, u32[]{:S(2)}) %collective-permute-start.10) | collective-permute-done | bytes 262176 | tf_op jit(solution)/shard_map/ppermute | solution.py:132
  58.1 2.2 %collective-permute-done.11 = bf16[256,512]{1,0:T(8,128)(2,1)S(1)} collective-permute-done((bf16[256,512]{1,0:T(8,128)(2,1)S(1)}, bf16[256,512]{1,0:T(8,128)(2,1)S(1)}, u32[]{:S(2)}, u32[]{:S(2)}) %collective-permute-start.11) | collective-permute-done | bytes 262176 | tf_op jit(solution)/shard_map/ppermute | solution.py:127
  61.4 1.9 %collective-permute-done.12 = bf16[256,512]{1,0:T(8,128)(2,1)S(1)} collective-permute-done((bf16[256,512]{1,0:T(8,128)(2,1)}, bf16[256,512]{1,0:T(8,128)(2,1)S(1)}, u32[]{:S(2)}, u32[]{:S(2)}) %collective-permute-start.12) | collective-permute-done | bytes 262176 | tf_op jit(solution)/shard_map/ppermute | solution.py:127
  65.1 8.3 %fusion.8 = f32[256,896]{1,0:T(8,128)} fusion(bf16[4096,7168]{1,0:T(8,128)(2,1)} %quant_ref.7, s32[]{:T(128)S(6)} %select_n.142, bf16[4096,56]{0,1:T(8,128)(2,1)S(1)} %copy-done.7, s32[896]{0:T(1024)S(1)} %add_select_fusion.2, bf16[256,2048]{1,0:T(8,128)(2,1)S(1)} %get-tuple-element.68, bf16[256,2048]{1,0:T(8,128)(2,1)S(1)} %get-tuple-element.67), kind=kOutput, calls=%fused_computation.8 | convolution fusion | flops 2312684544 | bytes 10817028 | tf_op jit(solution)/shard_map/dot_general | solution.py:140
  73.5 9.9 %collective-permute-start.13 = (f32[256,896]{1,0:T(8,128)}, f32[256,896]{1,0:T(8,128)}, u32[]{:S(2)}, u32[]{:S(2)}) collective-permute-start(f32[256,896]{1,0:T(8,128)} %fusion.8), channel_id=1, source_target_pairs={{0,8},{8,0},{16,24},{24,16},{1,9},{9,1},{17,25},{25,17},{2,10},{10... | collective-permute-start | bytes 2752520 | tf_op jit(solution)/shard_map/ppermute | solution.py:127
  83.4 4.9 %collective-permute-start.16 = (bf16[256,512]{1,0:T(8,128)(2,1)}, bf16[256,512]{1,0:T(8,128)(2,1)}, u32[]{:S(2)}, u32[]{:S(2)}) collective-permute-start(bf16[256,512]{1,0:T(8,128)(2,1)} %collective-permute-done.10), channel_id=1, source_target_pairs={{0,2},{2,4},{4,6},{1,3},{3,5},{5,7},{8,10},{10,12},{12,14},{9,11},... | collective-permute-start | bytes 786440 | tf_op jit(solution)/shard_map/ppermute | solution.py:132
  88.4 1.3 collective-permute-start.15
  89.7 8.3 %fusion.4 = f32[256,896]{1,0:T(8,128)} fusion(bf16[4096,7168]{1,0:T(8,128)(2,1)} %quant_ref.7, s32[]{:T(128)S(6)} %select_n.144, bf16[4096,56]{0,1:T(8,128)(2,1)S(1)} %copy-done.7, s32[896]{0:T(1024)S(1)} %add_select_fusion.1, bf16[256,2048]{1,0:T(8,128)(2,1)S(1)} %get-tuple-element.68, bf16[256,2048]{1,0:T(8,128)(2,1)S(1)} %get-tuple-element.67), kind=kOutput, calls=%fused_computation.4 | convolution fusion | flops 2312684544 | bytes 10817028 | tf_op jit(solution)/shard_map/dot_general | solution.py:140
  98.0 1.1 collective-permute-start.18
  99.1 2.0 %collective-permute-start.17 = (bf16[256,512]{1,0:T(8,128)(2,1)}, bf16[256,512]{1,0:T(8,128)(2,1)}, u32[]{:S(2)}, u32[]{:S(2)}) collective-permute-start(bf16[256,512]{1,0:T(8,128)(2,1)} %collective-permute-done.16), channel_id=1, source_target_pairs={{0,2},{2,4},{4,6},{1,3},{3,5},{5,7},{8,10},{10,12},{12,14},{9,11},... | collective-permute-start | bytes 786440 | tf_op jit(solution)/shard_map/ppermute | solution.py:132
  102.2 8.7 %fusion.32 = f32[256,896]{1,0:T(8,128)} fusion(f32[256,896]{1,0:T(8,128)} %collective-permute-done.13, bf16[4096,7168]{1,0:T(8,128)(2,1)} %quant_ref.7, s32[]{:T(128)S(6)} %select_n.140, bf16[4096,56]{0,1:T(8,128)(2,1)} %exponential_convert_fusion, s32[896]{0:T(1024)S(1)} %add_select_fusion.3, bf16[256,2048]{1,0:T(8,128)(2,1)S(1)} %get-tuple-element.68, ...), kind=kOutput, calls=%fused_computation.37 | convolution fusion | flops 2312913920 | bytes 11734532 | tf_op jit(solution)/shard_map/dot_general | solution.py:140
  111.3 8.9 %fusion.first_ref = f32[256,896]{1,0:T(8,128)} fusion(bf16[4096,7168]{1,0:T(8,128)(2,1)} %quant_ref.7, s32[]{:T(128)S(6)} %select_n.147, bf16[4096,56]{0,1:T(8,128)(2,1)} %exponential_convert_fusion, s32[896]{0:T(1024)S(1)} %add_select_fusion, bf16[256,2048]{1,0:T(8,128)(2,1)} %copy-done.3, bf16[256,2048]{1,0:T(8,128)(2,1)S(1)} %get-tuple-element.67), kind=kOutput, calls=%fused_computation | convolution fusion | flops 2312684544 | bytes 10817028 | tf_op jit(solution)/shard_map/dot_general | solution.py:140
  120.2 1.7 constant_dynamic-update-slice_fusion.15
  121.8 1.7 constant_dynamic-update-slice_fusion.14
  123.5 1.9 %dynamic-slice_bitcast_fusion = bf16[1024,256]{0,1:T(8,128)(2,1)} fusion(bf16[256,2560]{1,0:T(8,128)(2,1)} %constant_dynamic-update-slice_fusion.14, s32[]{:T(128)S(6)} %select_n.146), kind=kLoop, calls=%fused_computation.43 | loop fusion | bytes 1048580 | tf_op jit(solution)/shard_map/transpose | solution.py:208
  125.4 7.9 %shard_map.50.inverse_ref = f32[256,256]{1,0:T(8,128)S(1)} custom-call(f32[256,256]{1,0:T(8,128)S(1)} %add.203.head_ref), custom_call_target="tpu_custom_call" | custom-call | flops 5637144576 | bytes 524288 | tf_op jit(solution)/shard_map/pallas_call | solution.py:85
  136.3 3.6 %fusion.46 = f32[1024,896]{1,0:T(8,128)} fusion(bf16[1024,256]{0,1:T(8,128)(2,1)} %dynamic-slice_bitcast_fusion, bf16[512,896]{1,0:T(8,128)(2,1)S(1)} %get-tuple-element.49), kind=kOutput, calls=%fused_computation.51 | convolution fusion | flops 469762048 | bytes 4653056 | tf_op jit(solution)/shard_map/dot_general | solution.py:140
  139.9 7.3 %broadcast_in_dim.13 = bf16[1024,7168]{1,0:T(8,128)(2,1)} broadcast(bf16[]{:T(256)} %constant.62.clone.1), dimensions={} | broadcast | bytes 14680066 | tf_op jit(solution)/shard_map/broadcast_in_dim | solution.py:224
  147.2 4.7 %fusion.24 = bf16[1024,7168]{1,0:T(8,128)(2,1)} fusion(bf16[1024,7168]{1,0:T(8,128)(2,1)} %broadcast_in_dim.13, s32[]{:T(128)S(6)} %select_n.147, f32[1024,896]{1,0:T(8,128)} %fusion.46, bf16[1024,7168]{1,0:T(8,128)(2,1)} %param.6, bf16[1024,256]{0,1:T(8,128)(2,1)S(1)} %copy-done.1, bf16[512,896]{1,0:T(8,128)(2,1)S(1)} %get-tuple-element.49), kind=kOutput, calls=%fused_computation.29 | convolution fusion | flops 473432064 | bytes 8323076 | tf_op jit(solution)/shard_map/dot_general | solution.py:140
  152.7 3.7 %fusion.25 = bf16[1024,7168]{1,0:T(8,128)(2,1)} fusion(bf16[1024,7168]{1,0:T(8,128)(2,1)} %fusion.24, s32[]{:T(128)S(6)} %select_n.144, f32[1024,896]{1,0:T(8,128)S(1)} %fusion.40, bf16[1024,7168]{1,0:T(8,128)(2,1)} %param.6, bf16[1024,256]{0,1:T(8,128)(2,1)S(1)} %copy-done.1, bf16[512,896]{1,0:T(8,128)(2,1)S(1)} %collective-permute-done.22), kind=kOutput, calls=%fused_computation.30 | convolution fusion | flops 473432064 | bytes 8323076 | tf_op jit(solution)/shard_map/dot_general | solution.py:140
  158.2 1.2 collective-permute-start.24
  160.0 3.6 %fusion.26 = bf16[1024,7168]{1,0:T(8,128)(2,1)} fusion(bf16[1024,7168]{1,0:T(8,128)(2,1)} %fusion.25, s32[]{:T(128)S(6)} %select_n.140, bf16[1024,256]{0,1:T(8,128)(2,1)S(1)} %copy-done.1, bf16[256,896]{1,0:T(8,128)(2,1)} %collective-permute-done.20, bf16[1024,7168]{1,0:T(8,128)(2,1)} %param.6), kind=kOutput, calls=%fused_computation.31 | convolution fusion | flops 472514560 | bytes 4653060 | tf_op jit(solution)/shard_map/dot_general | solution.py:140
  163.6 3.5 %fusion.27 = bf16[1024,7168]{1,0:T(8,128)(2,1)} fusion(bf16[1024,7168]{1,0:T(8,128)(2,1)} %fusion.26, s32[]{:T(128)S(6)} %select_n.149, bf16[1024,256]{0,1:T(8,128)(2,1)S(1)} %copy-done.1, bf16[256,896]{1,0:T(8,128)(2,1)S(1)} %collective-permute-done.21, bf16[1024,7168]{1,0:T(8,128)(2,1)} %param.6), kind=kOutput, calls=%fused_computation.32 | convolution fusion | flops 472514560 | bytes 4653060 | tf_op jit(solution)/shard_map/dot_general | solution.py:140
  168.3 2.0 %fusion.28 = bf16[1024,7168]{1,0:T(8,128)(2,1)} fusion(bf16[1024,7168]{1,0:T(8,128)(2,1)} %fusion.27, s32[]{:T(128)S(6)} %select_n.142, bf16[1024,256]{0,1:T(8,128)(2,1)S(1)} %copy-done.1, bf16[256,896]{1,0:T(8,128)(2,1)S(1)} %collective-permute-done.25, bf16[1024,7168]{1,0:T(8,128)(2,1)S(1)} %bitcast.30), kind=kOutput, calls=%fused_computation.33 | convolution fusion | flops 472514560 | bytes 4653060 | tf_op jit(solution)/shard_map/dot_general | solution.py:140
  170.2 2.0 %fusion.29 = bf16[1024,7168]{1,0:T(8,128)(2,1)} fusion(bf16[1024,7168]{1,0:T(8,128)(2,1)} %fusion.28, s32[]{:T(128)S(6)} %select_n.150, bf16[1024,256]{0,1:T(8,128)(2,1)S(1)} %copy-done.1, bf16[256,896]{1,0:T(8,128)(2,1)S(1)} %collective-permute-done.26, bf16[1024,7168]{1,0:T(8,128)(2,1)S(1)} %bitcast.30), kind=kOutput, calls=%fused_computation.34 | convolution fusion | flops 472514560 | bytes 4653060 | tf_op jit(solution)/shard_map/dot_general | solution.py:140
  172.2 2.0 %fusion.30 = bf16[1024,7168]{1,0:T(8,128)(2,1)} fusion(bf16[1024,7168]{1,0:T(8,128)(2,1)} %fusion.29, s32[]{:T(128)S(6)} %select_n.151, bf16[1024,256]{0,1:T(8,128)(2,1)S(1)} %copy-done.1, bf16[256,896]{1,0:T(8,128)(2,1)S(1)} %pad_maximum_fusion.1, bf16[1024,7168]{1,0:T(8,128)(2,1)S(1)} %bitcast.30), kind=kOutput, calls=%fused_computation.35 | convolution fusion | flops 472514560 | bytes 4653060 | tf_op jit(solution)/shard_map/dot_general | solution.py:140
  174.2 2.0 %fusion.31 = bf16[1024,7168]{1,0:T(8,128)(2,1)} fusion(bf16[1024,7168]{1,0:T(8,128)(2,1)} %fusion.30, s32[]{:T(128)S(6)} %select_n.152, bf16[1024,256]{0,1:T(8,128)(2,1)S(1)} %copy-done.1, bf16[256,896]{1,0:T(8,128)(2,1)S(1)} %collective-permute-done.27, bf16[1024,7168]{1,0:T(8,128)(2,1)S(1)} %bitcast.30), kind=kOutput, calls=%fused_computation.36 | convolution fusion | flops 472514560 | bytes 4653060 | tf_op jit(solution)/shard_map/dot_general | solution.py:140
  (91 shorter events, 19.7 us)
Async XLA Ops:
  3.8 9.0 %collective-permute-start = (bf16[256,512]{1,0:T(8,128)(2,1)S(1)}, bf16[256,512]{1,0:T(8,128)(2,1)S(1)}, u32[]{:S(2)}, u32[]{:S(2)}) collective-permute-start(bf16[256,512]{1,0:T(8,128)(2,1)S(1)} %get-tuple-element.66), channel_id=1, source_target_pairs={{0,2},{2,4},{4,6},{1,3},{3,5},{5,7},{8,10},{10,12},{12,14},{9,11},... | collective-permute-start | bytes 786440 | tf_op jit(solution)/shard_map/ppermute | solution.py:132
  7.8 6.9 %collective-permute-start.1 = (bf16[256,512]{1,0:T(8,128)(2,1)S(1)}, bf16[256,512]{1,0:T(8,128)(2,1)S(1)}, u32[]{:S(2)}, u32[]{:S(2)}) collective-permute-start(bf16[256,512]{1,0:T(8,128)(2,1)S(1)} %get-tuple-element.66), channel_id=1, source_target_pairs={{0,1},{1,0},{2,3},{3,2},{4,5},{5,4},{6,7},{7,6},{8,9},{9,8},{10,11... | collective-permute-start | bytes 786440 | tf_op jit(solution)/shard_map/ppermute | solution.py:127
  14.8 6.9 %collective-permute-start.2 = (bf16[256,512]{1,0:T(8,128)(2,1)S(1)}, bf16[256,512]{1,0:T(8,128)(2,1)S(1)}, u32[]{:S(2)}, u32[]{:S(2)}) collective-permute-start(bf16[256,512]{1,0:T(8,128)(2,1)S(1)} %get-tuple-element.30), channel_id=1, source_target_pairs={{0,2},{2,4},{4,6},{1,3},{3,5},{5,7},{8,10},{10,12},{12,14},{9,11},... | collective-permute-start | bytes 786440 | tf_op jit(solution)/shard_map/ppermute | solution.py:132
  18.0 5.8 %collective-permute-start.3 = (bf16[256,512]{1,0:T(8,128)(2,1)S(1)}, bf16[256,512]{1,0:T(8,128)(2,1)S(1)}, u32[]{:S(2)}, u32[]{:S(2)}) collective-permute-start(bf16[256,512]{1,0:T(8,128)(2,1)S(1)} %get-tuple-element.30), channel_id=1, source_target_pairs={{0,1},{1,0},{2,3},{3,2},{4,5},{5,4},{6,7},{7,6},{8,9},{9,8},{10,11... | collective-permute-start | bytes 786440 | tf_op jit(solution)/shard_map/ppermute | solution.py:127
  19.3 9.3 %copy-start.2 = (s32[4096,56]{0,1:T(8,128)S(1)}, s32[4096,56]{0,1:T(8,128)}, u32[]{:S(2)}) copy-start(s32[4096,56]{0,1:T(8,128)} %param.5) | copy-start | bytes 2752516
  22.5 10.9 %collective-permute-start.5 = (bf16[256,512]{1,0:T(8,128)(2,1)}, bf16[256,512]{1,0:T(8,128)(2,1)}, u32[]{:S(2)}, u32[]{:S(2)}) collective-permute-start(bf16[256,512]{1,0:T(8,128)(2,1)} %get-tuple-element.31), channel_id=1, source_target_pairs={{0,1},{1,0},{2,3},{3,2},{4,5},{5,4},{6,7},{7,6},{8,9},{9,8},{10,11... | collective-permute-start | bytes 786440 | tf_op jit(solution)/shard_map/ppermute | solution.py:127
  23.8 8.8 %collective-permute-start.4 = (bf16[256,512]{1,0:T(8,128)(2,1)}, bf16[256,512]{1,0:T(8,128)(2,1)}, u32[]{:S(2)}, u32[]{:S(2)}) collective-permute-start(bf16[256,512]{1,0:T(8,128)(2,1)} %get-tuple-element.31), channel_id=1, source_target_pairs={{0,2},{2,4},{4,6},{1,3},{3,5},{5,7},{8,10},{10,12},{12,14},{9,11},... | collective-permute-start | bytes 786440 | tf_op jit(solution)/shard_map/ppermute | solution.py:132
  29.5 1.3 slice-start.4
  33.4 7.2 %collective-permute-start.6 = (bf16[256,512]{1,0:T(8,128)(2,1)S(1)}, bf16[256,512]{1,0:T(8,128)(2,1)S(1)}, u32[]{:S(2)}, u32[]{:S(2)}) collective-permute-start(bf16[256,512]{1,0:T(8,128)(2,1)S(1)} %get-tuple-element.33), channel_id=1, source_target_pairs={{0,2},{2,4},{4,6},{1,3},{3,5},{5,7},{8,10},{10,12},{12,14},{9,11},... | collective-permute-start | bytes 786440 | tf_op jit(solution)/shard_map/ppermute | solution.py:132
  37.5 5.3 %collective-permute-start.7 = (bf16[256,512]{1,0:T(8,128)(2,1)S(1)}, bf16[256,512]{1,0:T(8,128)(2,1)S(1)}, u32[]{:S(2)}, u32[]{:S(2)}) collective-permute-start(bf16[256,512]{1,0:T(8,128)(2,1)S(1)} %get-tuple-element.33), channel_id=1, source_target_pairs={{0,1},{1,0},{2,3},{3,2},{4,5},{5,4},{6,7},{7,6},{8,9},{9,8},{10,11... | collective-permute-start | bytes 786440 | tf_op jit(solution)/shard_map/ppermute | solution.py:127
  37.8 17.2 %copy-start.5 = (bf16[256,3584]{1,0:T(8,128)(2,1)S(1)}, bf16[256,3584]{1,0:T(8,128)(2,1)}, u32[]{:S(2)}) copy-start(bf16[256,3584]{1,0:T(8,128)(2,1)} %get-tuple-element.59) | copy-start | bytes 5505028
  42.7 6.5 %collective-permute-start.8 = (bf16[256,512]{1,0:T(8,128)(2,1)S(1)}, bf16[256,512]{1,0:T(8,128)(2,1)S(1)}, u32[]{:S(2)}, u32[]{:S(2)}) collective-permute-start(bf16[256,512]{1,0:T(8,128)(2,1)S(1)} %get-tuple-element.34), channel_id=1, source_target_pairs={{0,2},{2,4},{4,6},{1,3},{3,5},{5,7},{8,10},{10,12},{12,14},{9,11},... | collective-permute-start | bytes 786440 | tf_op jit(solution)/shard_map/ppermute | solution.py:132
  46.0 5.3 %collective-permute-start.9 = (bf16[256,512]{1,0:T(8,128)(2,1)S(1)}, bf16[256,512]{1,0:T(8,128)(2,1)S(1)}, u32[]{:S(2)}, u32[]{:S(2)}) collective-permute-start(bf16[256,512]{1,0:T(8,128)(2,1)S(1)} %get-tuple-element.34), channel_id=1, source_target_pairs={{0,1},{1,0},{2,3},{3,2},{4,5},{5,4},{6,7},{7,6},{8,9},{9,8},{10,11... | collective-permute-start | bytes 786440 | tf_op jit(solution)/shard_map/ppermute | solution.py:127
  51.3 6.6 %collective-permute-start.10 = (bf16[256,512]{1,0:T(8,128)(2,1)S(1)}, bf16[256,512]{1,0:T(8,128)(2,1)}, u32[]{:S(2)}, u32[]{:S(2)}) collective-permute-start(bf16[256,512]{1,0:T(8,128)(2,1)S(1)} %get-tuple-element.35), channel_id=1, source_target_pairs={{0,2},{2,4},{4,6},{1,3},{3,5},{5,7},{8,10},{10,12},{12,14},{9,11},... | collective-permute-start | bytes 786440 | tf_op jit(solution)/shard_map/ppermute | solution.py:132
  55.1 5.3 %collective-permute-start.11 = (bf16[256,512]{1,0:T(8,128)(2,1)S(1)}, bf16[256,512]{1,0:T(8,128)(2,1)S(1)}, u32[]{:S(2)}, u32[]{:S(2)}) collective-permute-start(bf16[256,512]{1,0:T(8,128)(2,1)S(1)} %get-tuple-element.35), channel_id=1, source_target_pairs={{0,1},{1,0},{2,3},{3,2},{4,5},{5,4},{6,7},{7,6},{8,9},{9,8},{10,11... | collective-permute-start | bytes 786440 | tf_op jit(solution)/shard_map/ppermute | solution.py:127
  57.9 5.4 %collective-permute-start.12 = (bf16[256,512]{1,0:T(8,128)(2,1)}, bf16[256,512]{1,0:T(8,128)(2,1)S(1)}, u32[]{:S(2)}, u32[]{:S(2)}) collective-permute-start(bf16[256,512]{1,0:T(8,128)(2,1)} %collective-permute-done.10), channel_id=1, source_target_pairs={{0,1},{1,0},{2,3},{3,2},{4,5},{5,4},{6,7},{7,6},{8,9},{9,8},{10,11... | collective-permute-start | bytes 786440 | tf_op jit(solution)/shard_map/ppermute | solution.py:127
  61.4 2.0 %copy-start.6 = (bf16[256,2560]{1,0:T(8,128)(2,1)}, bf16[256,2560]{1,0:T(8,128)(2,1)S(1)}, u32[]{:S(2)}) copy-start(bf16[256,2560]{1,0:T(8,128)(2,1)S(1)} %get-tuple-element.69) | copy-start | bytes 3932164
  63.8 38.5 %copy-start.3 = (bf16[256,2048]{1,0:T(8,128)(2,1)}, bf16[256,2048]{1,0:T(8,128)(2,1)S(1)}, u32[]{:S(2)}) copy-start(bf16[256,2048]{1,0:T(8,128)(2,1)S(1)} %get-tuple-element.68) | copy-start | bytes 3145732
  63.8 1.4 copy-start.7
  73.5 28.8 %collective-permute-start.13 = (f32[256,896]{1,0:T(8,128)}, f32[256,896]{1,0:T(8,128)}, u32[]{:S(2)}, u32[]{:S(2)}) collective-permute-start(f32[256,896]{1,0:T(8,128)} %fusion.8), channel_id=1, source_target_pairs={{0,8},{8,0},{16,24},{24,16},{1,9},{9,1},{17,25},{25,17},{2,10},{10... | collective-permute-start | bytes 2752520 | tf_op jit(solution)/shard_map/ppermute | solution.py:127
  83.4 5.0 %collective-permute-start.14 = (f32[256,256]{1,0:T(8,128)S(1)}, f32[256,256]{1,0:T(8,128)S(1)}, u32[]{:S(2)}, u32[]{:S(2)}) collective-permute-start(f32[256,256]{1,0:T(8,128)S(1)} %fusion.72), channel_id=1, source_target_pairs={{0,8},{8,0},{16,24},{24,16},{1,9},{9,1},{17,25},{25,17},{2,10},{10... | collective-permute-start | bytes 786440 | tf_op jit(solution)/shard_map/ppermute | solution.py:127
  83.4 15.7 %collective-permute-start.16 = (bf16[256,512]{1,0:T(8,128)(2,1)}, bf16[256,512]{1,0:T(8,128)(2,1)}, u32[]{:S(2)}, u32[]{:S(2)}) collective-permute-start(bf16[256,512]{1,0:T(8,128)(2,1)} %collective-permute-done.10), channel_id=1, source_target_pairs={{0,2},{2,4},{4,6},{1,3},{3,5},{5,7},{8,10},{10,12},{12,14},{9,11},... | collective-permute-start | bytes 786440 | tf_op jit(solution)/shard_map/ppermute | solution.py:132
  88.4 9.6 %copy-start.4 = (f32[256,256]{1,0:T(8,128)}, f32[256,256]{1,0:T(8,128)S(1)}, u32[]{:S(2)}) copy-start(f32[256,256]{1,0:T(8,128)S(1)} %add.202) | copy-start | bytes 786436
  88.4 12.7 %collective-permute-start.15 = (f32[256,256]{1,0:T(8,128)S(1)}, f32[256,256]{1,0:T(8,128)}, u32[]{:S(2)}, u32[]{:S(2)}) collective-permute-start(f32[256,256]{1,0:T(8,128)S(1)} %add.202), channel_id=1, source_target_pairs={{0,16},{8,24},{16,0},{24,8},{1,17},{9,25},{17,1},{25,9},{2,18},{10... | collective-permute-start | bytes 786440 | tf_op jit(solution)/shard_map/ppermute | solution.py:127
  98.0 35.2 %collective-permute-start.18 = (f32[256,896]{1,0:T(8,128)}, f32[256,896]{1,0:T(8,128)S(1)}, u32[]{:S(2)}, u32[]{:S(2)}) collective-permute-start(f32[256,896]{1,0:T(8,128)} %fusion.4), channel_id=1, source_target_pairs={{0,8},{8,0},{16,24},{24,16},{1,9},{9,1},{17,25},{25,17},{2,10},{10... | collective-permute-start | bytes 2752520 | tf_op jit(solution)/shard_map/ppermute | solution.py:127
  99.1 22.7 %collective-permute-start.17 = (bf16[256,512]{1,0:T(8,128)(2,1)}, bf16[256,512]{1,0:T(8,128)(2,1)}, u32[]{:S(2)}, u32[]{:S(2)}) collective-permute-start(bf16[256,512]{1,0:T(8,128)(2,1)} %collective-permute-done.16), channel_id=1, source_target_pairs={{0,2},{2,4},{4,6},{1,3},{3,5},{5,7},{8,10},{10,12},{12,14},{9,11},... | collective-permute-start | bytes 786440 | tf_op jit(solution)/shard_map/ppermute | solution.py:132
  111.0 22.3 %collective-permute-start.19 = (f32[256,896]{1,0:T(8,128)}, f32[256,896]{1,0:T(8,128)S(1)}, u32[]{:S(2)}, u32[]{:S(2)}) collective-permute-start(f32[256,896]{1,0:T(8,128)} %fusion.32), channel_id=1, source_target_pairs={{0,16},{8,24},{16,0},{24,8},{1,17},{9,25},{17,1},{25,9},{2,18},{10... | collective-permute-start | bytes 2752520 | tf_op jit(solution)/shard_map/ppermute | solution.py:127
  125.4 7.9 %copy-start = (f32[256,896]{1,0:T(8,128)S(1)}, f32[256,896]{1,0:T(8,128)}, u32[]{:S(2)}) copy-start(f32[256,896]{1,0:T(8,128)} %fusion.first_ref) | copy-start | bytes 2752516
  134.4 17.5 %collective-permute-start.22 = (bf16[512,896]{1,0:T(8,128)(2,1)S(1)}, bf16[512,896]{1,0:T(8,128)(2,1)S(1)}, u32[]{:S(2)}, u32[]{:S(2)}) collective-permute-start(bf16[512,896]{1,0:T(8,128)(2,1)S(1)} %get-tuple-element.49), channel_id=1, source_target_pairs={{0,8},{8,0},{16,24},{24,16},{1,9},{9,1},{17,25},{25,17},{2,10},{10... | collective-permute-start | bytes 2752520 | tf_op jit(solution)/shard_map/ppermute | solution.py:127
  135.1 21.3 %collective-permute-start.20 = (bf16[256,896]{1,0:T(8,128)(2,1)S(1)}, bf16[256,896]{1,0:T(8,128)(2,1)}, u32[]{:S(2)}, u32[]{:S(2)}) collective-permute-start(bf16[256,896]{1,0:T(8,128)(2,1)S(1)} %get-tuple-element.47), channel_id=1, source_target_pairs={{0,16},{8,24},{16,0},{24,8},{1,17},{9,25},{17,1},{25,9},{2,18},{10... | collective-permute-start | bytes 1376264 | tf_op jit(solution)/shard_map/ppermute | solution.py:127
  135.9 20.5 %collective-permute-start.21 = (bf16[256,896]{1,0:T(8,128)(2,1)S(1)}, bf16[256,896]{1,0:T(8,128)(2,1)S(1)}, u32[]{:S(2)}, u32[]{:S(2)}) collective-permute-start(bf16[256,896]{1,0:T(8,128)(2,1)S(1)} %get-tuple-element.47), channel_id=1, source_target_pairs={{0,1},{1,0},{2,3},{3,2},{4,5},{5,4},{6,7},{7,6},{8,9},{9,8},{10,11... | collective-permute-start | bytes 1376264 | tf_op jit(solution)/shard_map/ppermute | solution.py:127
  139.9 7.3 %copy-start.1 = (bf16[1024,256]{0,1:T(8,128)(2,1)S(1)}, bf16[1024,256]{0,1:T(8,128)(2,1)}, u32[]{:S(2)}) copy-start(bf16[1024,256]{0,1:T(8,128)(2,1)} %dynamic-slice_bitcast_fusion) | copy-start | bytes 1572868
  147.2 21.0 %slice-start = ((s8[14680064]{0:T(1024)(128)(4,1)}), s8[2097152]{0:T(1024)(128)(4,1)S(1)}, s32[]{:S(2)}) async-start(s8[14680064]{0:T(1024)(128)(4,1)} %bitcast.29), calls=%async_computation | async-start | bytes 4194304
  147.2 21.0 %slice-start.1 = ((s8[14680064]{0:T(1024)(128)(4,1)}), s8[4194304]{0:T(1024)(128)(4,1)S(1)}, s32[]{:S(2)}) async-start(s8[14680064]{0:T(1024)(128)(4,1)} %bitcast.29), calls=%async_computation.1 | async-start | bytes 8388608
  152.7 15.6 %slice-start.2 = ((s8[14680064]{0:T(1024)(128)(4,1)}), s8[4194304]{0:T(1024)(128)(4,1)S(1)}, s32[]{:S(2)}) async-start(s8[14680064]{0:T(1024)(128)(4,1)} %bitcast.29), calls=%async_computation.2 | async-start | bytes 8388608
  157.4 10.9 %collective-permute-start.25 = (bf16[256,896]{1,0:T(8,128)(2,1)}, bf16[256,896]{1,0:T(8,128)(2,1)S(1)}, u32[]{:S(2)}, u32[]{:S(2)}) collective-permute-start(bf16[256,896]{1,0:T(8,128)(2,1)} %collective-permute-done.20), channel_id=1, source_target_pairs={{0,8},{8,0},{16,24},{24,16},{1,9},{9,1},{17,25},{25,17},{2,10},{10... | collective-permute-start | bytes 1376264 | tf_op jit(solution)/shard_map/ppermute | solution.py:127
  158.1 10.2 %slice-start.3 = ((s8[14680064]{0:T(1024)(128)(4,1)}), s8[4194304]{0:T(1024)(128)(4,1)S(1)}, s32[]{:S(2)}) async-start(s8[14680064]{0:T(1024)(128)(4,1)} %bitcast.29), calls=%async_computation.3 | async-start | bytes 8388608
  158.1 12.1 %collective-permute-start.26 = (bf16[256,896]{1,0:T(8,128)(2,1)S(1)}, bf16[256,896]{1,0:T(8,128)(2,1)S(1)}, u32[]{:S(2)}, u32[]{:S(2)}) collective-permute-start(bf16[256,896]{1,0:T(8,128)(2,1)S(1)} %collective-permute-done.21), channel_id=1, source_target_pairs={{0,8},{8,0},{16,24},{24,16},{1,9},{9,1},{17,25},{25,17},{2,10},{10... | collective-permute-start | bytes 1376264 | tf_op jit(solution)/shard_map/ppermute | solution.py:127
  158.2 8.9 %collective-permute-start.24 = (bf16[128,896]{1,0:T(8,128)(2,1)S(1)}, bf16[128,896]{1,0:T(8,128)(2,1)S(1)}, u32[]{:S(2)}, u32[]{:S(2)}) collective-permute-start(bf16[128,896]{1,0:T(8,128)(2,1)S(1)} %slice.35), channel_id=1, source_target_pairs={{0,1},{1,0},{2,3},{3,2},{4,5},{5,4},{6,7},{7,6},{8,9},{9,8},{10,11... | collective-permute-start | bytes 688136 | tf_op jit(solution)/shard_map/ppermute | solution.py:127
  159.4 7.7 %collective-permute-start.23 = (bf16[128,896]{1,0:T(8,128)(2,1)S(1)}, bf16[128,896]{1,0:T(8,128)(2,1)S(1)}, u32[]{:S(2)}, u32[]{:S(2)}) collective-permute-start(bf16[128,896]{1,0:T(8,128)(2,1)S(1)} %slice.34), channel_id=1, source_target_pairs={{0,16},{8,24},{16,0},{24,8},{1,17},{9,25},{17,1},{25,9},{2,18},{10... | collective-permute-start | bytes 688136 | tf_op jit(solution)/shard_map/ppermute | solution.py:127
  167.2 7.1 %collective-permute-start.27 = (bf16[256,896]{1,0:T(8,128)(2,1)S(1)}, bf16[256,896]{1,0:T(8,128)(2,1)S(1)}, u32[]{:S(2)}, u32[]{:S(2)}) collective-permute-start(bf16[256,896]{1,0:T(8,128)(2,1)S(1)} %pad_maximum_fusion.1), channel_id=1, source_target_pairs={{0,8},{8,0},{16,24},{24,16},{1,9},{9,1},{17,25},{25,17},{2,10},{10... | collective-permute-start | bytes 1376264 | tf_op jit(solution)/shard_map/ppermute | solution.py:127

commit v5 on v4

--- a/solution.py
+++ b/solution.py
@@ -127,9 +127,8 @@
     return lax.ppermute(x, axis, [(i, i ^ bit) for i in range(size)])
 
 
-def forward(x, axis):
-    size = lax.axis_size(axis)
-    return lax.ppermute(x, axis, [(i, i + 1) for i in range(size - 1)])
+def hop(x, axis, start):
+    return lax.ppermute(x, axis, [(start, start + 1)])
 
 
 def after(x, *others):
@@ -138,6 +137,14 @@
 
 def dot(left, right):
     return jnp.dot(left, right, preferred_element_type=F32)
+
+
+def unwritten(shape, dtype):
+    return pl.pallas_call(
+        lambda out_ref: None,
+        out_shape=jax.ShapeDtypeStruct(shape, dtype),
+        out_specs=pl.BlockSpec(memory_space=pl.ANY),
+    )()
 
 
 def shards(quantized, exponents, weights, keep_mask):
@@ -146,44 +153,61 @@
     tok, row, feat = lax.axis_index("tok"), lax.axis_index("row"), lax.axis_index("feat")
     width = cols // (toks * rows)
     root = feat == 0
+    hops = feats - 1
 
     piece = tokens // rows // ROUNDS
-    sources = [
-        panel_piece(quantized, exponents, row * ROUNDS + c, piece) for c in range(ROUNDS)
+    got = [
+        [panel_piece(quantized, exponents, row * ROUNDS + c, piece)] for c in range(ROUNDS)
     ]
-    panel_weights = after(weights[:, :PANEL], sources[0])
-    error = jnp.where(keep_mask == 0, panel_weights, jnp.zeros((), BF16)).T
-    extras = -(-error.shape[1] // piece)
-    error = jnp.pad(error, ((0, 0), (0, extras * piece - error.shape[1])))
-    sources += [error[:, i * piece : (i + 1) * piece] for i in range(extras)]
-    panel_rounds = ROUNDS + feats - 1
-    held, swapped = [jnp.where(root, sources[0], jnp.zeros((), BF16))], []
-
-    def advance(*others):
-        r = len(held)
-        x = forward(after(held[-1], *others) if others else held[-1], "feat")
-        held.append(jnp.where(root, sources[r], x) if r < len(sources) else x)
-
-    for r in range(1, panel_rounds):
-        swapped.append(swap(held[r - 1], "row", 1))
-        advance(*swapped[r - 2 : r - 1])
-    swapped.append(swap(held[-1], "row", 1))
-
-    scale = jnp.exp2(after(exponents, sources[0]).astype(F32)).astype(BF16)
-    acts = []
-    for k, link in zip((3, 2, 1, 0), (1, 2, 3, 4)):
-        col = row * toks + (tok ^ k)
-        block = (col * width + lax.broadcasted_iota(jnp.int32, (1, width), 1)) // QBLOCK
+    for c in range(ROUNDS):
+        got[c].append(hop(got[c][0], "feat", 0))
+
+    def scaled(k, link):
+        scale = jnp.exp2(after(exponents, link).astype(F32)).astype(BF16)
+        start = (row * toks + (tok ^ k)) * width
+        block = (start + lax.broadcasted_iota(jnp.int32, (1, width), 1)) // QBLOCK
         spread = lax.broadcasted_iota(jnp.int32, (scale.shape[1], width), 0) == block
-        wide = dot(after(scale, held[link]), spread.astype(BF16)).astype(BF16)
-        acts.insert(0, lax.dynamic_slice_in_dim(quantized, col * width, width, 1) * wide)
-
-    def window(rounds, first, count):
-        rounds = jnp.concatenate(rounds, axis=1)
-        return lax.dynamic_slice_in_dim(rounds, first * piece, count * piece, 1)
-
-    own = window(held[:panel_rounds], feat, ROUNDS)
-    other = window(swapped, feat, ROUNDS)
+        wide = dot(scale, spread.astype(BF16)).astype(BF16)
+        return lax.dynamic_slice_in_dim(quantized, start, width, 1) * wide
+
+    acts = {3: scaled(3, got[-1][0])}
+
+    def settle(parts):
+        result = parts[0]
+        for h in range(hops):
+            result = jnp.where(feat == h + 1, parts[h + 1], result)
+        return result
+
+    events = sorted((5 * (c + 1) + 8 * h, c, h) for c in range(ROUNDS) for h in range(hops))
+    full, swapped, token, errors = [], [], acts[3], []
+    for _, c, h in events:
+        x = after(got[c][h + 1], token)
+        got[c][h + 1] = token = x
+        if h + 1 < hops:
+            got[c].append(hop(x, "feat", h + 1))
+        else:
+            full.append(settle(got[c]))
+            swapped.append(swap(full[-1], "row", 1))
+        if (c, h) == (1, 0):
+            acts[2] = token = scaled(2, x)
+        elif (c, h) == (1, 1):
+            acts[1] = token = scaled(1, x)
+        elif (c, h) == (0, 1):
+            panel_weights, mask = after(weights[:, :PANEL], x), after(keep_mask, x)
+            error = jnp.where(mask == 0, panel_weights, jnp.zeros((), BF16)).T
+            extras = -(-error.shape[1] // piece)
+            error = jnp.pad(error, ((0, 0), (0, extras * piece - error.shape[1])))
+            errors = [[error[:, i * piece : (i + 1) * piece]] for i in range(extras)]
+        elif (c, h) == (ROUNDS - 1, 0):
+            for parts in errors:
+                parts[0] = after(parts[0], x)
+                parts.append(hop(parts[0], "feat", 0))
+        elif (c, h) == (ROUNDS - 1, 1):
+            for parts in errors:
+                parts[1] = after(parts[1], x)
+                parts.append(hop(parts[1], "feat", 1))
+
+    own, other = jnp.concatenate(full, axis=1), jnp.concatenate(swapped, axis=1)
     panel = jnp.concatenate(
         [jnp.where(row == 0, own, other), jnp.where(row == 0, other, own)], axis=1
     )
@@ -195,18 +219,22 @@
     block3 = dot(panel, acts[3])
     from3 = swap(block3, "tok", 1)
     head = head + swap(head, "tok", 2)
-    advance(block3)
+    acts[2] = after(acts[2], from3)
     block2 = dot(panel, acts[2]) + from3
     block2, head = lax.optimization_barrier((block2, head))
     fromx = swap(block2, "tok", 2)
+    for parts in errors:
+        parts[2] = after(parts[2], block2)
+        for h in range(2, hops):
+            parts.append(hop(parts[h], "feat", h))
     block1 = dot(panel, acts[1])
     from1 = swap(block1, "tok", 1)
-    block0 = dot(panel, acts[0])
-    while len(held) < len(sources) + feats - 1:
-        advance(block1)
-    inverse = invert(after(head, held[-1]))
-    error = window(held[ROUNDS:], feat, extras)[:, : weights.shape[0]].T
-    inverse, error = lax.optimization_barrier((inverse, error))
+    block0 = dot(panel, scaled(0, block1))
+    error = jnp.concatenate([settle(parts) for parts in errors], axis=1)
+    error = error[:, : weights.shape[0]].T
+    twice = jnp.concatenate([error, error], axis=1)
+    head, twice = lax.optimization_barrier((head, twice))
+    inverse = invert(head)
     start = jnp.where(root, (row * toks + tok) * width, PANEL)
     high, pair = make_gains(inverse, (block0, from1, fromx), start)
 
@@ -215,17 +243,17 @@
     def update(out, gain, tok_bits, row_bit):
         start = ((row ^ row_bit) * toks + (tok ^ tok_bits)) * width
         total = lax.dynamic_slice_in_dim(weights, start, width, 1).astype(F32)
-        for top in range(0, gain.shape[0], PANEL):
-            total = total + dot(error, gain[top : top + PANEL])
+        total = total + dot(twice[:, : gain.shape[0]], gain)
         return lax.dynamic_update_slice_in_dim(out, total.astype(BF16), start, 1)
 
+    in_x, in_y = swap(high, "tok", 2), swap(high, "row", 1)
     near = swap(pair, "tok", 1)
-    in_x, in_y = swap(high, "tok", 2), swap(high, "row", 1)
-    out = jnp.zeros_like(weights)
+    out = unwritten(weights.shape, BF16)
     out = update(out, pair, 0, 0)
     out = update(out, near, 1, 0)
     in_x, in_y, out = lax.optimization_barrier((in_x, in_y, out))
-    far = jnp.concatenate([swap(in_y[:half], "tok", 2), swap(in_x[half:], "row", 1)], axis=0)
+    top, bottom, out = lax.optimization_barrier((in_y[:half], in_x[half:], out))
+    far = jnp.concatenate([swap(top, "tok", 2), swap(bottom, "row", 1)], axis=0)
     near_x, near_y = swap(in_x, "tok", 1), swap(in_y, "tok", 1)
     out = update(out, in_x, 2, 0)
     out = update(out, in_y, 0, 1)

time: 177 us -> 179 us (1.011)
  the two profiles are of different devices: /device:TPU:1 before, /device:TPU:9 now
where the time goes in v5:
time: 179 us; the launch traced here: 178 us
  matrix products  72 us (40%)
  starting transfers between devices  47.6 us (27%)
  waiting for transfers between devices  32.6 us (18%)
  Pallas kernels  13.9 us (8%)
  other arithmetic  7.21 us (4%)
  local copies, waits for them, and re-layouts  3.78 us (2%)
    dot_general x15, matrix products, dot(): return jnp.dot(left, right, preferred_element_type=F32)  71.3 us
    ppermute x17, waiting for transfers between devices, swap(): return lax.ppermute(x, axis, [(i, i ^ bit) for i in range(size)])  32.5 us
    ppermute x18, starting transfers between devices, hop(): return lax.ppermute(x, axis, [(start, start + 1)])  29.6 us
    ppermute x17, starting transfers between devices, swap(): return lax.ppermute(x, axis, [(i, i ^ bit) for i in range(size)])  18 us
    pallas_call x1, Pallas kernels, invert(): pl.pallas_call(inverse_kernel, out_shape=jax.ShapeDtypeStruct((PANEL, PAN...  7.86 us
    pallas_call x4, Pallas kernels, panel_piece(): pl.pallas_call(panel_kernel, out_shape=jax.ShapeDtypeStruct((PANEL, piece...  4.98 us
    select_n x6, other arithmetic, settle(): result = jnp.where(feat == h + 1, parts[h + 1], result)  4.16 us
  transfers between devices with their start and end apart: 35, of which 8 were waited for; matrix products, arithmetic and copies ran while one was open for 45% of the time, Pallas kernels for 7%

profile of v5, /device:TPU:9, one launch (start us, length us, event | category | flops | bytes accessed | tf_op | source)
XLA Modules:
  0.0 177.8 jit_solution(12192839367606939251)
XLA Ops:
  0.0 1.8 copy.5.exps_ref
  3.0 1.3 collective-permute-start
  5.6 1.3 collective-permute-start.2
  8.2 1.3 collective-permute-start.6
  10.7 1.3 collective-permute-start.4
  12.1 8.6 %convert_multiply_fusion.2 = bf16[4096,896]{1,0:T(8,128)(2,1)} fusion(bf16[4096,7168]{1,0:T(8,128)(2,1)} %quant_ref.7, s32[]{:T(128)S(6)} %select_n.173, s32[4096,56]{0,1:T(8,128)} %param.5, s32[896]{0:T(1024)S(1)} %add_select_fusion.3), kind=kOutput, calls=%fused_computation.6 | convolution fusion | flops 430130176 | bytes 15601156 | tf_op jit(solution)/shard_map/dot_general | solution.py:139
  21.0 2.1 %collective-permute-start.1 = (bf16[256,512]{1,0:T(8,128)(2,1)}, bf16[256,512]{1,0:T(8,128)(2,1)S(1)}, u32[]{:S(2)}, u32[]{:S(2)}) collective-permute-start(bf16[256,512]{1,0:T(8,128)(2,1)} %collective-permute-done), channel_id=1, source_target_pairs={{2,4},{3,5},{10,12},{11,13},{18,20},{19,21},{26,28},{27,29}} | collective-permute-start | bytes 786440 | tf_op jit(solution)/shard_map/ppermute | solution.py:131
  23.1 2.0 %collective-permute-start.5 = (bf16[256,512]{1,0:T(8,128)(2,1)}, bf16[256,512]{1,0:T(8,128)(2,1)}, u32[]{:S(2)}, u32[]{:S(2)}) collective-permute-start(bf16[256,512]{1,0:T(8,128)(2,1)} %collective-permute-done.2), channel_id=1, source_target_pairs={{2,4},{3,5},{10,12},{11,13},{18,20},{19,21},{26,28},{27,29}} | collective-permute-start | bytes 786440 | tf_op jit(solution)/shard_map/ppermute | solution.py:131
  25.1 8.2 %convert_multiply_fusion.1 = bf16[4096,896]{1,0:T(8,128)(2,1)} fusion(bf16[4096,7168]{1,0:T(8,128)(2,1)} %quant_ref.7, s32[]{:T(128)S(6)} %select_n.175, s32[4096,56]{0,1:T(8,128)S(1)} %copy-done, s32[896]{0:T(1024)S(1)} %add_select_fusion.2), kind=kOutput, calls=%fused_computation.5 | convolution fusion | flops 430130176 | bytes 15601156 | tf_op jit(solution)/shard_map/dot_general | solution.py:139
  33.3 1.4 collective-permute-start.3
  34.7 3.3 %collective-permute-start.8 = (bf16[256,512]{1,0:T(8,128)(2,1)S(1)}, bf16[256,512]{1,0:T(8,128)(2,1)}, u32[]{:S(2)}, u32[]{:S(2)}) collective-permute-start(bf16[256,512]{1,0:T(8,128)(2,1)S(1)} %collective-permute-done.6), channel_id=1, source_target_pairs={{2,4},{3,5},{10,12},{11,13},{18,20},{19,21},{26,28},{27,29}} | collective-permute-start | bytes 786440 | tf_op jit(solution)/shard_map/ppermute | solution.py:131
  38.0 1.4 collective-permute-start.7
  39.3 8.3 %convert_multiply_fusion = bf16[4096,896]{1,0:T(8,128)(2,1)} fusion(bf16[4096,7168]{1,0:T(8,128)(2,1)} %quant_ref.7, s32[]{:T(128)S(6)} %select_n.177, s32[4096,56]{0,1:T(8,128)S(1)} %copy-done, s32[896]{0:T(1024)S(1)} %add_select_fusion.1), kind=kOutput, calls=%fused_computation.4 | convolution fusion | flops 430130176 | bytes 15601156 | tf_op jit(solution)/shard_map/dot_general | solution.py:139
  47.6 2.0 %collective-permute-start.10 = (bf16[256,512]{1,0:T(8,128)(2,1)S(1)}, bf16[256,512]{1,0:T(8,128)(2,1)}, u32[]{:S(2)}, u32[]{:S(2)}) collective-permute-start(bf16[256,512]{1,0:T(8,128)(2,1)S(1)} %collective-permute-done.4), channel_id=1, source_target_pairs={{2,4},{3,5},{10,12},{11,13},{18,20},{19,21},{26,28},{27,29}} | collective-permute-start | bytes 786440 | tf_op jit(solution)/shard_map/ppermute | solution.py:131
  49.6 1.6 copy.9
  51.4 1.6 collective-permute-start.19
  52.9 1.3 collective-permute-start.22
  57.9 1.4 collective-permute-start.13
  59.5 1.4 collective-permute-start.14
  60.9 9.1 %collective-permute-done.12 = bf16[256,512]{1,0:T(8,128)(2,1)S(1)} collective-permute-done((bf16[256,512]{1,0:T(8,128)(2,1)S(1)}, bf16[256,512]{1,0:T(8,128)(2,1)S(1)}, u32[]{:S(2)}, u32[]{:S(2)}) %collective-permute-start.12) | collective-permute-done | bytes 262176 | tf_op jit(solution)/shard_map/ppermute | solution.py:127
  70.0 1.4 collective-permute-start.15
  71.5 4.2 %collective-permute-done.14 = bf16[256,512]{1,0:T(8,128)(2,1)S(1)} collective-permute-done((bf16[256,512]{1,0:T(8,128)(2,1)S(1)}, bf16[256,512]{1,0:T(8,128)(2,1)S(1)}, u32[]{:S(2)}, u32[]{:S(2)}) %collective-permute-start.14) | collective-permute-done | bytes 262176 | tf_op jit(solution)/shard_map/ppermute | solution.py:127
  75.7 5.6 %collective-permute-done.15 = bf16[256,512]{1,0:T(8,128)(2,1)S(1)} collective-permute-done((bf16[256,512]{1,0:T(8,128)(2,1)S(1)}, bf16[256,512]{1,0:T(8,128)(2,1)S(1)}, u32[]{:S(2)}, u32[]{:S(2)}) %collective-permute-start.15) | collective-permute-done | bytes 262176 | tf_op jit(solution)/shard_map/ppermute | solution.py:127
  81.8 3.4 %fusion.51 = f32[256,896]{1,0:T(8,128)} fusion(bf16[4096,896]{1,0:T(8,128)(2,1)S(1)} %bitcast.25, bf16[256,2048]{1,0:T(8,128)(2,1)S(1)} %get-tuple-element.84, bf16[256,2048]{1,0:T(8,128)(2,1)S(1)} %get-tuple-element.83), kind=kOutput, calls=%fused_computation.109 | convolution fusion | flops 1883242496 | bytes 10354688 | tf_op jit(solution)/shard_map/dot_general | solution.py:139
  85.2 2.2 %collective-permute-start.16 = (f32[256,896]{1,0:T(8,128)}, f32[256,896]{1,0:T(8,128)}, u32[]{:S(2)}, u32[]{:S(2)}) collective-permute-start(f32[256,896]{1,0:T(8,128)} %fusion.51), channel_id=1, source_target_pairs={{0,8},{8,0},{16,24},{24,16},{1,9},{9,1},{17,25},{25,17},{2,10},{10... | collective-permute-start | bytes 2752520 | tf_op jit(solution)/shard_map/ppermute | solution.py:127
  88.3 3.1 %collective-permute-start.20 = (bf16[256,512]{1,0:T(8,128)(2,1)}, bf16[256,512]{1,0:T(8,128)(2,1)}, u32[]{:S(2)}, u32[]{:S(2)}) collective-permute-start(bf16[256,512]{1,0:T(8,128)(2,1)} %collective-permute-done.19), channel_id=1, source_target_pairs={{2,4},{3,5},{10,12},{11,13},{18,20},{19,21},{26,28},{27,29}} | collective-permute-start | bytes 786440 | tf_op jit(solution)/shard_map/ppermute | solution.py:131
  91.4 2.0 %collective-permute-start.23 = (bf16[256,512]{1,0:T(8,128)(2,1)}, bf16[256,512]{1,0:T(8,128)(2,1)}, u32[]{:S(2)}, u32[]{:S(2)}) collective-permute-start(bf16[256,512]{1,0:T(8,128)(2,1)} %collective-permute-done.22), channel_id=1, source_target_pairs={{2,4},{3,5},{10,12},{11,13},{18,20},{19,21},{26,28},{27,29}} | collective-permute-start | bytes 786440 | tf_op jit(solution)/shard_map/ppermute | solution.py:131
  94.5 1.3 collective-permute-start.18
  95.8 6.4 %fusion.49 = f32[256,896]{1,0:T(8,128)} fusion(bf16[4096,896]{1,0:T(8,128)(2,1)} %convert_multiply_fusion, bf16[256,2048]{1,0:T(8,128)(2,1)S(1)} %get-tuple-element.84, bf16[256,2048]{1,0:T(8,128)(2,1)S(1)} %get-tuple-element.83), kind=kOutput, calls=%fused_computation.107 | convolution fusion | flops 1883242496 | bytes 10354688 | tf_op jit(solution)/shard_map/dot_general | solution.py:139
  103.4 4.8 %convolution_add_fusion = f32[256,896]{1,0:T(8,128)} fusion(f32[256,896]{1,0:T(8,128)} %collective-permute-done.16, bf16[4096,896]{1,0:T(8,128)(2,1)S(1)} %bitcast.23, bf16[256,2048]{1,0:T(8,128)(2,1)} %copy-done.3, bf16[256,2048]{1,0:T(8,128)(2,1)S(1)} %get-tuple-element.83), kind=kOutput, calls=%fused_computation.25 | convolution fusion | flops 1883471872 | bytes 11272192 | tf_op jit(solution)/shard_map/dot_general | solution.py:139
  108.2 1.5 collective-permute-start.21
  109.7 1.4 collective-permute-start.24
  111.1 8.1 %fusion.first_ref = f32[256,896]{1,0:T(8,128)S(1)} fusion(bf16[4096,7168]{1,0:T(8,128)(2,1)} %quant_ref.7, s32[]{:T(128)S(6)} %select_n.202, s32[4096,56]{0,1:T(8,128)S(1)} %copy-done.1, s32[896]{0:T(1024)S(1)} %add_select_fusion, bf16[256,2048]{1,0:T(8,128)(2,1)} %copy-done.3, bf16[256,2048]{1,0:T(8,128)(2,1)} %copy-done.2), kind=kOutput, calls=%fused_computation | convolution fusion | flops 2313372672 | bytes 11275780 | tf_op jit(solution)/shard_map/dot_general | solution.py:139
  123.2 7.9 %shard_map.50.inverse_ref = f32[256,256]{1,0:T(8,128)S(1)} custom-call(f32[256,256]{1,0:T(8,128)S(1)} %add.193.head_ref), custom_call_target="tpu_custom_call" | custom-call | flops 5637144576 | bytes 524288 | tf_op jit(solution)/shard_map/pallas_call | solution.py:85
  131.1 10.3 %collective-permute-done.26.third_ref = f32[256,896]{1,0:T(8,128)S(1)} collective-permute-done((f32[256,896]{1,0:T(8,128)}, f32[256,896]{1,0:T(8,128)S(1)}, u32[]{:S(2)}, u32[]{:S(2)}) %collective-permute-start.26) | collective-permute-done | bytes 917536 | tf_op jit(solution)/shard_map/ppermute | solution.py:127
  144.1 1.4 collective-permute-start.28
  145.5 4.2 %fusion.6 = bf16[1024,7168]{1,0:T(8,128)(2,1)} fusion(bf16[1024,7168]{1,0:T(8,128)(2,1)} %shard_map.52, s32[]{:T(128)S(6)} %select_n.202, bf16[1024,512]{0,1:T(8,128)(2,1)S(1)} %copy-done.4, bf16[512,896]{1,0:T(8,128)(2,1)S(1)} %get-tuple-element.74, bf16[1024,7168]{1,0:T(8,128)(2,1)} %param.6), kind=kOutput, calls=%fused_computation.17 | convolution fusion | flops 942276608 | bytes 5636100 | tf_op jit(solution)/shard_map/dot_general | solution.py:139
  149.7 4.2 %fusion.7 = bf16[1024,7168]{1,0:T(8,128)(2,1)} fusion(bf16[1024,7168]{1,0:T(8,128)(2,1)} %fusion.6, s32[]{:T(128)S(6)} %select_n.177, bf16[1024,512]{0,1:T(8,128)(2,1)S(1)} %copy-done.4, bf16[512,896]{1,0:T(8,128)(2,1)S(1)} %collective-permute-done.29, bf16[1024,7168]{1,0:T(8,128)(2,1)} %param.6), kind=kOutput, calls=%fused_computation.18 | convolution fusion | flops 942276608 | bytes 5636100 | tf_op jit(solution)/shard_map/dot_general | solution.py:139
  153.9 1.5 collective-permute-done.27
  155.8 1.3 collective-permute-start.32
  157.3 3.6 %fusion.8 = bf16[1024,7168]{1,0:T(8,128)(2,1)} fusion(bf16[1024,7168]{1,0:T(8,128)(2,1)} %fusion.7, s32[]{:T(128)S(6)} %select_n.175, bf16[256,896]{1,0:T(8,128)(2,1)S(1)} %collective-permute-done.27, bf16[1024,7168]{1,0:T(8,128)(2,1)} %param.6, bf16[1024,512]{0,1:T(8,128)(2,1)S(1)} %copy-done.4), kind=kOutput, calls=%fused_computation.19 | convolution fusion | flops 472514560 | bytes 4653060 | tf_op jit(solution)/shard_map/dot_general | solution.py:139
  161.7 1.3 collective-permute-start.31
  163.0 3.5 %fusion.9 = bf16[1024,7168]{1,0:T(8,128)(2,1)} fusion(bf16[1024,7168]{1,0:T(8,128)(2,1)} %fusion.8, s32[]{:T(128)S(6)} %select_n.204, bf16[256,896]{1,0:T(8,128)(2,1)S(1)} %collective-permute-done.28, bf16[1024,7168]{1,0:T(8,128)(2,1)} %param.6, bf16[1024,512]{0,1:T(8,128)(2,1)S(1)} %copy-done.4), kind=kOutput, calls=%fused_computation.20 | convolution fusion | flops 472514560 | bytes 4653060 | tf_op jit(solution)/shard_map/dot_general | solution.py:139
  167.9 1.9 %collective-permute-start.34 = (bf16[256,896]{1,0:T(8,128)(2,1)S(1)}, bf16[256,896]{1,0:T(8,128)(2,1)S(1)}, u32[]{:S(2)}, u32[]{:S(2)}) collective-permute-start(bf16[256,896]{1,0:T(8,128)(2,1)S(1)} %pad_maximum_fusion.3), channel_id=1, source_target_pairs={{0,8},{8,0},{16,24},{24,16},{1,9},{9,1},{17,25},{25,17},{2,10},{10... | collective-permute-start | bytes 1376264 | tf_op jit(solution)/shard_map/ppermute | solution.py:127
  169.8 2.0 %fusion.10 = bf16[1024,7168]{1,0:T(8,128)(2,1)} fusion(bf16[1024,7168]{1,0:T(8,128)(2,1)} %fusion.9, s32[]{:T(128)S(6)} %select_n.173, bf16[256,896]{1,0:T(8,128)(2,1)S(1)} %collective-permute-done.32, bf16[1024,7168]{1,0:T(8,128)(2,1)S(1)} %bitcast.27, bf16[1024,512]{0,1:T(8,128)(2,1)S(1)} %copy-done.4), kind=kOutput, calls=%fused_computation.21 | convolution fusion | flops 472514560 | bytes 4653060 | tf_op jit(solution)/shard_map/dot_general | solution.py:139
  171.8 2.0 %fusion.11 = bf16[1024,7168]{1,0:T(8,128)(2,1)} fusion(bf16[1024,7168]{1,0:T(8,128)(2,1)} %fusion.10, s32[]{:T(128)S(6)} %select_n.205, bf16[256,896]{1,0:T(8,128)(2,1)S(1)} %collective-permute-done.33, bf16[1024,7168]{1,0:T(8,128)(2,1)S(1)} %bitcast.27, bf16[1024,512]{0,1:T(8,128)(2,1)S(1)} %copy-done.4), kind=kOutput, calls=%fused_computation.22 | convolution fusion | flops 472514560 | bytes 4653060 | tf_op jit(solution)/shard_map/dot_general | solution.py:139
  173.8 2.0 %fusion.12 = bf16[1024,7168]{1,0:T(8,128)(2,1)} fusion(bf16[1024,7168]{1,0:T(8,128)(2,1)} %fusion.11, s32[]{:T(128)S(6)} %select_n.206, bf16[256,896]{1,0:T(8,128)(2,1)S(1)} %pad_maximum_fusion.3, bf16[1024,7168]{1,0:T(8,128)(2,1)S(1)} %bitcast.27, bf16[1024,512]{0,1:T(8,128)(2,1)S(1)} %copy-done.4), kind=kOutput, calls=%fused_computation.23 | convolution fusion | flops 472514560 | bytes 4653060 | tf_op jit(solution)/shard_map/dot_general | solution.py:139
  175.8 2.0 %fusion.13 = bf16[1024,7168]{1,0:T(8,128)(2,1)} fusion(bf16[1024,7168]{1,0:T(8,128)(2,1)} %fusion.12, s32[]{:T(128)S(6)} %select_n.207, bf16[256,896]{1,0:T(8,128)(2,1)S(1)} %collective-permute-done.34, bf16[1024,7168]{1,0:T(8,128)(2,1)S(1)} %bitcast.27, bf16[1024,512]{0,1:T(8,128)(2,1)S(1)} %copy-done.4), kind=kOutput, calls=%fused_computation.24 | convolution fusion | flops 472514560 | bytes 4653060 | tf_op jit(solution)/shard_map/dot_general | solution.py:139
  (109 shorter events, 22.4 us)
Async XLA Ops:
  3.0 17.9 %collective-permute-start = (bf16[256,512]{1,0:T(8,128)(2,1)S(1)}, bf16[256,512]{1,0:T(8,128)(2,1)}, u32[]{:S(2)}, u32[]{:S(2)}) collective-permute-start(bf16[256,512]{1,0:T(8,128)(2,1)S(1)} %shard_map.46), channel_id=1, source_target_pairs={{0,2},{1,3},{8,10},{9,11},{16,18},{17,19},{24,26},{25,27}} | collective-permute-start | bytes 786440 | tf_op jit(solution)/shard_map/ppermute | solution.py:131
  5.6 17.5 %collective-permute-start.2 = (bf16[256,512]{1,0:T(8,128)(2,1)S(1)}, bf16[256,512]{1,0:T(8,128)(2,1)}, u32[]{:S(2)}, u32[]{:S(2)}) collective-permute-start(bf16[256,512]{1,0:T(8,128)(2,1)S(1)} %shard_map.48), channel_id=1, source_target_pairs={{0,2},{1,3},{8,10},{9,11},{16,18},{17,19},{24,26},{25,27}} | collective-permute-start | bytes 786440 | tf_op jit(solution)/shard_map/ppermute | solution.py:131
  8.2 26.5 %collective-permute-start.6 = (bf16[256,512]{1,0:T(8,128)(2,1)S(1)}, bf16[256,512]{1,0:T(8,128)(2,1)S(1)}, u32[]{:S(2)}, u32[]{:S(2)}) collective-permute-start(bf16[256,512]{1,0:T(8,128)(2,1)S(1)} %shard_map.49), channel_id=1, source_target_pairs={{0,2},{1,3},{8,10},{9,11},{16,18},{17,19},{24,26},{25,27}} | collective-permute-start | bytes 786440 | tf_op jit(solution)/shard_map/ppermute | solution.py:131
  10.7 36.9 %collective-permute-start.4 = (bf16[256,512]{1,0:T(8,128)(2,1)S(1)}, bf16[256,512]{1,0:T(8,128)(2,1)S(1)}, u32[]{:S(2)}, u32[]{:S(2)}) collective-permute-start(bf16[256,512]{1,0:T(8,128)(2,1)S(1)} %shard_map.47), channel_id=1, source_target_pairs={{0,2},{1,3},{8,10},{9,11},{16,18},{17,19},{24,26},{25,27}} | collective-permute-start | bytes 786440 | tf_op jit(solution)/shard_map/ppermute | solution.py:131
  12.1 13.1 %copy-start = (s32[4096,56]{0,1:T(8,128)S(1)}, s32[4096,56]{0,1:T(8,128)}, u32[]{:S(2)}) copy-start(s32[4096,56]{0,1:T(8,128)} %param.5) | copy-start | bytes 2752516
  21.0 12.3 %collective-permute-start.1 = (bf16[256,512]{1,0:T(8,128)(2,1)}, bf16[256,512]{1,0:T(8,128)(2,1)S(1)}, u32[]{:S(2)}, u32[]{:S(2)}) collective-permute-start(bf16[256,512]{1,0:T(8,128)(2,1)} %collective-permute-done), channel_id=1, source_target_pairs={{2,4},{3,5},{10,12},{11,13},{18,20},{19,21},{26,28},{27,29}} | collective-permute-start | bytes 786440 | tf_op jit(solution)/shard_map/ppermute | solution.py:131
  23.1 14.8 %collective-permute-start.5 = (bf16[256,512]{1,0:T(8,128)(2,1)}, bf16[256,512]{1,0:T(8,128)(2,1)}, u32[]{:S(2)}, u32[]{:S(2)}) collective-permute-start(bf16[256,512]{1,0:T(8,128)(2,1)} %collective-permute-done.2), channel_id=1, source_target_pairs={{2,4},{3,5},{10,12},{11,13},{18,20},{19,21},{26,28},{27,29}} | collective-permute-start | bytes 786440 | tf_op jit(solution)/shard_map/ppermute | solution.py:131
  33.3 19.6 %collective-permute-start.3 = (bf16[256,512]{1,0:T(8,128)(2,1)S(1)}, bf16[256,512]{1,0:T(8,128)(2,1)}, u32[]{:S(2)}, u32[]{:S(2)}) collective-permute-start(bf16[256,512]{1,0:T(8,128)(2,1)S(1)} %collective-permute-done.1), channel_id=1, source_target_pairs={{4,6},{5,7},{12,14},{13,15},{20,22},{21,23},{28,30},{29,31}} | collective-permute-start | bytes 786440 | tf_op jit(solution)/shard_map/ppermute | solution.py:131
  34.7 19.6 %collective-permute-start.8 = (bf16[256,512]{1,0:T(8,128)(2,1)S(1)}, bf16[256,512]{1,0:T(8,128)(2,1)}, u32[]{:S(2)}, u32[]{:S(2)}) collective-permute-start(bf16[256,512]{1,0:T(8,128)(2,1)S(1)} %collective-permute-done.6), channel_id=1, source_target_pairs={{2,4},{3,5},{10,12},{11,13},{18,20},{19,21},{26,28},{27,29}} | collective-permute-start | bytes 786440 | tf_op jit(solution)/shard_map/ppermute | solution.py:131
  38.0 17.0 %collective-permute-start.7 = (bf16[256,512]{1,0:T(8,128)(2,1)}, bf16[256,512]{1,0:T(8,128)(2,1)}, u32[]{:S(2)}, u32[]{:S(2)}) collective-permute-start(bf16[256,512]{1,0:T(8,128)(2,1)} %collective-permute-done.5), channel_id=1, source_target_pairs={{4,6},{5,7},{12,14},{13,15},{20,22},{21,23},{28,30},{29,31}} | collective-permute-start | bytes 786440 | tf_op jit(solution)/shard_map/ppermute | solution.py:131
  47.6 7.3 %collective-permute-start.10 = (bf16[256,512]{1,0:T(8,128)(2,1)S(1)}, bf16[256,512]{1,0:T(8,128)(2,1)}, u32[]{:S(2)}, u32[]{:S(2)}) collective-permute-start(bf16[256,512]{1,0:T(8,128)(2,1)S(1)} %collective-permute-done.4), channel_id=1, source_target_pairs={{2,4},{3,5},{10,12},{11,13},{18,20},{19,21},{26,28},{27,29}} | collective-permute-start | bytes 786440 | tf_op jit(solution)/shard_map/ppermute | solution.py:131
  51.2 30.6 %slice-start.2 = ((s8[7340032]{0:T(1024)(128)(4,1)}), s8[4194304]{0:T(1024)(128)(4,1)S(1)}, s32[]{:S(2)}) async-start(s8[7340032]{0:T(1024)(128)(4,1)} %bitcast.24), calls=%async_computation.2 | async-start | bytes 8388608
  51.4 30.4 %copy-start.5 = (bf16[256,512]{1,0:T(8,128)(2,1)}, bf16[256,512]{1,0:T(8,128)(2,1)S(1)}, u32[]{:S(2)}) copy-start(bf16[256,512]{1,0:T(8,128)(2,1)S(1)} %get-tuple-element.67) | copy-start | bytes 786436
  51.4 30.4 %copy-start.7 = (bf16[256,512]{1,0:T(8,128)(2,1)}, bf16[256,512]{1,0:T(8,128)(2,1)S(1)}, u32[]{:S(2)}) copy-start(bf16[256,512]{1,0:T(8,128)(2,1)S(1)} %get-tuple-element.63) | copy-start | bytes 786436
  51.4 36.9 %collective-permute-start.19 = (bf16[256,512]{1,0:T(8,128)(2,1)S(1)}, bf16[256,512]{1,0:T(8,128)(2,1)}, u32[]{:S(2)}, u32[]{:S(2)}) collective-permute-start(bf16[256,512]{1,0:T(8,128)(2,1)S(1)} %get-tuple-element.63), channel_id=1, source_target_pairs={{0,2},{1,3},{8,10},{9,11},{16,18},{17,19},{24,26},{25,27}} | collective-permute-start | bytes 786440 | tf_op jit(solution)/shard_map/ppermute | solution.py:131
  52.9 38.4 %collective-permute-start.22 = (bf16[256,512]{1,0:T(8,128)(2,1)S(1)}, bf16[256,512]{1,0:T(8,128)(2,1)}, u32[]{:S(2)}, u32[]{:S(2)}) collective-permute-start(bf16[256,512]{1,0:T(8,128)(2,1)S(1)} %get-tuple-element.67), channel_id=1, source_target_pairs={{0,2},{1,3},{8,10},{9,11},{16,18},{17,19},{24,26},{25,27}} | collective-permute-start | bytes 786440 | tf_op jit(solution)/shard_map/ppermute | solution.py:131
  54.3 5.0 %collective-permute-start.9 = (bf16[256,512]{1,0:T(8,128)(2,1)}, bf16[256,512]{1,0:T(8,128)(2,1)S(1)}, u32[]{:S(2)}, u32[]{:S(2)}) collective-permute-start(bf16[256,512]{1,0:T(8,128)(2,1)} %collective-permute-done.8), channel_id=1, source_target_pairs={{4,6},{5,7},{12,14},{13,15},{20,22},{21,23},{28,30},{29,31}} | collective-permute-start | bytes 786440 | tf_op jit(solution)/shard_map/ppermute | solution.py:131
  55.0 4.5 %collective-permute-start.11 = (bf16[256,512]{1,0:T(8,128)(2,1)}, bf16[256,512]{1,0:T(8,128)(2,1)S(1)}, u32[]{:S(2)}, u32[]{:S(2)}) collective-permute-start(bf16[256,512]{1,0:T(8,128)(2,1)} %collective-permute-done.10), channel_id=1, source_target_pairs={{4,6},{5,7},{12,14},{13,15},{20,22},{21,23},{28,30},{29,31}} | collective-permute-start | bytes 786440 | tf_op jit(solution)/shard_map/ppermute | solution.py:131
  57.9 13.6 %collective-permute-start.13 = (bf16[256,512]{1,0:T(8,128)(2,1)S(1)}, bf16[256,512]{1,0:T(8,128)(2,1)S(1)}, u32[]{:S(2)}, u32[]{:S(2)}) collective-permute-start(bf16[256,512]{1,0:T(8,128)(2,1)S(1)} %select_select_fusion.4), channel_id=1, source_target_pairs={{0,1},{1,0},{2,3},{3,2},{4,5},{5,4},{6,7},{7,6},{8,9},{9,8},{10,11... | collective-permute-start | bytes 786440 | tf_op jit(solution)/shard_map/ppermute | solution.py:127
  59.2 10.8 %collective-permute-start.12 = (bf16[256,512]{1,0:T(8,128)(2,1)S(1)}, bf16[256,512]{1,0:T(8,128)(2,1)S(1)}, u32[]{:S(2)}, u32[]{:S(2)}) collective-permute-start(bf16[256,512]{1,0:T(8,128)(2,1)S(1)} %select_select_fusion.5), channel_id=1, source_target_pairs={{0,1},{1,0},{2,3},{3,2},{4,5},{5,4},{6,7},{7,6},{8,9},{9,8},{10,11... | collective-permute-start | bytes 786440 | tf_op jit(solution)/shard_map/ppermute | solution.py:127
  59.5 22.3 %slice-start.3 = ((s8[7340032]{0:T(1024)(128)(4,1)}), s8[3145728]{0:T(1024)(128)(4,1)S(1)}, s32[]{:S(2)}) async-start(s8[7340032]{0:T(1024)(128)(4,1)} %bitcast.24), calls=%async_computation.3 | async-start | bytes 6291456
  59.5 16.2 %collective-permute-start.14 = (bf16[256,512]{1,0:T(8,128)(2,1)S(1)}, bf16[256,512]{1,0:T(8,128)(2,1)S(1)}, u32[]{:S(2)}, u32[]{:S(2)}) collective-permute-start(bf16[256,512]{1,0:T(8,128)(2,1)S(1)} %select_select_fusion.3), channel_id=1, source_target_pairs={{0,1},{1,0},{2,3},{3,2},{4,5},{5,4},{6,7},{7,6},{8,9},{9,8},{10,11... | collective-permute-start | bytes 786440 | tf_op jit(solution)/shard_map/ppermute | solution.py:127
  70.0 11.2 %collective-permute-start.15 = (bf16[256,512]{1,0:T(8,128)(2,1)S(1)}, bf16[256,512]{1,0:T(8,128)(2,1)S(1)}, u32[]{:S(2)}, u32[]{:S(2)}) collective-permute-start(bf16[256,512]{1,0:T(8,128)(2,1)S(1)} %select_select_fusion.2), channel_id=1, source_target_pairs={{0,1},{1,0},{2,3},{3,2},{4,5},{5,4},{6,7},{7,6},{8,9},{9,8},{10,11... | collective-permute-start | bytes 786440 | tf_op jit(solution)/shard_map/ppermute | solution.py:127
  81.8 14.0 %copy-start.3 = (bf16[256,2048]{1,0:T(8,128)(2,1)}, bf16[256,2048]{1,0:T(8,128)(2,1)S(1)}, u32[]{:S(2)}) copy-start(bf16[256,2048]{1,0:T(8,128)(2,1)S(1)} %get-tuple-element.84) | copy-start | bytes 3145732
  81.8 21.5 %copy-start.2 = (bf16[256,2048]{1,0:T(8,128)(2,1)}, bf16[256,2048]{1,0:T(8,128)(2,1)S(1)}, u32[]{:S(2)}) copy-start(bf16[256,2048]{1,0:T(8,128)(2,1)S(1)} %get-tuple-element.83) | copy-start | bytes 3145732
  85.2 18.1 %collective-permute-start.16 = (f32[256,896]{1,0:T(8,128)}, f32[256,896]{1,0:T(8,128)}, u32[]{:S(2)}, u32[]{:S(2)}) collective-permute-start(f32[256,896]{1,0:T(8,128)} %fusion.51), channel_id=1, source_target_pairs={{0,8},{8,0},{16,24},{24,16},{1,9},{9,1},{17,25},{25,17},{2,10},{10... | collective-permute-start | bytes 2752520 | tf_op jit(solution)/shard_map/ppermute | solution.py:127
  88.2 5.2 %collective-permute-start.17 = (f32[256,256]{1,0:T(8,128)S(1)}, f32[256,256]{1,0:T(8,128)}, u32[]{:S(2)}, u32[]{:S(2)}) collective-permute-start(f32[256,256]{1,0:T(8,128)S(1)} %fusion.50), channel_id=1, source_target_pairs={{0,8},{8,0},{16,24},{24,16},{1,9},{9,1},{17,25},{25,17},{2,10},{10... | collective-permute-start | bytes 786440 | tf_op jit(solution)/shard_map/ppermute | solution.py:127
  88.3 19.9 %collective-permute-start.20 = (bf16[256,512]{1,0:T(8,128)(2,1)}, bf16[256,512]{1,0:T(8,128)(2,1)}, u32[]{:S(2)}, u32[]{:S(2)}) collective-permute-start(bf16[256,512]{1,0:T(8,128)(2,1)} %collective-permute-done.19), channel_id=1, source_target_pairs={{2,4},{3,5},{10,12},{11,13},{18,20},{19,21},{26,28},{27,29}} | collective-permute-start | bytes 786440 | tf_op jit(solution)/shard_map/ppermute | solution.py:131
  91.4 18.3 %collective-permute-start.23 = (bf16[256,512]{1,0:T(8,128)(2,1)}, bf16[256,512]{1,0:T(8,128)(2,1)}, u32[]{:S(2)}, u32[]{:S(2)}) collective-permute-start(bf16[256,512]{1,0:T(8,128)(2,1)} %collective-permute-done.22), channel_id=1, source_target_pairs={{2,4},{3,5},{10,12},{11,13},{18,20},{19,21},{26,28},{27,29}} | collective-permute-start | bytes 786440 | tf_op jit(solution)/shard_map/ppermute | solution.py:131
  93.4 10.0 %slice-start = ((s8[7340032]{0:T(1024)(128)(4,1)}), s8[4194304]{0:T(1024)(128)(4,1)S(1)}, s32[]{:S(2)}) async-start(s8[7340032]{0:T(1024)(128)(4,1)} %bitcast.22), calls=%async_computation | async-start | bytes 8388608
  94.5 8.7 %collective-permute-start.18 = (f32[256,256]{1,0:T(8,128)S(1)}, f32[256,256]{1,0:T(8,128)S(1)}, u32[]{:S(2)}, u32[]{:S(2)}) collective-permute-start(f32[256,256]{1,0:T(8,128)S(1)} %add.192), channel_id=1, source_target_pairs={{0,16},{8,24},{16,0},{24,8},{1,17},{9,25},{17,1},{25,9},{2,18},{10... | collective-permute-start | bytes 786440 | tf_op jit(solution)/shard_map/ppermute | solution.py:127
  102.2 28.9 %collective-permute-start.25 = (f32[256,896]{1,0:T(8,128)}, f32[256,896]{1,0:T(8,128)S(1)}, u32[]{:S(2)}, u32[]{:S(2)}) collective-permute-start(f32[256,896]{1,0:T(8,128)} %fusion.49), channel_id=1, source_target_pairs={{0,8},{8,0},{16,24},{24,16},{1,9},{9,1},{17,25},{25,17},{2,10},{10... | collective-permute-start | bytes 2752520 | tf_op jit(solution)/shard_map/ppermute | solution.py:127
  108.2 12.8 %copy-start.6 = (bf16[256,512]{1,0:T(8,128)(2,1)S(1)}, bf16[256,512]{1,0:T(8,128)(2,1)}, u32[]{:S(2)}) copy-start(bf16[256,512]{1,0:T(8,128)(2,1)} %copy-done.5) | copy-start | bytes 786436
  108.2 11.8 %collective-permute-start.21 = (bf16[256,512]{1,0:T(8,128)(2,1)}, bf16[256,512]{1,0:T(8,128)(2,1)}, u32[]{:S(2)}, u32[]{:S(2)}) collective-permute-start(bf16[256,512]{1,0:T(8,128)(2,1)} %collective-permute-done.20), channel_id=1, source_target_pairs={{4,6},{5,7},{12,14},{13,15},{20,22},{21,23},{28,30},{29,31}} | collective-permute-start | bytes 786440 | tf_op jit(solution)/shard_map/ppermute | solution.py:131
  109.7 11.3 %collective-permute-start.24 = (bf16[256,512]{1,0:T(8,128)(2,1)}, bf16[256,512]{1,0:T(8,128)(2,1)}, u32[]{:S(2)}, u32[]{:S(2)}) collective-permute-start(bf16[256,512]{1,0:T(8,128)(2,1)} %collective-permute-done.23), channel_id=1, source_target_pairs={{4,6},{5,7},{12,14},{13,15},{20,22},{21,23},{28,30},{29,31}} | collective-permute-start | bytes 786440 | tf_op jit(solution)/shard_map/ppermute | solution.py:131
  119.2 22.3 %collective-permute-start.26 = (f32[256,896]{1,0:T(8,128)}, f32[256,896]{1,0:T(8,128)S(1)}, u32[]{:S(2)}, u32[]{:S(2)}) collective-permute-start(f32[256,896]{1,0:T(8,128)} %convolution_add_fusion), channel_id=1, source_target_pairs={{0,16},{8,24},{16,0},{24,8},{1,17},{9,25},{17,1},{25,9},{2,18},{10... | collective-permute-start | bytes 2752520 | tf_op jit(solution)/shard_map/ppermute | solution.py:127
  142.5 7.1 %collective-permute-start.29 = (bf16[512,896]{1,0:T(8,128)(2,1)S(1)}, bf16[512,896]{1,0:T(8,128)(2,1)S(1)}, u32[]{:S(2)}, u32[]{:S(2)}) collective-permute-start(bf16[512,896]{1,0:T(8,128)(2,1)S(1)} %get-tuple-element.74), channel_id=1, source_target_pairs={{0,8},{8,0},{16,24},{24,16},{1,9},{9,1},{17,25},{25,17},{2,10},{10... | collective-permute-start | bytes 2752520 | tf_op jit(solution)/shard_map/ppermute | solution.py:127
  143.4 12.0 %collective-permute-start.27 = (bf16[256,896]{1,0:T(8,128)(2,1)S(1)}, bf16[256,896]{1,0:T(8,128)(2,1)S(1)}, u32[]{:S(2)}, u32[]{:S(2)}) collective-permute-start(bf16[256,896]{1,0:T(8,128)(2,1)S(1)} %get-tuple-element.72), channel_id=1, source_target_pairs={{0,16},{8,24},{16,0},{24,8},{1,17},{9,25},{17,1},{25,9},{2,18},{10... | collective-permute-start | bytes 1376264 | tf_op jit(solution)/shard_map/ppermute | solution.py:127
  144.1 11.7 %collective-permute-start.28 = (bf16[256,896]{1,0:T(8,128)(2,1)S(1)}, bf16[256,896]{1,0:T(8,128)(2,1)S(1)}, u32[]{:S(2)}, u32[]{:S(2)}) collective-permute-start(bf16[256,896]{1,0:T(8,128)(2,1)S(1)} %get-tuple-element.72), channel_id=1, source_target_pairs={{0,1},{1,0},{2,3},{3,2},{4,5},{5,4},{6,7},{7,6},{8,9},{9,8},{10,11... | collective-permute-start | bytes 1376264 | tf_op jit(solution)/shard_map/ppermute | solution.py:127
  145.5 24.3 %slice-start.4 = ((s8[14680064]{0:T(1024)(128)(4,1)}), s8[2097152]{0:T(1024)(128)(4,1)S(1)}, s32[]{:S(2)}) async-start(s8[14680064]{0:T(1024)(128)(4,1)} %bitcast.26), calls=%async_computation.4 | async-start | bytes 4194304
  145.5 24.3 %slice-start.5 = ((s8[14680064]{0:T(1024)(128)(4,1)}), s8[4194304]{0:T(1024)(128)(4,1)S(1)}, s32[]{:S(2)}) async-start(s8[14680064]{0:T(1024)(128)(4,1)} %bitcast.26), calls=%async_computation.5 | async-start | bytes 8388608
  149.7 20.1 %slice-start.6 = ((s8[14680064]{0:T(1024)(128)(4,1)}), s8[4194304]{0:T(1024)(128)(4,1)S(1)}, s32[]{:S(2)}) async-start(s8[14680064]{0:T(1024)(128)(4,1)} %bitcast.26), calls=%async_computation.6 | async-start | bytes 8388608
  155.8 14.0 %collective-permute-start.32 = (bf16[256,896]{1,0:T(8,128)(2,1)S(1)}, bf16[256,896]{1,0:T(8,128)(2,1)S(1)}, u32[]{:S(2)}, u32[]{:S(2)}) collective-permute-start(bf16[256,896]{1,0:T(8,128)(2,1)S(1)} %collective-permute-done.27), channel_id=1, source_target_pairs={{0,8},{8,0},{16,24},{24,16},{1,9},{9,1},{17,25},{25,17},{2,10},{10... | collective-permute-start | bytes 1376264 | tf_op jit(solution)/shard_map/ppermute | solution.py:127
  157.2 12.6 %slice-start.7 = ((s8[14680064]{0:T(1024)(128)(4,1)}), s8[4194304]{0:T(1024)(128)(4,1)S(1)}, s32[]{:S(2)}) async-start(s8[14680064]{0:T(1024)(128)(4,1)} %bitcast.26), calls=%async_computation.7 | async-start | bytes 8388608
  157.2 14.6 %collective-permute-start.33 = (bf16[256,896]{1,0:T(8,128)(2,1)S(1)}, bf16[256,896]{1,0:T(8,128)(2,1)S(1)}, u32[]{:S(2)}, u32[]{:S(2)}) collective-permute-start(bf16[256,896]{1,0:T(8,128)(2,1)S(1)} %collective-permute-done.28), channel_id=1, source_target_pairs={{0,8},{8,0},{16,24},{24,16},{1,9},{9,1},{17,25},{25,17},{2,10},{10... | collective-permute-start | bytes 1376264 | tf_op jit(solution)/shard_map/ppermute | solution.py:127
  160.9 6.5 %collective-permute-start.30 = (bf16[128,896]{1,0:T(8,128)(2,1)S(1)}, bf16[128,896]{1,0:T(8,128)(2,1)S(1)}, u32[]{:S(2)}, u32[]{:S(2)}) collective-permute-start(bf16[128,896]{1,0:T(8,128)(2,1)S(1)} %slice.26), channel_id=1, source_target_pairs={{0,16},{8,24},{16,0},{24,8},{1,17},{9,25},{17,1},{25,9},{2,18},{10... | collective-permute-start | bytes 688136 | tf_op jit(solution)/shard_map/ppermute | solution.py:127
  161.7 6.2 %collective-permute-start.31 = (bf16[128,896]{1,0:T(8,128)(2,1)S(1)}, bf16[128,896]{1,0:T(8,128)(2,1)S(1)}, u32[]{:S(2)}, u32[]{:S(2)}) collective-permute-start(bf16[128,896]{1,0:T(8,128)(2,1)S(1)} %slice.27), channel_id=1, source_target_pairs={{0,1},{1,0},{2,3},{3,2},{4,5},{5,4},{6,7},{7,6},{8,9},{9,8},{10,11... | collective-permute-start | bytes 688136 | tf_op jit(solution)/shard_map/ppermute | solution.py:127
  167.9 7.9 %collective-permute-start.34 = (bf16[256,896]{1,0:T(8,128)(2,1)S(1)}, bf16[256,896]{1,0:T(8,128)(2,1)S(1)}, u32[]{:S(2)}, u32[]{:S(2)}) collective-permute-start(bf16[256,896]{1,0:T(8,128)(2,1)S(1)} %pad_maximum_fusion.3), channel_id=1, source_target_pairs={{0,8},{8,0},{16,24},{24,16},{1,9},{9,1},{17,25},{25,17},{2,10},{10... | collective-permute-start | bytes 1376264 | tf_op jit(solution)/shard_map/ppermute | solution.py:127
  (4 other events, 28.2 us)

commit v6 on v5

--- a/solution.py
+++ b/solution.py
@@ -43,11 +43,100 @@
             ],
             out_specs=pl.BlockSpec((PANEL, piece), lambda i, place: (0, 0)),
         ),
-        compiler_params=pltpu.CompilerParams(vmem_limit_bytes=48 * MIB),
+        compiler_params=pltpu.CompilerParams(vmem_limit_bytes=8 * MIB),
         cost_estimate=pl.CostEstimate(
             flops=piece * PANEL, bytes_accessed=4 * piece * PANEL, transcendentals=0
         ),
     )(at.reshape(1).astype(jnp.int32), quantized, exponents)
+
+
+def scale_kernel(place_ref, exps_ref, quant_ref, out_ref, held_ref, sems):
+    parts, step, cols = held_ref.shape
+    slots, tokens, width = out_ref.shape
+    blocks, half = width // QBLOCK, cols // QBLOCK
+    tok, row = place_ref[0], place_ref[1]
+    base = pl.multiple_of(place_ref[2] * tokens, tokens)
+
+    def read(i):
+        return pltpu.make_async_copy(
+            quant_ref.at[
+                pl.ds(pl.multiple_of(base + i * step, step), step),
+                pl.ds(pl.multiple_of(row * cols, QBLOCK), cols),
+            ],
+            held_ref.at[i],
+            sems.at[i],
+        )
+
+    for i in range(parts):
+        read(i).start()
+
+    @pl.loop(0, parts)
+    def _(i):
+        read(i).wait()
+        exps = exps_ref[pl.ds(pl.multiple_of(base + i * step, step), step), :]
+        mine = exps[:, :half]
+        for other in range(1, exps.shape[1] // half):
+            mine = jnp.where(row == other, exps[:, other * half : (other + 1) * half], mine)
+        scale = jnp.exp2(mine.astype(F32))
+        rows = pl.ds(pl.multiple_of(i * step, step), step)
+        for slot in range(slots):
+            for c in range(blocks):
+                at = slot * blocks + c
+                wide = jnp.broadcast_to(scale[:, at : at + 1], (step, QBLOCK)).astype(BF16)
+                out_ref[tok ^ slot, rows, c * QBLOCK : (c + 1) * QBLOCK] = (
+                    held_ref[i, :, at * QBLOCK : (at + 1) * QBLOCK] * wide
+                )
+
+
+def scaled_quarter(quantized, exponents, place, link, slots, width, tokens):
+    parts = 8
+    return pl.pallas_call(
+        scale_kernel,
+        out_shape=jax.ShapeDtypeStruct((slots, tokens, width), BF16),
+        in_specs=[
+            pl.BlockSpec(memory_space=pltpu.SMEM),
+            pl.BlockSpec(memory_space=pltpu.VMEM),
+            pl.BlockSpec(memory_space=pl.ANY),
+        ],
+        out_specs=pl.BlockSpec(memory_space=pltpu.VMEM),
+        scratch_shapes=[
+            pltpu.VMEM((parts, tokens // parts, slots * width), BF16),
+            pltpu.SemaphoreType.DMA((parts,)),
+        ],
+        compiler_params=pltpu.CompilerParams(vmem_limit_bytes=12 * MIB),
+        cost_estimate=pl.CostEstimate(
+            flops=tokens * width, bytes_accessed=tokens * width, transcendentals=0
+        ),
+    )(after(jnp.stack(place).astype(jnp.int32), link), exponents, quantized)
+
+
+def gram_kernel(block, quarters, panel_ref, *refs):
+    tokens = panel_ref.shape[1] // quarters
+    total = None
+    for q in range(quarters):
+        part = jnp.dot(
+            panel_ref[:, q * tokens : (q + 1) * tokens],
+            refs[q][block],
+            preferred_element_type=F32,
+        )
+        total = part if total is None else total + part
+    refs[-1][...] = total if len(refs) == quarters + 1 else total + refs[quarters][...]
+
+
+def gram_block(panel, acts, block, extra=None):
+    width = acts[0].shape[2]
+    args = [panel, *acts] + ([] if extra is None else [extra])
+    vmem = pl.BlockSpec(memory_space=pltpu.VMEM)
+    return pl.pallas_call(
+        functools.partial(gram_kernel, block, len(acts)),
+        out_shape=jax.ShapeDtypeStruct((PANEL, width), F32),
+        in_specs=[vmem] * len(args),
+        out_specs=vmem,
+        compiler_params=pltpu.CompilerParams(vmem_limit_bytes=12 * MIB),
+        cost_estimate=pl.CostEstimate(
+            flops=PANEL * PANEL * width, bytes_accessed=4 * PANEL * width, transcendentals=0
+        ),
+    )(*args)
 
 
 def inverse_kernel(head_ref, out_ref, pair_ref):
@@ -86,9 +175,9 @@
         inverse_kernel,
         out_shape=jax.ShapeDtypeStruct((PANEL, PANEL), F32),
         scratch_shapes=[pltpu.VMEM((2 * PANEL, PANEL), F32)],
-        compiler_params=pltpu.CompilerParams(vmem_limit_bytes=32 * MIB),
-        cost_estimate=pl.CostEstimate(
-            flops=28 * 12 * PANEL**3, bytes_accessed=8 * PANEL * PANEL, transcendentals=0
+        compiler_params=pltpu.CompilerParams(vmem_limit_bytes=8 * MIB),
+        cost_estimate=pl.CostEstimate(
+            flops=2 * PANEL**3, bytes_accessed=8 * PANEL * PANEL, transcendentals=0
         ),
     )(head)
 
@@ -115,7 +204,7 @@
             jax.ShapeDtypeStruct((2 * PANEL, width), BF16),
         ),
         in_specs=[pl.BlockSpec(memory_space=pltpu.SMEM)] + [vmem] * 4,
-        compiler_params=pltpu.CompilerParams(vmem_limit_bytes=32 * MIB),
+        compiler_params=pltpu.CompilerParams(vmem_limit_bytes=8 * MIB),
         cost_estimate=pl.CostEstimate(
             flops=12 * PANEL * PANEL * width, bytes_accessed=16 * PANEL * width, transcendentals=0
         ),
@@ -162,15 +251,28 @@
     for c in range(ROUNDS):
         got[c].append(hop(got[c][0], "feat", 0))
 
-    def scaled(k, link):
-        scale = jnp.exp2(after(exponents, link).astype(F32)).astype(BF16)
-        start = (row * toks + (tok ^ k)) * width
-        block = (start + lax.broadcasted_iota(jnp.int32, (1, width), 1)) // QBLOCK
-        spread = lax.broadcasted_iota(jnp.int32, (scale.shape[1], width), 0) == block
-        wide = dot(scale, spread.astype(BF16)).astype(BF16)
-        return lax.dynamic_slice_in_dim(quantized, start, width, 1) * wide
-
-    acts = {3: scaled(3, got[-1][0])}
+    quarters = 4
+    kernels = width % QBLOCK == 0
+
+    def scaled(q, link):
+        if kernels:
+            place = (tok, row, jnp.int32(q))
+            return scaled_quarter(
+                quantized, exponents, place, link, toks, width, tokens // quarters
+            )
+        span = slice(q * tokens // quarters, (q + 1) * tokens // quarters)
+        scale = jnp.exp2(after(exponents, link)[span].astype(F32)).astype(BF16)
+        acts = quantized[span] * jnp.repeat(scale, QBLOCK, axis=1)
+        starts = [(row * toks + (tok ^ k)) * width for k in range(toks)]
+        return jnp.stack([lax.dynamic_slice_in_dim(acts, at, width, 1) for at in starts])
+
+    def gram(k, *extra):
+        if kernels:
+            return gram_block(panel, acts, k, *extra)
+        block = jnp.concatenate([part[k] for part in acts], axis=0)
+        return sum(extra, dot(panel, block))
+
+    acts = [scaled(0, got[-1][0])]
 
     def settle(parts):
         result = parts[0]
@@ -179,7 +281,7 @@
         return result
 
     events = sorted((5 * (c + 1) + 8 * h, c, h) for c in range(ROUNDS) for h in range(hops))
-    full, swapped, token, errors = [], [], acts[3], []
+    full, swapped, token = [], [], acts[0]
     for _, c, h in events:
         x = after(got[c][h + 1], token)
         got[c][h + 1] = token = x
@@ -188,24 +290,19 @@
         else:
             full.append(settle(got[c]))
             swapped.append(swap(full[-1], "row", 1))
-        if (c, h) == (1, 0):
-            acts[2] = token = scaled(2, x)
-        elif (c, h) == (1, 1):
-            acts[1] = token = scaled(1, x)
-        elif (c, h) == (0, 1):
-            panel_weights, mask = after(weights[:, :PANEL], x), after(keep_mask, x)
-            error = jnp.where(mask == 0, panel_weights, jnp.zeros((), BF16)).T
-            extras = -(-error.shape[1] // piece)
-            error = jnp.pad(error, ((0, 0), (0, extras * piece - error.shape[1])))
-            errors = [[error[:, i * piece : (i + 1) * piece]] for i in range(extras)]
-        elif (c, h) == (ROUNDS - 1, 0):
-            for parts in errors:
-                parts[0] = after(parts[0], x)
-                parts.append(hop(parts[0], "feat", 0))
-        elif (c, h) == (ROUNDS - 1, 1):
-            for parts in errors:
-                parts[1] = after(parts[1], x)
-                parts.append(hop(parts[1], "feat", 1))
+        if (c, h) in ((1, 0), (2, 0), (2, 1)):
+            acts.append(scaled(len(acts), x))
+            token = acts[-1]
+    panel_weights, mask = after(weights[:, :PANEL], full[0]), after(keep_mask, full[0])
+    error = jnp.where(mask == 0, panel_weights, jnp.zeros((), BF16)).T
+    extras = -(-error.shape[1] // piece)
+    error = jnp.pad(error, ((0, 0), (0, extras * piece - error.shape[1])))
+    errors = [
+        [after(error[:, i * piece : (i + 1) * piece], full[-1], swapped[0])]
+        for i in range(extras)
+    ]
+    for parts in errors:
+        parts.append(hop(parts[0], "feat", 0))
 
     own, other = jnp.concatenate(full, axis=1), jnp.concatenate(swapped, axis=1)
     panel = jnp.concatenate(
@@ -216,25 +313,29 @@
         panel, panel, (((1,), (1,)), ((), ())), preferred_element_type=F32
     )
     head = head + swap(head, "tok", 1)
-    block3 = dot(panel, acts[3])
+    block3 = gram(3)
     from3 = swap(block3, "tok", 1)
+    for parts in errors:
+        parts[1] = after(parts[1], block3)
+        parts.append(hop(parts[1], "feat", 1))
     head = head + swap(head, "tok", 2)
-    acts[2] = after(acts[2], from3)
-    block2 = dot(panel, acts[2]) + from3
+    block2 = gram(2, from3)
     block2, head = lax.optimization_barrier((block2, head))
     fromx = swap(block2, "tok", 2)
+    panel = after(panel, block2)
+    block1 = gram(1)
+    from1 = swap(block1, "tok", 1)
     for parts in errors:
-        parts[2] = after(parts[2], block2)
+        parts[2] = after(parts[2], block1)
         for h in range(2, hops):
             parts.append(hop(parts[h], "feat", h))
-    block1 = dot(panel, acts[1])
-    from1 = swap(block1, "tok", 1)
-    block0 = dot(panel, scaled(0, block1))
+    panel = after(panel, block1)
+    block0 = gram(0)
+    inverse = invert(after(head, block0))
     error = jnp.concatenate([settle(parts) for parts in errors], axis=1)
-    error = error[:, : weights.shape[0]].T
+    error = after(error[:, : weights.shape[0]].T, inverse)
     twice = jnp.concatenate([error, error], axis=1)
-    head, twice = lax.optimization_barrier((head, twice))
-    inverse = invert(head)
+    inverse, twice = lax.optimization_barrier((inverse, twice))
     start = jnp.where(root, (row * toks + tok) * width, PANEL)
     high, pair = make_gains(inverse, (block0, from1, fromx), start)
 
@@ -253,11 +354,12 @@
     out = update(out, near, 1, 0)
     in_x, in_y, out = lax.optimization_barrier((in_x, in_y, out))
     top, bottom, out = lax.optimization_barrier((in_y[:half], in_x[half:], out))
-    far = jnp.concatenate([swap(top, "tok", 2), swap(bottom, "row", 1)], axis=0)
+    far = [swap(top, "tok", 2), swap(bottom, "row", 1)]
     near_x, near_y = swap(in_x, "tok", 1), swap(in_y, "tok", 1)
-    out = update(out, in_x, 2, 0)
+    out = update(after(out, near_x, near_y), in_x, 2, 0)
     out = update(out, in_y, 0, 1)
-    far, out = lax.optimization_barrier((far, out))
+    far[0], far[1], out = lax.optimization_barrier((far[0], far[1], out))
+    far = jnp.concatenate(far, axis=0)
     near_far = swap(far, "tok", 1)
     out = update(out, near_x, 3, 0)
     out = update(out, near_y, 1, 1)

time: 179 us -> 206 us (1.15)
  local copies, waits for them, and re-layouts: 3.78 us -> 47.3 us
  matrix products: 72 us -> 30.1 us
  Pallas kernels: 13.9 us -> 46.4 us
  waiting for transfers between devices: 32.6 us -> 26.8 us
  starting transfers between devices: 47.6 us -> 44 us
  other arithmetic: 7.21 us -> 9.84 us
    dot_general x15 -> x8, matrix products: 71.3 us -> 29.3 us  [dot(): return jnp.dot(left, right, preferred_element_type=F32)]
    unnamed x36 -> x77, local copies, waits for them, and re-layouts: 1.91 us -> 41.6 us
    pallas_call x0 -> x8, Pallas kernels: none -> 32.5 us  [the longest x4 21.1 us: scaled_quarter(): pl.pallas_call(scale_kernel, out_shape=jax.ShapeDtypeStruct((slots, token...]
    ppermute x17, waiting for transfers between devices: 32.5 us -> 17.7 us  [swap(): return lax.ppermute(x, axis, [(i, i ^ bit) for i in range(size)])]
    ppermute x18, waiting for transfers between devices: 0.05 us -> 9.13 us  [hop(): return lax.ppermute(x, axis, [(start, start + 1)])]
    ppermute x17, starting transfers between devices: 18 us -> 13.9 us  [swap(): return lax.ppermute(x, axis, [(i, i ^ bit) for i in range(size)])]
    select_n x6, other arithmetic: 4.16 us -> 6.64 us  [settle(): result = jnp.where(feat == h + 1, parts[h + 1], result)]
  transfers between devices with their start and end apart: 35 -> 35, of which waited for: 8 -> 7; matrix products, arithmetic and copies ran while one was open for 45% -> 21% of each run, Pallas kernels for 7% -> 20%
where the time goes in v6:
time: 206 us; the launch traced here: 205 us
  local copies, waits for them, and re-layouts  47.3 us (23%)
  Pallas kernels  46.4 us (23%)
  starting transfers between devices  44 us (21%)
  matrix products  30.1 us (15%)
  waiting for transfers between devices  26.8 us (13%)
  other arithmetic  9.84 us (5%)
    unnamed x77, local copies, waits for them, and re-layouts  41.6 us
    ppermute x18, starting transfers between devices, hop(): return lax.ppermute(x, axis, [(start, start + 1)])  30 us
    dot_general x8, matrix products, dot(): return jnp.dot(left, right, preferred_element_type=F32)  29.3 us
    pallas_call x4, Pallas kernels, scaled_quarter(): pl.pallas_call(scale_kernel, out_shape=jax.ShapeDtypeStruct((slots, token...  21.1 us
    ppermute x17, waiting for transfers between devices, swap(): return lax.ppermute(x, axis, [(i, i ^ bit) for i in range(size)])  17.7 us
    ppermute x17, starting transfers between devices, swap(): return lax.ppermute(x, axis, [(i, i ^ bit) for i in range(size)])  13.9 us
    pallas_call x4, Pallas kernels, gram_block(): pl.pallas_call(functools.partial(gram_kernel, block, len(acts)), out_shap...  11.4 us
    ppermute x18, waiting for transfers between devices, hop(): return lax.ppermute(x, axis, [(start, start + 1)])  9.13 us
  transfers between devices with their start and end apart: 35, of which 7 were waited for; matrix products, arithmetic and copies ran while one was open for 21% of the time, Pallas kernels for 20%

profile of v6, /device:TPU:9, one launch (start us, length us, event | category | flops | bytes accessed | tf_op | source)
XLA Modules:
  0.0 205.0 jit_solution(17889591253135160823)
XLA Ops:
  0.0 1.8 copy.5.exps_ref
  8.3 5.3 %shard_map.48.refs_0_ = bf16[4,1024,896]{2,1,0:T(8,128)(2,1)S(1)} custom-call(s32[3]{0:T(128)S(1)} %get-tuple-element.49.place_ref, s32[4096,56]{1,0:T(8,128)S(1)} %copy.5.exps_ref, bf16[4096,7168]{1,0:T(8,128)(2,1)} %quant_ref.15), custom_call_target="tpu_custom_call" | custom-call | flops 917504 | bytes 917504 | tf_op jit(solution)/shard_map/pallas_call | solution.py:93
  13.6 3.0 %copy-done = bf16[4,1024,896]{2,1,0:T(8,128)(2,1)} copy-done((bf16[4,1024,896]{2,1,0:T(8,128)(2,1)}, bf16[4,1024,896]{2,1,0:T(8,128)(2,1)S(1)}, u32[]{:S(2)}) %copy-start) | copy-done | bytes 7340056
  16.7 4.0 %collective-permute-start.1 = (bf16[256,512]{1,0:T(8,128)(2,1)}, bf16[256,512]{1,0:T(8,128)(2,1)}, u32[]{:S(2)}, u32[]{:S(2)}) collective-permute-start(bf16[256,512]{1,0:T(8,128)(2,1)} %collective-permute-done), channel_id=1, source_target_pairs={{2,4},{3,5},{10,12},{11,13},{18,20},{19,21},{26,28},{27,29}} | collective-permute-start | bytes 786440 | tf_op jit(solution)/shard_map/ppermute | solution.py:220
  23.3 2.0 collective-permute-start.5
  26.6 5.3 %shard_map.50.refs_1_ = bf16[4,1024,896]{2,1,0:T(8,128)(2,1)S(1)} custom-call(s32[3]{0:T(128)S(1)} %get-tuple-element.52.place_ref, s32[4096,56]{1,0:T(8,128)S(1)} %copy.5.exps_ref, bf16[4096,7168]{1,0:T(8,128)(2,1)} %quant_ref.15), custom_call_target="tpu_custom_call" | custom-call | flops 917504 | bytes 917504 | tf_op jit(solution)/shard_map/pallas_call | solution.py:93
  31.9 2.9 %copy-done.2 = bf16[4,1024,896]{2,1,0:T(8,128)(2,1)} copy-done((bf16[4,1024,896]{2,1,0:T(8,128)(2,1)}, bf16[4,1024,896]{2,1,0:T(8,128)(2,1)S(1)}, u32[]{:S(2)}) %copy-start.2) | copy-done | bytes 7340056
  36.2 3.5 %collective-permute-start.8 = (bf16[256,512]{1,0:T(8,128)(2,1)}, bf16[256,512]{1,0:T(8,128)(2,1)}, u32[]{:S(2)}, u32[]{:S(2)}) collective-permute-start(bf16[256,512]{1,0:T(8,128)(2,1)} %collective-permute-done.6), channel_id=1, source_target_pairs={{2,4},{3,5},{10,12},{11,13},{18,20},{19,21},{26,28},{27,29}} | collective-permute-start | bytes 786440 | tf_op jit(solution)/shard_map/ppermute | solution.py:220
  39.6 5.3 %shard_map.52.refs_2_ = bf16[4,1024,896]{2,1,0:T(8,128)(2,1)S(1)} custom-call(s32[3]{0:T(128)S(1)} %get-tuple-element.55.place_ref, s32[4096,56]{1,0:T(8,128)S(1)} %copy.5.exps_ref, bf16[4096,7168]{1,0:T(8,128)(2,1)} %quant_ref.15), custom_call_target="tpu_custom_call" | custom-call | flops 917504 | bytes 917504 | tf_op jit(solution)/shard_map/pallas_call | solution.py:93
  44.9 3.0 %copy-done.6 = bf16[4,1024,896]{2,1,0:T(8,128)(2,1)} copy-done((bf16[4,1024,896]{2,1,0:T(8,128)(2,1)}, bf16[4,1024,896]{2,1,0:T(8,128)(2,1)S(1)}, u32[]{:S(2)}) %copy-start.6) | copy-done | bytes 7340056
  49.3 2.0 collective-permute-start.10
  53.6 5.3 %shard_map.53.refs_3_ = bf16[4,1024,896]{2,1,0:T(8,128)(2,1)S(1)} custom-call(s32[3]{0:T(128)S(1)} %get-tuple-element.60.place_ref, s32[4096,56]{1,0:T(8,128)S(1)} %copy.5.exps_ref, bf16[4096,7168]{1,0:T(8,128)(2,1)} %quant_ref.15), custom_call_target="tpu_custom_call" | custom-call | flops 917504 | bytes 917504 | tf_op jit(solution)/shard_map/pallas_call | solution.py:93
  58.9 3.0 %copy-done.9 = bf16[4,1024,896]{2,1,0:T(8,128)(2,1)} copy-done((bf16[4,1024,896]{2,1,0:T(8,128)(2,1)}, bf16[4,1024,896]{2,1,0:T(8,128)(2,1)S(1)}, u32[]{:S(2)}) %copy-start.9) | copy-done | bytes 7340056
  63.3 1.7 select_select_fusion.5
  65.0 1.9 select_select_fusion.4
  68.1 2.6 %copy.13 = s32[1024,256]{0,1:T(8,128)} copy(s32[1024,256]{1,0:T(8,128)} %param.7) | data formatting | bytes 2097152 | tf_op jit(solution)/shard_map/optimization_barrier | solution.py:224
  75.5 3.8 %collective-permute-done.13 = bf16[256,512]{1,0:T(8,128)(2,1)S(1)} collective-permute-done((bf16[256,512]{1,0:T(8,128)(2,1)}, bf16[256,512]{1,0:T(8,128)(2,1)S(1)}, u32[]{:S(2)}, u32[]{:S(2)}) %collective-permute-start.13) | collective-permute-done | bytes 262176 | tf_op jit(solution)/shard_map/ppermute | solution.py:216
  79.3 5.6 %collective-permute-done.14 = bf16[256,512]{1,0:T(8,128)(2,1)S(1)} collective-permute-done((bf16[256,512]{1,0:T(8,128)(2,1)S(1)}, bf16[256,512]{1,0:T(8,128)(2,1)S(1)}, u32[]{:S(2)}, u32[]{:S(2)}) %collective-permute-start.14) | collective-permute-done | bytes 262176 | tf_op jit(solution)/shard_map/ppermute | solution.py:216
  84.9 5.6 %collective-permute-done.15 = bf16[256,512]{1,0:T(8,128)(2,1)S(1)} collective-permute-done((bf16[256,512]{1,0:T(8,128)(2,1)S(1)}, bf16[256,512]{1,0:T(8,128)(2,1)S(1)}, u32[]{:S(2)}, u32[]{:S(2)}) %collective-permute-start.15) | collective-permute-done | bytes 262176 | tf_op jit(solution)/shard_map/ppermute | solution.py:216
  90.6 1.5 broadcast_select_fusion.1
  92.8 3.1 %copy-done.3 = bf16[4,1024,896]{2,1,0:T(8,128)(2,1)S(1)} copy-done((bf16[4,1024,896]{2,1,0:T(8,128)(2,1)S(1)}, bf16[4,1024,896]{2,1,0:T(8,128)(2,1)}, u32[]{:S(2)}) %copy-start.3) | copy-done | bytes 7340056
  95.9 3.1 %copy-done.7 = bf16[4,1024,896]{2,1,0:T(8,128)(2,1)S(1)} copy-done((bf16[4,1024,896]{2,1,0:T(8,128)(2,1)S(1)}, bf16[4,1024,896]{2,1,0:T(8,128)(2,1)}, u32[]{:S(2)}) %copy-start.7) | copy-done | bytes 7340056
  99.0 3.1 %copy-done.10 = bf16[4,1024,896]{2,1,0:T(8,128)(2,1)S(1)} copy-done((bf16[4,1024,896]{2,1,0:T(8,128)(2,1)S(1)}, bf16[4,1024,896]{2,1,0:T(8,128)(2,1)}, u32[]{:S(2)}) %copy-start.10) | copy-done | bytes 7340056
  102.1 2.4 %shard_map.54 = f32[256,896]{1,0:T(8,128)S(1)} custom-call(bf16[256,4096]{1,0:T(8,128)(2,1)S(1)} %pad_maximum_fusion.panel_ref, bf16[4,1024,896]{2,1,0:T(8,128)(2,1)S(1)} %bitcast.22, bf16[4,1024,896]{2,1,0:T(8,128)(2,1)S(1)} %copy-done.3, bf16[4,1024,896]{2,1,0:T(8,128)(2,1)S(1)} %copy-done.7, bf16[4,1024,896]{2,1,0:T(8,128)(2,1)S(1)} %copy-done.10), custom_call_target="tpu_custom_call" | custom-call | flops 58720256 | bytes 917504 | tf_op jit(solution)/shard_map/pallas_call | solution.py:130
  104.5 2.1 %collective-permute-start.16 = (f32[256,896]{1,0:T(8,128)S(1)}, f32[256,896]{1,0:T(8,128)S(1)}, u32[]{:S(2)}, u32[]{:S(2)}) collective-permute-start(f32[256,896]{1,0:T(8,128)S(1)} %shard_map.54), channel_id=1, source_target_pairs={{0,8},{8,0},{16,24},{24,16},{1,9},{9,1},{17,25},{25,17},{2,10},{10... | collective-permute-start | bytes 2752520 | tf_op jit(solution)/shard_map/ppermute | solution.py:216
  111.6 5.3 %collective-permute-done.19 = bf16[256,512]{1,0:T(8,128)(2,1)S(1)} collective-permute-done((bf16[256,512]{1,0:T(8,128)(2,1)S(1)}, bf16[256,512]{1,0:T(8,128)(2,1)S(1)}, u32[]{:S(2)}, u32[]{:S(2)}) %collective-permute-start.19) | collective-permute-done | bytes 262176 | tf_op jit(solution)/shard_map/ppermute | solution.py:220
  117.0 2.0 collective-permute-start.20
  118.9 3.7 %collective-permute-done.22 = bf16[256,512]{1,0:T(8,128)(2,1)} collective-permute-done((bf16[256,512]{1,0:T(8,128)(2,1)S(1)}, bf16[256,512]{1,0:T(8,128)(2,1)}, u32[]{:S(2)}, u32[]{:S(2)}) %collective-permute-start.22) | collective-permute-done | bytes 262176 | tf_op jit(solution)/shard_map/ppermute | solution.py:220
  122.7 2.0 collective-permute-start.23
  124.8 3.1 %copy-done.4 = bf16[4,1024,896]{2,1,0:T(8,128)(2,1)S(1)} copy-done((bf16[4,1024,896]{2,1,0:T(8,128)(2,1)S(1)}, bf16[4,1024,896]{2,1,0:T(8,128)(2,1)}, u32[]{:S(2)}) %copy-start.4) | copy-done | bytes 7340056
  127.8 3.4 %shard_map.55 = f32[256,896]{1,0:T(8,128)} custom-call(bf16[256,4096]{1,0:T(8,128)(2,1)S(1)} %pad_maximum_fusion.panel_ref, bf16[4,1024,896]{2,1,0:T(8,128)(2,1)S(1)} %bitcast.22, bf16[4,1024,896]{2,1,0:T(8,128)(2,1)S(1)} %copy-done.4, bf16[4,1024,896]{2,1,0:T(8,128)(2,1)S(1)} %bitcast.24, bf16[4,1024,896]{2,1,0:T(8,128)(2,1)S(1)} %copy-done.10, ...), custom_call_target="tpu_custom_call" | custom-call | flops 58720256 | bytes 917504 | tf_op jit(solution)/shard_map/pallas_call | solution.py:130
  131.2 3.3 %shard_map.56 = f32[256,896]{1,0:T(8,128)} custom-call(bf16[256,4096]{1,0:T(8,128)(2,1)S(1)} %pad_maximum_fusion.panel_ref, bf16[4,1024,896]{2,1,0:T(8,128)(2,1)S(1)} %bitcast.22, bf16[4,1024,896]{2,1,0:T(8,128)(2,1)S(1)} %copy-done.4, bf16[4,1024,896]{2,1,0:T(8,128)(2,1)S(1)} %bitcast.24, bf16[4,1024,896]{2,1,0:T(8,128)(2,1)S(1)} %copy-done.10), custom_call_target="tpu_custom_call" | custom-call | flops 58720256 | bytes 917504 | tf_op jit(solution)/shard_map/pallas_call | solution.py:130
  138.5 3.1 %copy-done.1 = bf16[4,1024,896]{2,1,0:T(8,128)(2,1)S(1)} copy-done((bf16[4,1024,896]{2,1,0:T(8,128)(2,1)S(1)}, bf16[4,1024,896]{2,1,0:T(8,128)(2,1)}, u32[]{:S(2)}) %copy-start.1) | copy-done | bytes 7340056
  141.6 3.1 %copy-done.5 = bf16[4,1024,896]{2,1,0:T(8,128)(2,1)S(1)} copy-done((bf16[4,1024,896]{2,1,0:T(8,128)(2,1)S(1)}, bf16[4,1024,896]{2,1,0:T(8,128)(2,1)}, u32[]{:S(2)}) %copy-start.5) | copy-done | bytes 7340056
  144.7 3.1 %copy-done.8 = bf16[4,1024,896]{2,1,0:T(8,128)(2,1)S(1)} copy-done((bf16[4,1024,896]{2,1,0:T(8,128)(2,1)S(1)}, bf16[4,1024,896]{2,1,0:T(8,128)(2,1)}, u32[]{:S(2)}) %copy-start.8) | copy-done | bytes 7340056
  147.8 3.1 %copy-done.11 = bf16[4,1024,896]{2,1,0:T(8,128)(2,1)S(1)} copy-done((bf16[4,1024,896]{2,1,0:T(8,128)(2,1)S(1)}, bf16[4,1024,896]{2,1,0:T(8,128)(2,1)}, u32[]{:S(2)}) %copy-start.11) | copy-done | bytes 7340056
  150.9 1.6 copy-done.13
  152.4 2.3 %shard_map.57.first_ref = f32[256,896]{1,0:T(8,128)S(1)} custom-call(bf16[256,4096]{1,0:T(8,128)(2,1)S(1)} %copy-done.13, bf16[4,1024,896]{2,1,0:T(8,128)(2,1)S(1)} %copy-done.1, bf16[4,1024,896]{2,1,0:T(8,128)(2,1)S(1)} %copy-done.5, bf16[4,1024,896]{2,1,0:T(8,128)(2,1)S(1)} %copy-done.8, bf16[4,1024,896]{2,1,0:T(8,128)(2,1)S(1)} %copy-done.11), custom_call_target="tpu_custom_call" | custom-call | flops 58720256 | bytes 917504 | tf_op jit(solution)/shard_map/pallas_call | solution.py:130
  154.8 7.9 %shard_map.58.inverse_ref = f32[256,256]{1,0:T(8,128)S(1)} custom-call(f32[256,256]{1,0:T(8,128)S(1)} %add.101.head_ref), custom_call_target="tpu_custom_call" | custom-call | flops 33554432 | bytes 524288 | tf_op jit(solution)/shard_map/pallas_call | solution.py:174
  168.0 4.0 %fusion = bf16[1024,7168]{1,0:T(8,128)(2,1)} fusion(bf16[1024,7168]{1,0:T(8,128)(2,1)} %shard_map.60, s32[]{:T(128)S(6)} %select_n.158, bf16[1024,512]{0,1:T(8,128)(2,1)S(1)} %copy-done.19, bf16[512,896]{1,0:T(8,128)(2,1)S(1)} %get-tuple-element.82, bf16[1024,7168]{1,0:T(8,128)(2,1)} %param.6), kind=kOutput, calls=%fused_computation.9 | convolution fusion | flops 942276608 | bytes 5636100 | tf_op jit(solution)/shard_map/dot_general | solution.py:228
  172.0 4.8 %fusion.1 = bf16[1024,7168]{1,0:T(8,128)(2,1)} fusion(bf16[1024,7168]{1,0:T(8,128)(2,1)} %fusion, s32[]{:T(128)S(6)} %select_n.159, bf16[1024,512]{0,1:T(8,128)(2,1)} %pad_maximum_fusion.2, bf16[512,896]{1,0:T(8,128)(2,1)} %collective-permute-done.29, bf16[1024,7168]{1,0:T(8,128)(2,1)} %param.6), kind=kOutput, calls=%fused_computation.10 | convolution fusion | flops 942276608 | bytes 5636100 | tf_op jit(solution)/shard_map/dot_general | solution.py:228
  176.8 1.8 collective-permute-done.28
  183.3 4.0 %fusion.2 = bf16[1024,7168]{1,0:T(8,128)(2,1)} fusion(bf16[1024,7168]{1,0:T(8,128)(2,1)} %fusion.1, s32[]{:T(128)S(6)} %select_n.160, bf16[256,896]{1,0:T(8,128)(2,1)} %collective-permute-done.27, bf16[1024,7168]{1,0:T(8,128)(2,1)} %param.6, bf16[1024,512]{0,1:T(8,128)(2,1)} %pad_maximum_fusion.2), kind=kOutput, calls=%fused_computation.11 | convolution fusion | flops 472514560 | bytes 4653060 | tf_op jit(solution)/shard_map/dot_general | solution.py:228
  187.3 3.9 %fusion.3 = bf16[1024,7168]{1,0:T(8,128)(2,1)} fusion(bf16[1024,7168]{1,0:T(8,128)(2,1)} %fusion.2, s32[]{:T(128)S(6)} %select_n.161, bf16[256,896]{1,0:T(8,128)(2,1)} %collective-permute-done.28, bf16[1024,7168]{1,0:T(8,128)(2,1)} %param.6, bf16[1024,512]{0,1:T(8,128)(2,1)} %pad_maximum_fusion.2), kind=kOutput, calls=%fused_computation.12 | convolution fusion | flops 472514560 | bytes 4653060 | tf_op jit(solution)/shard_map/dot_general | solution.py:228
  192.3 3.5 %fusion.4 = bf16[1024,7168]{1,0:T(8,128)(2,1)} fusion(bf16[1024,7168]{1,0:T(8,128)(2,1)} %fusion.3, s32[]{:T(128)S(6)} %select_n.162, bf16[256,896]{1,0:T(8,128)(2,1)S(1)} %collective-permute-done.32, bf16[1024,7168]{1,0:T(8,128)(2,1)} %param.6, bf16[1024,512]{0,1:T(8,128)(2,1)S(1)} %copy-done.20), kind=kOutput, calls=%fused_computation.13 | convolution fusion | flops 472514560 | bytes 4653060 | tf_op jit(solution)/shard_map/dot_general | solution.py:228
  195.8 3.6 %fusion.5 = bf16[1024,7168]{1,0:T(8,128)(2,1)} fusion(bf16[1024,7168]{1,0:T(8,128)(2,1)} %fusion.4, s32[]{:T(128)S(6)} %select_n.163, bf16[256,896]{1,0:T(8,128)(2,1)S(1)} %collective-permute-done.33, bf16[1024,7168]{1,0:T(8,128)(2,1)} %param.6, bf16[1024,512]{0,1:T(8,128)(2,1)S(1)} %copy-done.20), kind=kOutput, calls=%fused_computation.14 | convolution fusion | flops 472514560 | bytes 4653060 | tf_op jit(solution)/shard_map/dot_general | solution.py:228
  199.5 3.5 %fusion.6 = bf16[1024,7168]{1,0:T(8,128)(2,1)} fusion(bf16[1024,7168]{1,0:T(8,128)(2,1)} %fusion.5, s32[]{:T(128)S(6)} %select_n.164, bf16[256,896]{1,0:T(8,128)(2,1)S(1)} %constant_dynamic-update-slice_fusion.4, bf16[1024,7168]{1,0:T(8,128)(2,1)} %param.6, bf16[1024,512]{0,1:T(8,128)(2,1)S(1)} %copy-done.20), kind=kOutput, calls=%fused_computation.15 | convolution fusion | flops 472514560 | bytes 4653060 | tf_op jit(solution)/shard_map/dot_general | solution.py:228
  203.0 2.0 fusion.7
  (150 shorter events, 43.7 us)
Async XLA Ops:
  3.0 13.6 %collective-permute-start = (bf16[256,512]{1,0:T(8,128)(2,1)S(1)}, bf16[256,512]{1,0:T(8,128)(2,1)}, u32[]{:S(2)}, u32[]{:S(2)}) collective-permute-start(bf16[256,512]{1,0:T(8,128)(2,1)S(1)} %shard_map.46), channel_id=1, source_target_pairs={{0,2},{1,3},{8,10},{9,11},{16,18},{17,19},{24,26},{25,27}} | collective-permute-start | bytes 786440 | tf_op jit(solution)/shard_map/ppermute | solution.py:220
  5.6 17.7 %collective-permute-start.2 = (bf16[256,512]{1,0:T(8,128)(2,1)S(1)}, bf16[256,512]{1,0:T(8,128)(2,1)}, u32[]{:S(2)}, u32[]{:S(2)}) collective-permute-start(bf16[256,512]{1,0:T(8,128)(2,1)S(1)} %shard_map.49), channel_id=1, source_target_pairs={{0,2},{1,3},{8,10},{9,11},{16,18},{17,19},{24,26},{25,27}} | collective-permute-start | bytes 786440 | tf_op jit(solution)/shard_map/ppermute | solution.py:220
  16.7 18.1 %collective-permute-start.1 = (bf16[256,512]{1,0:T(8,128)(2,1)}, bf16[256,512]{1,0:T(8,128)(2,1)}, u32[]{:S(2)}, u32[]{:S(2)}) collective-permute-start(bf16[256,512]{1,0:T(8,128)(2,1)} %collective-permute-done), channel_id=1, source_target_pairs={{2,4},{3,5},{10,12},{11,13},{18,20},{19,21},{26,28},{27,29}} | collective-permute-start | bytes 786440 | tf_op jit(solution)/shard_map/ppermute | solution.py:220
  22.0 14.2 %collective-permute-start.6 = (bf16[256,512]{1,0:T(8,128)(2,1)S(1)}, bf16[256,512]{1,0:T(8,128)(2,1)}, u32[]{:S(2)}, u32[]{:S(2)}) collective-permute-start(bf16[256,512]{1,0:T(8,128)(2,1)S(1)} %shard_map.51), channel_id=1, source_target_pairs={{0,2},{1,3},{8,10},{9,11},{16,18},{17,19},{24,26},{25,27}} | collective-permute-start | bytes 786440 | tf_op jit(solution)/shard_map/ppermute | solution.py:220
  23.3 24.6 %collective-permute-start.5 = (bf16[256,512]{1,0:T(8,128)(2,1)}, bf16[256,512]{1,0:T(8,128)(2,1)}, u32[]{:S(2)}, u32[]{:S(2)}) collective-permute-start(bf16[256,512]{1,0:T(8,128)(2,1)} %collective-permute-done.2), channel_id=1, source_target_pairs={{2,4},{3,5},{10,12},{11,13},{18,20},{19,21},{26,28},{27,29}} | collective-permute-start | bytes 786440 | tf_op jit(solution)/shard_map/ppermute | solution.py:220
  25.3 24.0 %collective-permute-start.4 = (bf16[256,512]{1,0:T(8,128)(2,1)S(1)}, bf16[256,512]{1,0:T(8,128)(2,1)}, u32[]{:S(2)}, u32[]{:S(2)}) collective-permute-start(bf16[256,512]{1,0:T(8,128)(2,1)S(1)} %shard_map.47), channel_id=1, source_target_pairs={{0,2},{1,3},{8,10},{9,11},{16,18},{17,19},{24,26},{25,27}} | collective-permute-start | bytes 786440 | tf_op jit(solution)/shard_map/ppermute | solution.py:220
  34.8 17.5 %collective-permute-start.3 = (bf16[256,512]{1,0:T(8,128)(2,1)}, bf16[256,512]{1,0:T(8,128)(2,1)}, u32[]{:S(2)}, u32[]{:S(2)}) collective-permute-start(bf16[256,512]{1,0:T(8,128)(2,1)} %collective-permute-done.1), channel_id=1, source_target_pairs={{4,6},{5,7},{12,14},{13,15},{20,22},{21,23},{28,30},{29,31}} | collective-permute-start | bytes 786440 | tf_op jit(solution)/shard_map/ppermute | solution.py:220
  36.2 16.1 %collective-permute-start.8 = (bf16[256,512]{1,0:T(8,128)(2,1)}, bf16[256,512]{1,0:T(8,128)(2,1)}, u32[]{:S(2)}, u32[]{:S(2)}) collective-permute-start(bf16[256,512]{1,0:T(8,128)(2,1)} %collective-permute-done.6), channel_id=1, source_target_pairs={{2,4},{3,5},{10,12},{11,13},{18,20},{19,21},{26,28},{27,29}} | collective-permute-start | bytes 786440 | tf_op jit(solution)/shard_map/ppermute | solution.py:220
  39.6 11.7 %slice-start.8 = ((bf16[1024,7168]{1,0:T(8,128)(2,1)}), bf16[1024,256]{1,0:T(8,128)(2,1)S(1)}, s32[]{:S(2)}) async-start(bf16[1024,7168]{1,0:T(8,128)(2,1)} %param.6), calls=%async_computation.8 | async-start | bytes 1048576 | tf_op jit(solution)/shard_map/slice | solution.py:296
  47.9 14.0 %collective-permute-start.7 = (bf16[256,512]{1,0:T(8,128)(2,1)}, bf16[256,512]{1,0:T(8,128)(2,1)}, u32[]{:S(2)}, u32[]{:S(2)}) collective-permute-start(bf16[256,512]{1,0:T(8,128)(2,1)} %collective-permute-done.5), channel_id=1, source_target_pairs={{4,6},{5,7},{12,14},{13,15},{20,22},{21,23},{28,30},{29,31}} | collective-permute-start | bytes 786440 | tf_op jit(solution)/shard_map/ppermute | solution.py:220
  49.3 12.6 %collective-permute-start.10 = (bf16[256,512]{1,0:T(8,128)(2,1)}, bf16[256,512]{1,0:T(8,128)(2,1)}, u32[]{:S(2)}, u32[]{:S(2)}) collective-permute-start(bf16[256,512]{1,0:T(8,128)(2,1)} %collective-permute-done.4), channel_id=1, source_target_pairs={{2,4},{3,5},{10,12},{11,13},{18,20},{19,21},{26,28},{27,29}} | collective-permute-start | bytes 786440 | tf_op jit(solution)/shard_map/ppermute | solution.py:220
  52.3 18.6 %collective-permute-start.9 = (bf16[256,512]{1,0:T(8,128)(2,1)}, bf16[256,512]{1,0:T(8,128)(2,1)}, u32[]{:S(2)}, u32[]{:S(2)}) collective-permute-start(bf16[256,512]{1,0:T(8,128)(2,1)} %collective-permute-done.8), channel_id=1, source_target_pairs={{4,6},{5,7},{12,14},{13,15},{20,22},{21,23},{28,30},{29,31}} | collective-permute-start | bytes 786440 | tf_op jit(solution)/shard_map/ppermute | solution.py:220
  53.6 11.3 %copy-start.15 = (bf16[256,512]{1,0:T(8,128)(2,1)S(1)}, bf16[256,512]{1,0:T(8,128)(2,1)}, u32[]{:S(2)}) copy-start(bf16[256,512]{1,0:T(8,128)(2,1)} %copy-done.14) | copy-start | bytes 786436
  61.9 11.3 %collective-permute-start.11 = (bf16[256,512]{1,0:T(8,128)(2,1)}, bf16[256,512]{1,0:T(8,128)(2,1)}, u32[]{:S(2)}, u32[]{:S(2)}) collective-permute-start(bf16[256,512]{1,0:T(8,128)(2,1)} %collective-permute-done.10), channel_id=1, source_target_pairs={{4,6},{5,7},{12,14},{13,15},{20,22},{21,23},{28,30},{29,31}} | collective-permute-start | bytes 786440 | tf_op jit(solution)/shard_map/ppermute | solution.py:220
  65.0 27.3 %slice-start = ((s8[7340032]{0:T(1024)(128)(4,1)}), s8[3145728]{0:T(1024)(128)(4,1)S(1)}, s32[]{:S(2)}) async-start(s8[7340032]{0:T(1024)(128)(4,1)} %bitcast.21), calls=%async_computation | async-start | bytes 6291456
  66.8 7.7 %collective-permute-start.12 = (bf16[256,512]{1,0:T(8,128)(2,1)}, bf16[256,512]{1,0:T(8,128)(2,1)}, u32[]{:S(2)}, u32[]{:S(2)}) collective-permute-start(bf16[256,512]{1,0:T(8,128)(2,1)} %select_select_fusion.5), channel_id=1, source_target_pairs={{0,1},{1,0},{2,3},{3,2},{4,5},{5,4},{6,7},{7,6},{8,9},{9,8},{10,11... | collective-permute-start | bytes 786440 | tf_op jit(solution)/shard_map/ppermute | solution.py:216
  70.7 19.9 %copy-start.21 = (bf16[256,512]{1,0:T(8,128)(2,1)S(1)}, bf16[256,512]{1,0:T(8,128)(2,1)}, u32[]{:S(2)}) copy-start(bf16[256,512]{1,0:T(8,128)(2,1)} %select_select_fusion.4) | copy-start | bytes 786436
  70.7 8.6 %collective-permute-start.13 = (bf16[256,512]{1,0:T(8,128)(2,1)}, bf16[256,512]{1,0:T(8,128)(2,1)S(1)}, u32[]{:S(2)}, u32[]{:S(2)}) collective-permute-start(bf16[256,512]{1,0:T(8,128)(2,1)} %select_select_fusion.4), channel_id=1, source_target_pairs={{0,1},{1,0},{2,3},{3,2},{4,5},{5,4},{6,7},{7,6},{8,9},{9,8},{10,11... | collective-permute-start | bytes 786440 | tf_op jit(solution)/shard_map/ppermute | solution.py:216
  71.9 13.0 %collective-permute-start.14 = (bf16[256,512]{1,0:T(8,128)(2,1)S(1)}, bf16[256,512]{1,0:T(8,128)(2,1)S(1)}, u32[]{:S(2)}, u32[]{:S(2)}) collective-permute-start(bf16[256,512]{1,0:T(8,128)(2,1)S(1)} %select_select_fusion.3), channel_id=1, source_target_pairs={{0,1},{1,0},{2,3},{3,2},{4,5},{5,4},{6,7},{7,6},{8,9},{9,8},{10,11... | collective-permute-start | bytes 786440 | tf_op jit(solution)/shard_map/ppermute | solution.py:216
  74.2 16.3 %collective-permute-start.15 = (bf16[256,512]{1,0:T(8,128)(2,1)S(1)}, bf16[256,512]{1,0:T(8,128)(2,1)S(1)}, u32[]{:S(2)}, u32[]{:S(2)}) collective-permute-start(bf16[256,512]{1,0:T(8,128)(2,1)S(1)} %select_select_fusion.2), channel_id=1, source_target_pairs={{0,1},{1,0},{2,3},{3,2},{4,5},{5,4},{6,7},{7,6},{8,9},{9,8},{10,11... | collective-permute-start | bytes 786440 | tf_op jit(solution)/shard_map/ppermute | solution.py:216
  79.3 45.4 %slice-start.2 = ((s8[7340032]{0:T(1024)(128)(4,1)}), s8[3145728]{0:T(1024)(128)(4,1)S(1)}, s32[]{:S(2)}) async-start(s8[7340032]{0:T(1024)(128)(4,1)} %bitcast.23), calls=%async_computation.2 | async-start | bytes 6291456
  102.1 29.1 %copy-start.12 = (bf16[256,4096]{1,0:T(8,128)(2,1)}, bf16[256,4096]{1,0:T(8,128)(2,1)S(1)}, u32[]{:S(2)}) copy-start(bf16[256,4096]{1,0:T(8,128)(2,1)S(1)} %pad_maximum_fusion.panel_ref) | copy-start | bytes 6291460
  102.1 22.6 %slice-start.3 = ((s8[7340032]{0:T(1024)(128)(4,1)}), s8[4194304]{0:T(1024)(128)(4,1)S(1)}, s32[]{:S(2)}) async-start(s8[7340032]{0:T(1024)(128)(4,1)} %bitcast.23), calls=%async_computation.3 | async-start | bytes 8388608
  104.5 20.2 %collective-permute-start.16 = (f32[256,896]{1,0:T(8,128)S(1)}, f32[256,896]{1,0:T(8,128)S(1)}, u32[]{:S(2)}, u32[]{:S(2)}) collective-permute-start(f32[256,896]{1,0:T(8,128)S(1)} %shard_map.54), channel_id=1, source_target_pairs={{0,8},{8,0},{16,24},{24,16},{1,9},{9,1},{17,25},{25,17},{2,10},{10... | collective-permute-start | bytes 2752520 | tf_op jit(solution)/shard_map/ppermute | solution.py:216
  107.5 2.8 %collective-permute-start.17 = (f32[256,256]{1,0:T(8,128)S(1)}, f32[256,256]{1,0:T(8,128)S(1)}, u32[]{:S(2)}, u32[]{:S(2)}) collective-permute-start(f32[256,256]{1,0:T(8,128)S(1)} %fusion.15), channel_id=1, source_target_pairs={{0,8},{8,0},{16,24},{24,16},{1,9},{9,1},{17,25},{25,17},{2,10},{10... | collective-permute-start | bytes 786440 | tf_op jit(solution)/shard_map/ppermute | solution.py:216
  107.7 23.6 %copy-start.22 = (bf16[256,512]{1,0:T(8,128)(2,1)}, bf16[256,512]{1,0:T(8,128)(2,1)S(1)}, u32[]{:S(2)}) copy-start(bf16[256,512]{1,0:T(8,128)(2,1)S(1)} %get-tuple-element.75) | copy-start | bytes 786436
  107.7 23.6 %copy-start.24 = (bf16[256,512]{1,0:T(8,128)(2,1)}, bf16[256,512]{1,0:T(8,128)(2,1)S(1)}, u32[]{:S(2)}) copy-start(bf16[256,512]{1,0:T(8,128)(2,1)S(1)} %get-tuple-element.72) | copy-start | bytes 786436
  107.7 9.3 %collective-permute-start.19 = (bf16[256,512]{1,0:T(8,128)(2,1)S(1)}, bf16[256,512]{1,0:T(8,128)(2,1)S(1)}, u32[]{:S(2)}, u32[]{:S(2)}) collective-permute-start(bf16[256,512]{1,0:T(8,128)(2,1)S(1)} %get-tuple-element.72), channel_id=1, source_target_pairs={{0,2},{1,3},{8,10},{9,11},{16,18},{17,19},{24,26},{25,27}} | collective-permute-start | bytes 786440 | tf_op jit(solution)/shard_map/ppermute | solution.py:220
  109.0 13.7 %collective-permute-start.22 = (bf16[256,512]{1,0:T(8,128)(2,1)S(1)}, bf16[256,512]{1,0:T(8,128)(2,1)}, u32[]{:S(2)}, u32[]{:S(2)}) collective-permute-start(bf16[256,512]{1,0:T(8,128)(2,1)S(1)} %get-tuple-element.75), channel_id=1, source_target_pairs={{0,2},{1,3},{8,10},{9,11},{16,18},{17,19},{24,26},{25,27}} | collective-permute-start | bytes 786440 | tf_op jit(solution)/shard_map/ppermute | solution.py:220
  110.3 14.3 %collective-permute-start.18 = (f32[256,256]{1,0:T(8,128)S(1)}, f32[256,256]{1,0:T(8,128)S(1)}, u32[]{:S(2)}, u32[]{:S(2)}) collective-permute-start(f32[256,256]{1,0:T(8,128)S(1)} %add.100), channel_id=1, source_target_pairs={{0,16},{8,24},{16,0},{24,8},{1,17},{9,25},{17,1},{25,9},{2,18},{10... | collective-permute-start | bytes 786440 | tf_op jit(solution)/shard_map/ppermute | solution.py:216
  117.0 14.3 %copy-start.26 = (bf16[256,512]{1,0:T(8,128)(2,1)}, bf16[256,512]{1,0:T(8,128)(2,1)S(1)}, u32[]{:S(2)}) copy-start(bf16[256,512]{1,0:T(8,128)(2,1)S(1)} %collective-permute-done.19) | copy-start | bytes 786436
  117.0 17.6 %collective-permute-start.20 = (bf16[256,512]{1,0:T(8,128)(2,1)S(1)}, bf16[256,512]{1,0:T(8,128)(2,1)}, u32[]{:S(2)}, u32[]{:S(2)}) collective-permute-start(bf16[256,512]{1,0:T(8,128)(2,1)S(1)} %collective-permute-done.19), channel_id=1, source_target_pairs={{2,4},{3,5},{10,12},{11,13},{18,20},{19,21},{26,28},{27,29}} | collective-permute-start | bytes 786440 | tf_op jit(solution)/shard_map/ppermute | solution.py:220
  122.7 15.2 %collective-permute-start.23 = (bf16[256,512]{1,0:T(8,128)(2,1)}, bf16[256,512]{1,0:T(8,128)(2,1)}, u32[]{:S(2)}, u32[]{:S(2)}) collective-permute-start(bf16[256,512]{1,0:T(8,128)(2,1)} %collective-permute-done.22), channel_id=1, source_target_pairs={{2,4},{3,5},{10,12},{11,13},{18,20},{19,21},{26,28},{27,29}} | collective-permute-start | bytes 786440 | tf_op jit(solution)/shard_map/ppermute | solution.py:220
  134.5 28.1 %collective-permute-start.21 = (bf16[256,512]{1,0:T(8,128)(2,1)}, bf16[256,512]{1,0:T(8,128)(2,1)S(1)}, u32[]{:S(2)}, u32[]{:S(2)}) collective-permute-start(bf16[256,512]{1,0:T(8,128)(2,1)} %collective-permute-done.20), channel_id=1, source_target_pairs={{4,6},{5,7},{12,14},{13,15},{20,22},{21,23},{28,30},{29,31}} | collective-permute-start | bytes 786440 | tf_op jit(solution)/shard_map/ppermute | solution.py:220
  135.2 29.8 %collective-permute-start.25 = (f32[256,896]{1,0:T(8,128)}, f32[256,896]{1,0:T(8,128)S(1)}, u32[]{:S(2)}, u32[]{:S(2)}) collective-permute-start(f32[256,896]{1,0:T(8,128)} %shard_map.56), channel_id=1, source_target_pairs={{0,8},{8,0},{16,24},{24,16},{1,9},{9,1},{17,25},{25,17},{2,10},{10... | collective-permute-start | bytes 2752520 | tf_op jit(solution)/shard_map/ppermute | solution.py:216
  136.6 28.4 %collective-permute-start.26 = (f32[256,896]{1,0:T(8,128)}, f32[256,896]{1,0:T(8,128)S(1)}, u32[]{:S(2)}, u32[]{:S(2)}) collective-permute-start(f32[256,896]{1,0:T(8,128)} %shard_map.55), channel_id=1, source_target_pairs={{0,16},{8,24},{16,0},{24,8},{1,17},{9,25},{17,1},{25,9},{2,18},{10... | collective-permute-start | bytes 2752520 | tf_op jit(solution)/shard_map/ppermute | solution.py:216
  137.8 24.9 %collective-permute-start.24 = (bf16[256,512]{1,0:T(8,128)(2,1)}, bf16[256,512]{1,0:T(8,128)(2,1)S(1)}, u32[]{:S(2)}, u32[]{:S(2)}) collective-permute-start(bf16[256,512]{1,0:T(8,128)(2,1)} %collective-permute-done.23), channel_id=1, source_target_pairs={{4,6},{5,7},{12,14},{13,15},{20,22},{21,23},{28,30},{29,31}} | collective-permute-start | bytes 786440 | tf_op jit(solution)/shard_map/ppermute | solution.py:220
  166.1 5.9 %collective-permute-start.29 = (bf16[512,896]{1,0:T(8,128)(2,1)S(1)}, bf16[512,896]{1,0:T(8,128)(2,1)}, u32[]{:S(2)}, u32[]{:S(2)}) collective-permute-start(bf16[512,896]{1,0:T(8,128)(2,1)S(1)} %get-tuple-element.82), channel_id=1, source_target_pairs={{0,8},{8,0},{16,24},{24,16},{1,9},{9,1},{17,25},{25,17},{2,10},{10... | collective-permute-start | bytes 2752520 | tf_op jit(solution)/shard_map/ppermute | solution.py:216
  166.5 12.1 %collective-permute-start.28 = (bf16[256,896]{1,0:T(8,128)(2,1)S(1)}, bf16[256,896]{1,0:T(8,128)(2,1)}, u32[]{:S(2)}, u32[]{:S(2)}) collective-permute-start(bf16[256,896]{1,0:T(8,128)(2,1)S(1)} %get-tuple-element.80), channel_id=1, source_target_pairs={{0,1},{1,0},{2,3},{3,2},{4,5},{5,4},{6,7},{7,6},{8,9},{9,8},{10,11... | collective-permute-start | bytes 1376264 | tf_op jit(solution)/shard_map/ppermute | solution.py:216
  167.8 11.8 %collective-permute-start.27 = (bf16[256,896]{1,0:T(8,128)(2,1)S(1)}, bf16[256,896]{1,0:T(8,128)(2,1)}, u32[]{:S(2)}, u32[]{:S(2)}) collective-permute-start(bf16[256,896]{1,0:T(8,128)(2,1)S(1)} %get-tuple-element.80), channel_id=1, source_target_pairs={{0,16},{8,24},{16,0},{24,8},{1,17},{9,25},{17,1},{25,9},{2,18},{10... | collective-permute-start | bytes 1376264 | tf_op jit(solution)/shard_map/ppermute | solution.py:216
  172.0 30.9 %slice-start.4 = ((s8[14680064]{0:T(1024)(128)(4,1)}), s8[2097152]{0:T(1024)(128)(4,1)S(1)}, s32[]{:S(2)}) async-start(s8[14680064]{0:T(1024)(128)(4,1)} %bitcast.25), calls=%async_computation.4 | async-start | bytes 4194304
  179.5 3.8 %collective-permute-start.33 = (bf16[256,896]{1,0:T(8,128)(2,1)}, bf16[256,896]{1,0:T(8,128)(2,1)S(1)}, u32[]{:S(2)}, u32[]{:S(2)}) collective-permute-start(bf16[256,896]{1,0:T(8,128)(2,1)} %collective-permute-done.28), channel_id=1, source_target_pairs={{0,8},{8,0},{16,24},{24,16},{1,9},{9,1},{17,25},{25,17},{2,10},{10... | collective-permute-start | bytes 1376264 | tf_op jit(solution)/shard_map/ppermute | solution.py:216
  180.8 2.5 %collective-permute-start.32 = (bf16[256,896]{1,0:T(8,128)(2,1)}, bf16[256,896]{1,0:T(8,128)(2,1)S(1)}, u32[]{:S(2)}, u32[]{:S(2)}) collective-permute-start(bf16[256,896]{1,0:T(8,128)(2,1)} %collective-permute-done.27), channel_id=1, source_target_pairs={{0,8},{8,0},{16,24},{24,16},{1,9},{9,1},{17,25},{25,17},{2,10},{10... | collective-permute-start | bytes 1376264 | tf_op jit(solution)/shard_map/ppermute | solution.py:216
  182.7 20.2 %slice-start.5 = ((s8[14680064]{0:T(1024)(128)(4,1)}), s8[4194304]{0:T(1024)(128)(4,1)S(1)}, s32[]{:S(2)}) async-start(s8[14680064]{0:T(1024)(128)(4,1)} %bitcast.25), calls=%async_computation.5 | async-start | bytes 8388608
  182.7 8.5 %collective-permute-start.30 = (bf16[128,896]{1,0:T(8,128)(2,1)S(1)}, bf16[128,896]{1,0:T(8,128)(2,1)S(1)}, u32[]{:S(2)}, u32[]{:S(2)}) collective-permute-start(bf16[128,896]{1,0:T(8,128)(2,1)S(1)} %slice.26), channel_id=1, source_target_pairs={{0,16},{8,24},{16,0},{24,8},{1,17},{9,25},{17,1},{25,9},{2,18},{10... | collective-permute-start | bytes 688136 | tf_op jit(solution)/shard_map/ppermute | solution.py:216
  183.1 8.2 %collective-permute-start.31 = (bf16[128,896]{1,0:T(8,128)(2,1)S(1)}, bf16[128,896]{1,0:T(8,128)(2,1)S(1)}, u32[]{:S(2)}, u32[]{:S(2)}) collective-permute-start(bf16[128,896]{1,0:T(8,128)(2,1)S(1)} %slice.27), channel_id=1, source_target_pairs={{0,1},{1,0},{2,3},{3,2},{4,5},{5,4},{6,7},{7,6},{8,9},{9,8},{10,11... | collective-permute-start | bytes 688136 | tf_op jit(solution)/shard_map/ppermute | solution.py:216
  187.3 15.6 %slice-start.6 = ((s8[14680064]{0:T(1024)(128)(4,1)}), s8[4194304]{0:T(1024)(128)(4,1)S(1)}, s32[]{:S(2)}) async-start(s8[14680064]{0:T(1024)(128)(4,1)} %bitcast.25), calls=%async_computation.6 | async-start | bytes 8388608
  191.3 11.6 %collective-permute-start.34 = (bf16[256,896]{1,0:T(8,128)(2,1)S(1)}, bf16[256,896]{1,0:T(8,128)(2,1)S(1)}, u32[]{:S(2)}, u32[]{:S(2)}) collective-permute-start(bf16[256,896]{1,0:T(8,128)(2,1)S(1)} %constant_dynamic-update-slice_fusion.4), channel_id=1, source_target_pairs={{0,8},{8,0},{16,24},{24,16},{1,9},{9,1},{17,25},{25,17},{2,10},{10... | collective-permute-start | bytes 1376264 | tf_op jit(solution)/shard_map/ppermute | solution.py:216
  (24 other events, 106.5 us)

commit v7 on v5

--- a/solution.py
+++ b/solution.py
@@ -43,11 +43,78 @@
             ],
             out_specs=pl.BlockSpec((PANEL, piece), lambda i, place: (0, 0)),
         ),
-        compiler_params=pltpu.CompilerParams(vmem_limit_bytes=48 * MIB),
+        compiler_params=pltpu.CompilerParams(vmem_limit_bytes=8 * MIB),
         cost_estimate=pl.CostEstimate(
             flops=piece * PANEL, bytes_accessed=4 * piece * PANEL, transcendentals=0
         ),
     )(at.reshape(1).astype(jnp.int32), quantized, exponents)
+
+
+def gram_kernel(blocks, place_ref, *refs):
+    acts_ref, out_ref = refs[-1], refs[-2]
+    step, width = refs[0].shape
+    shift = lax.rem(QBLOCK - lax.rem(place_ref[1] * blocks, QBLOCK), QBLOCK)
+
+    @pl.when(pl.program_id(0) == 0)
+    def _():
+        out_ref[...] = refs[6][...] if len(refs) > 8 else jnp.zeros_like(out_ref)
+
+    for side in range(2):
+        quant_ref, exps_ref, _ = refs[3 * side : 3 * side + 3]
+        scale = jnp.exp2(exps_ref[...].astype(F32))
+        rest = jnp.zeros((step, QBLOCK - scale.shape[1]), F32)
+        scale = pltpu.roll(jnp.concatenate([scale, rest], axis=1), shift, 1)
+        rows = slice(side * step, (side + 1) * step)
+        for c in range(blocks):
+            span = slice(c * QBLOCK, (c + 1) * QBLOCK)
+            wide = jnp.broadcast_to(scale[:, c : c + 1], (step, QBLOCK)).astype(BF16)
+            acts_ref[rows, span] = quant_ref[:, span] * wide
+    panel = jnp.concatenate([refs[2][...], refs[5][...]], axis=1)
+    out_ref[...] += jnp.dot(panel, acts_ref[...], preferred_element_type=F32)
+
+
+def gram_block(quantized, exponents, own, other, row, col, width, extra=None):
+    tokens, cols = quantized.shape
+    if width % QBLOCK or cols // QBLOCK >= QBLOCK:
+        panel = jnp.concatenate([own, other], axis=1)
+        quant = lax.dynamic_slice_in_dim(quantized, col * width, width, 1)
+        scale = jnp.exp2(exponents.astype(F32)).astype(BF16)
+        acts = quant * jnp.take(scale, (col * width + jnp.arange(width)) // QBLOCK, axis=1)
+        acts = jnp.roll(acts, -row * (tokens // 2), axis=0)
+        total = jnp.dot(panel, acts, preferred_element_type=F32)
+        return total if extra is None else total + extra
+    step = tokens // 2 // ROUNDS
+    place = jnp.stack([row, col]).astype(jnp.int32)
+    specs, args = [], [place]
+    for side, panel in enumerate((own, other)):
+
+        def at(k, place, side=side):
+            return lax.rem(place[0] + side, 2) * ROUNDS + k
+
+        specs += [
+            pl.BlockSpec((step, width), lambda k, place, at=at: (at(k, place), place[1])),
+            pl.BlockSpec((step, cols // QBLOCK), lambda k, place, at=at: (at(k, place), 0)),
+            pl.BlockSpec((PANEL, step), lambda k, place: (0, k)),
+        ]
+        args += [quantized, exponents, panel]
+    if extra is not None:
+        specs.append(pl.BlockSpec((PANEL, width), lambda k, place: (0, 0)))
+        args.append(extra)
+    return pl.pallas_call(
+        functools.partial(gram_kernel, width // QBLOCK),
+        out_shape=jax.ShapeDtypeStruct((PANEL, width), F32),
+        grid_spec=pltpu.PrefetchScalarGridSpec(
+            num_scalar_prefetch=1,
+            grid=(ROUNDS,),
+            in_specs=specs,
+            out_specs=pl.BlockSpec((PANEL, width), lambda k, place: (0, 0)),
+            scratch_shapes=[pltpu.VMEM((2 * step, width), BF16)],
+        ),
+        compiler_params=pltpu.CompilerParams(vmem_limit_bytes=24 * MIB),
+        cost_estimate=pl.CostEstimate(
+            flops=PANEL * PANEL * width, bytes_accessed=4 * PANEL * width, transcendentals=0
+        ),
+    )(*args)
 
 
 def inverse_kernel(head_ref, out_ref, pair_ref):
@@ -86,9 +153,9 @@
         inverse_kernel,
         out_shape=jax.ShapeDtypeStruct((PANEL, PANEL), F32),
         scratch_shapes=[pltpu.VMEM((2 * PANEL, PANEL), F32)],
-        compiler_params=pltpu.CompilerParams(vmem_limit_bytes=32 * MIB),
-        cost_estimate=pl.CostEstimate(
-            flops=28 * 12 * PANEL**3, bytes_accessed=8 * PANEL * PANEL, transcendentals=0
+        compiler_params=pltpu.CompilerParams(vmem_limit_bytes=8 * MIB),
+        cost_estimate=pl.CostEstimate(
+            flops=2 * PANEL**3, bytes_accessed=8 * PANEL * PANEL, transcendentals=0
         ),
     )(head)
 
@@ -115,11 +182,95 @@
             jax.ShapeDtypeStruct((2 * PANEL, width), BF16),
         ),
         in_specs=[pl.BlockSpec(memory_space=pltpu.SMEM)] + [vmem] * 4,
-        compiler_params=pltpu.CompilerParams(vmem_limit_bytes=32 * MIB),
+        compiler_params=pltpu.CompilerParams(vmem_limit_bytes=8 * MIB),
         cost_estimate=pl.CostEstimate(
             flops=12 * PANEL * PANEL * width, bytes_accessed=16 * PANEL * width, transcendentals=0
         ),
     )(start.reshape(1).astype(jnp.int32), inverse, *parts)
+
+
+def update_kernel(shapes, place_ref, error_ref, weights_ref, *refs):
+    count = len(shapes)
+    groups, at = [], 0
+    for pieces in shapes:
+        groups.append(refs[at : at + len(pieces)])
+        at += len(pieces)
+    out_ref, read_ref, made_ref, read_sems, made_sems = refs[-5:]
+    _, parts, step, width = read_ref.shape
+
+    def window(ref, j, i):
+        col = pl.multiple_of(place_ref[j] * width, QBLOCK)
+        return ref.at[pl.ds(i * step, step), pl.ds(col, width)]
+
+    def read(j, i):
+        return pltpu.make_async_copy(window(weights_ref, j, i), read_ref.at[j, i], read_sems.at[j, i])
+
+    def made(j, i):
+        return pltpu.make_async_copy(made_ref.at[j, i], window(out_ref, j, i), made_sems.at[j, i])
+
+    spots = [(j, i) for j in range(count) for i in range(parts)]
+    for j, i in spots:
+        read(j, i).start()
+    for j, i in spots:
+        read(j, i).wait()
+        error = error_ref[i * step : (i + 1) * step, :]
+        total = read_ref[j, i].astype(F32)
+        row = 0
+        for gain in groups[j]:
+            for top in range(0, gain.shape[0], PANEL):
+                size = min(PANEL, gain.shape[0])
+                total += jnp.dot(
+                    error[:, row : row + size],
+                    gain[top : top + size, :],
+                    preferred_element_type=F32,
+                )
+                row = (row + size) % PANEL
+        made_ref[j, i] = total.astype(BF16)
+        made(j, i).start()
+    for j, i in spots:
+        made(j, i).wait()
+
+
+def update_blocks(out, weights, error, gains, spots):
+    rows, cols = weights.shape
+    width = gains[0][0].shape[1]
+    count = len(gains)
+    if width % QBLOCK or width < PANEL:
+        out = jnp.zeros_like(weights) if out is None else out
+        for pieces, col in zip(gains, spots):
+            total = lax.dynamic_slice_in_dim(weights, col * width, width, 1).astype(F32)
+            gain = jnp.concatenate(pieces, axis=0)
+            for at in range(0, gain.shape[0], PANEL):
+                total += jnp.dot(error, gain[at : at + PANEL], preferred_element_type=F32)
+            out = lax.dynamic_update_slice_in_dim(out, total.astype(BF16), col * width, 1)
+        return out
+    parts = 4 if rows % 64 == 0 else 1
+    place = jnp.stack(spots).astype(jnp.int32)
+    flat = [piece for pieces in gains for piece in pieces]
+    vmem, anywhere = pl.BlockSpec(memory_space=pltpu.VMEM), pl.BlockSpec(memory_space=pl.ANY)
+    specs = [pl.BlockSpec(memory_space=pltpu.SMEM), vmem, anywhere] + [vmem] * len(flat)
+    args = [place, error, weights, *flat]
+    aliases = {}
+    if out is not None:
+        specs.append(anywhere)
+        aliases = {len(args): 0}
+        args.append(out)
+    buffer = pltpu.VMEM((count, parts, rows // parts, width), BF16)
+    sems = pltpu.SemaphoreType.DMA((count, parts))
+    return pl.pallas_call(
+        functools.partial(update_kernel, [[p.shape for p in pieces] for pieces in gains]),
+        out_shape=jax.ShapeDtypeStruct((rows, cols), BF16),
+        in_specs=specs,
+        out_specs=anywhere,
+        scratch_shapes=[buffer, buffer, sems, sems],
+        input_output_aliases=aliases,
+        compiler_params=pltpu.CompilerParams(vmem_limit_bytes=36 * MIB),
+        cost_estimate=pl.CostEstimate(
+            flops=2 * rows * width * PANEL * count,
+            bytes_accessed=4 * rows * width * count,
+            transcendentals=0,
+        ),
+    )(*args)
 
 
 def swap(x, axis, bit):
@@ -137,14 +288,6 @@
 
 def dot(left, right):
     return jnp.dot(left, right, preferred_element_type=F32)
-
-
-def unwritten(shape, dtype):
-    return pl.pallas_call(
-        lambda out_ref: None,
-        out_shape=jax.ShapeDtypeStruct(shape, dtype),
-        out_specs=pl.BlockSpec(memory_space=pl.ANY),
-    )()
 
 
 def shards(quantized, exponents, weights, keep_mask):
@@ -162,16 +305,6 @@
     for c in range(ROUNDS):
         got[c].append(hop(got[c][0], "feat", 0))
 
-    def scaled(k, link):
-        scale = jnp.exp2(after(exponents, link).astype(F32)).astype(BF16)
-        start = (row * toks + (tok ^ k)) * width
-        block = (start + lax.broadcasted_iota(jnp.int32, (1, width), 1)) // QBLOCK
-        spread = lax.broadcasted_iota(jnp.int32, (scale.shape[1], width), 0) == block
-        wide = dot(scale, spread.astype(BF16)).astype(BF16)
-        return lax.dynamic_slice_in_dim(quantized, start, width, 1) * wide
-
-    acts = {3: scaled(3, got[-1][0])}
-
     def settle(parts):
         result = parts[0]
         for h in range(hops):
@@ -179,90 +312,76 @@
         return result
 
     events = sorted((5 * (c + 1) + 8 * h, c, h) for c in range(ROUNDS) for h in range(hops))
-    full, swapped, token, errors = [], [], acts[3], []
+    full, swapped, token, errors = [], [], None, None
     for _, c, h in events:
-        x = after(got[c][h + 1], token)
+        x = got[c][h + 1]
+        if token is not None:
+            x = after(x, token)
+        if h + 1 == hops and c > 1:
+            x = after(x, swapped[c - 2])
         got[c][h + 1] = token = x
         if h + 1 < hops:
             got[c].append(hop(x, "feat", h + 1))
         else:
             full.append(settle(got[c]))
             swapped.append(swap(full[-1], "row", 1))
-        if (c, h) == (1, 0):
-            acts[2] = token = scaled(2, x)
-        elif (c, h) == (1, 1):
-            acts[1] = token = scaled(1, x)
-        elif (c, h) == (0, 1):
+        if (c, h) == (0, 1):
             panel_weights, mask = after(weights[:, :PANEL], x), after(keep_mask, x)
-            error = jnp.where(mask == 0, panel_weights, jnp.zeros((), BF16)).T
-            extras = -(-error.shape[1] // piece)
-            error = jnp.pad(error, ((0, 0), (0, extras * piece - error.shape[1])))
-            errors = [[error[:, i * piece : (i + 1) * piece]] for i in range(extras)]
-        elif (c, h) == (ROUNDS - 1, 0):
-            for parts in errors:
-                parts[0] = after(parts[0], x)
-                parts.append(hop(parts[0], "feat", 0))
+            error = jnp.where(mask == 0, panel_weights, jnp.zeros((), BF16))
         elif (c, h) == (ROUNDS - 1, 1):
-            for parts in errors:
-                parts[1] = after(parts[1], x)
-                parts.append(hop(parts[1], "feat", 1))
-
+            errors = [after(error, x)]
+            errors.append(hop(errors[0], "feat", 0))
     own, other = jnp.concatenate(full, axis=1), jnp.concatenate(swapped, axis=1)
-    panel = jnp.concatenate(
-        [jnp.where(row == 0, own, other), jnp.where(row == 0, other, own)], axis=1
-    )
-
-    head = lax.dot_general(
-        panel, panel, (((1,), (1,)), ((), ())), preferred_element_type=F32
+
+    def gram(k, link, extra=None):
+        col = row * toks + (tok ^ k)
+        if link is not None:
+            col = after(col, link)
+        return gram_block(quantized, exponents, own, other, row, col, width, extra)
+
+    head = sum(
+        lax.dot_general(x, x, (((1,), (1,)), ((), ())), preferred_element_type=F32)
+        for x in (own, other)
     )
     head = head + swap(head, "tok", 1)
-    block3 = dot(panel, acts[3])
+    block3 = gram(3, None)
     from3 = swap(block3, "tok", 1)
+    errors[1] = after(errors[1], block3)
+    errors.append(hop(errors[1], "feat", 1))
     head = head + swap(head, "tok", 2)
-    acts[2] = after(acts[2], from3)
-    block2 = dot(panel, acts[2]) + from3
+    block2 = gram(2, None, from3)
     block2, head = lax.optimization_barrier((block2, head))
     fromx = swap(block2, "tok", 2)
-    for parts in errors:
-        parts[2] = after(parts[2], block2)
-        for h in range(2, hops):
-            parts.append(hop(parts[h], "feat", h))
-    block1 = dot(panel, acts[1])
+    block1 = gram(1, block2)
     from1 = swap(block1, "tok", 1)
-    block0 = dot(panel, scaled(0, block1))
-    error = jnp.concatenate([settle(parts) for parts in errors], axis=1)
-    error = error[:, : weights.shape[0]].T
-    twice = jnp.concatenate([error, error], axis=1)
-    head, twice = lax.optimization_barrier((head, twice))
-    inverse = invert(head)
+    errors[2] = after(errors[2], block1)
+    for h in range(2, hops):
+        errors.append(hop(errors[h], "feat", h))
+    block0 = gram(0, block1)
+    inverse = invert(after(head, block0))
+    inverse, last = lax.optimization_barrier((inverse, errors[-1]))
+    error = settle(errors[:-1] + [last])
     start = jnp.where(root, (row * toks + tok) * width, PANEL)
     high, pair = make_gains(inverse, (block0, from1, fromx), start)
 
     half = PANEL // 2
 
-    def update(out, gain, tok_bits, row_bit):
-        start = ((row ^ row_bit) * toks + (tok ^ tok_bits)) * width
-        total = lax.dynamic_slice_in_dim(weights, start, width, 1).astype(F32)
-        total = total + dot(twice[:, : gain.shape[0]], gain)
-        return lax.dynamic_update_slice_in_dim(out, total.astype(BF16), start, 1)
+    def update(out, group):
+        spots = [(row ^ row_bit) * toks + (tok ^ tok_bits) for _, tok_bits, row_bit in group]
+        return update_blocks(out, weights, error, [gain for gain, _, _ in group], spots)
 
     in_x, in_y = swap(high, "tok", 2), swap(high, "row", 1)
     near = swap(pair, "tok", 1)
-    out = unwritten(weights.shape, BF16)
-    out = update(out, pair, 0, 0)
-    out = update(out, near, 1, 0)
+    out = update(None, [((pair,), 0, 0), ((near,), 1, 0)])
     in_x, in_y, out = lax.optimization_barrier((in_x, in_y, out))
     top, bottom, out = lax.optimization_barrier((in_y[:half], in_x[half:], out))
-    far = jnp.concatenate([swap(top, "tok", 2), swap(bottom, "row", 1)], axis=0)
+    far = [swap(top, "tok", 2), swap(bottom, "row", 1)]
     near_x, near_y = swap(in_x, "tok", 1), swap(in_y, "tok", 1)
-    out = update(out, in_x, 2, 0)
-    out = update(out, in_y, 0, 1)
-    far, out = lax.optimization_barrier((far, out))
-    near_far = swap(far, "tok", 1)
-    out = update(out, near_x, 3, 0)
-    out = update(out, near_y, 1, 1)
-    out = update(out, far, 2, 1)
-    return update(out, near_far, 3, 1)
+    out = update(after(out, near_x, near_y), [((in_x,), 2, 0), ((in_y,), 0, 1)])
+    far[0], far[1], out = lax.optimization_barrier((far[0], far[1], out))
+    near_far = tuple(swap(x, "tok", 1) for x in far)
+    last = [((near_x,), 3, 0), ((near_y,), 1, 1), (tuple(far), 2, 1), (near_far, 3, 1)]
+    return update(out, last)
 
 
 def solution(mesh):

time: 179 us -> 167 us (0.933)
  matrix products: 72 us -> 0.94 us
  Pallas kernels: 13.9 us -> 66.4 us
  local copies, waits for them, and re-layouts: 3.78 us -> 14.9 us
  starting transfers between devices: 47.6 us -> 39.5 us
  waiting for transfers between devices: 32.6 us -> 35.5 us
    dot_general x16 -> x2, matrix products: 72 us -> 0.94 us  [shards(): lax.dot_general(x, x, (((1,), (1,)), ((), ())), preferred_element_type=F32)]
    pallas_call x1 -> x7, Pallas kernels: 0.01 us -> 51 us  [the longest x4 33.1 us: gram_block(): pl.pallas_call(functools.partial(gram_kernel, width // QBLOCK), out_shape...]
    unnamed x36 -> x28, local copies, waits for them, and re-layouts: 1.91 us -> 14.8 us
    ppermute x18 -> x15, waiting for transfers between devices: 0.05 us -> 8.77 us  [hop(): return lax.ppermute(x, axis, [(start, start + 1)])]
    ppermute x18 -> x15, starting transfers between devices: 29.6 us -> 21.5 us  [hop(): return lax.ppermute(x, axis, [(start, start + 1)])]
    ppermute x17 -> x18, waiting for transfers between devices: 32.5 us -> 26.7 us  [swap(): return lax.ppermute(x, axis, [(i, i ^ bit) for i in range(size)])]
    select_n x6 -> x5, other arithmetic: 4.16 us -> 5.19 us  [settle(): result = jnp.where(feat == h + 1, parts[h + 1], result)]
    ppermute x17 -> x18, starting transfers between devices: 18 us -> 17.9 us  [swap(): return lax.ppermute(x, axis, [(i, i ^ bit) for i in range(size)])]
  transfers between devices with their start and end apart: 35 -> 33, of which waited for: 8 -> 13; matrix products, arithmetic and copies ran while one was open for 45% -> 5% of each run, Pallas kernels for 7% -> 33%
where the time goes in v7:
time: 167 us; the launch traced here: 166 us
  Pallas kernels  66.4 us (40%)
  starting transfers between devices  39.5 us (24%)
  waiting for transfers between devices  35.5 us (21%)
  local copies, waits for them, and re-layouts  14.9 us (9%)
  other arithmetic  7.84 us (5%)
    pallas_call x4, Pallas kernels, gram_block(): pl.pallas_call(functools.partial(gram_kernel, width // QBLOCK), out_shape...  33.1 us
    ppermute x18, waiting for transfers between devices, swap(): return lax.ppermute(x, axis, [(i, i ^ bit) for i in range(size)])  26.7 us
    ppermute x15, starting transfers between devices, hop(): return lax.ppermute(x, axis, [(start, start + 1)])  21.5 us
    ppermute x18, starting transfers between devices, swap(): return lax.ppermute(x, axis, [(i, i ^ bit) for i in range(size)])  17.9 us
    pallas_call x3, Pallas kernels, update_blocks(): pl.pallas_call(functools.partial(update_kernel, [[p.shape for p in pieces...  17.9 us
    unnamed x28, local copies, waits for them, and re-layouts  14.8 us
    ppermute x15, waiting for transfers between devices, hop(): return lax.ppermute(x, axis, [(start, start + 1)])  8.77 us
    pallas_call x1, Pallas kernels, invert(): pl.pallas_call(inverse_kernel, out_shape=jax.ShapeDtypeStruct((PANEL, PAN...  7.82 us
  transfers between devices with their start and end apart: 33, of which 13 were waited for; matrix products, arithmetic and copies ran while one was open for 5% of the time, Pallas kernels for 33%

profile of v7, /device:TPU:9, one launch (start us, length us, event | category | flops | bytes accessed | tf_op | source)
XLA Modules:
  0.0 165.7 jit_solution(541085742484260152)
XLA Ops:
  0.0 1.8 %copy.13.exps_ref.refs_1_.refs_4_ = s32[4096,56]{1,0:T(8,128)S(1)} copy(s32[4096,56]{0,1:T(8,128)} %param.5) | data formatting | bytes 1835008 | tf_op args[1]
  1.8 1.2 shard_map.46
  3.1 1.3 collective-permute-start
  4.4 1.2 shard_map.47
  5.6 1.3 collective-permute-start.2
  6.9 5.3 %collective-permute-done = bf16[256,512]{1,0:T(8,128)(2,1)} collective-permute-done((bf16[256,512]{1,0:T(8,128)(2,1)S(1)}, bf16[256,512]{1,0:T(8,128)(2,1)}, u32[]{:S(2)}, u32[]{:S(2)}) %collective-permute-start) | collective-permute-done | bytes 262176 | tf_op jit(solution)/shard_map/ppermute | solution.py:282
  12.2 2.0 %collective-permute-start.1 = (bf16[256,512]{1,0:T(8,128)(2,1)}, bf16[256,512]{1,0:T(8,128)(2,1)}, u32[]{:S(2)}, u32[]{:S(2)}) collective-permute-start(bf16[256,512]{1,0:T(8,128)(2,1)} %collective-permute-done), channel_id=1, source_target_pairs={{2,4},{3,5},{10,12},{11,13},{18,20},{19,21},{26,28},{27,29}} | collective-permute-start | bytes 786440 | tf_op jit(solution)/shard_map/ppermute | solution.py:282
  14.2 1.2 shard_map.49
  15.5 1.3 collective-permute-start.6
  17.8 2.0 %collective-permute-start.5 = (bf16[256,512]{1,0:T(8,128)(2,1)}, bf16[256,512]{1,0:T(8,128)(2,1)}, u32[]{:S(2)}, u32[]{:S(2)}) collective-permute-start(bf16[256,512]{1,0:T(8,128)(2,1)} %collective-permute-done.2), channel_id=1, source_target_pairs={{2,4},{3,5},{10,12},{11,13},{18,20},{19,21},{26,28},{27,29}} | collective-permute-start | bytes 786440 | tf_op jit(solution)/shard_map/ppermute | solution.py:282
  19.9 1.2 shard_map.48
  21.1 1.4 collective-permute-start.4
  22.6 1.4 collective-permute-start.3
  24.0 2.0 %collective-permute-start.8 = (bf16[256,512]{1,0:T(8,128)(2,1)}, bf16[256,512]{1,0:T(8,128)(2,1)}, u32[]{:S(2)}, u32[]{:S(2)}) collective-permute-start(bf16[256,512]{1,0:T(8,128)(2,1)} %collective-permute-done.6), channel_id=1, source_target_pairs={{2,4},{3,5},{10,12},{11,13},{18,20},{19,21},{26,28},{27,29}} | collective-permute-start | bytes 786440 | tf_op jit(solution)/shard_map/ppermute | solution.py:282
  25.9 1.4 collective-permute-start.7
  27.4 2.4 %collective-permute-done.4 = bf16[256,512]{1,0:T(8,128)(2,1)} collective-permute-done((bf16[256,512]{1,0:T(8,128)(2,1)S(1)}, bf16[256,512]{1,0:T(8,128)(2,1)}, u32[]{:S(2)}, u32[]{:S(2)}) %collective-permute-start.4) | collective-permute-done | bytes 262176 | tf_op jit(solution)/shard_map/ppermute | solution.py:282
  29.7 1.3 collective-permute-start.10
  32.1 1.3 collective-permute-start.11
  37.7 1.3 collective-permute-start.19
  40.0 4.1 %collective-permute-done.13 = bf16[256,512]{1,0:T(8,128)(2,1)S(1)} collective-permute-done((bf16[256,512]{1,0:T(8,128)(2,1)S(1)}, bf16[256,512]{1,0:T(8,128)(2,1)S(1)}, u32[]{:S(2)}, u32[]{:S(2)}) %collective-permute-start.13) | collective-permute-done | bytes 262176 | tf_op jit(solution)/shard_map/ppermute | solution.py:278
  46.9 9.4 %collective-permute-done.14 = bf16[256,512]{1,0:T(8,128)(2,1)S(1)} collective-permute-done((bf16[256,512]{1,0:T(8,128)(2,1)S(1)}, bf16[256,512]{1,0:T(8,128)(2,1)S(1)}, u32[]{:S(2)}, u32[]{:S(2)}) %collective-permute-start.14) | collective-permute-done | bytes 262176 | tf_op jit(solution)/shard_map/ppermute | solution.py:278
  56.3 8.2 %shard_map.50 = f32[256,896]{1,0:T(8,128)} custom-call(s32[2]{0:T(128)S(1)} %pad_add_fusion.2.place_ref, bf16[4096,7168]{1,0:T(8,128)(2,1)} %refs_3_.7, s32[4096,56]{1,0:T(8,128)S(1)} %copy.13.exps_ref.refs_1_.refs_4_, bf16[256,2048]{1,0:T(8,128)(2,1)S(1)} %pad_maximum_fusion.refs_2_, bf16[4096,7168]{1,0:T(8,128)(2,1)} %refs_3_.7, ...), custom_call_target="tpu_custom_call" | custom-call | flops 58720256 | bytes 917504 | tf_op jit(solution)/shard_map/pallas_call | solution.py:103
  64.5 3.3 %collective-permute-start.16 = (f32[256,896]{1,0:T(8,128)}, f32[256,896]{1,0:T(8,128)}, u32[]{:S(2)}, u32[]{:S(2)}) collective-permute-start(f32[256,896]{1,0:T(8,128)} %shard_map.50), channel_id=1, source_target_pairs={{0,8},{8,0},{16,24},{24,16},{1,9},{9,1},{17,25},{25,17},{2,10},{10... | collective-permute-start | bytes 2752520 | tf_op jit(solution)/shard_map/ppermute | solution.py:278
  68.9 1.5 collective-permute-done.17
  70.5 1.3 collective-permute-start.18
  71.7 2.1 %collective-permute-start.20 = (bf16[1024,256]{1,0:T(8,128)(2,1)}, bf16[1024,256]{1,0:T(8,128)(2,1)}, u32[]{:S(2)}, u32[]{:S(2)}) collective-permute-start(bf16[1024,256]{1,0:T(8,128)(2,1)} %collective-permute-done.19), channel_id=1, source_target_pairs={{2,4},{3,5},{10,12},{11,13},{18,20},{19,21},{26,28},{27,29}} | collective-permute-start | bytes 1572872 | tf_op jit(solution)/shard_map/ppermute | solution.py:282
  73.9 4.3 %collective-permute-done.18 = f32[256,256]{1,0:T(8,128)} collective-permute-done((f32[256,256]{1,0:T(8,128)S(1)}, f32[256,256]{1,0:T(8,128)}, u32[]{:S(2)}, u32[]{:S(2)}) %collective-permute-start.18) | collective-permute-done | bytes 262176 | tf_op jit(solution)/shard_map/ppermute | solution.py:278
  79.3 1.2 copy-done.3
  80.6 8.5 %shard_map.51 = f32[256,896]{1,0:T(8,128)} custom-call(s32[2]{0:T(128)S(1)} %pad_add_fusion.1.place_ref, bf16[4096,7168]{1,0:T(8,128)(2,1)} %refs_3_.7, s32[4096,56]{1,0:T(8,128)S(1)} %copy.13.exps_ref.refs_1_.refs_4_, bf16[256,2048]{1,0:T(8,128)(2,1)S(1)} %pad_maximum_fusion.refs_2_, bf16[4096,7168]{1,0:T(8,128)(2,1)} %refs_3_.7, ...), custom_call_target="tpu_custom_call" | custom-call | flops 58720256 | bytes 917504 | tf_op jit(solution)/shard_map/pallas_call | solution.py:103
  89.1 8.2 %shard_map.52 = f32[256,896]{1,0:T(8,128)} custom-call(s32[2]{0:T(128)S(1)} %pad_add_fusion.3.place_ref, bf16[4096,7168]{1,0:T(8,128)(2,1)} %refs_3_.7, s32[4096,56]{1,0:T(8,128)S(1)} %copy.13.exps_ref.refs_1_.refs_4_, bf16[256,2048]{1,0:T(8,128)(2,1)S(1)} %pad_maximum_fusion.refs_2_, bf16[4096,7168]{1,0:T(8,128)(2,1)} %refs_3_.7, ...), custom_call_target="tpu_custom_call" | custom-call | flops 58720256 | bytes 917504 | tf_op jit(solution)/shard_map/pallas_call | solution.py:103
  97.4 1.1 collective-permute-start.22
  98.5 1.2 collective-permute-start.23
  99.7 1.5 collective-permute-start.21
  101.2 1.4 copy-done.4
  102.6 8.2 %shard_map.53.first_ref = f32[256,896]{1,0:T(8,128)S(1)} custom-call(s32[2]{0:T(128)S(1)} %pad_add_fusion.4.place_ref, bf16[4096,7168]{1,0:T(8,128)(2,1)} %refs_3_.7, s32[4096,56]{1,0:T(8,128)S(1)} %copy.13.exps_ref.refs_1_.refs_4_, bf16[256,2048]{1,0:T(8,128)(2,1)S(1)} %pad_maximum_fusion.refs_2_, bf16[4096,7168]{1,0:T(8,128)(2,1)} %refs_3_.7, ...), custom_call_target="tpu_custom_call" | custom-call | flops 58720256 | bytes 917504 | tf_op jit(solution)/shard_map/pallas_call | solution.py:103
  110.8 7.8 %shard_map.54.inverse_ref = f32[256,256]{1,0:T(8,128)S(1)} custom-call(f32[256,256]{1,0:T(8,128)S(1)} %add.57.head_ref), custom_call_target="tpu_custom_call" | custom-call | flops 33554432 | bytes 524288 | tf_op jit(solution)/shard_map/pallas_call | solution.py:152
  118.6 2.2 %collective-permute-done.23.third_ref = f32[256,896]{1,0:T(8,128)} collective-permute-done((f32[256,896]{1,0:T(8,128)}, f32[256,896]{1,0:T(8,128)}, u32[]{:S(2)}, u32[]{:S(2)}) %collective-permute-start.23) | collective-permute-done | bytes 917536 | tf_op jit(solution)/shard_map/ppermute | solution.py:278
  120.8 2.6 %shard_map.55 = (bf16[256,896]{1,0:T(8,128)(2,1)S(1)}, bf16[512,896]{1,0:T(8,128)(2,1)S(1)}) custom-call(s32[1]{0:T(128)} %bitcast.12.place_ref, f32[256,256]{1,0:T(8,128)S(1)} %shard_map.54.inverse_ref, f32[256,896]{1,0:T(8,128)S(1)} %shard_map.53.first_ref, f32[256,896]{1,0:T(8,128)} %collective-permute-done.22.second_ref, ...), custom_call_target="tpu_custom_call" | custom-call | flops 704643072 | bytes 3670016 | tf_op jit(solution)/shard_map/pallas_call | solution.py:178
  125.1 1.3 collective-permute-start.24
  126.4 1.1 select_select_fusion.error_ref
  127.6 5.4 %shard_map.56.refs_2_ = bf16[1024,7168]{1,0:T(8,128)(2,1)} custom-call(s32[2]{0:T(128)S(1)} %pad_add_fusion.5.place_ref, bf16[1024,256]{1,0:T(8,128)(2,1)S(1)} %select_select_fusion.error_ref, bf16[1024,7168]{1,0:T(8,128)(2,1)S(1)} %bitcast.21, bf16[512,896]{1,0:T(8,128)(2,1)S(1)} %get-tuple-element.68.refs_0_, ...), custom_call_target="tpu_custom_call" | custom-call | flops 939524096 | bytes 7340032 | tf_op jit(solution)/shard_map/pallas_call | solution.py:260
  133.0 3.3 %collective-permute-done.25.refs_1_ = bf16[256,896]{1,0:T(8,128)(2,1)S(1)} collective-permute-done((bf16[256,896]{1,0:T(8,128)(2,1)S(1)}, bf16[256,896]{1,0:T(8,128)(2,1)S(1)}, u32[]{:S(2)}, u32[]{:S(2)}) %collective-permute-start.25) | collective-permute-done | bytes 458784 | tf_op jit(solution)/shard_map/ppermute | solution.py:278
  136.8 1.2 collective-permute-start.27
  138.1 1.3 collective-permute-start.29
  140.1 5.2 %copy-done = bf16[1024,7168]{1,0:T(8,128)(2,1)S(1)} copy-done((bf16[1024,7168]{1,0:T(8,128)(2,1)S(1)}, bf16[1024,7168]{1,0:T(8,128)(2,1)}, u32[]{:S(2)}) %copy-start) | copy-done | bytes 14680088
  145.3 4.3 %shard_map.57.refs_6_ = bf16[1024,7168]{1,0:T(8,128)(2,1)} custom-call(s32[2]{0:T(128)S(1)} %pad_add_fusion.6.place_ref, bf16[1024,256]{1,0:T(8,128)(2,1)S(1)} %select_select_fusion.error_ref, bf16[1024,7168]{1,0:T(8,128)(2,1)S(1)} %copy-done, bf16[256,896]{1,0:T(8,128)(2,1)S(1)} %collective-permute-done.24.refs_0_, ...), custom_call_target="tpu_custom_call", output_to_operand_aliasing={{}: (5, {})} | custom-call | flops 939524096 | bytes 7340032 | tf_op jit(solution)/shard_map/pallas_call | solution.py:260
  152.1 5.2 %copy-done.1 = bf16[1024,7168]{1,0:T(8,128)(2,1)S(1)} copy-done((bf16[1024,7168]{1,0:T(8,128)(2,1)S(1)}, bf16[1024,7168]{1,0:T(8,128)(2,1)}, u32[]{:S(2)}) %copy-start.1) | copy-done | bytes 14680088
  157.3 8.2 %shard_map.58 = bf16[1024,7168]{1,0:T(8,128)(2,1)} custom-call(s32[4]{0:T(128)S(1)} %pad_add_fusion.place_ref, bf16[1024,256]{1,0:T(8,128)(2,1)S(1)} %select_select_fusion.error_ref, bf16[1024,7168]{1,0:T(8,128)(2,1)S(1)} %copy-done.1, bf16[256,896]{1,0:T(8,128)(2,1)S(1)} %collective-permute-done.27.refs_0_, ...), custom_call_target="tpu_custom_call", output_to_operand_aliasing={{}: (9, {})} | custom-call | flops 1879048192 | bytes 14680064 | tf_op jit(solution)/shard_map/pallas_call | solution.py:260
  (83 shorter events, 18.3 us)
Async XLA Ops:
  3.0 2.6 %copy-start.5 = (bf16[256,512]{1,0:T(8,128)(2,1)}, bf16[256,512]{1,0:T(8,128)(2,1)S(1)}, u32[]{:S(2)}) copy-start(bf16[256,512]{1,0:T(8,128)(2,1)S(1)} %shard_map.46) | copy-start | bytes 786436
  3.1 9.2 %collective-permute-start = (bf16[256,512]{1,0:T(8,128)(2,1)S(1)}, bf16[256,512]{1,0:T(8,128)(2,1)}, u32[]{:S(2)}, u32[]{:S(2)}) collective-permute-start(bf16[256,512]{1,0:T(8,128)(2,1)S(1)} %shard_map.46), channel_id=1, source_target_pairs={{0,2},{1,3},{8,10},{9,11},{16,18},{17,19},{24,26},{25,27}} | collective-permute-start | bytes 786440 | tf_op jit(solution)/shard_map/ppermute | solution.py:282
  5.6 12.2 %collective-permute-start.2 = (bf16[256,512]{1,0:T(8,128)(2,1)S(1)}, bf16[256,512]{1,0:T(8,128)(2,1)}, u32[]{:S(2)}, u32[]{:S(2)}) collective-permute-start(bf16[256,512]{1,0:T(8,128)(2,1)S(1)} %shard_map.47), channel_id=1, source_target_pairs={{0,2},{1,3},{8,10},{9,11},{16,18},{17,19},{24,26},{25,27}} | collective-permute-start | bytes 786440 | tf_op jit(solution)/shard_map/ppermute | solution.py:282
  12.2 10.3 %collective-permute-start.1 = (bf16[256,512]{1,0:T(8,128)(2,1)}, bf16[256,512]{1,0:T(8,128)(2,1)}, u32[]{:S(2)}, u32[]{:S(2)}) collective-permute-start(bf16[256,512]{1,0:T(8,128)(2,1)} %collective-permute-done), channel_id=1, source_target_pairs={{2,4},{3,5},{10,12},{11,13},{18,20},{19,21},{26,28},{27,29}} | collective-permute-start | bytes 786440 | tf_op jit(solution)/shard_map/ppermute | solution.py:282
  15.5 8.5 %collective-permute-start.6 = (bf16[256,512]{1,0:T(8,128)(2,1)S(1)}, bf16[256,512]{1,0:T(8,128)(2,1)}, u32[]{:S(2)}, u32[]{:S(2)}) collective-permute-start(bf16[256,512]{1,0:T(8,128)(2,1)S(1)} %shard_map.49), channel_id=1, source_target_pairs={{0,2},{1,3},{8,10},{9,11},{16,18},{17,19},{24,26},{25,27}} | collective-permute-start | bytes 786440 | tf_op jit(solution)/shard_map/ppermute | solution.py:282
  17.8 8.1 %collective-permute-start.5 = (bf16[256,512]{1,0:T(8,128)(2,1)}, bf16[256,512]{1,0:T(8,128)(2,1)}, u32[]{:S(2)}, u32[]{:S(2)}) collective-permute-start(bf16[256,512]{1,0:T(8,128)(2,1)} %collective-permute-done.2), channel_id=1, source_target_pairs={{2,4},{3,5},{10,12},{11,13},{18,20},{19,21},{26,28},{27,29}} | collective-permute-start | bytes 786440 | tf_op jit(solution)/shard_map/ppermute | solution.py:282
  21.1 15.6 %slice-start.4 = ((bf16[1024,7168]{1,0:T(8,128)(2,1)}), bf16[1024,256]{1,0:T(8,128)(2,1)S(1)}, s32[]{:S(2)}) async-start(bf16[1024,7168]{1,0:T(8,128)(2,1)} %weights_ref.5), calls=%async_computation.4 | async-start | bytes 1048576 | tf_op jit(solution)/shard_map/slice | solution.py:329
  21.1 8.6 %collective-permute-start.4 = (bf16[256,512]{1,0:T(8,128)(2,1)S(1)}, bf16[256,512]{1,0:T(8,128)(2,1)}, u32[]{:S(2)}, u32[]{:S(2)}) collective-permute-start(bf16[256,512]{1,0:T(8,128)(2,1)S(1)} %shard_map.48), channel_id=1, source_target_pairs={{0,2},{1,3},{8,10},{9,11},{16,18},{17,19},{24,26},{25,27}} | collective-permute-start | bytes 786440 | tf_op jit(solution)/shard_map/ppermute | solution.py:282
  22.6 8.5 %collective-permute-start.3 = (bf16[256,512]{1,0:T(8,128)(2,1)}, bf16[256,512]{1,0:T(8,128)(2,1)}, u32[]{:S(2)}, u32[]{:S(2)}) collective-permute-start(bf16[256,512]{1,0:T(8,128)(2,1)} %collective-permute-done.1), channel_id=1, source_target_pairs={{4,6},{5,7},{12,14},{13,15},{20,22},{21,23},{28,30},{29,31}} | collective-permute-start | bytes 786440 | tf_op jit(solution)/shard_map/ppermute | solution.py:282
  24.0 9.4 %collective-permute-start.8 = (bf16[256,512]{1,0:T(8,128)(2,1)}, bf16[256,512]{1,0:T(8,128)(2,1)}, u32[]{:S(2)}, u32[]{:S(2)}) collective-permute-start(bf16[256,512]{1,0:T(8,128)(2,1)} %collective-permute-done.6), channel_id=1, source_target_pairs={{2,4},{3,5},{10,12},{11,13},{18,20},{19,21},{26,28},{27,29}} | collective-permute-start | bytes 786440 | tf_op jit(solution)/shard_map/ppermute | solution.py:282
  25.9 8.1 %collective-permute-start.7 = (bf16[256,512]{1,0:T(8,128)(2,1)}, bf16[256,512]{1,0:T(8,128)(2,1)}, u32[]{:S(2)}, u32[]{:S(2)}) collective-permute-start(bf16[256,512]{1,0:T(8,128)(2,1)} %collective-permute-done.5), channel_id=1, source_target_pairs={{4,6},{5,7},{12,14},{13,15},{20,22},{21,23},{28,30},{29,31}} | collective-permute-start | bytes 786440 | tf_op jit(solution)/shard_map/ppermute | solution.py:282
  27.4 9.4 %copy-start.7 = (s32[1024,256]{1,0:T(8,128)S(1)}, s32[1024,256]{1,0:T(8,128)}, u32[]{:S(2)}) copy-start(s32[1024,256]{1,0:T(8,128)} %param.7) | copy-start | bytes 3145732
  29.7 5.4 %collective-permute-start.10 = (bf16[256,512]{1,0:T(8,128)(2,1)}, bf16[256,512]{1,0:T(8,128)(2,1)S(1)}, u32[]{:S(2)}, u32[]{:S(2)}) collective-permute-start(bf16[256,512]{1,0:T(8,128)(2,1)} %collective-permute-done.4), channel_id=1, source_target_pairs={{2,4},{3,5},{10,12},{11,13},{18,20},{19,21},{26,28},{27,29}} | collective-permute-start | bytes 786440 | tf_op jit(solution)/shard_map/ppermute | solution.py:282
  32.1 6.9 %collective-permute-start.11 = (bf16[256,512]{1,0:T(8,128)(2,1)S(1)}, bf16[256,512]{1,0:T(8,128)(2,1)S(1)}, u32[]{:S(2)}, u32[]{:S(2)}) collective-permute-start(bf16[256,512]{1,0:T(8,128)(2,1)S(1)} %select_select_fusion.4), channel_id=1, source_target_pairs={{0,1},{1,0},{2,3},{3,2},{4,5},{5,4},{6,7},{7,6},{8,9},{9,8},{10,11... | collective-permute-start | bytes 786440 | tf_op jit(solution)/shard_map/ppermute | solution.py:278
  33.4 5.6 %collective-permute-start.9 = (bf16[256,512]{1,0:T(8,128)(2,1)}, bf16[256,512]{1,0:T(8,128)(2,1)S(1)}, u32[]{:S(2)}, u32[]{:S(2)}) collective-permute-start(bf16[256,512]{1,0:T(8,128)(2,1)} %collective-permute-done.8), channel_id=1, source_target_pairs={{4,6},{5,7},{12,14},{13,15},{20,22},{21,23},{28,30},{29,31}} | collective-permute-start | bytes 786440 | tf_op jit(solution)/shard_map/ppermute | solution.py:282
  35.1 3.9 %collective-permute-start.12 = (bf16[256,512]{1,0:T(8,128)(2,1)S(1)}, bf16[256,512]{1,0:T(8,128)(2,1)S(1)}, u32[]{:S(2)}, u32[]{:S(2)}) collective-permute-start(bf16[256,512]{1,0:T(8,128)(2,1)S(1)} %collective-permute-done.10), channel_id=1, source_target_pairs={{4,6},{5,7},{12,14},{13,15},{20,22},{21,23},{28,30},{29,31}} | collective-permute-start | bytes 786440 | tf_op jit(solution)/shard_map/ppermute | solution.py:282
  35.8 8.4 %collective-permute-start.13 = (bf16[256,512]{1,0:T(8,128)(2,1)S(1)}, bf16[256,512]{1,0:T(8,128)(2,1)S(1)}, u32[]{:S(2)}, u32[]{:S(2)}) collective-permute-start(bf16[256,512]{1,0:T(8,128)(2,1)S(1)} %select_select_fusion.3), channel_id=1, source_target_pairs={{0,1},{1,0},{2,3},{3,2},{4,5},{5,4},{6,7},{7,6},{8,9},{9,8},{10,11... | collective-permute-start | bytes 786440 | tf_op jit(solution)/shard_map/ppermute | solution.py:278
  37.7 34.1 %collective-permute-start.19 = (bf16[1024,256]{1,0:T(8,128)(2,1)}, bf16[1024,256]{1,0:T(8,128)(2,1)}, u32[]{:S(2)}, u32[]{:S(2)}) collective-permute-start(bf16[1024,256]{1,0:T(8,128)(2,1)} %compare_select_fusion), channel_id=1, source_target_pairs={{0,2},{1,3},{8,10},{9,11},{16,18},{17,19},{24,26},{25,27}} | collective-permute-start | bytes 1572872 | tf_op jit(solution)/shard_map/ppermute | solution.py:282
  45.1 11.1 %collective-permute-start.15 = (bf16[256,512]{1,0:T(8,128)(2,1)S(1)}, bf16[256,512]{1,0:T(8,128)(2,1)S(1)}, u32[]{:S(2)}, u32[]{:S(2)}) collective-permute-start(bf16[256,512]{1,0:T(8,128)(2,1)S(1)} %select_select_fusion.1), channel_id=1, source_target_pairs={{0,1},{1,0},{2,3},{3,2},{4,5},{5,4},{6,7},{7,6},{8,9},{9,8},{10,11... | collective-permute-start | bytes 786440 | tf_op jit(solution)/shard_map/ppermute | solution.py:278
  46.1 10.1 %collective-permute-start.14 = (bf16[256,512]{1,0:T(8,128)(2,1)S(1)}, bf16[256,512]{1,0:T(8,128)(2,1)S(1)}, u32[]{:S(2)}, u32[]{:S(2)}) collective-permute-start(bf16[256,512]{1,0:T(8,128)(2,1)S(1)} %select_select_fusion.2), channel_id=1, source_target_pairs={{0,1},{1,0},{2,3},{3,2},{4,5},{5,4},{6,7},{7,6},{8,9},{9,8},{10,11... | collective-permute-start | bytes 786440 | tf_op jit(solution)/shard_map/ppermute | solution.py:278
  56.3 12.0 %copy-start.2 = (bf16[256,2048]{1,0:T(8,128)(2,1)}, bf16[256,2048]{1,0:T(8,128)(2,1)S(1)}, u32[]{:S(2)}) copy-start(bf16[256,2048]{1,0:T(8,128)(2,1)S(1)} %constant_dynamic-update-slice_fusion.refs_5_) | copy-start | bytes 3145732
  64.5 14.8 %collective-permute-start.16 = (f32[256,896]{1,0:T(8,128)}, f32[256,896]{1,0:T(8,128)}, u32[]{:S(2)}, u32[]{:S(2)}) collective-permute-start(f32[256,896]{1,0:T(8,128)} %shard_map.50), channel_id=1, source_target_pairs={{0,8},{8,0},{16,24},{24,16},{1,9},{9,1},{17,25},{25,17},{2,10},{10... | collective-permute-start | bytes 2752520 | tf_op jit(solution)/shard_map/ppermute | solution.py:278
  68.8 1.6 collective-permute-start.17
  70.4 3.5 %copy-start.6 = (f32[256,256]{1,0:T(8,128)}, f32[256,256]{1,0:T(8,128)S(1)}, u32[]{:S(2)}) copy-start(f32[256,256]{1,0:T(8,128)S(1)} %add.56) | copy-start | bytes 786436
  70.5 7.8 %collective-permute-start.18 = (f32[256,256]{1,0:T(8,128)S(1)}, f32[256,256]{1,0:T(8,128)}, u32[]{:S(2)}, u32[]{:S(2)}) collective-permute-start(f32[256,256]{1,0:T(8,128)S(1)} %add.56), channel_id=1, source_target_pairs={{0,16},{8,24},{16,0},{24,8},{1,17},{9,25},{17,1},{25,9},{2,18},{10... | collective-permute-start | bytes 786440 | tf_op jit(solution)/shard_map/ppermute | solution.py:278
  71.7 27.9 %collective-permute-start.20 = (bf16[1024,256]{1,0:T(8,128)(2,1)}, bf16[1024,256]{1,0:T(8,128)(2,1)}, u32[]{:S(2)}, u32[]{:S(2)}) collective-permute-start(bf16[1024,256]{1,0:T(8,128)(2,1)} %collective-permute-done.19), channel_id=1, source_target_pairs={{2,4},{3,5},{10,12},{11,13},{18,20},{19,21},{26,28},{27,29}} | collective-permute-start | bytes 1572872 | tf_op jit(solution)/shard_map/ppermute | solution.py:282
  79.3 1.2 copy-start.3
  97.4 21.2 %collective-permute-start.22 = (f32[256,896]{1,0:T(8,128)}, f32[256,896]{1,0:T(8,128)}, u32[]{:S(2)}, u32[]{:S(2)}) collective-permute-start(f32[256,896]{1,0:T(8,128)} %shard_map.52), channel_id=1, source_target_pairs={{0,8},{8,0},{16,24},{24,16},{1,9},{9,1},{17,25},{25,17},{2,10},{10... | collective-permute-start | bytes 2752520 | tf_op jit(solution)/shard_map/ppermute | solution.py:278
  98.5 22.3 %collective-permute-start.23 = (f32[256,896]{1,0:T(8,128)}, f32[256,896]{1,0:T(8,128)}, u32[]{:S(2)}, u32[]{:S(2)}) collective-permute-start(f32[256,896]{1,0:T(8,128)} %shard_map.51), channel_id=1, source_target_pairs={{0,16},{8,24},{16,0},{24,8},{1,17},{9,25},{17,1},{25,9},{2,18},{10... | collective-permute-start | bytes 2752520 | tf_op jit(solution)/shard_map/ppermute | solution.py:278
  99.7 18.9 %collective-permute-start.21 = (bf16[1024,256]{1,0:T(8,128)(2,1)}, bf16[1024,256]{1,0:T(8,128)(2,1)}, u32[]{:S(2)}, u32[]{:S(2)}) collective-permute-start(bf16[1024,256]{1,0:T(8,128)(2,1)} %collective-permute-done.20), channel_id=1, source_target_pairs={{4,6},{5,7},{12,14},{13,15},{20,22},{21,23},{28,30},{29,31}} | collective-permute-start | bytes 1572872 | tf_op jit(solution)/shard_map/ppermute | solution.py:282
  101.2 26.4 %slice-start = ((s8[14680064]{0:T(1024)(128)(4,1)}), s8[4194304]{0:T(1024)(128)(4,1)S(1)}, s32[]{:S(2)}) async-start(s8[14680064]{0:T(1024)(128)(4,1)} %bitcast.20), calls=%async_computation | async-start | bytes 8388608
  101.2 1.4 copy-start.4
  102.6 25.0 %slice-start.1 = ((s8[14680064]{0:T(1024)(128)(4,1)}), s8[4194304]{0:T(1024)(128)(4,1)S(1)}, s32[]{:S(2)}) async-start(s8[14680064]{0:T(1024)(128)(4,1)} %bitcast.20), calls=%async_computation.1 | async-start | bytes 8388608
  102.6 25.0 %slice-start.2 = ((s8[14680064]{0:T(1024)(128)(4,1)}), s8[4194304]{0:T(1024)(128)(4,1)S(1)}, s32[]{:S(2)}) async-start(s8[14680064]{0:T(1024)(128)(4,1)} %bitcast.20), calls=%async_computation.2 | async-start | bytes 8388608
  102.6 25.0 %slice-start.3 = ((s8[14680064]{0:T(1024)(128)(4,1)}), s8[2097152]{0:T(1024)(128)(4,1)S(1)}, s32[]{:S(2)}) async-start(s8[14680064]{0:T(1024)(128)(4,1)} %bitcast.20), calls=%async_computation.3 | async-start | bytes 4194304
  123.3 4.2 %collective-permute-start.26 = (bf16[512,896]{1,0:T(8,128)(2,1)S(1)}, bf16[512,896]{1,0:T(8,128)(2,1)S(1)}, u32[]{:S(2)}, u32[]{:S(2)}) collective-permute-start(bf16[512,896]{1,0:T(8,128)(2,1)S(1)} %get-tuple-element.68.refs_0_), channel_id=1, source_target_pairs={{0,8},{8,0},{16,24},{24,16},{1,9},{9,1},{17,25},{25,17},{2,10},{10... | collective-permute-start | bytes 2752520 | tf_op jit(solution)/shard_map/ppermute | solution.py:278
  124.2 12.1 %collective-permute-start.25 = (bf16[256,896]{1,0:T(8,128)(2,1)S(1)}, bf16[256,896]{1,0:T(8,128)(2,1)S(1)}, u32[]{:S(2)}, u32[]{:S(2)}) collective-permute-start(bf16[256,896]{1,0:T(8,128)(2,1)S(1)} %get-tuple-element.67), channel_id=1, source_target_pairs={{0,1},{1,0},{2,3},{3,2},{4,5},{5,4},{6,7},{7,6},{8,9},{9,8},{10,11... | collective-permute-start | bytes 1376264 | tf_op jit(solution)/shard_map/ppermute | solution.py:278
  125.1 11.8 %collective-permute-start.24 = (bf16[256,896]{1,0:T(8,128)(2,1)S(1)}, bf16[256,896]{1,0:T(8,128)(2,1)S(1)}, u32[]{:S(2)}, u32[]{:S(2)}) collective-permute-start(bf16[256,896]{1,0:T(8,128)(2,1)S(1)} %get-tuple-element.67), channel_id=1, source_target_pairs={{0,16},{8,24},{16,0},{24,8},{1,17},{9,25},{17,1},{25,9},{2,18},{10... | collective-permute-start | bytes 1376264 | tf_op jit(solution)/shard_map/ppermute | solution.py:278
  136.8 3.2 %collective-permute-start.27 = (bf16[256,896]{1,0:T(8,128)(2,1)S(1)}, bf16[256,896]{1,0:T(8,128)(2,1)S(1)}, u32[]{:S(2)}, u32[]{:S(2)}) collective-permute-start(bf16[256,896]{1,0:T(8,128)(2,1)S(1)} %collective-permute-done.24.refs_0_), channel_id=1, source_target_pairs={{0,8},{8,0},{16,24},{24,16},{1,9},{9,1},{17,25},{25,17},{2,10},{10... | collective-permute-start | bytes 1376264 | tf_op jit(solution)/shard_map/ppermute | solution.py:278
  138.0 2.1 %collective-permute-start.28 = (bf16[256,896]{1,0:T(8,128)(2,1)S(1)}, bf16[256,896]{1,0:T(8,128)(2,1)S(1)}, u32[]{:S(2)}, u32[]{:S(2)}) collective-permute-start(bf16[256,896]{1,0:T(8,128)(2,1)S(1)} %collective-permute-done.25.refs_1_), channel_id=1, source_target_pairs={{0,8},{8,0},{16,24},{24,16},{1,9},{9,1},{17,25},{25,17},{2,10},{10... | collective-permute-start | bytes 1376264 | tf_op jit(solution)/shard_map/ppermute | solution.py:278
  138.1 11.5 %collective-permute-start.29 = (bf16[128,896]{1,0:T(8,128)(2,1)S(1)}, bf16[128,896]{1,0:T(8,128)(2,1)S(1)}, u32[]{:S(2)}, u32[]{:S(2)}) collective-permute-start(bf16[128,896]{1,0:T(8,128)(2,1)S(1)} %slice.10), channel_id=1, source_target_pairs={{0,16},{8,24},{16,0},{24,8},{1,17},{9,25},{17,1},{25,9},{2,18},{10... | collective-permute-start | bytes 688136 | tf_op jit(solution)/shard_map/ppermute | solution.py:278
  139.4 10.2 %collective-permute-start.30 = (bf16[128,896]{1,0:T(8,128)(2,1)S(1)}, bf16[128,896]{1,0:T(8,128)(2,1)S(1)}, u32[]{:S(2)}, u32[]{:S(2)}) collective-permute-start(bf16[128,896]{1,0:T(8,128)(2,1)S(1)} %slice.11), channel_id=1, source_target_pairs={{0,1},{1,0},{2,3},{3,2},{4,5},{5,4},{6,7},{7,6},{8,9},{9,8},{10,11... | collective-permute-start | bytes 688136 | tf_op jit(solution)/shard_map/ppermute | solution.py:278
  140.1 5.2 %copy-start = (bf16[1024,7168]{1,0:T(8,128)(2,1)S(1)}, bf16[1024,7168]{1,0:T(8,128)(2,1)}, u32[]{:S(2)}) copy-start(bf16[1024,7168]{1,0:T(8,128)(2,1)} %weights_ref.5) | copy-start | bytes 44040196
  149.6 2.1 %collective-permute-start.31 = (bf16[128,896]{1,0:T(8,128)(2,1)S(1)}, bf16[128,896]{1,0:T(8,128)(2,1)S(1)}, u32[]{:S(2)}, u32[]{:S(2)}) collective-permute-start(bf16[128,896]{1,0:T(8,128)(2,1)S(1)} %collective-permute-done.29.refs_2_), channel_id=1, source_target_pairs={{0,8},{8,0},{16,24},{24,16},{1,9},{9,1},{17,25},{25,17},{2,10},{10... | collective-permute-start | bytes 688136 | tf_op jit(solution)/shard_map/ppermute | solution.py:278
  150.6 1.5 collective-permute-start.32
  152.1 5.2 %copy-start.1 = (bf16[1024,7168]{1,0:T(8,128)(2,1)S(1)}, bf16[1024,7168]{1,0:T(8,128)(2,1)}, u32[]{:S(2)}) copy-start(bf16[1024,7168]{1,0:T(8,128)(2,1)} %weights_ref.5) | copy-start | bytes 44040196

commit v8 on v7

--- a/solution.py
+++ b/solution.py
@@ -60,10 +60,8 @@
         out_ref[...] = refs[6][...] if len(refs) > 8 else jnp.zeros_like(out_ref)
 
     for side in range(2):
-        quant_ref, exps_ref, _ = refs[3 * side : 3 * side + 3]
-        scale = jnp.exp2(exps_ref[...].astype(F32))
-        rest = jnp.zeros((step, QBLOCK - scale.shape[1]), F32)
-        scale = pltpu.roll(jnp.concatenate([scale, rest], axis=1), shift, 1)
+        quant_ref, scale_ref, _ = refs[3 * side : 3 * side + 3]
+        scale = pltpu.roll(scale_ref[...], shift, 1)
         rows = slice(side * step, (side + 1) * step)
         for c in range(blocks):
             span = slice(c * QBLOCK, (c + 1) * QBLOCK)
@@ -73,30 +71,32 @@
     out_ref[...] += jnp.dot(panel, acts_ref[...], preferred_element_type=F32)
 
 
-def gram_block(quantized, exponents, own, other, row, col, width, extra=None):
+def gram_block(quantized, scale_pad, own, other, row, col, width, first, extra=None):
     tokens, cols = quantized.shape
-    if width % QBLOCK or cols // QBLOCK >= QBLOCK:
-        panel = jnp.concatenate([own, other], axis=1)
-        quant = lax.dynamic_slice_in_dim(quantized, col * width, width, 1)
-        scale = jnp.exp2(exponents.astype(F32)).astype(BF16)
-        acts = quant * jnp.take(scale, (col * width + jnp.arange(width)) // QBLOCK, axis=1)
-        acts = jnp.roll(acts, -row * (tokens // 2), axis=0)
-        total = jnp.dot(panel, acts, preferred_element_type=F32)
-        return total if extra is None else total + extra
+    if width % QBLOCK or cols // QBLOCK > QBLOCK:
+        total = 0.0 if extra is None else extra
+        for side, panel in enumerate((own, other)):
+            at = (row + side) % 2 * (tokens // 2) + first * (tokens // 2 // ROUNDS)
+            size = (panel.shape[1], width)
+            quant = lax.dynamic_slice(quantized, (at, col * width), size)
+            scale = lax.dynamic_slice_in_dim(scale_pad, at, size[0], 0).astype(BF16)
+            acts = quant * jnp.take(scale, (col * width + jnp.arange(width)) // QBLOCK, axis=1)
+            total = total + jnp.dot(panel, acts, preferred_element_type=F32)
+        return total
     step = tokens // 2 // ROUNDS
     place = jnp.stack([row, col]).astype(jnp.int32)
     specs, args = [], [place]
     for side, panel in enumerate((own, other)):
 
         def at(k, place, side=side):
-            return lax.rem(place[0] + side, 2) * ROUNDS + k
+            return lax.rem(place[0] + side, 2) * ROUNDS + first + k
 
         specs += [
             pl.BlockSpec((step, width), lambda k, place, at=at: (at(k, place), place[1])),
-            pl.BlockSpec((step, cols // QBLOCK), lambda k, place, at=at: (at(k, place), 0)),
+            pl.BlockSpec((step, QBLOCK), lambda k, place, at=at: (at(k, place), 0)),
             pl.BlockSpec((PANEL, step), lambda k, place: (0, k)),
         ]
-        args += [quantized, exponents, panel]
+        args += [quantized, scale_pad, panel]
     if extra is not None:
         specs.append(pl.BlockSpec((PANEL, width), lambda k, place: (0, 0)))
         args.append(extra)
@@ -105,7 +105,7 @@
         out_shape=jax.ShapeDtypeStruct((PANEL, width), F32),
         grid_spec=pltpu.PrefetchScalarGridSpec(
             num_scalar_prefetch=1,
-            grid=(ROUNDS,),
+            grid=(own.shape[1] // step,),
             in_specs=specs,
             out_specs=pl.BlockSpec((PANEL, width), lambda k, place: (0, 0)),
             scratch_shapes=[pltpu.VMEM((2 * step, width), BF16)],
@@ -264,7 +264,7 @@
         out_specs=anywhere,
         scratch_shapes=[buffer, buffer, sems, sems],
         input_output_aliases=aliases,
-        compiler_params=pltpu.CompilerParams(vmem_limit_bytes=36 * MIB),
+        compiler_params=pltpu.CompilerParams(vmem_limit_bytes=52 * MIB),
         cost_estimate=pl.CostEstimate(
             flops=2 * rows * width * PANEL * count,
             bytes_accessed=4 * rows * width * count,
@@ -312,7 +312,17 @@
         return result
 
     events = sorted((5 * (c + 1) + 8 * h, c, h) for c in range(ROUNDS) for h in range(hops))
-    full, swapped, token, errors = [], [], None, None
+    early = ROUNDS // 2
+    full, swapped, token, errors, begun, scale_pad = [], [], got[-1][0], None, {}, None
+
+    def gram(k, first, last, link, extra=None):
+        own = jnp.concatenate(full[first:last], axis=1)
+        other = jnp.concatenate(swapped[first:last], axis=1)
+        col = row * toks + (tok ^ k)
+        if link is not None:
+            col = after(col, link)
+        return gram_block(quantized, scale_pad, own, other, row, col, width, first, extra)
+
     for _, c, h in events:
         x = got[c][h + 1]
         if token is not None:
@@ -325,39 +335,39 @@
         else:
             full.append(settle(got[c]))
             swapped.append(swap(full[-1], "row", 1))
-        if (c, h) == (0, 1):
+        if (c, h) == (1, 0):
+            scale = jnp.exp2(after(exponents, x).astype(F32))
+            scale_pad = jnp.pad(scale, ((0, 0), (0, -scale.shape[1] % QBLOCK)))
+        elif (c, h) == (0, 1):
             panel_weights, mask = after(weights[:, :PANEL], x), after(keep_mask, x)
             error = jnp.where(mask == 0, panel_weights, jnp.zeros((), BF16))
         elif (c, h) == (ROUNDS - 1, 1):
             errors = [after(error, x)]
             errors.append(hop(errors[0], "feat", 0))
+    begun[3] = gram(3, 0, early, full[-1])
+    begun[2] = gram(2, 0, early, begun[3])
+    swapped[-1] = after(swapped[-1], begun[2], errors[1])
     own, other = jnp.concatenate(full, axis=1), jnp.concatenate(swapped, axis=1)
-
-    def gram(k, link, extra=None):
-        col = row * toks + (tok ^ k)
-        if link is not None:
-            col = after(col, link)
-        return gram_block(quantized, exponents, own, other, row, col, width, extra)
 
     head = sum(
         lax.dot_general(x, x, (((1,), (1,)), ((), ())), preferred_element_type=F32)
         for x in (own, other)
     )
     head = head + swap(head, "tok", 1)
-    block3 = gram(3, None)
+    block3 = gram(3, early, ROUNDS, head, begun[3])
     from3 = swap(block3, "tok", 1)
     errors[1] = after(errors[1], block3)
     errors.append(hop(errors[1], "feat", 1))
     head = head + swap(head, "tok", 2)
-    block2 = gram(2, None, from3)
+    block2 = gram(2, early, ROUNDS, from3, begun[2] + from3)
     block2, head = lax.optimization_barrier((block2, head))
     fromx = swap(block2, "tok", 2)
-    block1 = gram(1, block2)
+    block1 = gram(1, 0, ROUNDS, block2)
     from1 = swap(block1, "tok", 1)
     errors[2] = after(errors[2], block1)
     for h in range(2, hops):
         errors.append(hop(errors[h], "feat", h))
-    block0 = gram(0, block1)
+    block0 = gram(0, 0, ROUNDS, block1)
     inverse = invert(after(head, block0))
     inverse, last = lax.optimization_barrier((inverse, errors[-1]))
     error = settle(errors[:-1] + [last])

time: 167 us -> 157 us (0.940)
  waiting for transfers between devices: 35.5 us -> 18.1 us
  starting transfers between devices: 39.5 us -> 47.9 us
  local copies, waits for them, and re-layouts: 14.9 us -> 6.63 us
  Pallas kernels: 66.4 us -> 71 us
    ppermute x18, waiting for transfers between devices: 26.7 us -> 12 us  [swap(): return lax.ppermute(x, axis, [(i, i ^ bit) for i in range(size)])]
    unnamed x28 -> x35, local copies, waits for them, and re-layouts: 14.8 us -> 4.57 us
    ppermute x18, starting transfers between devices: 17.9 us -> 24.3 us  [swap(): return lax.ppermute(x, axis, [(i, i ^ bit) for i in range(size)])]
    ppermute x15, waiting for transfers between devices: 8.77 us -> 6.02 us  [hop(): return lax.ppermute(x, axis, [(start, start + 1)])]
    pallas_call x3, Pallas kernels: 17.9 us -> 20.5 us  [update_blocks(): pl.pallas_call(functools.partial(update_kernel, [[p.shape for p in pieces...]
    pallas_call x4 -> x6, Pallas kernels: 33.1 us -> 35.3 us  [gram_block(): pl.pallas_call(functools.partial(gram_kernel, width // QBLOCK), out_shape...]
    convert_element_type x0 -> x1, other arithmetic: none -> 2.16 us  [shards(): scale = jnp.exp2(after(exponents, x).astype(F32))]
    ppermute x15, starting transfers between devices: 21.5 us -> 23.6 us  [hop(): return lax.ppermute(x, axis, [(start, start + 1)])]
  transfers between devices with their start and end apart: 33 -> 33, of which waited for: 13 -> 14; matrix products, arithmetic and copies ran while one was open for 5% -> 8% of each run, Pallas kernels for 33% -> 34%
where the time goes in v8:
time: 157 us; the launch traced here: 155 us
  Pallas kernels  71 us (45%)
  starting transfers between devices  47.9 us (31%)
  waiting for transfers between devices  18.1 us (12%)
  other arithmetic  9.38 us (6%)
  local copies, waits for them, and re-layouts  6.63 us (4%)
    pallas_call x6, Pallas kernels, gram_block(): pl.pallas_call(functools.partial(gram_kernel, width // QBLOCK), out_shape...  35.3 us
    ppermute x18, starting transfers between devices, swap(): return lax.ppermute(x, axis, [(i, i ^ bit) for i in range(size)])  24.3 us
    ppermute x15, starting transfers between devices, hop(): return lax.ppermute(x, axis, [(start, start + 1)])  23.6 us
    pallas_call x3, Pallas kernels, update_blocks(): pl.pallas_call(functools.partial(update_kernel, [[p.shape for p in pieces...  20.5 us
    ppermute x18, waiting for transfers between devices, swap(): return lax.ppermute(x, axis, [(i, i ^ bit) for i in range(size)])  12 us
    pallas_call x1, Pallas kernels, invert(): pl.pallas_call(inverse_kernel, out_shape=jax.ShapeDtypeStruct((PANEL, PAN...  7.64 us
    ppermute x15, waiting for transfers between devices, hop(): return lax.ppermute(x, axis, [(start, start + 1)])  6.02 us
    pallas_call x4, Pallas kernels, panel_piece(): pl.pallas_call(panel_kernel, out_shape=jax.ShapeDtypeStruct((PANEL, piece...  4.98 us
  transfers between devices with their start and end apart: 33, of which 14 were waited for; matrix products, arithmetic and copies ran while one was open for 8% of the time, Pallas kernels for 34%

profile of v8, /device:TPU:9, one launch (start us, length us, event | category | flops | bytes accessed | tf_op | source)
XLA Modules:
  0.0 154.7 jit_solution(3940981802455113224)
XLA Ops:
  0.0 1.8 %copy.12.exps_ref = s32[4096,56]{1,0:T(8,128)S(1)} copy(s32[4096,56]{0,1:T(8,128)} %param.5) | data formatting | bytes 1835008 | tf_op args[1]
  1.8 1.2 shard_map.46
  3.0 1.3 collective-permute-start
  4.3 1.2 shard_map.48
  5.6 1.3 collective-permute-start.2
  6.9 1.2 shard_map.49
  8.2 1.3 collective-permute-start.6
  9.5 1.2 shard_map.47
  10.7 1.3 collective-permute-start.4
  12.2 3.3 %collective-permute-start.1 = (bf16[256,512]{1,0:T(8,128)(2,1)}, bf16[256,512]{1,0:T(8,128)(2,1)}, u32[]{:S(2)}, u32[]{:S(2)}) collective-permute-start(bf16[256,512]{1,0:T(8,128)(2,1)} %collective-permute-done), channel_id=1, source_target_pairs={{2,4},{3,5},{10,12},{11,13},{18,20},{19,21},{26,28},{27,29}} | collective-permute-start | bytes 786440 | tf_op jit(solution)/shard_map/ppermute | solution.py:282
  15.5 2.3 %collective-permute-done.2 = bf16[256,512]{1,0:T(8,128)(2,1)} collective-permute-done((bf16[256,512]{1,0:T(8,128)(2,1)S(1)}, bf16[256,512]{1,0:T(8,128)(2,1)}, u32[]{:S(2)}, u32[]{:S(2)}) %collective-permute-start.2) | collective-permute-done | bytes 262176 | tf_op jit(solution)/shard_map/ppermute | solution.py:282
  17.8 2.0 %collective-permute-start.5 = (bf16[256,512]{1,0:T(8,128)(2,1)}, bf16[256,512]{1,0:T(8,128)(2,1)}, u32[]{:S(2)}, u32[]{:S(2)}) collective-permute-start(bf16[256,512]{1,0:T(8,128)(2,1)} %collective-permute-done.2), channel_id=1, source_target_pairs={{2,4},{3,5},{10,12},{11,13},{18,20},{19,21},{26,28},{27,29}} | collective-permute-start | bytes 786440 | tf_op jit(solution)/shard_map/ppermute | solution.py:282
  19.8 2.2 %convert_element_type.5 = f32[4096,56]{0,1:T(8,128)} convert(s32[4096,56]{0,1:T(8,128)} %param.5) | non-fusion elementwise | flops 229376 | bytes 1835008 | tf_op jit(solution)/shard_map/convert_element_type | solution.py:339
  22.0 1.8 %copy.16 = f32[4096,56]{1,0:T(8,128)S(1)} copy(f32[4096,56]{0,1:T(8,128)} %convert_element_type.5) | data formatting | bytes 1835008 | tf_op jit(solution)/shard_map/convert_element_type | solution.py:339
  25.1 1.3 collective-permute-start.8
  27.1 1.9 %collective-permute-done.4 = bf16[256,512]{1,0:T(8,128)(2,1)S(1)} collective-permute-done((bf16[256,512]{1,0:T(8,128)(2,1)S(1)}, bf16[256,512]{1,0:T(8,128)(2,1)S(1)}, u32[]{:S(2)}, u32[]{:S(2)}) %collective-permute-start.4) | collective-permute-done | bytes 262176 | tf_op jit(solution)/shard_map/ppermute | solution.py:282
  29.0 1.7 %collective-permute-start.10 = (bf16[256,512]{1,0:T(8,128)(2,1)S(1)}, bf16[256,512]{1,0:T(8,128)(2,1)S(1)}, u32[]{:S(2)}, u32[]{:S(2)}) collective-permute-start(bf16[256,512]{1,0:T(8,128)(2,1)S(1)} %collective-permute-done.4), channel_id=1, source_target_pairs={{2,4},{3,5},{10,12},{11,13},{18,20},{19,21},{26,28},{27,29}} | collective-permute-start | bytes 786440 | tf_op jit(solution)/shard_map/ppermute | solution.py:282
  32.6 1.3 collective-permute-start.11
  35.2 1.6 %collective-permute-done.10 = bf16[256,512]{1,0:T(8,128)(2,1)S(1)} collective-permute-done((bf16[256,512]{1,0:T(8,128)(2,1)S(1)}, bf16[256,512]{1,0:T(8,128)(2,1)S(1)}, u32[]{:S(2)}, u32[]{:S(2)}) %collective-permute-start.10) | collective-permute-done | bytes 262176 | tf_op jit(solution)/shard_map/ppermute | solution.py:282
  37.5 1.3 collective-permute-start.16
  39.9 1.3 collective-permute-start.14
  42.3 1.3 collective-permute-start.15
  43.7 4.5 %shard_map.50.refs_6_ = f32[256,896]{1,0:T(8,128)S(1)} custom-call(s32[2]{0:T(128)S(1)} %pad_add_fusion.1.place_ref, bf16[4096,7168]{1,0:T(8,128)(2,1)} %refs_3_.11, f32[4096,128]{1,0:T(8,128)S(1)} %pad.4.refs_1_.refs_4_, bf16[256,1024]{1,0:T(8,128)(2,1)S(1)} %pad_maximum_fusion.1.refs_2_, bf16[4096,7168]{1,0:T(8,128)(2,1)} %refs_3_.11, ...), custom_call_target="tpu_custom_call" | custom-call | flops 58720256 | bytes 917504 | tf_op jit(solution)/shard_map/pallas_call | solution.py:103
  48.3 4.5 %shard_map.51 = f32[256,896]{1,0:T(8,128)S(1)} custom-call(s32[2]{0:T(128)S(1)} %pad_add_fusion.2.place_ref, bf16[4096,7168]{1,0:T(8,128)(2,1)} %refs_3_.11, f32[4096,128]{1,0:T(8,128)S(1)} %pad.4.refs_1_.refs_4_, bf16[256,1024]{1,0:T(8,128)(2,1)S(1)} %pad_maximum_fusion.1.refs_2_, bf16[4096,7168]{1,0:T(8,128)(2,1)} %refs_3_.11, ...), custom_call_target="tpu_custom_call" | custom-call | flops 58720256 | bytes 917504 | tf_op jit(solution)/shard_map/pallas_call | solution.py:103
  54.8 8.8 %collective-permute-start.17 = (f32[256,256]{1,0:T(8,128)S(1)}, f32[256,256]{1,0:T(8,128)S(1)}, u32[]{:S(2)}, u32[]{:S(2)}) collective-permute-start(f32[256,256]{1,0:T(8,128)S(1)} %convolution_add_fusion), channel_id=1, source_target_pairs={{0,8},{8,0},{16,24},{24,16},{1,9},{9,1},{17,25},{25,17},{2,10},{10... | collective-permute-start | bytes 786440 | tf_op jit(solution)/shard_map/ppermute | solution.py:278
  63.6 1.1 collective-permute-done.17
  64.9 5.5 %shard_map.52 = f32[256,896]{1,0:T(8,128)} custom-call(s32[2]{0:T(128)S(1)} %pad_add_fusion.3.place_ref, bf16[4096,7168]{1,0:T(8,128)(2,1)} %refs_3_.11, f32[4096,128]{1,0:T(8,128)S(1)} %pad.4.refs_1_.refs_4_, bf16[256,1024]{1,0:T(8,128)(2,1)S(1)} %pad_maximum_fusion.2.refs_2_, bf16[4096,7168]{1,0:T(8,128)(2,1)} %refs_3_.11, ...), custom_call_target="tpu_custom_call" | custom-call | flops 58720256 | bytes 917504 | tf_op jit(solution)/shard_map/pallas_call | solution.py:103
  70.7 1.2 collective-permute-start.19
  71.9 4.6 %collective-permute-start.20 = (bf16[1024,256]{1,0:T(8,128)(2,1)}, bf16[1024,256]{1,0:T(8,128)(2,1)}, u32[]{:S(2)}, u32[]{:S(2)}) collective-permute-start(bf16[1024,256]{1,0:T(8,128)(2,1)} %copy-done.14), channel_id=1, source_target_pairs={{2,4},{3,5},{10,12},{11,13},{18,20},{19,21},{26,28},{27,29}} | collective-permute-start | bytes 1572872 | tf_op jit(solution)/shard_map/ppermute | solution.py:282
  76.5 2.1 %collective-permute-done.19 = f32[256,256]{1,0:T(8,128)} collective-permute-done((f32[256,256]{1,0:T(8,128)S(1)}, f32[256,256]{1,0:T(8,128)}, u32[]{:S(2)}, u32[]{:S(2)}) %collective-permute-start.19) | collective-permute-done | bytes 262176 | tf_op jit(solution)/shard_map/ppermute | solution.py:278
  79.7 1.5 %add.64.refs_6_ = f32[256,896]{1,0:T(8,128)S(1)} add(f32[256,896]{1,0:T(8,128)} %copy-done.6, f32[256,896]{1,0:T(8,128)} %collective-permute-done.18) | non-fusion elementwise | flops 229376 | bytes 2752512 | tf_op jit(solution)/shard_map/add | solution.py:362
  81.3 5.4 %shard_map.53 = f32[256,896]{1,0:T(8,128)} custom-call(s32[2]{0:T(128)S(1)} %pad_add_fusion.4.place_ref, bf16[4096,7168]{1,0:T(8,128)(2,1)} %refs_3_.11, f32[4096,128]{1,0:T(8,128)S(1)} %pad.4.refs_1_.refs_4_, bf16[256,1024]{1,0:T(8,128)(2,1)S(1)} %copy-done.5, bf16[4096,7168]{1,0:T(8,128)(2,1)} %refs_3_.11, f32[4096,128]{1,0:T(8,128)S(1)} %pad.4.refs_1_.refs_4_, ...), custom_call_target="tpu_custom_call" | custom-call | flops 58720256 | bytes 917504 | tf_op jit(solution)/shard_map/pallas_call | solution.py:103
  86.8 8.1 %shard_map.54 = f32[256,896]{1,0:T(8,128)} custom-call(s32[2]{0:T(128)S(1)} %pad_add_fusion.5.place_ref, bf16[4096,7168]{1,0:T(8,128)(2,1)} %refs_3_.11, f32[4096,128]{1,0:T(8,128)S(1)} %pad.4.refs_1_.refs_4_, bf16[256,2048]{1,0:T(8,128)(2,1)S(1)} %pad_maximum_fusion.refs_2_, bf16[4096,7168]{1,0:T(8,128)(2,1)} %refs_3_.11, ...), custom_call_target="tpu_custom_call" | custom-call | flops 58720256 | bytes 917504 | tf_op jit(solution)/shard_map/pallas_call | solution.py:103
  95.9 1.2 collective-permute-start.23
  97.1 1.5 collective-permute-start.21
  98.7 1.2 copy-done.2
  99.9 7.2 %shard_map.55.first_ref = f32[256,896]{1,0:T(8,128)S(1)} custom-call(s32[2]{0:T(128)S(1)} %pad_add_fusion.6.place_ref, bf16[4096,7168]{1,0:T(8,128)(2,1)} %refs_3_.11, f32[4096,128]{1,0:T(8,128)S(1)} %pad.4.refs_1_.refs_4_, bf16[256,2048]{1,0:T(8,128)(2,1)S(1)} %pad_maximum_fusion.refs_2_, bf16[4096,7168]{1,0:T(8,128)(2,1)} %refs_3_.11, ...), custom_call_target="tpu_custom_call" | custom-call | flops 58720256 | bytes 917504 | tf_op jit(solution)/shard_map/pallas_call | solution.py:103
  107.2 7.6 %shard_map.56.inverse_ref = f32[256,256]{1,0:T(8,128)S(1)} custom-call(f32[256,256]{1,0:T(8,128)S(1)} %add.65.head_ref), custom_call_target="tpu_custom_call" | custom-call | flops 33554432 | bytes 524288 | tf_op jit(solution)/shard_map/pallas_call | solution.py:152
  114.8 3.4 %collective-permute-done.23.third_ref = f32[256,896]{1,0:T(8,128)} collective-permute-done((f32[256,896]{1,0:T(8,128)}, f32[256,896]{1,0:T(8,128)}, u32[]{:S(2)}, u32[]{:S(2)}) %collective-permute-start.23) | collective-permute-done | bytes 917536 | tf_op jit(solution)/shard_map/ppermute | solution.py:278
  118.2 2.6 %shard_map.57 = (bf16[256,896]{1,0:T(8,128)(2,1)S(1)}, bf16[512,896]{1,0:T(8,128)(2,1)S(1)}) custom-call(s32[1]{0:T(128)} %bitcast.15.place_ref, f32[256,256]{1,0:T(8,128)S(1)} %shard_map.56.inverse_ref, f32[256,896]{1,0:T(8,128)S(1)} %shard_map.55.first_ref, f32[256,896]{1,0:T(8,128)} %collective-permute-done.22.second_ref, ...), custom_call_target="tpu_custom_call" | custom-call | flops 704643072 | bytes 3670016 | tf_op jit(solution)/shard_map/pallas_call | solution.py:178
  121.9 1.2 collective-permute-start.24
  124.6 6.7 %shard_map.58.refs_2_ = bf16[1024,7168]{1,0:T(8,128)(2,1)} custom-call(s32[2]{0:T(128)S(1)} %pad_add_fusion.7.place_ref, bf16[1024,256]{1,0:T(8,128)(2,1)S(1)} %select_select_fusion.error_ref, bf16[1024,7168]{1,0:T(8,128)(2,1)} %weights_ref.5, bf16[512,896]{1,0:T(8,128)(2,1)S(1)} %get-tuple-element.82.refs_0_, bf16[512,896]{1,0:T(8,128)(2,1)} %copy-done.13), custom_call_target="tpu_custom_call" | custom-call | flops 939524096 | bytes 7340032 | tf_op jit(solution)/shard_map/pallas_call | solution.py:260
  131.3 2.4 %collective-permute-done.25.refs_1_ = bf16[256,896]{1,0:T(8,128)(2,1)S(1)} collective-permute-done((bf16[256,896]{1,0:T(8,128)(2,1)S(1)}, bf16[256,896]{1,0:T(8,128)(2,1)S(1)}, u32[]{:S(2)}, u32[]{:S(2)}) %collective-permute-start.25) | collective-permute-done | bytes 458784 | tf_op jit(solution)/shard_map/ppermute | solution.py:278
  134.9 1.3 collective-permute-start.29
  136.1 1.2 collective-permute-start.30
  137.5 4.9 %shard_map.59.refs_6_ = bf16[1024,7168]{1,0:T(8,128)(2,1)} custom-call(s32[2]{0:T(128)S(1)} %pad_add_fusion.8.place_ref, bf16[1024,256]{1,0:T(8,128)(2,1)S(1)} %select_select_fusion.error_ref, bf16[1024,7168]{1,0:T(8,128)(2,1)} %weights_ref.5, bf16[256,896]{1,0:T(8,128)(2,1)S(1)} %collective-permute-done.24.refs_0_, ...), custom_call_target="tpu_custom_call", output_to_operand_aliasing={{}: (5, {})} | custom-call | flops 939524096 | bytes 7340032 | tf_op jit(solution)/shard_map/pallas_call | solution.py:260
  142.5 1.7 %collective-permute-start.31 = (bf16[128,896]{1,0:T(8,128)(2,1)S(1)}, bf16[128,896]{1,0:T(8,128)(2,1)S(1)}, u32[]{:S(2)}, u32[]{:S(2)}) collective-permute-start(bf16[128,896]{1,0:T(8,128)(2,1)S(1)} %collective-permute-done.29.refs_2_), channel_id=1, source_target_pairs={{0,8},{8,0},{16,24},{24,16},{1,9},{9,1},{17,25},{25,17},{2,10},{10... | collective-permute-start | bytes 688136 | tf_op jit(solution)/shard_map/ppermute | solution.py:278
  145.6 8.9 %shard_map.60 = bf16[1024,7168]{1,0:T(8,128)(2,1)} custom-call(s32[4]{0:T(128)S(1)} %pad_add_fusion.place_ref, bf16[1024,256]{1,0:T(8,128)(2,1)} %copy-done.3, bf16[1024,7168]{1,0:T(8,128)(2,1)} %weights_ref.5, bf16[256,896]{1,0:T(8,128)(2,1)S(1)} %collective-permute-done.27.refs_0_, ...), custom_call_target="tpu_custom_call", output_to_operand_aliasing={{}: (9, {})} | custom-call | flops 1879048192 | bytes 14680064 | tf_op jit(solution)/shard_map/pallas_call | solution.py:260
  (101 shorter events, 18.4 us)
Async XLA Ops:
  3.0 9.2 %collective-permute-start = (bf16[256,512]{1,0:T(8,128)(2,1)S(1)}, bf16[256,512]{1,0:T(8,128)(2,1)}, u32[]{:S(2)}, u32[]{:S(2)}) collective-permute-start(bf16[256,512]{1,0:T(8,128)(2,1)S(1)} %shard_map.46), channel_id=1, source_target_pairs={{0,2},{1,3},{8,10},{9,11},{16,18},{17,19},{24,26},{25,27}} | collective-permute-start | bytes 786440 | tf_op jit(solution)/shard_map/ppermute | solution.py:282
  5.6 12.2 %collective-permute-start.2 = (bf16[256,512]{1,0:T(8,128)(2,1)S(1)}, bf16[256,512]{1,0:T(8,128)(2,1)}, u32[]{:S(2)}, u32[]{:S(2)}) collective-permute-start(bf16[256,512]{1,0:T(8,128)(2,1)S(1)} %shard_map.48), channel_id=1, source_target_pairs={{0,2},{1,3},{8,10},{9,11},{16,18},{17,19},{24,26},{25,27}} | collective-permute-start | bytes 786440 | tf_op jit(solution)/shard_map/ppermute | solution.py:282
  8.2 16.9 %collective-permute-start.6 = (bf16[256,512]{1,0:T(8,128)(2,1)S(1)}, bf16[256,512]{1,0:T(8,128)(2,1)}, u32[]{:S(2)}, u32[]{:S(2)}) collective-permute-start(bf16[256,512]{1,0:T(8,128)(2,1)S(1)} %shard_map.49), channel_id=1, source_target_pairs={{0,2},{1,3},{8,10},{9,11},{16,18},{17,19},{24,26},{25,27}} | collective-permute-start | bytes 786440 | tf_op jit(solution)/shard_map/ppermute | solution.py:282
  10.7 18.3 %collective-permute-start.4 = (bf16[256,512]{1,0:T(8,128)(2,1)S(1)}, bf16[256,512]{1,0:T(8,128)(2,1)S(1)}, u32[]{:S(2)}, u32[]{:S(2)}) collective-permute-start(bf16[256,512]{1,0:T(8,128)(2,1)S(1)} %shard_map.47), channel_id=1, source_target_pairs={{0,2},{1,3},{8,10},{9,11},{16,18},{17,19},{24,26},{25,27}} | collective-permute-start | bytes 786440 | tf_op jit(solution)/shard_map/ppermute | solution.py:282
  12.2 12.0 %collective-permute-start.1 = (bf16[256,512]{1,0:T(8,128)(2,1)}, bf16[256,512]{1,0:T(8,128)(2,1)}, u32[]{:S(2)}, u32[]{:S(2)}) collective-permute-start(bf16[256,512]{1,0:T(8,128)(2,1)} %collective-permute-done), channel_id=1, source_target_pairs={{2,4},{3,5},{10,12},{11,13},{18,20},{19,21},{26,28},{27,29}} | collective-permute-start | bytes 786440 | tf_op jit(solution)/shard_map/ppermute | solution.py:282
  17.8 8.5 %collective-permute-start.5 = (bf16[256,512]{1,0:T(8,128)(2,1)}, bf16[256,512]{1,0:T(8,128)(2,1)}, u32[]{:S(2)}, u32[]{:S(2)}) collective-permute-start(bf16[256,512]{1,0:T(8,128)(2,1)} %collective-permute-done.2), channel_id=1, source_target_pairs={{2,4},{3,5},{10,12},{11,13},{18,20},{19,21},{26,28},{27,29}} | collective-permute-start | bytes 786440 | tf_op jit(solution)/shard_map/ppermute | solution.py:282
  24.0 6.6 %slice-start = ((bf16[1024,7168]{1,0:T(8,128)(2,1)}), bf16[1024,256]{1,0:T(8,128)(2,1)S(1)}, s32[]{:S(2)}) async-start(bf16[1024,7168]{1,0:T(8,128)(2,1)} %weights_ref.5), calls=%async_computation | async-start | bytes 1048576 | tf_op jit(solution)/shard_map/slice | solution.py:342
  24.1 6.6 %copy-start.12 = (s32[1024,256]{1,0:T(8,128)S(1)}, s32[1024,256]{1,0:T(8,128)}, u32[]{:S(2)}) copy-start(s32[1024,256]{1,0:T(8,128)} %param.7) | copy-start | bytes 3145732
  24.2 6.6 %collective-permute-start.3 = (bf16[256,512]{1,0:T(8,128)(2,1)}, bf16[256,512]{1,0:T(8,128)(2,1)S(1)}, u32[]{:S(2)}, u32[]{:S(2)}) collective-permute-start(bf16[256,512]{1,0:T(8,128)(2,1)} %collective-permute-done.1), channel_id=1, source_target_pairs={{4,6},{5,7},{12,14},{13,15},{20,22},{21,23},{28,30},{29,31}} | collective-permute-start | bytes 786440 | tf_op jit(solution)/shard_map/ppermute | solution.py:282
  25.1 5.8 %collective-permute-start.8 = (bf16[256,512]{1,0:T(8,128)(2,1)}, bf16[256,512]{1,0:T(8,128)(2,1)S(1)}, u32[]{:S(2)}, u32[]{:S(2)}) collective-permute-start(bf16[256,512]{1,0:T(8,128)(2,1)} %collective-permute-done.6), channel_id=1, source_target_pairs={{2,4},{3,5},{10,12},{11,13},{18,20},{19,21},{26,28},{27,29}} | collective-permute-start | bytes 786440 | tf_op jit(solution)/shard_map/ppermute | solution.py:282
  26.4 6.2 %collective-permute-start.7 = (bf16[256,512]{1,0:T(8,128)(2,1)}, bf16[256,512]{1,0:T(8,128)(2,1)S(1)}, u32[]{:S(2)}, u32[]{:S(2)}) collective-permute-start(bf16[256,512]{1,0:T(8,128)(2,1)} %collective-permute-done.5), channel_id=1, source_target_pairs={{4,6},{5,7},{12,14},{13,15},{20,22},{21,23},{28,30},{29,31}} | collective-permute-start | bytes 786440 | tf_op jit(solution)/shard_map/ppermute | solution.py:282
  29.0 7.8 %collective-permute-start.10 = (bf16[256,512]{1,0:T(8,128)(2,1)S(1)}, bf16[256,512]{1,0:T(8,128)(2,1)S(1)}, u32[]{:S(2)}, u32[]{:S(2)}) collective-permute-start(bf16[256,512]{1,0:T(8,128)(2,1)S(1)} %collective-permute-done.4), channel_id=1, source_target_pairs={{2,4},{3,5},{10,12},{11,13},{18,20},{19,21},{26,28},{27,29}} | collective-permute-start | bytes 786440 | tf_op jit(solution)/shard_map/ppermute | solution.py:282
  30.8 9.1 %copy-start.9 = (bf16[1024,256]{1,0:T(8,128)(2,1)}, bf16[1024,256]{1,0:T(8,128)(2,1)S(1)}, u32[]{:S(2)}) copy-start(bf16[1024,256]{1,0:T(8,128)(2,1)S(1)} %compare_select_fusion) | copy-start | bytes 1572868
  30.9 8.0 %collective-permute-start.9 = (bf16[256,512]{1,0:T(8,128)(2,1)S(1)}, bf16[256,512]{1,0:T(8,128)(2,1)S(1)}, u32[]{:S(2)}, u32[]{:S(2)}) collective-permute-start(bf16[256,512]{1,0:T(8,128)(2,1)S(1)} %collective-permute-done.8), channel_id=1, source_target_pairs={{4,6},{5,7},{12,14},{13,15},{20,22},{21,23},{28,30},{29,31}} | collective-permute-start | bytes 786440 | tf_op jit(solution)/shard_map/ppermute | solution.py:282
  32.6 6.2 %collective-permute-start.11 = (bf16[256,512]{1,0:T(8,128)(2,1)S(1)}, bf16[256,512]{1,0:T(8,128)(2,1)S(1)}, u32[]{:S(2)}, u32[]{:S(2)}) collective-permute-start(bf16[256,512]{1,0:T(8,128)(2,1)S(1)} %select_select_fusion.4), channel_id=1, source_target_pairs={{0,1},{1,0},{2,3},{3,2},{4,5},{5,4},{6,7},{7,6},{8,9},{9,8},{10,11... | collective-permute-start | bytes 786440 | tf_op jit(solution)/shard_map/ppermute | solution.py:278
  34.9 7.3 %collective-permute-start.13 = (bf16[256,512]{1,0:T(8,128)(2,1)S(1)}, bf16[256,512]{1,0:T(8,128)(2,1)S(1)}, u32[]{:S(2)}, u32[]{:S(2)}) collective-permute-start(bf16[256,512]{1,0:T(8,128)(2,1)S(1)} %select_select_fusion.3), channel_id=1, source_target_pairs={{0,1},{1,0},{2,3},{3,2},{4,5},{5,4},{6,7},{7,6},{8,9},{9,8},{10,11... | collective-permute-start | bytes 786440 | tf_op jit(solution)/shard_map/ppermute | solution.py:278
  36.8 4.4 %collective-permute-start.12 = (bf16[256,512]{1,0:T(8,128)(2,1)S(1)}, bf16[256,512]{1,0:T(8,128)(2,1)S(1)}, u32[]{:S(2)}, u32[]{:S(2)}) collective-permute-start(bf16[256,512]{1,0:T(8,128)(2,1)S(1)} %collective-permute-done.10), channel_id=1, source_target_pairs={{4,6},{5,7},{12,14},{13,15},{20,22},{21,23},{28,30},{29,31}} | collective-permute-start | bytes 786440 | tf_op jit(solution)/shard_map/ppermute | solution.py:282
  37.5 16.5 %collective-permute-start.16 = (bf16[1024,256]{1,0:T(8,128)(2,1)S(1)}, bf16[1024,256]{1,0:T(8,128)(2,1)S(1)}, u32[]{:S(2)}, u32[]{:S(2)}) collective-permute-start(bf16[1024,256]{1,0:T(8,128)(2,1)S(1)} %compare_select_fusion), channel_id=1, source_target_pairs={{0,2},{1,3},{8,10},{9,11},{16,18},{17,19},{24,26},{25,27}} | collective-permute-start | bytes 1572872 | tf_op jit(solution)/shard_map/ppermute | solution.py:282
  39.9 14.1 %collective-permute-start.14 = (bf16[256,512]{1,0:T(8,128)(2,1)S(1)}, bf16[256,512]{1,0:T(8,128)(2,1)S(1)}, u32[]{:S(2)}, u32[]{:S(2)}) collective-permute-start(bf16[256,512]{1,0:T(8,128)(2,1)S(1)} %select_select_fusion.2), channel_id=1, source_target_pairs={{0,1},{1,0},{2,3},{3,2},{4,5},{5,4},{6,7},{7,6},{8,9},{9,8},{10,11... | collective-permute-start | bytes 786440 | tf_op jit(solution)/shard_map/ppermute | solution.py:278
  42.3 11.7 %collective-permute-start.15 = (bf16[256,512]{1,0:T(8,128)(2,1)S(1)}, bf16[256,512]{1,0:T(8,128)(2,1)S(1)}, u32[]{:S(2)}, u32[]{:S(2)}) collective-permute-start(bf16[256,512]{1,0:T(8,128)(2,1)S(1)} %select_select_fusion.1), channel_id=1, source_target_pairs={{0,1},{1,0},{2,3},{3,2},{4,5},{5,4},{6,7},{7,6},{8,9},{9,8},{10,11... | collective-permute-start | bytes 786440 | tf_op jit(solution)/shard_map/ppermute | solution.py:278
  52.9 0.9 copy-start.6
  54.1 10.6 %copy-start = (bf16[256,2048]{1,0:T(8,128)(2,1)}, bf16[256,2048]{1,0:T(8,128)(2,1)S(1)}, u32[]{:S(2)}) copy-start(bf16[256,2048]{1,0:T(8,128)(2,1)S(1)} %get-tuple-element.94.refs_5_) | copy-start | bytes 3145732
  54.1 10.7 %copy-start.7 = (bf16[256,1024]{1,0:T(8,128)(2,1)}, bf16[256,1024]{1,0:T(8,128)(2,1)S(1)}, u32[]{:S(2)}) copy-start(bf16[256,1024]{1,0:T(8,128)(2,1)S(1)} %get-tuple-element.93.refs_5_) | copy-start | bytes 1572868
  54.8 9.9 %collective-permute-start.17 = (f32[256,256]{1,0:T(8,128)S(1)}, f32[256,256]{1,0:T(8,128)S(1)}, u32[]{:S(2)}, u32[]{:S(2)}) collective-permute-start(f32[256,256]{1,0:T(8,128)S(1)} %convolution_add_fusion), channel_id=1, source_target_pairs={{0,8},{8,0},{16,24},{24,16},{1,9},{9,1},{17,25},{25,17},{2,10},{10... | collective-permute-start | bytes 786440 | tf_op jit(solution)/shard_map/ppermute | solution.py:278
  63.6 6.7 %copy-start.4 = (bf16[256,1024]{1,0:T(8,128)(2,1)}, bf16[256,1024]{1,0:T(8,128)(2,1)S(1)}, u32[]{:S(2)}) copy-start(bf16[256,1024]{1,0:T(8,128)(2,1)S(1)} %pad_maximum_fusion.2.refs_2_) | copy-start | bytes 1572868
  64.8 5.9 %copy-start.11 = (f32[256,256]{1,0:T(8,128)}, f32[256,256]{1,0:T(8,128)S(1)}, u32[]{:S(2)}) copy-start(f32[256,256]{1,0:T(8,128)S(1)} %add.63) | copy-start | bytes 786436
  70.3 9.3 %collective-permute-start.18 = (f32[256,896]{1,0:T(8,128)}, f32[256,896]{1,0:T(8,128)}, u32[]{:S(2)}, u32[]{:S(2)}) collective-permute-start(f32[256,896]{1,0:T(8,128)} %shard_map.52), channel_id=1, source_target_pairs={{0,8},{8,0},{16,24},{24,16},{1,9},{9,1},{17,25},{25,17},{2,10},{10... | collective-permute-start | bytes 2752520 | tf_op jit(solution)/shard_map/ppermute | solution.py:278
  70.7 7.9 %collective-permute-start.19 = (f32[256,256]{1,0:T(8,128)S(1)}, f32[256,256]{1,0:T(8,128)}, u32[]{:S(2)}, u32[]{:S(2)}) collective-permute-start(f32[256,256]{1,0:T(8,128)S(1)} %add.63), channel_id=1, source_target_pairs={{0,16},{8,24},{16,0},{24,8},{1,17},{9,25},{17,1},{25,9},{2,18},{10... | collective-permute-start | bytes 786440 | tf_op jit(solution)/shard_map/ppermute | solution.py:278
  71.9 9.4 %copy-start.5 = (bf16[256,1024]{1,0:T(8,128)(2,1)S(1)}, bf16[256,1024]{1,0:T(8,128)(2,1)}, u32[]{:S(2)}) copy-start(bf16[256,1024]{1,0:T(8,128)(2,1)} %copy-done.4) | copy-start | bytes 1572868
  71.9 9.4 %copy-start.8 = (bf16[256,1024]{1,0:T(8,128)(2,1)S(1)}, bf16[256,1024]{1,0:T(8,128)(2,1)}, u32[]{:S(2)}) copy-start(bf16[256,1024]{1,0:T(8,128)(2,1)} %copy-done.7) | copy-start | bytes 1572868
  71.9 25.2 %collective-permute-start.20 = (bf16[1024,256]{1,0:T(8,128)(2,1)}, bf16[1024,256]{1,0:T(8,128)(2,1)}, u32[]{:S(2)}, u32[]{:S(2)}) collective-permute-start(bf16[1024,256]{1,0:T(8,128)(2,1)} %copy-done.14), channel_id=1, source_target_pairs={{2,4},{3,5},{10,12},{11,13},{18,20},{19,21},{26,28},{27,29}} | collective-permute-start | bytes 1572872 | tf_op jit(solution)/shard_map/ppermute | solution.py:282
  81.3 5.5 %copy-start.1 = (bf16[256,2048]{1,0:T(8,128)(2,1)S(1)}, bf16[256,2048]{1,0:T(8,128)(2,1)}, u32[]{:S(2)}) copy-start(bf16[256,2048]{1,0:T(8,128)(2,1)} %copy-done) | copy-start | bytes 3145732
  95.0 19.9 %collective-permute-start.22 = (f32[256,896]{1,0:T(8,128)}, f32[256,896]{1,0:T(8,128)}, u32[]{:S(2)}, u32[]{:S(2)}) collective-permute-start(f32[256,896]{1,0:T(8,128)} %shard_map.54), channel_id=1, source_target_pairs={{0,8},{8,0},{16,24},{24,16},{1,9},{9,1},{17,25},{25,17},{2,10},{10... | collective-permute-start | bytes 2752520 | tf_op jit(solution)/shard_map/ppermute | solution.py:278
  95.9 22.3 %collective-permute-start.23 = (f32[256,896]{1,0:T(8,128)}, f32[256,896]{1,0:T(8,128)}, u32[]{:S(2)}, u32[]{:S(2)}) collective-permute-start(f32[256,896]{1,0:T(8,128)} %shard_map.53), channel_id=1, source_target_pairs={{0,16},{8,24},{16,0},{24,8},{1,17},{9,25},{17,1},{25,9},{2,18},{10... | collective-permute-start | bytes 2752520 | tf_op jit(solution)/shard_map/ppermute | solution.py:278
  97.1 17.7 %collective-permute-start.21 = (bf16[1024,256]{1,0:T(8,128)(2,1)}, bf16[1024,256]{1,0:T(8,128)(2,1)}, u32[]{:S(2)}, u32[]{:S(2)}) collective-permute-start(bf16[1024,256]{1,0:T(8,128)(2,1)} %collective-permute-done.20), channel_id=1, source_target_pairs={{4,6},{5,7},{12,14},{13,15},{20,22},{21,23},{28,30},{29,31}} | collective-permute-start | bytes 1572872 | tf_op jit(solution)/shard_map/ppermute | solution.py:282
  98.7 1.2 copy-start.2
  107.2 16.0 %copy-start.10 = (bf16[1024,256]{1,0:T(8,128)(2,1)S(1)}, bf16[1024,256]{1,0:T(8,128)(2,1)}, u32[]{:S(2)}) copy-start(bf16[1024,256]{1,0:T(8,128)(2,1)} %copy-done.9) | copy-start | bytes 1572868
  107.2 16.0 %copy-start.15 = (bf16[1024,256]{1,0:T(8,128)(2,1)S(1)}, bf16[1024,256]{1,0:T(8,128)(2,1)}, u32[]{:S(2)}) copy-start(bf16[1024,256]{1,0:T(8,128)(2,1)} %copy-done.14) | copy-start | bytes 1572868
  120.8 2.9 %collective-permute-start.26 = (bf16[512,896]{1,0:T(8,128)(2,1)S(1)}, bf16[512,896]{1,0:T(8,128)(2,1)S(1)}, u32[]{:S(2)}, u32[]{:S(2)}) collective-permute-start(bf16[512,896]{1,0:T(8,128)(2,1)S(1)} %get-tuple-element.82.refs_0_), channel_id=1, source_target_pairs={{0,8},{8,0},{16,24},{24,16},{1,9},{9,1},{17,25},{25,17},{2,10},{10... | collective-permute-start | bytes 2752520 | tf_op jit(solution)/shard_map/ppermute | solution.py:278
  121.6 12.1 %collective-permute-start.25 = (bf16[256,896]{1,0:T(8,128)(2,1)S(1)}, bf16[256,896]{1,0:T(8,128)(2,1)S(1)}, u32[]{:S(2)}, u32[]{:S(2)}) collective-permute-start(bf16[256,896]{1,0:T(8,128)(2,1)S(1)} %get-tuple-element.81), channel_id=1, source_target_pairs={{0,1},{1,0},{2,3},{3,2},{4,5},{5,4},{6,7},{7,6},{8,9},{9,8},{10,11... | collective-permute-start | bytes 1376264 | tf_op jit(solution)/shard_map/ppermute | solution.py:278
  121.9 11.8 %collective-permute-start.24 = (bf16[256,896]{1,0:T(8,128)(2,1)S(1)}, bf16[256,896]{1,0:T(8,128)(2,1)S(1)}, u32[]{:S(2)}, u32[]{:S(2)}) collective-permute-start(bf16[256,896]{1,0:T(8,128)(2,1)S(1)} %get-tuple-element.81), channel_id=1, source_target_pairs={{0,16},{8,24},{16,0},{24,8},{1,17},{9,25},{17,1},{25,9},{2,18},{10... | collective-permute-start | bytes 1376264 | tf_op jit(solution)/shard_map/ppermute | solution.py:278
  123.3 14.2 %copy-start.3 = (bf16[1024,256]{1,0:T(8,128)(2,1)}, bf16[1024,256]{1,0:T(8,128)(2,1)S(1)}, u32[]{:S(2)}) copy-start(bf16[1024,256]{1,0:T(8,128)(2,1)S(1)} %select_select_fusion.error_ref) | copy-start | bytes 1572868
  133.7 3.7 %collective-permute-start.27 = (bf16[256,896]{1,0:T(8,128)(2,1)S(1)}, bf16[256,896]{1,0:T(8,128)(2,1)S(1)}, u32[]{:S(2)}, u32[]{:S(2)}) collective-permute-start(bf16[256,896]{1,0:T(8,128)(2,1)S(1)} %collective-permute-done.24.refs_0_), channel_id=1, source_target_pairs={{0,8},{8,0},{16,24},{24,16},{1,9},{9,1},{17,25},{25,17},{2,10},{10... | collective-permute-start | bytes 1376264 | tf_op jit(solution)/shard_map/ppermute | solution.py:278
  134.8 2.6 %collective-permute-start.28 = (bf16[256,896]{1,0:T(8,128)(2,1)S(1)}, bf16[256,896]{1,0:T(8,128)(2,1)S(1)}, u32[]{:S(2)}, u32[]{:S(2)}) collective-permute-start(bf16[256,896]{1,0:T(8,128)(2,1)S(1)} %collective-permute-done.25.refs_1_), channel_id=1, source_target_pairs={{0,8},{8,0},{16,24},{24,16},{1,9},{9,1},{17,25},{25,17},{2,10},{10... | collective-permute-start | bytes 1376264 | tf_op jit(solution)/shard_map/ppermute | solution.py:278
  134.9 7.5 %collective-permute-start.29 = (bf16[128,896]{1,0:T(8,128)(2,1)S(1)}, bf16[128,896]{1,0:T(8,128)(2,1)S(1)}, u32[]{:S(2)}, u32[]{:S(2)}) collective-permute-start(bf16[128,896]{1,0:T(8,128)(2,1)S(1)} %slice.10), channel_id=1, source_target_pairs={{0,16},{8,24},{16,0},{24,8},{1,17},{9,25},{17,1},{25,9},{2,18},{10... | collective-permute-start | bytes 688136 | tf_op jit(solution)/shard_map/ppermute | solution.py:278
  136.1 6.3 %collective-permute-start.30 = (bf16[128,896]{1,0:T(8,128)(2,1)S(1)}, bf16[128,896]{1,0:T(8,128)(2,1)S(1)}, u32[]{:S(2)}, u32[]{:S(2)}) collective-permute-start(bf16[128,896]{1,0:T(8,128)(2,1)S(1)} %slice.11), channel_id=1, source_target_pairs={{0,1},{1,0},{2,3},{3,2},{4,5},{5,4},{6,7},{7,6},{8,9},{9,8},{10,11... | collective-permute-start | bytes 688136 | tf_op jit(solution)/shard_map/ppermute | solution.py:278
  142.5 2.8 %collective-permute-start.31 = (bf16[128,896]{1,0:T(8,128)(2,1)S(1)}, bf16[128,896]{1,0:T(8,128)(2,1)S(1)}, u32[]{:S(2)}, u32[]{:S(2)}) collective-permute-start(bf16[128,896]{1,0:T(8,128)(2,1)S(1)} %collective-permute-done.29.refs_2_), channel_id=1, source_target_pairs={{0,8},{8,0},{16,24},{24,16},{1,9},{9,1},{17,25},{25,17},{2,10},{10... | collective-permute-start | bytes 688136 | tf_op jit(solution)/shard_map/ppermute | solution.py:278
  144.2 1.5 collective-permute-start.32
  (2 other events, 1.7 us)

commit v9 on v8

--- a/solution.py
+++ b/solution.py
@@ -57,7 +57,7 @@
 
     @pl.when(pl.program_id(0) == 0)
     def _():
-        out_ref[...] = refs[6][...] if len(refs) > 8 else jnp.zeros_like(out_ref)
+        out_ref[...] = sum((ref[...] for ref in refs[6:-2]), jnp.zeros_like(out_ref))
 
     for side in range(2):
         quant_ref, scale_ref, _ = refs[3 * side : 3 * side + 3]
@@ -71,10 +71,10 @@
     out_ref[...] += jnp.dot(panel, acts_ref[...], preferred_element_type=F32)
 
 
-def gram_block(quantized, scale_pad, own, other, row, col, width, first, extra=None):
+def gram_block(quantized, scale_pad, own, other, row, col, width, first, *extras):
     tokens, cols = quantized.shape
     if width % QBLOCK or cols // QBLOCK > QBLOCK:
-        total = 0.0 if extra is None else extra
+        total = sum(extras)
         for side, panel in enumerate((own, other)):
             at = (row + side) % 2 * (tokens // 2) + first * (tokens // 2 // ROUNDS)
             size = (panel.shape[1], width)
@@ -97,9 +97,8 @@
             pl.BlockSpec((PANEL, step), lambda k, place: (0, k)),
         ]
         args += [quantized, scale_pad, panel]
-    if extra is not None:
-        specs.append(pl.BlockSpec((PANEL, width), lambda k, place: (0, 0)))
-        args.append(extra)
+    specs += [pl.BlockSpec((PANEL, width), lambda k, place: (0, 0))] * len(extras)
+    args += extras
     return pl.pallas_call(
         functools.partial(gram_kernel, width // QBLOCK),
         out_shape=jax.ShapeDtypeStruct((PANEL, width), F32),
@@ -315,20 +314,20 @@
     early = ROUNDS // 2
     full, swapped, token, errors, begun, scale_pad = [], [], got[-1][0], None, {}, None
 
-    def gram(k, first, last, link, extra=None):
+    def gram(k, first, last, link, *extras):
         own = jnp.concatenate(full[first:last], axis=1)
         other = jnp.concatenate(swapped[first:last], axis=1)
         col = row * toks + (tok ^ k)
         if link is not None:
             col = after(col, link)
-        return gram_block(quantized, scale_pad, own, other, row, col, width, first, extra)
+        return gram_block(quantized, scale_pad, own, other, row, col, width, first, *extras)
 
     for _, c, h in events:
         x = got[c][h + 1]
         if token is not None:
             x = after(x, token)
-        if h + 1 == hops and c > 1:
-            x = after(x, swapped[c - 2])
+        if h + 1 == hops and c > 0:
+            x = after(x, swapped[max(c - 2, 0)])
         got[c][h + 1] = token = x
         if h + 1 < hops:
             got[c].append(hop(x, "feat", h + 1))
@@ -359,15 +358,15 @@
     errors[1] = after(errors[1], block3)
     errors.append(hop(errors[1], "feat", 1))
     head = head + swap(head, "tok", 2)
-    block2 = gram(2, early, ROUNDS, from3, begun[2] + from3)
+    block1 = gram(1, 0, ROUNDS, block3)
+    from1 = swap(block1, "tok", 1)
+    block2 = gram(2, early, ROUNDS, block1, begun[2], from3)
     block2, head = lax.optimization_barrier((block2, head))
     fromx = swap(block2, "tok", 2)
-    block1 = gram(1, 0, ROUNDS, block2)
-    from1 = swap(block1, "tok", 1)
-    errors[2] = after(errors[2], block1)
+    errors[2] = after(errors[2], block2)
     for h in range(2, hops):
         errors.append(hop(errors[h], "feat", h))
-    block0 = gram(0, 0, ROUNDS, block1)
+    block0 = gram(0, 0, ROUNDS, block2)
     inverse = invert(after(head, block0))
     inverse, last = lax.optimization_barrier((inverse, errors[-1]))
     error = settle(errors[:-1] + [last])
@@ -387,11 +386,11 @@
     top, bottom, out = lax.optimization_barrier((in_y[:half], in_x[half:], out))
     far = [swap(top, "tok", 2), swap(bottom, "row", 1)]
     near_x, near_y = swap(in_x, "tok", 1), swap(in_y, "tok", 1)
-    out = update(after(out, near_x, near_y), [((in_x,), 2, 0), ((in_y,), 0, 1)])
+    middle = [((in_x,), 2, 0), ((in_y,), 0, 1), ((near_x,), 3, 0), ((near_y,), 1, 1)]
+    out = update(out, middle)
     far[0], far[1], out = lax.optimization_barrier((far[0], far[1], out))
     near_far = tuple(swap(x, "tok", 1) for x in far)
-    last = [((near_x,), 3, 0), ((near_y,), 1, 1), (tuple(far), 2, 1), (near_far, 3, 1)]
-    return update(out, last)
+    return update(out, [(tuple(far), 2, 1), (near_far, 3, 1)])
 
 
 def solution(mesh):

time: 157 us -> 157 us (level)
  waiting for transfers between devices: 18.1 us -> 23 us
  starting transfers between devices: 47.9 us -> 44 us
  other arithmetic: 9.38 us -> 7.78 us
    ppermute x18, waiting for transfers between devices: 12 us -> 17.9 us  [swap(): return lax.ppermute(x, axis, [(i, i ^ bit) for i in range(size)])]
    ppermute x18, starting transfers between devices: 24.3 us -> 21.3 us  [swap(): return lax.ppermute(x, axis, [(i, i ^ bit) for i in range(size)])]
    unnamed x35 -> x41, local copies, waits for them, and re-layouts: 4.57 us -> 5.58 us
  transfers between devices with their start and end apart: 33 -> 33, of which waited for: 14 -> 12; matrix products, arithmetic and copies ran while one was open for 8% -> 7% of each run, Pallas kernels for 34% -> 36%
where the time goes in v9:
time: 157 us; the launch traced here: 156 us
  Pallas kernels  71.5 us (46%)
  starting transfers between devices  44 us (28%)
  waiting for transfers between devices  23 us (15%)
  other arithmetic  7.78 us (5%)
  local copies, waits for them, and re-layouts  7.65 us (5%)
    pallas_call x6, Pallas kernels, gram_block(): pl.pallas_call(functools.partial(gram_kernel, width // QBLOCK), out_shape...  35.8 us
    ppermute x15, starting transfers between devices, hop(): return lax.ppermute(x, axis, [(start, start + 1)])  22.8 us
    ppermute x18, starting transfers between devices, swap(): return lax.ppermute(x, axis, [(i, i ^ bit) for i in range(size)])  21.3 us
    pallas_call x3, Pallas kernels, update_blocks(): pl.pallas_call(functools.partial(update_kernel, [[p.shape for p in pieces...  20.5 us
    ppermute x18, waiting for transfers between devices, swap(): return lax.ppermute(x, axis, [(i, i ^ bit) for i in range(size)])  17.9 us
    pallas_call x1, Pallas kernels, invert(): pl.pallas_call(inverse_kernel, out_shape=jax.ShapeDtypeStruct((PANEL, PAN...  7.65 us
    unnamed x41, local copies, waits for them, and re-layouts  5.58 us
    ppermute x15, waiting for transfers between devices, hop(): return lax.ppermute(x, axis, [(start, start + 1)])  5.09 us
  transfers between devices with their start and end apart: 33, of which 12 were waited for; matrix products, arithmetic and copies ran while one was open for 7% of the time, Pallas kernels for 36%

profile of v9, /device:TPU:9, one launch (start us, length us, event | category | flops | bytes accessed | tf_op | source)
XLA Modules:
  0.0 155.7 jit_solution(223667899128246026)
XLA Ops:
  0.0 1.8 %copy.12.exps_ref = s32[4096,56]{1,0:T(8,128)S(1)} copy(s32[4096,56]{0,1:T(8,128)} %param.5) | data formatting | bytes 1835008 | tf_op args[1]
  1.8 1.2 shard_map.46
  3.0 1.3 collective-permute-start
  4.3 1.2 shard_map.48
  5.6 1.3 collective-permute-start.2
  6.9 1.2 shard_map.47
  8.2 4.1 %collective-permute-done = bf16[256,512]{1,0:T(8,128)(2,1)} collective-permute-done((bf16[256,512]{1,0:T(8,128)(2,1)S(1)}, bf16[256,512]{1,0:T(8,128)(2,1)}, u32[]{:S(2)}, u32[]{:S(2)}) %collective-permute-start) | collective-permute-done | bytes 262176 | tf_op jit(solution)/shard_map/ppermute | solution.py:281
  12.2 2.0 %collective-permute-start.1 = (bf16[256,512]{1,0:T(8,128)(2,1)}, bf16[256,512]{1,0:T(8,128)(2,1)}, u32[]{:S(2)}, u32[]{:S(2)}) collective-permute-start(bf16[256,512]{1,0:T(8,128)(2,1)} %collective-permute-done), channel_id=1, source_target_pairs={{2,4},{3,5},{10,12},{11,13},{18,20},{19,21},{26,28},{27,29}} | collective-permute-start | bytes 786440 | tf_op jit(solution)/shard_map/ppermute | solution.py:281
  14.2 1.2 shard_map.49
  15.5 1.3 collective-permute-start.6
  16.8 1.3 collective-permute-start.4
  18.1 2.0 %collective-permute-start.5 = (bf16[256,512]{1,0:T(8,128)(2,1)}, bf16[256,512]{1,0:T(8,128)(2,1)}, u32[]{:S(2)}, u32[]{:S(2)}) collective-permute-start(bf16[256,512]{1,0:T(8,128)(2,1)} %collective-permute-done.2), channel_id=1, source_target_pairs={{2,4},{3,5},{10,12},{11,13},{18,20},{19,21},{26,28},{27,29}} | collective-permute-start | bytes 786440 | tf_op jit(solution)/shard_map/ppermute | solution.py:281
  20.1 2.2 %convert_element_type.5 = f32[4096,56]{0,1:T(8,128)} convert(s32[4096,56]{0,1:T(8,128)} %param.5) | non-fusion elementwise | flops 229376 | bytes 1835008 | tf_op jit(solution)/shard_map/convert_element_type | solution.py:338
  22.3 1.8 %copy.16 = f32[4096,56]{1,0:T(8,128)S(1)} copy(f32[4096,56]{0,1:T(8,128)} %convert_element_type.5) | data formatting | bytes 1835008 | tf_op jit(solution)/shard_map/convert_element_type | solution.py:338
  24.8 1.3 collective-permute-start.8
  28.2 1.3 collective-permute-start.11
  30.3 1.0 select_select_fusion.4
  31.4 1.3 collective-permute-start.9
  32.9 3.8 %collective-permute-done.9 = bf16[256,512]{1,0:T(8,128)(2,1)S(1)} collective-permute-done((bf16[256,512]{1,0:T(8,128)(2,1)S(1)}, bf16[256,512]{1,0:T(8,128)(2,1)S(1)}, u32[]{:S(2)}, u32[]{:S(2)}) %collective-permute-start.9) | collective-permute-done | bytes 262176 | tf_op jit(solution)/shard_map/ppermute | solution.py:277
  36.7 1.0 select_select_fusion.3
  37.7 1.3 collective-permute-start.13
  39.7 1.0 select_select_fusion.2
  41.0 1.3 collective-permute-start.16
  42.5 3.2 %collective-permute-done.13 = bf16[256,512]{1,0:T(8,128)(2,1)S(1)} collective-permute-done((bf16[256,512]{1,0:T(8,128)(2,1)S(1)}, bf16[256,512]{1,0:T(8,128)(2,1)S(1)}, u32[]{:S(2)}, u32[]{:S(2)}) %collective-permute-start.13) | collective-permute-done | bytes 262176 | tf_op jit(solution)/shard_map/ppermute | solution.py:277
  45.7 1.3 collective-permute-start.15
  47.2 4.5 %shard_map.50.refs_6_ = f32[256,896]{1,0:T(8,128)S(1)} custom-call(s32[2]{0:T(128)S(1)} %pad_add_fusion.1.place_ref, bf16[4096,7168]{1,0:T(8,128)(2,1)} %refs_3_.11, f32[4096,128]{1,0:T(8,128)S(1)} %pad.4.refs_1_.refs_4_, bf16[256,1024]{1,0:T(8,128)(2,1)S(1)} %pad_maximum_fusion.1.refs_2_, bf16[4096,7168]{1,0:T(8,128)(2,1)} %refs_3_.11, ...), custom_call_target="tpu_custom_call" | custom-call | flops 58720256 | bytes 917504 | tf_op jit(solution)/shard_map/pallas_call | solution.py:102
  51.8 4.5 %shard_map.51.refs_6_ = f32[256,896]{1,0:T(8,128)S(1)} custom-call(s32[2]{0:T(128)S(1)} %pad_add_fusion.2.place_ref, bf16[4096,7168]{1,0:T(8,128)(2,1)} %refs_3_.11, f32[4096,128]{1,0:T(8,128)S(1)} %pad.4.refs_1_.refs_4_, bf16[256,1024]{1,0:T(8,128)(2,1)S(1)} %pad_maximum_fusion.1.refs_2_, bf16[4096,7168]{1,0:T(8,128)(2,1)} %refs_3_.11, ...), custom_call_target="tpu_custom_call" | custom-call | flops 58720256 | bytes 917504 | tf_op jit(solution)/shard_map/pallas_call | solution.py:102
  57.9 9.6 %collective-permute-start.17 = (f32[256,256]{1,0:T(8,128)S(1)}, f32[256,256]{1,0:T(8,128)S(1)}, u32[]{:S(2)}, u32[]{:S(2)}) collective-permute-start(f32[256,256]{1,0:T(8,128)S(1)} %convolution_add_fusion), channel_id=1, source_target_pairs={{0,8},{8,0},{16,24},{24,16},{1,9},{9,1},{17,25},{25,17},{2,10},{10... | collective-permute-start | bytes 786440 | tf_op jit(solution)/shard_map/ppermute | solution.py:277
  67.6 1.1 collective-permute-done.17
  68.8 5.4 %shard_map.52 = f32[256,896]{1,0:T(8,128)} custom-call(s32[2]{0:T(128)S(1)} %pad_add_fusion.3.place_ref, bf16[4096,7168]{1,0:T(8,128)(2,1)} %refs_3_.11, f32[4096,128]{1,0:T(8,128)S(1)} %pad.4.refs_1_.refs_4_, bf16[256,1024]{1,0:T(8,128)(2,1)S(1)} %pad_maximum_fusion.2.refs_2_, bf16[4096,7168]{1,0:T(8,128)(2,1)} %refs_3_.11, ...), custom_call_target="tpu_custom_call" | custom-call | flops 58720256 | bytes 917504 | tf_op jit(solution)/shard_map/pallas_call | solution.py:102
  74.6 1.2 collective-permute-start.19
  75.8 5.4 %collective-permute-start.20 = (bf16[1024,256]{1,0:T(8,128)(2,1)}, bf16[1024,256]{1,0:T(8,128)(2,1)}, u32[]{:S(2)}, u32[]{:S(2)}) collective-permute-start(bf16[1024,256]{1,0:T(8,128)(2,1)} %copy-done.17), channel_id=1, source_target_pairs={{2,4},{3,5},{10,12},{11,13},{18,20},{19,21},{26,28},{27,29}} | collective-permute-start | bytes 1572872 | tf_op jit(solution)/shard_map/ppermute | solution.py:281
  81.3 1.2 copy-done.1
  82.5 8.2 %shard_map.53 = f32[256,896]{1,0:T(8,128)} custom-call(s32[2]{0:T(128)S(1)} %pad_add_fusion.4.place_ref, bf16[4096,7168]{1,0:T(8,128)(2,1)} %refs_3_.11, f32[4096,128]{1,0:T(8,128)S(1)} %pad.4.refs_1_.refs_4_, bf16[256,2048]{1,0:T(8,128)(2,1)S(1)} %pad_maximum_fusion.refs_2_, bf16[4096,7168]{1,0:T(8,128)(2,1)} %refs_3_.11, ...), custom_call_target="tpu_custom_call" | custom-call | flops 58720256 | bytes 917504 | tf_op jit(solution)/shard_map/pallas_call | solution.py:102
  92.6 5.7 %shard_map.54 = f32[256,896]{1,0:T(8,128)} custom-call(s32[2]{0:T(128)S(1)} %pad_add_fusion.5.place_ref, bf16[4096,7168]{1,0:T(8,128)(2,1)} %refs_3_.11, f32[4096,128]{1,0:T(8,128)S(1)} %pad.4.refs_1_.refs_4_, bf16[256,1024]{1,0:T(8,128)(2,1)S(1)} %copy-done.6, bf16[4096,7168]{1,0:T(8,128)(2,1)} %refs_3_.11, f32[4096,128]{1,0:T(8,128)S(1)} %pad.4.refs_1_.refs_4_, ...), custom_call_target="tpu_custom_call" | custom-call | flops 58720256 | bytes 917504 | tf_op jit(solution)/shard_map/pallas_call | solution.py:102
  98.6 1.5 collective-permute-start.21
  100.1 1.2 copy-done.2
  101.4 7.3 %shard_map.55.first_ref = f32[256,896]{1,0:T(8,128)S(1)} custom-call(s32[2]{0:T(128)S(1)} %pad_add_fusion.6.place_ref, bf16[4096,7168]{1,0:T(8,128)(2,1)} %refs_3_.11, f32[4096,128]{1,0:T(8,128)S(1)} %pad.4.refs_1_.refs_4_, bf16[256,2048]{1,0:T(8,128)(2,1)S(1)} %pad_maximum_fusion.refs_2_, bf16[4096,7168]{1,0:T(8,128)(2,1)} %refs_3_.11, ...), custom_call_target="tpu_custom_call" | custom-call | flops 58720256 | bytes 917504 | tf_op jit(solution)/shard_map/pallas_call | solution.py:102
  108.7 7.6 %shard_map.56.inverse_ref = f32[256,256]{1,0:T(8,128)S(1)} custom-call(f32[256,256]{1,0:T(8,128)S(1)} %add.61.head_ref), custom_call_target="tpu_custom_call" | custom-call | flops 33554432 | bytes 524288 | tf_op jit(solution)/shard_map/pallas_call | solution.py:151
  116.4 4.3 %collective-permute-done.23.third_ref = f32[256,896]{1,0:T(8,128)} collective-permute-done((f32[256,896]{1,0:T(8,128)}, f32[256,896]{1,0:T(8,128)}, u32[]{:S(2)}, u32[]{:S(2)}) %collective-permute-start.23) | collective-permute-done | bytes 917536 | tf_op jit(solution)/shard_map/ppermute | solution.py:277
  120.6 2.6 %shard_map.57 = (bf16[256,896]{1,0:T(8,128)(2,1)S(1)}, bf16[512,896]{1,0:T(8,128)(2,1)S(1)}) custom-call(s32[1]{0:T(128)} %bitcast.13.place_ref, f32[256,256]{1,0:T(8,128)S(1)} %shard_map.56.inverse_ref, f32[256,896]{1,0:T(8,128)S(1)} %shard_map.55.first_ref, f32[256,896]{1,0:T(8,128)} %collective-permute-done.22.second_ref, ...), custom_call_target="tpu_custom_call" | custom-call | flops 704643072 | bytes 3670016 | tf_op jit(solution)/shard_map/pallas_call | solution.py:177
  124.8 1.4 collective-permute-done.26.refs_1_
  127.2 6.7 %shard_map.58.refs_4_ = bf16[1024,7168]{1,0:T(8,128)(2,1)} custom-call(s32[2]{0:T(128)S(1)} %pad_add_fusion.7.place_ref, bf16[1024,256]{1,0:T(8,128)(2,1)S(1)} %select_select_fusion.error_ref, bf16[1024,7168]{1,0:T(8,128)(2,1)} %weights_ref.5, bf16[512,896]{1,0:T(8,128)(2,1)S(1)} %get-tuple-element.83.refs_0_, bf16[512,896]{1,0:T(8,128)(2,1)} %copy-done.16), custom_call_target="tpu_custom_call" | custom-call | flops 939524096 | bytes 7340032 | tf_op jit(solution)/shard_map/pallas_call | solution.py:259
  133.9 2.3 %collective-permute-done.25.refs_1_ = bf16[256,896]{1,0:T(8,128)(2,1)S(1)} collective-permute-done((bf16[256,896]{1,0:T(8,128)(2,1)S(1)}, bf16[256,896]{1,0:T(8,128)(2,1)S(1)}, u32[]{:S(2)}, u32[]{:S(2)}) %collective-permute-start.25) | collective-permute-done | bytes 458784 | tf_op jit(solution)/shard_map/ppermute | solution.py:277
  136.2 1.1 collective-permute-start.30
  137.6 1.2 collective-permute-start.28
  139.4 8.0 %shard_map.59.refs_4_ = bf16[1024,7168]{1,0:T(8,128)(2,1)} custom-call(s32[4]{0:T(128)S(1)} %pad_add_fusion.8.place_ref, bf16[1024,256]{1,0:T(8,128)(2,1)} %copy-done.3, bf16[1024,7168]{1,0:T(8,128)(2,1)} %weights_ref.5, bf16[256,896]{1,0:T(8,128)(2,1)S(1)} %collective-permute-done.24.refs_0_, ...), custom_call_target="tpu_custom_call", output_to_operand_aliasing={{}: (7, {})} | custom-call | flops 1879048192 | bytes 14680064 | tf_op jit(solution)/shard_map/pallas_call | solution.py:259
  149.7 5.8 %shard_map.60 = bf16[1024,7168]{1,0:T(8,128)(2,1)} custom-call(s32[2]{0:T(128)S(1)} %pad_add_fusion.place_ref, bf16[1024,256]{1,0:T(8,128)(2,1)S(1)} %copy-done.4, bf16[1024,7168]{1,0:T(8,128)(2,1)} %weights_ref.5, bf16[128,896]{1,0:T(8,128)(2,1)S(1)} %collective-permute-done.27.refs_0_, ...), custom_call_target="tpu_custom_call", output_to_operand_aliasing={{}: (7, {})} | custom-call | flops 939524096 | bytes 7340032 | tf_op jit(solution)/shard_map/pallas_call | solution.py:259
  (106 shorter events, 14.9 us)
Async XLA Ops:
  3.0 9.2 %collective-permute-start = (bf16[256,512]{1,0:T(8,128)(2,1)S(1)}, bf16[256,512]{1,0:T(8,128)(2,1)}, u32[]{:S(2)}, u32[]{:S(2)}) collective-permute-start(bf16[256,512]{1,0:T(8,128)(2,1)S(1)} %shard_map.46), channel_id=1, source_target_pairs={{0,2},{1,3},{8,10},{9,11},{16,18},{17,19},{24,26},{25,27}} | collective-permute-start | bytes 786440 | tf_op jit(solution)/shard_map/ppermute | solution.py:281
  5.6 12.5 %collective-permute-start.2 = (bf16[256,512]{1,0:T(8,128)(2,1)S(1)}, bf16[256,512]{1,0:T(8,128)(2,1)}, u32[]{:S(2)}, u32[]{:S(2)}) collective-permute-start(bf16[256,512]{1,0:T(8,128)(2,1)S(1)} %shard_map.48), channel_id=1, source_target_pairs={{0,2},{1,3},{8,10},{9,11},{16,18},{17,19},{24,26},{25,27}} | collective-permute-start | bytes 786440 | tf_op jit(solution)/shard_map/ppermute | solution.py:281
  12.2 11.8 %collective-permute-start.1 = (bf16[256,512]{1,0:T(8,128)(2,1)}, bf16[256,512]{1,0:T(8,128)(2,1)}, u32[]{:S(2)}, u32[]{:S(2)}) collective-permute-start(bf16[256,512]{1,0:T(8,128)(2,1)} %collective-permute-done), channel_id=1, source_target_pairs={{2,4},{3,5},{10,12},{11,13},{18,20},{19,21},{26,28},{27,29}} | collective-permute-start | bytes 786440 | tf_op jit(solution)/shard_map/ppermute | solution.py:281
  15.5 9.3 %collective-permute-start.6 = (bf16[256,512]{1,0:T(8,128)(2,1)S(1)}, bf16[256,512]{1,0:T(8,128)(2,1)}, u32[]{:S(2)}, u32[]{:S(2)}) collective-permute-start(bf16[256,512]{1,0:T(8,128)(2,1)S(1)} %shard_map.49), channel_id=1, source_target_pairs={{0,2},{1,3},{8,10},{9,11},{16,18},{17,19},{24,26},{25,27}} | collective-permute-start | bytes 786440 | tf_op jit(solution)/shard_map/ppermute | solution.py:281
  16.8 11.4 %collective-permute-start.4 = (bf16[256,512]{1,0:T(8,128)(2,1)S(1)}, bf16[256,512]{1,0:T(8,128)(2,1)S(1)}, u32[]{:S(2)}, u32[]{:S(2)}) collective-permute-start(bf16[256,512]{1,0:T(8,128)(2,1)S(1)} %shard_map.47), channel_id=1, source_target_pairs={{0,2},{1,3},{8,10},{9,11},{16,18},{17,19},{24,26},{25,27}} | collective-permute-start | bytes 786440 | tf_op jit(solution)/shard_map/ppermute | solution.py:281
  18.1 8.4 %collective-permute-start.5 = (bf16[256,512]{1,0:T(8,128)(2,1)}, bf16[256,512]{1,0:T(8,128)(2,1)}, u32[]{:S(2)}, u32[]{:S(2)}) collective-permute-start(bf16[256,512]{1,0:T(8,128)(2,1)} %collective-permute-done.2), channel_id=1, source_target_pairs={{2,4},{3,5},{10,12},{11,13},{18,20},{19,21},{26,28},{27,29}} | collective-permute-start | bytes 786440 | tf_op jit(solution)/shard_map/ppermute | solution.py:281
  24.1 5.4 %collective-permute-start.3 = (bf16[256,512]{1,0:T(8,128)(2,1)}, bf16[256,512]{1,0:T(8,128)(2,1)S(1)}, u32[]{:S(2)}, u32[]{:S(2)}) collective-permute-start(bf16[256,512]{1,0:T(8,128)(2,1)} %collective-permute-done.1), channel_id=1, source_target_pairs={{4,6},{5,7},{12,14},{13,15},{20,22},{21,23},{28,30},{29,31}} | collective-permute-start | bytes 786440 | tf_op jit(solution)/shard_map/ppermute | solution.py:281
  24.8 4.9 %collective-permute-start.8 = (bf16[256,512]{1,0:T(8,128)(2,1)}, bf16[256,512]{1,0:T(8,128)(2,1)S(1)}, u32[]{:S(2)}, u32[]{:S(2)}) collective-permute-start(bf16[256,512]{1,0:T(8,128)(2,1)} %collective-permute-done.6), channel_id=1, source_target_pairs={{2,4},{3,5},{10,12},{11,13},{18,20},{19,21},{26,28},{27,29}} | collective-permute-start | bytes 786440 | tf_op jit(solution)/shard_map/ppermute | solution.py:281
  26.4 6.3 %slice-start = ((bf16[1024,7168]{1,0:T(8,128)(2,1)}), bf16[1024,256]{1,0:T(8,128)(2,1)S(1)}, s32[]{:S(2)}) async-start(bf16[1024,7168]{1,0:T(8,128)(2,1)} %weights_ref.5), calls=%async_computation | async-start | bytes 1048576 | tf_op jit(solution)/shard_map/slice | solution.py:341
  26.4 6.3 %copy-start.15 = (s32[1024,256]{1,0:T(8,128)S(1)}, s32[1024,256]{1,0:T(8,128)}, u32[]{:S(2)}) copy-start(s32[1024,256]{1,0:T(8,128)} %param.7) | copy-start | bytes 3145732
  26.5 6.3 %collective-permute-start.7 = (bf16[256,512]{1,0:T(8,128)(2,1)}, bf16[256,512]{1,0:T(8,128)(2,1)S(1)}, u32[]{:S(2)}, u32[]{:S(2)}) collective-permute-start(bf16[256,512]{1,0:T(8,128)(2,1)} %collective-permute-done.5), channel_id=1, source_target_pairs={{4,6},{5,7},{12,14},{13,15},{20,22},{21,23},{28,30},{29,31}} | collective-permute-start | bytes 786440 | tf_op jit(solution)/shard_map/ppermute | solution.py:281
  28.2 10.8 %collective-permute-start.11 = (bf16[256,512]{1,0:T(8,128)(2,1)S(1)}, bf16[256,512]{1,0:T(8,128)(2,1)S(1)}, u32[]{:S(2)}, u32[]{:S(2)}) collective-permute-start(bf16[256,512]{1,0:T(8,128)(2,1)S(1)} %collective-permute-done.4), channel_id=1, source_target_pairs={{2,4},{3,5},{10,12},{11,13},{18,20},{19,21},{26,28},{27,29}} | collective-permute-start | bytes 786440 | tf_op jit(solution)/shard_map/ppermute | solution.py:281
  29.7 10.0 %collective-permute-start.10 = (bf16[256,512]{1,0:T(8,128)(2,1)S(1)}, bf16[256,512]{1,0:T(8,128)(2,1)S(1)}, u32[]{:S(2)}, u32[]{:S(2)}) collective-permute-start(bf16[256,512]{1,0:T(8,128)(2,1)S(1)} %collective-permute-done.8), channel_id=1, source_target_pairs={{4,6},{5,7},{12,14},{13,15},{20,22},{21,23},{28,30},{29,31}} | collective-permute-start | bytes 786440 | tf_op jit(solution)/shard_map/ppermute | solution.py:281
  31.4 5.3 %collective-permute-start.9 = (bf16[256,512]{1,0:T(8,128)(2,1)S(1)}, bf16[256,512]{1,0:T(8,128)(2,1)S(1)}, u32[]{:S(2)}, u32[]{:S(2)}) collective-permute-start(bf16[256,512]{1,0:T(8,128)(2,1)S(1)} %select_select_fusion.4), channel_id=1, source_target_pairs={{0,1},{1,0},{2,3},{3,2},{4,5},{5,4},{6,7},{7,6},{8,9},{9,8},{10,11... | collective-permute-start | bytes 786440 | tf_op jit(solution)/shard_map/ppermute | solution.py:277
  32.8 9.6 %copy-start.11 = (bf16[1024,256]{1,0:T(8,128)(2,1)}, bf16[1024,256]{1,0:T(8,128)(2,1)S(1)}, u32[]{:S(2)}) copy-start(bf16[1024,256]{1,0:T(8,128)(2,1)S(1)} %compare_select_fusion) | copy-start | bytes 1572868
  37.7 7.9 %collective-permute-start.13 = (bf16[256,512]{1,0:T(8,128)(2,1)S(1)}, bf16[256,512]{1,0:T(8,128)(2,1)S(1)}, u32[]{:S(2)}, u32[]{:S(2)}) collective-permute-start(bf16[256,512]{1,0:T(8,128)(2,1)S(1)} %select_select_fusion.3), channel_id=1, source_target_pairs={{0,1},{1,0},{2,3},{3,2},{4,5},{5,4},{6,7},{7,6},{8,9},{9,8},{10,11... | collective-permute-start | bytes 786440 | tf_op jit(solution)/shard_map/ppermute | solution.py:277
  39.0 3.4 %collective-permute-start.12 = (bf16[256,512]{1,0:T(8,128)(2,1)S(1)}, bf16[256,512]{1,0:T(8,128)(2,1)S(1)}, u32[]{:S(2)}, u32[]{:S(2)}) collective-permute-start(bf16[256,512]{1,0:T(8,128)(2,1)S(1)} %collective-permute-done.11), channel_id=1, source_target_pairs={{4,6},{5,7},{12,14},{13,15},{20,22},{21,23},{28,30},{29,31}} | collective-permute-start | bytes 786440 | tf_op jit(solution)/shard_map/ppermute | solution.py:281
  40.7 15.6 %collective-permute-start.14 = (bf16[256,512]{1,0:T(8,128)(2,1)S(1)}, bf16[256,512]{1,0:T(8,128)(2,1)S(1)}, u32[]{:S(2)}, u32[]{:S(2)}) collective-permute-start(bf16[256,512]{1,0:T(8,128)(2,1)S(1)} %select_select_fusion.2), channel_id=1, source_target_pairs={{0,1},{1,0},{2,3},{3,2},{4,5},{5,4},{6,7},{7,6},{8,9},{9,8},{10,11... | collective-permute-start | bytes 786440 | tf_op jit(solution)/shard_map/ppermute | solution.py:277
  41.0 16.3 %collective-permute-start.16 = (bf16[1024,256]{1,0:T(8,128)(2,1)S(1)}, bf16[1024,256]{1,0:T(8,128)(2,1)S(1)}, u32[]{:S(2)}, u32[]{:S(2)}) collective-permute-start(bf16[1024,256]{1,0:T(8,128)(2,1)S(1)} %compare_select_fusion), channel_id=1, source_target_pairs={{0,2},{1,3},{8,10},{9,11},{16,18},{17,19},{24,26},{25,27}} | collective-permute-start | bytes 1572872 | tf_op jit(solution)/shard_map/ppermute | solution.py:281
  45.7 11.6 %collective-permute-start.15 = (bf16[256,512]{1,0:T(8,128)(2,1)S(1)}, bf16[256,512]{1,0:T(8,128)(2,1)S(1)}, u32[]{:S(2)}, u32[]{:S(2)}) collective-permute-start(bf16[256,512]{1,0:T(8,128)(2,1)S(1)} %select_select_fusion.1), channel_id=1, source_target_pairs={{0,1},{1,0},{2,3},{3,2},{4,5},{5,4},{6,7},{7,6},{8,9},{9,8},{10,11... | collective-permute-start | bytes 786440 | tf_op jit(solution)/shard_map/ppermute | solution.py:277
  57.3 10.3 %copy-start.17 = (bf16[1024,256]{1,0:T(8,128)(2,1)}, bf16[1024,256]{1,0:T(8,128)(2,1)S(1)}, u32[]{:S(2)}) copy-start(bf16[1024,256]{1,0:T(8,128)(2,1)S(1)} %collective-permute-done.16) | copy-start | bytes 1572868
  57.4 11.3 %copy-start = (bf16[256,2048]{1,0:T(8,128)(2,1)}, bf16[256,2048]{1,0:T(8,128)(2,1)S(1)}, u32[]{:S(2)}) copy-start(bf16[256,2048]{1,0:T(8,128)(2,1)S(1)} %get-tuple-element.94.refs_5_) | copy-start | bytes 3145732
  57.4 11.4 %copy-start.9 = (bf16[256,1024]{1,0:T(8,128)(2,1)}, bf16[256,1024]{1,0:T(8,128)(2,1)S(1)}, u32[]{:S(2)}) copy-start(bf16[256,1024]{1,0:T(8,128)(2,1)S(1)} %get-tuple-element.93.refs_5_) | copy-start | bytes 1572868
  57.9 10.8 %collective-permute-start.17 = (f32[256,256]{1,0:T(8,128)S(1)}, f32[256,256]{1,0:T(8,128)S(1)}, u32[]{:S(2)}, u32[]{:S(2)}) collective-permute-start(f32[256,256]{1,0:T(8,128)S(1)} %convolution_add_fusion), channel_id=1, source_target_pairs={{0,8},{8,0},{16,24},{24,16},{1,9},{9,1},{17,25},{25,17},{2,10},{10... | collective-permute-start | bytes 786440 | tf_op jit(solution)/shard_map/ppermute | solution.py:277
  67.6 6.6 %copy-start.5 = (bf16[256,1024]{1,0:T(8,128)(2,1)}, bf16[256,1024]{1,0:T(8,128)(2,1)S(1)}, u32[]{:S(2)}) copy-start(bf16[256,1024]{1,0:T(8,128)(2,1)S(1)} %pad_maximum_fusion.2.refs_2_) | copy-start | bytes 1572868
  74.2 18.3 %collective-permute-start.18 = (f32[256,896]{1,0:T(8,128)}, f32[256,896]{1,0:T(8,128)}, u32[]{:S(2)}, u32[]{:S(2)}) collective-permute-start(f32[256,896]{1,0:T(8,128)} %shard_map.52), channel_id=1, source_target_pairs={{0,8},{8,0},{16,24},{24,16},{1,9},{9,1},{17,25},{25,17},{2,10},{10... | collective-permute-start | bytes 2752520 | tf_op jit(solution)/shard_map/ppermute | solution.py:277
  74.6 17.0 %collective-permute-start.19 = (f32[256,256]{1,0:T(8,128)S(1)}, f32[256,256]{1,0:T(8,128)}, u32[]{:S(2)}, u32[]{:S(2)}) collective-permute-start(f32[256,256]{1,0:T(8,128)S(1)} %add.60), channel_id=1, source_target_pairs={{0,16},{8,24},{16,0},{24,8},{1,17},{9,25},{17,1},{25,9},{2,18},{10... | collective-permute-start | bytes 786440 | tf_op jit(solution)/shard_map/ppermute | solution.py:277
  75.8 22.8 %collective-permute-start.20 = (bf16[1024,256]{1,0:T(8,128)(2,1)}, bf16[1024,256]{1,0:T(8,128)(2,1)}, u32[]{:S(2)}, u32[]{:S(2)}) collective-permute-start(bf16[1024,256]{1,0:T(8,128)(2,1)} %copy-done.17), channel_id=1, source_target_pairs={{2,4},{3,5},{10,12},{11,13},{18,20},{19,21},{26,28},{27,29}} | collective-permute-start | bytes 1572872 | tf_op jit(solution)/shard_map/ppermute | solution.py:281
  82.5 9.0 %copy-start.14 = (f32[256,256]{1,0:T(8,128)S(1)}, f32[256,256]{1,0:T(8,128)}, u32[]{:S(2)}) copy-start(f32[256,256]{1,0:T(8,128)} %copy-done.13) | copy-start | bytes 786436
  82.5 10.0 %copy-start.6 = (bf16[256,1024]{1,0:T(8,128)(2,1)S(1)}, bf16[256,1024]{1,0:T(8,128)(2,1)}, u32[]{:S(2)}) copy-start(bf16[256,1024]{1,0:T(8,128)(2,1)} %copy-done.5) | copy-start | bytes 1572868
  82.5 10.1 %copy-start.8 = (f32[256,896]{1,0:T(8,128)S(1)}, f32[256,896]{1,0:T(8,128)}, u32[]{:S(2)}) copy-start(f32[256,896]{1,0:T(8,128)} %copy-done.7) | copy-start | bytes 2752516
  82.5 10.1 %copy-start.10 = (bf16[256,1024]{1,0:T(8,128)(2,1)S(1)}, bf16[256,1024]{1,0:T(8,128)(2,1)}, u32[]{:S(2)}) copy-start(bf16[256,1024]{1,0:T(8,128)(2,1)} %copy-done.9) | copy-start | bytes 1572868
  90.8 25.6 %collective-permute-start.22 = (f32[256,896]{1,0:T(8,128)}, f32[256,896]{1,0:T(8,128)}, u32[]{:S(2)}, u32[]{:S(2)}) collective-permute-start(f32[256,896]{1,0:T(8,128)} %shard_map.53), channel_id=1, source_target_pairs={{0,8},{8,0},{16,24},{24,16},{1,9},{9,1},{17,25},{25,17},{2,10},{10... | collective-permute-start | bytes 2752520 | tf_op jit(solution)/shard_map/ppermute | solution.py:277
  98.3 22.3 %collective-permute-start.23 = (f32[256,896]{1,0:T(8,128)}, f32[256,896]{1,0:T(8,128)}, u32[]{:S(2)}, u32[]{:S(2)}) collective-permute-start(f32[256,896]{1,0:T(8,128)} %shard_map.54), channel_id=1, source_target_pairs={{0,16},{8,24},{16,0},{24,8},{1,17},{9,25},{17,1},{25,9},{2,18},{10... | collective-permute-start | bytes 2752520 | tf_op jit(solution)/shard_map/ppermute | solution.py:277
  98.6 17.7 %collective-permute-start.21 = (bf16[1024,256]{1,0:T(8,128)(2,1)}, bf16[1024,256]{1,0:T(8,128)(2,1)}, u32[]{:S(2)}, u32[]{:S(2)}) collective-permute-start(bf16[1024,256]{1,0:T(8,128)(2,1)} %collective-permute-done.20), channel_id=1, source_target_pairs={{4,6},{5,7},{12,14},{13,15},{20,22},{21,23},{28,30},{29,31}} | collective-permute-start | bytes 1572872 | tf_op jit(solution)/shard_map/ppermute | solution.py:281
  108.7 16.0 %copy-start.12 = (bf16[1024,256]{1,0:T(8,128)(2,1)S(1)}, bf16[1024,256]{1,0:T(8,128)(2,1)}, u32[]{:S(2)}) copy-start(bf16[1024,256]{1,0:T(8,128)(2,1)} %copy-done.11) | copy-start | bytes 1572868
  108.7 16.0 %copy-start.18 = (bf16[1024,256]{1,0:T(8,128)(2,1)S(1)}, bf16[1024,256]{1,0:T(8,128)(2,1)}, u32[]{:S(2)}) copy-start(bf16[1024,256]{1,0:T(8,128)(2,1)} %copy-done.17) | copy-start | bytes 1572868
  123.3 3.0 %collective-permute-start.26 = (bf16[512,896]{1,0:T(8,128)(2,1)S(1)}, bf16[512,896]{1,0:T(8,128)(2,1)S(1)}, u32[]{:S(2)}, u32[]{:S(2)}) collective-permute-start(bf16[512,896]{1,0:T(8,128)(2,1)S(1)} %get-tuple-element.83.refs_0_), channel_id=1, source_target_pairs={{0,8},{8,0},{16,24},{24,16},{1,9},{9,1},{17,25},{25,17},{2,10},{10... | collective-permute-start | bytes 2752520 | tf_op jit(solution)/shard_map/ppermute | solution.py:277
  124.1 12.1 %collective-permute-start.25 = (bf16[256,896]{1,0:T(8,128)(2,1)S(1)}, bf16[256,896]{1,0:T(8,128)(2,1)S(1)}, u32[]{:S(2)}, u32[]{:S(2)}) collective-permute-start(bf16[256,896]{1,0:T(8,128)(2,1)S(1)} %get-tuple-element.82), channel_id=1, source_target_pairs={{0,1},{1,0},{2,3},{3,2},{4,5},{5,4},{6,7},{7,6},{8,9},{9,8},{10,11... | collective-permute-start | bytes 1376264 | tf_op jit(solution)/shard_map/ppermute | solution.py:277
  124.4 11.9 %collective-permute-start.24 = (bf16[256,896]{1,0:T(8,128)(2,1)S(1)}, bf16[256,896]{1,0:T(8,128)(2,1)S(1)}, u32[]{:S(2)}, u32[]{:S(2)}) collective-permute-start(bf16[256,896]{1,0:T(8,128)(2,1)S(1)} %get-tuple-element.82), channel_id=1, source_target_pairs={{0,16},{8,24},{16,0},{24,8},{1,17},{9,25},{17,1},{25,9},{2,18},{10... | collective-permute-start | bytes 1376264 | tf_op jit(solution)/shard_map/ppermute | solution.py:277
  124.8 9.1 %copy-start.3 = (bf16[1024,256]{1,0:T(8,128)(2,1)}, bf16[1024,256]{1,0:T(8,128)(2,1)S(1)}, u32[]{:S(2)}) copy-start(bf16[1024,256]{1,0:T(8,128)(2,1)S(1)} %select_select_fusion.error_ref) | copy-start | bytes 1572868
  136.2 2.8 %collective-permute-start.30 = (bf16[256,896]{1,0:T(8,128)(2,1)S(1)}, bf16[256,896]{1,0:T(8,128)(2,1)S(1)}, u32[]{:S(2)}, u32[]{:S(2)}) collective-permute-start(bf16[256,896]{1,0:T(8,128)(2,1)S(1)} %collective-permute-done.25.refs_1_), channel_id=1, source_target_pairs={{0,8},{8,0},{16,24},{24,16},{1,9},{9,1},{17,25},{25,17},{2,10},{10... | collective-permute-start | bytes 1376264 | tf_op jit(solution)/shard_map/ppermute | solution.py:277
  137.3 2.1 %collective-permute-start.29 = (bf16[256,896]{1,0:T(8,128)(2,1)S(1)}, bf16[256,896]{1,0:T(8,128)(2,1)S(1)}, u32[]{:S(2)}, u32[]{:S(2)}) collective-permute-start(bf16[256,896]{1,0:T(8,128)(2,1)S(1)} %collective-permute-done.24.refs_0_), channel_id=1, source_target_pairs={{0,8},{8,0},{16,24},{24,16},{1,9},{9,1},{17,25},{25,17},{2,10},{10... | collective-permute-start | bytes 1376264 | tf_op jit(solution)/shard_map/ppermute | solution.py:277
  137.3 10.1 %collective-permute-start.27 = (bf16[128,896]{1,0:T(8,128)(2,1)S(1)}, bf16[128,896]{1,0:T(8,128)(2,1)S(1)}, u32[]{:S(2)}, u32[]{:S(2)}) collective-permute-start(bf16[128,896]{1,0:T(8,128)(2,1)S(1)} %slice.10), channel_id=1, source_target_pairs={{0,16},{8,24},{16,0},{24,8},{1,17},{9,25},{17,1},{25,9},{2,18},{10... | collective-permute-start | bytes 688136 | tf_op jit(solution)/shard_map/ppermute | solution.py:277
  137.6 9.8 %collective-permute-start.28 = (bf16[128,896]{1,0:T(8,128)(2,1)S(1)}, bf16[128,896]{1,0:T(8,128)(2,1)S(1)}, u32[]{:S(2)}, u32[]{:S(2)}) collective-permute-start(bf16[128,896]{1,0:T(8,128)(2,1)S(1)} %slice.11), channel_id=1, source_target_pairs={{0,1},{1,0},{2,3},{3,2},{4,5},{5,4},{6,7},{7,6},{8,9},{9,8},{10,11... | collective-permute-start | bytes 688136 | tf_op jit(solution)/shard_map/ppermute | solution.py:277
  139.0 10.7 %copy-start.4 = (bf16[1024,256]{1,0:T(8,128)(2,1)S(1)}, bf16[1024,256]{1,0:T(8,128)(2,1)}, u32[]{:S(2)}) copy-start(bf16[1024,256]{1,0:T(8,128)(2,1)} %copy-done.3) | copy-start | bytes 1572868
  147.4 1.9 %collective-permute-start.31 = (bf16[128,896]{1,0:T(8,128)(2,1)S(1)}, bf16[128,896]{1,0:T(8,128)(2,1)S(1)}, u32[]{:S(2)}, u32[]{:S(2)}) collective-permute-start(bf16[128,896]{1,0:T(8,128)(2,1)S(1)} %collective-permute-done.27.refs_0_), channel_id=1, source_target_pairs={{0,8},{8,0},{16,24},{24,16},{1,9},{9,1},{17,25},{25,17},{2,10},{10... | collective-permute-start | bytes 688136 | tf_op jit(solution)/shard_map/ppermute | solution.py:277
  148.2 1.5 collective-permute-start.32
  (5 other events, 10.2 us)

commit v10 on v9

--- a/solution.py
+++ b/solution.py
@@ -326,8 +326,8 @@
         x = got[c][h + 1]
         if token is not None:
             x = after(x, token)
-        if h + 1 == hops and c > 0:
-            x = after(x, swapped[max(c - 2, 0)])
+        if h + 1 == hops and c > 1:
+            x = after(x, swapped[c - 2])
         got[c][h + 1] = token = x
         if h + 1 < hops:
             got[c].append(hop(x, "feat", h + 1))

time: 157 us -> 152 us (0.968)
  waiting for transfers between devices: 23 us -> 18 us
    ppermute x18, waiting for transfers between devices: 17.9 us -> 12 us  [swap(): return lax.ppermute(x, axis, [(i, i ^ bit) for i in range(size)])]
  transfers between devices with their start and end apart: 33 -> 33, of which waited for: 12 -> 13; matrix products, arithmetic and copies ran while one was open for 7% -> 7% of each run, Pallas kernels for 36% -> 37%
where the time goes in v10:
time: 152 us; the launch traced here: 151 us
  Pallas kernels  71.5 us (47%)
  starting transfers between devices  44 us (29%)
  waiting for transfers between devices  18 us (12%)
  local copies, waits for them, and re-layouts  7.9 us (5%)
  other arithmetic  7.71 us (5%)
    pallas_call x6, Pallas kernels, gram_block(): pl.pallas_call(functools.partial(gram_kernel, width // QBLOCK), out_shape...  35.8 us
    ppermute x15, starting transfers between devices, hop(): return lax.ppermute(x, axis, [(start, start + 1)])  23.6 us
    pallas_call x3, Pallas kernels, update_blocks(): pl.pallas_call(functools.partial(update_kernel, [[p.shape for p in pieces...  20.5 us
    ppermute x18, starting transfers between devices, swap(): return lax.ppermute(x, axis, [(i, i ^ bit) for i in range(size)])  20.5 us
    ppermute x18, waiting for transfers between devices, swap(): return lax.ppermute(x, axis, [(i, i ^ bit) for i in range(size)])  12 us
    pallas_call x1, Pallas kernels, invert(): pl.pallas_call(inverse_kernel, out_shape=jax.ShapeDtypeStruct((PANEL, PAN...  7.64 us
    ppermute x15, waiting for transfers between devices, hop(): return lax.ppermute(x, axis, [(start, start + 1)])  5.98 us
    unnamed x41, local copies, waits for them, and re-layouts  5.82 us
  transfers between devices with their start and end apart: 33, of which 13 were waited for; matrix products, arithmetic and copies ran while one was open for 7% of the time, Pallas kernels for 37%

profile of v10, /device:TPU:9, one launch (start us, length us, event | category | flops | bytes accessed | tf_op | source)
XLA Modules:
  0.0 150.9 jit_solution(18039237864353576581)
XLA Ops:
  0.0 1.8 %copy.12.exps_ref = s32[4096,56]{1,0:T(8,128)S(1)} copy(s32[4096,56]{0,1:T(8,128)} %param.5) | data formatting | bytes 1835008 | tf_op args[1]
  1.8 1.2 shard_map.46
  3.0 1.3 collective-permute-start
  4.3 1.2 shard_map.48
  5.6 1.3 collective-permute-start.2
  6.9 1.2 shard_map.49
  8.2 1.3 collective-permute-start.6
  9.5 1.2 shard_map.47
  10.7 1.3 collective-permute-start.4
  12.2 3.3 %collective-permute-start.1 = (bf16[256,512]{1,0:T(8,128)(2,1)}, bf16[256,512]{1,0:T(8,128)(2,1)}, u32[]{:S(2)}, u32[]{:S(2)}) collective-permute-start(bf16[256,512]{1,0:T(8,128)(2,1)} %collective-permute-done), channel_id=1, source_target_pairs={{2,4},{3,5},{10,12},{11,13},{18,20},{19,21},{26,28},{27,29}} | collective-permute-start | bytes 786440 | tf_op jit(solution)/shard_map/ppermute | solution.py:281
  15.6 2.3 %collective-permute-done.2 = bf16[256,512]{1,0:T(8,128)(2,1)} collective-permute-done((bf16[256,512]{1,0:T(8,128)(2,1)S(1)}, bf16[256,512]{1,0:T(8,128)(2,1)}, u32[]{:S(2)}, u32[]{:S(2)}) %collective-permute-start.2) | collective-permute-done | bytes 262176 | tf_op jit(solution)/shard_map/ppermute | solution.py:281
  17.8 2.0 %collective-permute-start.5 = (bf16[256,512]{1,0:T(8,128)(2,1)}, bf16[256,512]{1,0:T(8,128)(2,1)}, u32[]{:S(2)}, u32[]{:S(2)}) collective-permute-start(bf16[256,512]{1,0:T(8,128)(2,1)} %collective-permute-done.2), channel_id=1, source_target_pairs={{2,4},{3,5},{10,12},{11,13},{18,20},{19,21},{26,28},{27,29}} | collective-permute-start | bytes 786440 | tf_op jit(solution)/shard_map/ppermute | solution.py:281
  19.8 2.2 %convert_element_type.5 = f32[4096,56]{0,1:T(8,128)} convert(s32[4096,56]{0,1:T(8,128)} %param.5) | non-fusion elementwise | flops 229376 | bytes 1835008 | tf_op jit(solution)/shard_map/convert_element_type | solution.py:338
  22.0 1.8 %copy.16 = f32[4096,56]{1,0:T(8,128)S(1)} copy(f32[4096,56]{0,1:T(8,128)} %convert_element_type.5) | data formatting | bytes 1835008 | tf_op jit(solution)/shard_map/convert_element_type | solution.py:338
  25.1 1.3 collective-permute-start.8
  27.1 1.9 %collective-permute-done.4 = bf16[256,512]{1,0:T(8,128)(2,1)S(1)} collective-permute-done((bf16[256,512]{1,0:T(8,128)(2,1)S(1)}, bf16[256,512]{1,0:T(8,128)(2,1)S(1)}, u32[]{:S(2)}, u32[]{:S(2)}) %collective-permute-start.4) | collective-permute-done | bytes 262176 | tf_op jit(solution)/shard_map/ppermute | solution.py:281
  29.0 1.7 %collective-permute-start.10 = (bf16[256,512]{1,0:T(8,128)(2,1)S(1)}, bf16[256,512]{1,0:T(8,128)(2,1)S(1)}, u32[]{:S(2)}, u32[]{:S(2)}) collective-permute-start(bf16[256,512]{1,0:T(8,128)(2,1)S(1)} %collective-permute-done.4), channel_id=1, source_target_pairs={{2,4},{3,5},{10,12},{11,13},{18,20},{19,21},{26,28},{27,29}} | collective-permute-start | bytes 786440 | tf_op jit(solution)/shard_map/ppermute | solution.py:281
  31.6 1.0 select_select_fusion.4
  32.6 1.3 collective-permute-start.11
  33.9 1.0 select_select_fusion.3
  35.2 1.6 %collective-permute-done.10 = bf16[256,512]{1,0:T(8,128)(2,1)S(1)} collective-permute-done((bf16[256,512]{1,0:T(8,128)(2,1)S(1)}, bf16[256,512]{1,0:T(8,128)(2,1)S(1)}, u32[]{:S(2)}, u32[]{:S(2)}) %collective-permute-start.10) | collective-permute-done | bytes 262176 | tf_op jit(solution)/shard_map/ppermute | solution.py:281
  37.6 1.3 collective-permute-start.16
  38.9 1.0 select_select_fusion.2
  39.9 1.3 collective-permute-start.14
  42.2 1.3 collective-permute-start.15
  43.7 4.5 %shard_map.50.refs_6_ = f32[256,896]{1,0:T(8,128)S(1)} custom-call(s32[2]{0:T(128)S(1)} %pad_add_fusion.1.place_ref, bf16[4096,7168]{1,0:T(8,128)(2,1)} %refs_3_.11, f32[4096,128]{1,0:T(8,128)S(1)} %pad.4.refs_1_.refs_4_, bf16[256,1024]{1,0:T(8,128)(2,1)S(1)} %pad_maximum_fusion.1.refs_2_, bf16[4096,7168]{1,0:T(8,128)(2,1)} %refs_3_.11, ...), custom_call_target="tpu_custom_call" | custom-call | flops 58720256 | bytes 917504 | tf_op jit(solution)/shard_map/pallas_call | solution.py:102
  48.4 4.5 %shard_map.51.refs_6_ = f32[256,896]{1,0:T(8,128)S(1)} custom-call(s32[2]{0:T(128)S(1)} %pad_add_fusion.2.place_ref, bf16[4096,7168]{1,0:T(8,128)(2,1)} %refs_3_.11, f32[4096,128]{1,0:T(8,128)S(1)} %pad.4.refs_1_.refs_4_, bf16[256,1024]{1,0:T(8,128)(2,1)S(1)} %pad_maximum_fusion.1.refs_2_, bf16[4096,7168]{1,0:T(8,128)(2,1)} %refs_3_.11, ...), custom_call_target="tpu_custom_call" | custom-call | flops 58720256 | bytes 917504 | tf_op jit(solution)/shard_map/pallas_call | solution.py:102
  54.8 8.8 %collective-permute-start.17 = (f32[256,256]{1,0:T(8,128)S(1)}, f32[256,256]{1,0:T(8,128)S(1)}, u32[]{:S(2)}, u32[]{:S(2)}) collective-permute-start(f32[256,256]{1,0:T(8,128)S(1)} %convolution_add_fusion), channel_id=1, source_target_pairs={{0,8},{8,0},{16,24},{24,16},{1,9},{9,1},{17,25},{25,17},{2,10},{10... | collective-permute-start | bytes 786440 | tf_op jit(solution)/shard_map/ppermute | solution.py:277
  63.7 1.1 collective-permute-done.17
  64.9 5.4 %shard_map.52 = f32[256,896]{1,0:T(8,128)} custom-call(s32[2]{0:T(128)S(1)} %pad_add_fusion.3.place_ref, bf16[4096,7168]{1,0:T(8,128)(2,1)} %refs_3_.11, f32[4096,128]{1,0:T(8,128)S(1)} %pad.4.refs_1_.refs_4_, bf16[256,1024]{1,0:T(8,128)(2,1)S(1)} %pad_maximum_fusion.2.refs_2_, bf16[4096,7168]{1,0:T(8,128)(2,1)} %refs_3_.11, ...), custom_call_target="tpu_custom_call" | custom-call | flops 58720256 | bytes 917504 | tf_op jit(solution)/shard_map/pallas_call | solution.py:102
  70.7 1.2 collective-permute-start.19
  71.9 4.5 %collective-permute-start.20 = (bf16[1024,256]{1,0:T(8,128)(2,1)}, bf16[1024,256]{1,0:T(8,128)(2,1)}, u32[]{:S(2)}, u32[]{:S(2)}) collective-permute-start(bf16[1024,256]{1,0:T(8,128)(2,1)} %copy-done.17), channel_id=1, source_target_pairs={{2,4},{3,5},{10,12},{11,13},{18,20},{19,21},{26,28},{27,29}} | collective-permute-start | bytes 1572872 | tf_op jit(solution)/shard_map/ppermute | solution.py:281
  76.5 1.2 copy-done.1
  77.7 8.2 %shard_map.53 = f32[256,896]{1,0:T(8,128)} custom-call(s32[2]{0:T(128)S(1)} %pad_add_fusion.4.place_ref, bf16[4096,7168]{1,0:T(8,128)(2,1)} %refs_3_.11, f32[4096,128]{1,0:T(8,128)S(1)} %pad.4.refs_1_.refs_4_, bf16[256,2048]{1,0:T(8,128)(2,1)S(1)} %pad_maximum_fusion.refs_2_, bf16[4096,7168]{1,0:T(8,128)(2,1)} %refs_3_.11, ...), custom_call_target="tpu_custom_call" | custom-call | flops 58720256 | bytes 917504 | tf_op jit(solution)/shard_map/pallas_call | solution.py:102
  87.8 5.7 %shard_map.54 = f32[256,896]{1,0:T(8,128)} custom-call(s32[2]{0:T(128)S(1)} %pad_add_fusion.5.place_ref, bf16[4096,7168]{1,0:T(8,128)(2,1)} %refs_3_.11, f32[4096,128]{1,0:T(8,128)S(1)} %pad.4.refs_1_.refs_4_, bf16[256,1024]{1,0:T(8,128)(2,1)S(1)} %copy-done.6, bf16[4096,7168]{1,0:T(8,128)(2,1)} %refs_3_.11, f32[4096,128]{1,0:T(8,128)S(1)} %pad.4.refs_1_.refs_4_, ...), custom_call_target="tpu_custom_call" | custom-call | flops 58720256 | bytes 917504 | tf_op jit(solution)/shard_map/pallas_call | solution.py:102
  93.8 1.5 collective-permute-start.21
  95.3 1.2 copy-done.2
  96.5 7.3 %shard_map.55.first_ref = f32[256,896]{1,0:T(8,128)S(1)} custom-call(s32[2]{0:T(128)S(1)} %pad_add_fusion.6.place_ref, bf16[4096,7168]{1,0:T(8,128)(2,1)} %refs_3_.11, f32[4096,128]{1,0:T(8,128)S(1)} %pad.4.refs_1_.refs_4_, bf16[256,2048]{1,0:T(8,128)(2,1)S(1)} %pad_maximum_fusion.refs_2_, bf16[4096,7168]{1,0:T(8,128)(2,1)} %refs_3_.11, ...), custom_call_target="tpu_custom_call" | custom-call | flops 58720256 | bytes 917504 | tf_op jit(solution)/shard_map/pallas_call | solution.py:102
  103.9 7.6 %shard_map.56.inverse_ref = f32[256,256]{1,0:T(8,128)S(1)} custom-call(f32[256,256]{1,0:T(8,128)S(1)} %add.61.head_ref), custom_call_target="tpu_custom_call" | custom-call | flops 33554432 | bytes 524288 | tf_op jit(solution)/shard_map/pallas_call | solution.py:151
  111.5 4.3 %collective-permute-done.23.third_ref = f32[256,896]{1,0:T(8,128)} collective-permute-done((f32[256,896]{1,0:T(8,128)}, f32[256,896]{1,0:T(8,128)}, u32[]{:S(2)}, u32[]{:S(2)}) %collective-permute-start.23) | collective-permute-done | bytes 917536 | tf_op jit(solution)/shard_map/ppermute | solution.py:277
  115.8 2.6 %shard_map.57 = (bf16[256,896]{1,0:T(8,128)(2,1)S(1)}, bf16[512,896]{1,0:T(8,128)(2,1)S(1)}) custom-call(s32[1]{0:T(128)} %bitcast.13.place_ref, f32[256,256]{1,0:T(8,128)S(1)} %shard_map.56.inverse_ref, f32[256,896]{1,0:T(8,128)S(1)} %shard_map.55.first_ref, f32[256,896]{1,0:T(8,128)} %collective-permute-done.22.second_ref, ...), custom_call_target="tpu_custom_call" | custom-call | flops 704643072 | bytes 3670016 | tf_op jit(solution)/shard_map/pallas_call | solution.py:177
  120.0 1.4 collective-permute-done.26.refs_1_
  122.3 6.7 %shard_map.58.refs_4_ = bf16[1024,7168]{1,0:T(8,128)(2,1)} custom-call(s32[2]{0:T(128)S(1)} %pad_add_fusion.7.place_ref, bf16[1024,256]{1,0:T(8,128)(2,1)S(1)} %select_select_fusion.error_ref, bf16[1024,7168]{1,0:T(8,128)(2,1)} %weights_ref.5, bf16[512,896]{1,0:T(8,128)(2,1)S(1)} %get-tuple-element.81.refs_0_, bf16[512,896]{1,0:T(8,128)(2,1)} %copy-done.16), custom_call_target="tpu_custom_call" | custom-call | flops 939524096 | bytes 7340032 | tf_op jit(solution)/shard_map/pallas_call | solution.py:259
  129.0 2.3 %collective-permute-done.25.refs_1_ = bf16[256,896]{1,0:T(8,128)(2,1)S(1)} collective-permute-done((bf16[256,896]{1,0:T(8,128)(2,1)S(1)}, bf16[256,896]{1,0:T(8,128)(2,1)S(1)}, u32[]{:S(2)}, u32[]{:S(2)}) %collective-permute-start.25) | collective-permute-done | bytes 458784 | tf_op jit(solution)/shard_map/ppermute | solution.py:277
  131.4 1.1 collective-permute-start.30
  132.8 1.2 collective-permute-start.28
  134.6 8.0 %shard_map.59.refs_4_ = bf16[1024,7168]{1,0:T(8,128)(2,1)} custom-call(s32[4]{0:T(128)S(1)} %pad_add_fusion.8.place_ref, bf16[1024,256]{1,0:T(8,128)(2,1)} %copy-done.3, bf16[1024,7168]{1,0:T(8,128)(2,1)} %weights_ref.5, bf16[256,896]{1,0:T(8,128)(2,1)S(1)} %collective-permute-done.24.refs_0_, ...), custom_call_target="tpu_custom_call", output_to_operand_aliasing={{}: (7, {})} | custom-call | flops 1879048192 | bytes 14680064 | tf_op jit(solution)/shard_map/pallas_call | solution.py:259
  144.9 5.8 %shard_map.60 = bf16[1024,7168]{1,0:T(8,128)(2,1)} custom-call(s32[2]{0:T(128)S(1)} %pad_add_fusion.place_ref, bf16[1024,256]{1,0:T(8,128)(2,1)S(1)} %copy-done.4, bf16[1024,7168]{1,0:T(8,128)(2,1)} %weights_ref.5, bf16[128,896]{1,0:T(8,128)(2,1)S(1)} %collective-permute-done.27.refs_0_, ...), custom_call_target="tpu_custom_call", output_to_operand_aliasing={{}: (7, {})} | custom-call | flops 939524096 | bytes 7340032 | tf_op jit(solution)/shard_map/pallas_call | solution.py:259
  (106 shorter events, 15.4 us)
Async XLA Ops:
  3.0 9.2 %collective-permute-start = (bf16[256,512]{1,0:T(8,128)(2,1)S(1)}, bf16[256,512]{1,0:T(8,128)(2,1)}, u32[]{:S(2)}, u32[]{:S(2)}) collective-permute-start(bf16[256,512]{1,0:T(8,128)(2,1)S(1)} %shard_map.46), channel_id=1, source_target_pairs={{0,2},{1,3},{8,10},{9,11},{16,18},{17,19},{24,26},{25,27}} | collective-permute-start | bytes 786440 | tf_op jit(solution)/shard_map/ppermute | solution.py:281
  5.6 12.2 %collective-permute-start.2 = (bf16[256,512]{1,0:T(8,128)(2,1)S(1)}, bf16[256,512]{1,0:T(8,128)(2,1)}, u32[]{:S(2)}, u32[]{:S(2)}) collective-permute-start(bf16[256,512]{1,0:T(8,128)(2,1)S(1)} %shard_map.48), channel_id=1, source_target_pairs={{0,2},{1,3},{8,10},{9,11},{16,18},{17,19},{24,26},{25,27}} | collective-permute-start | bytes 786440 | tf_op jit(solution)/shard_map/ppermute | solution.py:281
  8.2 16.9 %collective-permute-start.6 = (bf16[256,512]{1,0:T(8,128)(2,1)S(1)}, bf16[256,512]{1,0:T(8,128)(2,1)}, u32[]{:S(2)}, u32[]{:S(2)}) collective-permute-start(bf16[256,512]{1,0:T(8,128)(2,1)S(1)} %shard_map.49), channel_id=1, source_target_pairs={{0,2},{1,3},{8,10},{9,11},{16,18},{17,19},{24,26},{25,27}} | collective-permute-start | bytes 786440 | tf_op jit(solution)/shard_map/ppermute | solution.py:281
  10.7 18.3 %collective-permute-start.4 = (bf16[256,512]{1,0:T(8,128)(2,1)S(1)}, bf16[256,512]{1,0:T(8,128)(2,1)S(1)}, u32[]{:S(2)}, u32[]{:S(2)}) collective-permute-start(bf16[256,512]{1,0:T(8,128)(2,1)S(1)} %shard_map.47), channel_id=1, source_target_pairs={{0,2},{1,3},{8,10},{9,11},{16,18},{17,19},{24,26},{25,27}} | collective-permute-start | bytes 786440 | tf_op jit(solution)/shard_map/ppermute | solution.py:281
  12.2 12.0 %collective-permute-start.1 = (bf16[256,512]{1,0:T(8,128)(2,1)}, bf16[256,512]{1,0:T(8,128)(2,1)}, u32[]{:S(2)}, u32[]{:S(2)}) collective-permute-start(bf16[256,512]{1,0:T(8,128)(2,1)} %collective-permute-done), channel_id=1, source_target_pairs={{2,4},{3,5},{10,12},{11,13},{18,20},{19,21},{26,28},{27,29}} | collective-permute-start | bytes 786440 | tf_op jit(solution)/shard_map/ppermute | solution.py:281
  17.8 8.6 %collective-permute-start.5 = (bf16[256,512]{1,0:T(8,128)(2,1)}, bf16[256,512]{1,0:T(8,128)(2,1)}, u32[]{:S(2)}, u32[]{:S(2)}) collective-permute-start(bf16[256,512]{1,0:T(8,128)(2,1)} %collective-permute-done.2), channel_id=1, source_target_pairs={{2,4},{3,5},{10,12},{11,13},{18,20},{19,21},{26,28},{27,29}} | collective-permute-start | bytes 786440 | tf_op jit(solution)/shard_map/ppermute | solution.py:281
  24.1 6.6 %slice-start = ((bf16[1024,7168]{1,0:T(8,128)(2,1)}), bf16[1024,256]{1,0:T(8,128)(2,1)S(1)}, s32[]{:S(2)}) async-start(bf16[1024,7168]{1,0:T(8,128)(2,1)} %weights_ref.5), calls=%async_computation | async-start | bytes 1048576 | tf_op jit(solution)/shard_map/slice | solution.py:341
  24.1 6.6 %copy-start.15 = (s32[1024,256]{1,0:T(8,128)S(1)}, s32[1024,256]{1,0:T(8,128)}, u32[]{:S(2)}) copy-start(s32[1024,256]{1,0:T(8,128)} %param.7) | copy-start | bytes 3145732
  24.2 6.6 %collective-permute-start.3 = (bf16[256,512]{1,0:T(8,128)(2,1)}, bf16[256,512]{1,0:T(8,128)(2,1)S(1)}, u32[]{:S(2)}, u32[]{:S(2)}) collective-permute-start(bf16[256,512]{1,0:T(8,128)(2,1)} %collective-permute-done.1), channel_id=1, source_target_pairs={{4,6},{5,7},{12,14},{13,15},{20,22},{21,23},{28,30},{29,31}} | collective-permute-start | bytes 786440 | tf_op jit(solution)/shard_map/ppermute | solution.py:281
  25.1 5.8 %collective-permute-start.8 = (bf16[256,512]{1,0:T(8,128)(2,1)}, bf16[256,512]{1,0:T(8,128)(2,1)S(1)}, u32[]{:S(2)}, u32[]{:S(2)}) collective-permute-start(bf16[256,512]{1,0:T(8,128)(2,1)} %collective-permute-done.6), channel_id=1, source_target_pairs={{2,4},{3,5},{10,12},{11,13},{18,20},{19,21},{26,28},{27,29}} | collective-permute-start | bytes 786440 | tf_op jit(solution)/shard_map/ppermute | solution.py:281
  26.4 6.2 %collective-permute-start.7 = (bf16[256,512]{1,0:T(8,128)(2,1)}, bf16[256,512]{1,0:T(8,128)(2,1)S(1)}, u32[]{:S(2)}, u32[]{:S(2)}) collective-permute-start(bf16[256,512]{1,0:T(8,128)(2,1)} %collective-permute-done.5), channel_id=1, source_target_pairs={{4,6},{5,7},{12,14},{13,15},{20,22},{21,23},{28,30},{29,31}} | collective-permute-start | bytes 786440 | tf_op jit(solution)/shard_map/ppermute | solution.py:281
  29.0 7.9 %collective-permute-start.10 = (bf16[256,512]{1,0:T(8,128)(2,1)S(1)}, bf16[256,512]{1,0:T(8,128)(2,1)S(1)}, u32[]{:S(2)}, u32[]{:S(2)}) collective-permute-start(bf16[256,512]{1,0:T(8,128)(2,1)S(1)} %collective-permute-done.4), channel_id=1, source_target_pairs={{2,4},{3,5},{10,12},{11,13},{18,20},{19,21},{26,28},{27,29}} | collective-permute-start | bytes 786440 | tf_op jit(solution)/shard_map/ppermute | solution.py:281
  30.8 9.0 %copy-start.11 = (bf16[1024,256]{1,0:T(8,128)(2,1)}, bf16[1024,256]{1,0:T(8,128)(2,1)S(1)}, u32[]{:S(2)}) copy-start(bf16[1024,256]{1,0:T(8,128)(2,1)S(1)} %compare_select_fusion) | copy-start | bytes 1572868
  30.9 8.0 %collective-permute-start.9 = (bf16[256,512]{1,0:T(8,128)(2,1)S(1)}, bf16[256,512]{1,0:T(8,128)(2,1)S(1)}, u32[]{:S(2)}, u32[]{:S(2)}) collective-permute-start(bf16[256,512]{1,0:T(8,128)(2,1)S(1)} %collective-permute-done.8), channel_id=1, source_target_pairs={{4,6},{5,7},{12,14},{13,15},{20,22},{21,23},{28,30},{29,31}} | collective-permute-start | bytes 786440 | tf_op jit(solution)/shard_map/ppermute | solution.py:281
  32.6 6.3 %collective-permute-start.11 = (bf16[256,512]{1,0:T(8,128)(2,1)S(1)}, bf16[256,512]{1,0:T(8,128)(2,1)S(1)}, u32[]{:S(2)}, u32[]{:S(2)}) collective-permute-start(bf16[256,512]{1,0:T(8,128)(2,1)S(1)} %select_select_fusion.4), channel_id=1, source_target_pairs={{0,1},{1,0},{2,3},{3,2},{4,5},{5,4},{6,7},{7,6},{8,9},{9,8},{10,11... | collective-permute-start | bytes 786440 | tf_op jit(solution)/shard_map/ppermute | solution.py:277
  34.9 7.2 %collective-permute-start.13 = (bf16[256,512]{1,0:T(8,128)(2,1)S(1)}, bf16[256,512]{1,0:T(8,128)(2,1)S(1)}, u32[]{:S(2)}, u32[]{:S(2)}) collective-permute-start(bf16[256,512]{1,0:T(8,128)(2,1)S(1)} %select_select_fusion.3), channel_id=1, source_target_pairs={{0,1},{1,0},{2,3},{3,2},{4,5},{5,4},{6,7},{7,6},{8,9},{9,8},{10,11... | collective-permute-start | bytes 786440 | tf_op jit(solution)/shard_map/ppermute | solution.py:277
  36.8 4.4 %collective-permute-start.12 = (bf16[256,512]{1,0:T(8,128)(2,1)S(1)}, bf16[256,512]{1,0:T(8,128)(2,1)S(1)}, u32[]{:S(2)}, u32[]{:S(2)}) collective-permute-start(bf16[256,512]{1,0:T(8,128)(2,1)S(1)} %collective-permute-done.10), channel_id=1, source_target_pairs={{4,6},{5,7},{12,14},{13,15},{20,22},{21,23},{28,30},{29,31}} | collective-permute-start | bytes 786440 | tf_op jit(solution)/shard_map/ppermute | solution.py:281
  37.6 16.4 %collective-permute-start.16 = (bf16[1024,256]{1,0:T(8,128)(2,1)S(1)}, bf16[1024,256]{1,0:T(8,128)(2,1)S(1)}, u32[]{:S(2)}, u32[]{:S(2)}) collective-permute-start(bf16[1024,256]{1,0:T(8,128)(2,1)S(1)} %compare_select_fusion), channel_id=1, source_target_pairs={{0,2},{1,3},{8,10},{9,11},{16,18},{17,19},{24,26},{25,27}} | collective-permute-start | bytes 1572872 | tf_op jit(solution)/shard_map/ppermute | solution.py:281
  39.9 14.1 %collective-permute-start.14 = (bf16[256,512]{1,0:T(8,128)(2,1)S(1)}, bf16[256,512]{1,0:T(8,128)(2,1)S(1)}, u32[]{:S(2)}, u32[]{:S(2)}) collective-permute-start(bf16[256,512]{1,0:T(8,128)(2,1)S(1)} %select_select_fusion.2), channel_id=1, source_target_pairs={{0,1},{1,0},{2,3},{3,2},{4,5},{5,4},{6,7},{7,6},{8,9},{9,8},{10,11... | collective-permute-start | bytes 786440 | tf_op jit(solution)/shard_map/ppermute | solution.py:277
  42.2 11.7 %collective-permute-start.15 = (bf16[256,512]{1,0:T(8,128)(2,1)S(1)}, bf16[256,512]{1,0:T(8,128)(2,1)S(1)}, u32[]{:S(2)}, u32[]{:S(2)}) collective-permute-start(bf16[256,512]{1,0:T(8,128)(2,1)S(1)} %select_select_fusion.1), channel_id=1, source_target_pairs={{0,1},{1,0},{2,3},{3,2},{4,5},{5,4},{6,7},{7,6},{8,9},{9,8},{10,11... | collective-permute-start | bytes 786440 | tf_op jit(solution)/shard_map/ppermute | solution.py:277
  54.1 10.7 %copy-start = (bf16[256,2048]{1,0:T(8,128)(2,1)}, bf16[256,2048]{1,0:T(8,128)(2,1)S(1)}, u32[]{:S(2)}) copy-start(bf16[256,2048]{1,0:T(8,128)(2,1)S(1)} %get-tuple-element.92.refs_5_) | copy-start | bytes 3145732
  54.1 10.8 %copy-start.9 = (bf16[256,1024]{1,0:T(8,128)(2,1)}, bf16[256,1024]{1,0:T(8,128)(2,1)S(1)}, u32[]{:S(2)}) copy-start(bf16[256,1024]{1,0:T(8,128)(2,1)S(1)} %get-tuple-element.91.refs_5_) | copy-start | bytes 1572868
  54.8 10.0 %collective-permute-start.17 = (f32[256,256]{1,0:T(8,128)S(1)}, f32[256,256]{1,0:T(8,128)S(1)}, u32[]{:S(2)}, u32[]{:S(2)}) collective-permute-start(f32[256,256]{1,0:T(8,128)S(1)} %convolution_add_fusion), channel_id=1, source_target_pairs={{0,8},{8,0},{16,24},{24,16},{1,9},{9,1},{17,25},{25,17},{2,10},{10... | collective-permute-start | bytes 786440 | tf_op jit(solution)/shard_map/ppermute | solution.py:277
  63.7 6.7 %copy-start.5 = (bf16[256,1024]{1,0:T(8,128)(2,1)}, bf16[256,1024]{1,0:T(8,128)(2,1)S(1)}, u32[]{:S(2)}) copy-start(bf16[256,1024]{1,0:T(8,128)(2,1)S(1)} %pad_maximum_fusion.2.refs_2_) | copy-start | bytes 1572868
  64.8 5.9 %copy-start.13 = (f32[256,256]{1,0:T(8,128)}, f32[256,256]{1,0:T(8,128)S(1)}, u32[]{:S(2)}) copy-start(f32[256,256]{1,0:T(8,128)S(1)} %add.60) | copy-start | bytes 786436
  70.4 17.4 %collective-permute-start.18 = (f32[256,896]{1,0:T(8,128)}, f32[256,896]{1,0:T(8,128)}, u32[]{:S(2)}, u32[]{:S(2)}) collective-permute-start(f32[256,896]{1,0:T(8,128)} %shard_map.52), channel_id=1, source_target_pairs={{0,8},{8,0},{16,24},{24,16},{1,9},{9,1},{17,25},{25,17},{2,10},{10... | collective-permute-start | bytes 2752520 | tf_op jit(solution)/shard_map/ppermute | solution.py:277
  70.7 16.0 %collective-permute-start.19 = (f32[256,256]{1,0:T(8,128)S(1)}, f32[256,256]{1,0:T(8,128)}, u32[]{:S(2)}, u32[]{:S(2)}) collective-permute-start(f32[256,256]{1,0:T(8,128)S(1)} %add.60), channel_id=1, source_target_pairs={{0,16},{8,24},{16,0},{24,8},{1,17},{9,25},{17,1},{25,9},{2,18},{10... | collective-permute-start | bytes 786440 | tf_op jit(solution)/shard_map/ppermute | solution.py:277
  71.9 21.8 %collective-permute-start.20 = (bf16[1024,256]{1,0:T(8,128)(2,1)}, bf16[1024,256]{1,0:T(8,128)(2,1)}, u32[]{:S(2)}, u32[]{:S(2)}) collective-permute-start(bf16[1024,256]{1,0:T(8,128)(2,1)} %copy-done.17), channel_id=1, source_target_pairs={{2,4},{3,5},{10,12},{11,13},{18,20},{19,21},{26,28},{27,29}} | collective-permute-start | bytes 1572872 | tf_op jit(solution)/shard_map/ppermute | solution.py:281
  77.7 9.1 %copy-start.14 = (f32[256,256]{1,0:T(8,128)S(1)}, f32[256,256]{1,0:T(8,128)}, u32[]{:S(2)}) copy-start(f32[256,256]{1,0:T(8,128)} %copy-done.13) | copy-start | bytes 786436
  77.7 10.0 %copy-start.6 = (bf16[256,1024]{1,0:T(8,128)(2,1)S(1)}, bf16[256,1024]{1,0:T(8,128)(2,1)}, u32[]{:S(2)}) copy-start(bf16[256,1024]{1,0:T(8,128)(2,1)} %copy-done.5) | copy-start | bytes 1572868
  77.7 10.1 %copy-start.8 = (f32[256,896]{1,0:T(8,128)S(1)}, f32[256,896]{1,0:T(8,128)}, u32[]{:S(2)}) copy-start(f32[256,896]{1,0:T(8,128)} %copy-done.7) | copy-start | bytes 2752516
  77.7 10.1 %copy-start.10 = (bf16[256,1024]{1,0:T(8,128)(2,1)S(1)}, bf16[256,1024]{1,0:T(8,128)(2,1)}, u32[]{:S(2)}) copy-start(bf16[256,1024]{1,0:T(8,128)(2,1)} %copy-done.9) | copy-start | bytes 1572868
  86.0 25.6 %collective-permute-start.22 = (f32[256,896]{1,0:T(8,128)}, f32[256,896]{1,0:T(8,128)}, u32[]{:S(2)}, u32[]{:S(2)}) collective-permute-start(f32[256,896]{1,0:T(8,128)} %shard_map.53), channel_id=1, source_target_pairs={{0,8},{8,0},{16,24},{24,16},{1,9},{9,1},{17,25},{25,17},{2,10},{10... | collective-permute-start | bytes 2752520 | tf_op jit(solution)/shard_map/ppermute | solution.py:277
  93.5 22.3 %collective-permute-start.23 = (f32[256,896]{1,0:T(8,128)}, f32[256,896]{1,0:T(8,128)}, u32[]{:S(2)}, u32[]{:S(2)}) collective-permute-start(f32[256,896]{1,0:T(8,128)} %shard_map.54), channel_id=1, source_target_pairs={{0,16},{8,24},{16,0},{24,8},{1,17},{9,25},{17,1},{25,9},{2,18},{10... | collective-permute-start | bytes 2752520 | tf_op jit(solution)/shard_map/ppermute | solution.py:277
  93.8 17.7 %collective-permute-start.21 = (bf16[1024,256]{1,0:T(8,128)(2,1)}, bf16[1024,256]{1,0:T(8,128)(2,1)}, u32[]{:S(2)}, u32[]{:S(2)}) collective-permute-start(bf16[1024,256]{1,0:T(8,128)(2,1)} %collective-permute-done.20), channel_id=1, source_target_pairs={{4,6},{5,7},{12,14},{13,15},{20,22},{21,23},{28,30},{29,31}} | collective-permute-start | bytes 1572872 | tf_op jit(solution)/shard_map/ppermute | solution.py:281
  103.8 16.0 %copy-start.12 = (bf16[1024,256]{1,0:T(8,128)(2,1)S(1)}, bf16[1024,256]{1,0:T(8,128)(2,1)}, u32[]{:S(2)}) copy-start(bf16[1024,256]{1,0:T(8,128)(2,1)} %copy-done.11) | copy-start | bytes 1572868
  103.9 16.0 %copy-start.18 = (bf16[1024,256]{1,0:T(8,128)(2,1)S(1)}, bf16[1024,256]{1,0:T(8,128)(2,1)}, u32[]{:S(2)}) copy-start(bf16[1024,256]{1,0:T(8,128)(2,1)} %copy-done.17) | copy-start | bytes 1572868
  118.4 2.9 %collective-permute-start.26 = (bf16[512,896]{1,0:T(8,128)(2,1)S(1)}, bf16[512,896]{1,0:T(8,128)(2,1)S(1)}, u32[]{:S(2)}, u32[]{:S(2)}) collective-permute-start(bf16[512,896]{1,0:T(8,128)(2,1)S(1)} %get-tuple-element.81.refs_0_), channel_id=1, source_target_pairs={{0,8},{8,0},{16,24},{24,16},{1,9},{9,1},{17,25},{25,17},{2,10},{10... | collective-permute-start | bytes 2752520 | tf_op jit(solution)/shard_map/ppermute | solution.py:277
  119.3 12.1 %collective-permute-start.25 = (bf16[256,896]{1,0:T(8,128)(2,1)S(1)}, bf16[256,896]{1,0:T(8,128)(2,1)S(1)}, u32[]{:S(2)}, u32[]{:S(2)}) collective-permute-start(bf16[256,896]{1,0:T(8,128)(2,1)S(1)} %get-tuple-element.80), channel_id=1, source_target_pairs={{0,1},{1,0},{2,3},{3,2},{4,5},{5,4},{6,7},{7,6},{8,9},{9,8},{10,11... | collective-permute-start | bytes 1376264 | tf_op jit(solution)/shard_map/ppermute | solution.py:277
  119.5 11.9 %collective-permute-start.24 = (bf16[256,896]{1,0:T(8,128)(2,1)S(1)}, bf16[256,896]{1,0:T(8,128)(2,1)S(1)}, u32[]{:S(2)}, u32[]{:S(2)}) collective-permute-start(bf16[256,896]{1,0:T(8,128)(2,1)S(1)} %get-tuple-element.80), channel_id=1, source_target_pairs={{0,16},{8,24},{16,0},{24,8},{1,17},{9,25},{17,1},{25,9},{2,18},{10... | collective-permute-start | bytes 1376264 | tf_op jit(solution)/shard_map/ppermute | solution.py:277
  120.0 9.1 %copy-start.3 = (bf16[1024,256]{1,0:T(8,128)(2,1)}, bf16[1024,256]{1,0:T(8,128)(2,1)S(1)}, u32[]{:S(2)}) copy-start(bf16[1024,256]{1,0:T(8,128)(2,1)S(1)} %select_select_fusion.error_ref) | copy-start | bytes 1572868
  131.4 2.8 %collective-permute-start.30 = (bf16[256,896]{1,0:T(8,128)(2,1)S(1)}, bf16[256,896]{1,0:T(8,128)(2,1)S(1)}, u32[]{:S(2)}, u32[]{:S(2)}) collective-permute-start(bf16[256,896]{1,0:T(8,128)(2,1)S(1)} %collective-permute-done.25.refs_1_), channel_id=1, source_target_pairs={{0,8},{8,0},{16,24},{24,16},{1,9},{9,1},{17,25},{25,17},{2,10},{10... | collective-permute-start | bytes 1376264 | tf_op jit(solution)/shard_map/ppermute | solution.py:277
  132.5 2.1 %collective-permute-start.29 = (bf16[256,896]{1,0:T(8,128)(2,1)S(1)}, bf16[256,896]{1,0:T(8,128)(2,1)S(1)}, u32[]{:S(2)}, u32[]{:S(2)}) collective-permute-start(bf16[256,896]{1,0:T(8,128)(2,1)S(1)} %collective-permute-done.24.refs_0_), channel_id=1, source_target_pairs={{0,8},{8,0},{16,24},{24,16},{1,9},{9,1},{17,25},{25,17},{2,10},{10... | collective-permute-start | bytes 1376264 | tf_op jit(solution)/shard_map/ppermute | solution.py:277
  132.5 10.1 %collective-permute-start.27 = (bf16[128,896]{1,0:T(8,128)(2,1)S(1)}, bf16[128,896]{1,0:T(8,128)(2,1)S(1)}, u32[]{:S(2)}, u32[]{:S(2)}) collective-permute-start(bf16[128,896]{1,0:T(8,128)(2,1)S(1)} %slice.10), channel_id=1, source_target_pairs={{0,16},{8,24},{16,0},{24,8},{1,17},{9,25},{17,1},{25,9},{2,18},{10... | collective-permute-start | bytes 688136 | tf_op jit(solution)/shard_map/ppermute | solution.py:277
  132.8 9.8 %collective-permute-start.28 = (bf16[128,896]{1,0:T(8,128)(2,1)S(1)}, bf16[128,896]{1,0:T(8,128)(2,1)S(1)}, u32[]{:S(2)}, u32[]{:S(2)}) collective-permute-start(bf16[128,896]{1,0:T(8,128)(2,1)S(1)} %slice.11), channel_id=1, source_target_pairs={{0,1},{1,0},{2,3},{3,2},{4,5},{5,4},{6,7},{7,6},{8,9},{9,8},{10,11... | collective-permute-start | bytes 688136 | tf_op jit(solution)/shard_map/ppermute | solution.py:277
  134.2 10.7 %copy-start.4 = (bf16[1024,256]{1,0:T(8,128)(2,1)S(1)}, bf16[1024,256]{1,0:T(8,128)(2,1)}, u32[]{:S(2)}) copy-start(bf16[1024,256]{1,0:T(8,128)(2,1)} %copy-done.3) | copy-start | bytes 1572868
  142.6 1.9 %collective-permute-start.31 = (bf16[128,896]{1,0:T(8,128)(2,1)S(1)}, bf16[128,896]{1,0:T(8,128)(2,1)S(1)}, u32[]{:S(2)}, u32[]{:S(2)}) collective-permute-start(bf16[128,896]{1,0:T(8,128)(2,1)S(1)} %collective-permute-done.27.refs_0_), channel_id=1, source_target_pairs={{0,8},{8,0},{16,24},{24,16},{1,9},{9,1},{17,25},{25,17},{2,10},{10... | collective-permute-start | bytes 688136 | tf_op jit(solution)/shard_map/ppermute | solution.py:277
  143.4 1.5 collective-permute-start.32
  (5 other events, 5.1 us)

commit v11 on v10

--- a/solution.py
+++ b/solution.py
@@ -327,7 +327,7 @@
         if token is not None:
             x = after(x, token)
         if h + 1 == hops and c > 1:
-            x = after(x, swapped[c - 2])
+            x = after(x, swapped[0])
         got[c][h + 1] = token = x
         if h + 1 < hops:
             got[c].append(hop(x, "feat", h + 1))

time: 152 us -> 151 us (level)
  starting transfers between devices: 44 us -> 41 us
  waiting for transfers between devices: 18 us -> 19.9 us
    ppermute x18, starting transfers between devices: 20.5 us -> 17.4 us  [swap(): return lax.ppermute(x, axis, [(i, i ^ bit) for i in range(size)])]
    ppermute x18, waiting for transfers between devices: 12 us -> 13.9 us  [swap(): return lax.ppermute(x, axis, [(i, i ^ bit) for i in range(size)])]
  transfers between devices with their start and end apart: 33 -> 33, of which waited for: 13 -> 15; matrix products, arithmetic and copies ran while one was open for 7% -> 7% of each run, Pallas kernels for 37% -> 38%
where the time goes in v11:
time: 151 us; the launch traced here: 150 us
  Pallas kernels  71.5 us (47%)
  starting transfers between devices  41 us (27%)
  waiting for transfers between devices  19.9 us (13%)
  local copies, waits for them, and re-layouts  7.89 us (5%)
  other arithmetic  7.71 us (5%)
    pallas_call x6, Pallas kernels, gram_block(): pl.pallas_call(functools.partial(gram_kernel, width // QBLOCK), out_shape...  35.8 us
    ppermute x15, starting transfers between devices, hop(): return lax.ppermute(x, axis, [(start, start + 1)])  23.6 us
    pallas_call x3, Pallas kernels, update_blocks(): pl.pallas_call(functools.partial(update_kernel, [[p.shape for p in pieces...  20.5 us
    ppermute x18, starting transfers between devices, swap(): return lax.ppermute(x, axis, [(i, i ^ bit) for i in range(size)])  17.4 us
    ppermute x18, waiting for transfers between devices, swap(): return lax.ppermute(x, axis, [(i, i ^ bit) for i in range(size)])  13.9 us
    pallas_call x1, Pallas kernels, invert(): pl.pallas_call(inverse_kernel, out_shape=jax.ShapeDtypeStruct((PANEL, PAN...  7.65 us
    ppermute x15, waiting for transfers between devices, hop(): return lax.ppermute(x, axis, [(start, start + 1)])  5.98 us
    unnamed x41, local copies, waits for them, and re-layouts  5.82 us
  transfers between devices with their start and end apart: 33, of which 15 were waited for; matrix products, arithmetic and copies ran while one was open for 7% of the time, Pallas kernels for 38%

profile of v11, /device:TPU:9, one launch (start us, length us, event | category | flops | bytes accessed | tf_op | source)
XLA Modules:
  0.0 149.8 jit_solution(5481625349712421765)
XLA Ops:
  0.0 1.8 %copy.12.exps_ref = s32[4096,56]{1,0:T(8,128)S(1)} copy(s32[4096,56]{0,1:T(8,128)} %param.5) | data formatting | bytes 1835008 | tf_op args[1]
  1.8 1.2 shard_map.46
  3.0 1.3 collective-permute-start
  4.3 1.2 shard_map.48
  5.6 1.3 collective-permute-start.2
  6.9 1.2 shard_map.49
  8.2 1.3 collective-permute-start.6
  9.5 1.2 shard_map.47
  10.7 1.3 collective-permute-start.4
  12.2 3.3 %collective-permute-start.1 = (bf16[256,512]{1,0:T(8,128)(2,1)}, bf16[256,512]{1,0:T(8,128)(2,1)}, u32[]{:S(2)}, u32[]{:S(2)}) collective-permute-start(bf16[256,512]{1,0:T(8,128)(2,1)} %collective-permute-done), channel_id=1, source_target_pairs={{2,4},{3,5},{10,12},{11,13},{18,20},{19,21},{26,28},{27,29}} | collective-permute-start | bytes 786440 | tf_op jit(solution)/shard_map/ppermute | solution.py:281
  15.6 2.3 %collective-permute-done.2 = bf16[256,512]{1,0:T(8,128)(2,1)} collective-permute-done((bf16[256,512]{1,0:T(8,128)(2,1)S(1)}, bf16[256,512]{1,0:T(8,128)(2,1)}, u32[]{:S(2)}, u32[]{:S(2)}) %collective-permute-start.2) | collective-permute-done | bytes 262176 | tf_op jit(solution)/shard_map/ppermute | solution.py:281
  17.8 2.0 %collective-permute-start.5 = (bf16[256,512]{1,0:T(8,128)(2,1)}, bf16[256,512]{1,0:T(8,128)(2,1)}, u32[]{:S(2)}, u32[]{:S(2)}) collective-permute-start(bf16[256,512]{1,0:T(8,128)(2,1)} %collective-permute-done.2), channel_id=1, source_target_pairs={{2,4},{3,5},{10,12},{11,13},{18,20},{19,21},{26,28},{27,29}} | collective-permute-start | bytes 786440 | tf_op jit(solution)/shard_map/ppermute | solution.py:281
  19.8 2.2 %convert_element_type.5 = f32[4096,56]{0,1:T(8,128)} convert(s32[4096,56]{0,1:T(8,128)} %param.5) | non-fusion elementwise | flops 229376 | bytes 1835008 | tf_op jit(solution)/shard_map/convert_element_type | solution.py:338
  22.0 1.8 %copy.16 = f32[4096,56]{1,0:T(8,128)S(1)} copy(f32[4096,56]{0,1:T(8,128)} %convert_element_type.5) | data formatting | bytes 1835008 | tf_op jit(solution)/shard_map/convert_element_type | solution.py:338
  25.1 1.3 collective-permute-start.8
  27.1 1.9 %collective-permute-done.4 = bf16[256,512]{1,0:T(8,128)(2,1)S(1)} collective-permute-done((bf16[256,512]{1,0:T(8,128)(2,1)S(1)}, bf16[256,512]{1,0:T(8,128)(2,1)S(1)}, u32[]{:S(2)}, u32[]{:S(2)}) %collective-permute-start.4) | collective-permute-done | bytes 262176 | tf_op jit(solution)/shard_map/ppermute | solution.py:281
  29.0 1.7 %collective-permute-start.10 = (bf16[256,512]{1,0:T(8,128)(2,1)S(1)}, bf16[256,512]{1,0:T(8,128)(2,1)S(1)}, u32[]{:S(2)}, u32[]{:S(2)}) collective-permute-start(bf16[256,512]{1,0:T(8,128)(2,1)S(1)} %collective-permute-done.4), channel_id=1, source_target_pairs={{2,4},{3,5},{10,12},{11,13},{18,20},{19,21},{26,28},{27,29}} | collective-permute-start | bytes 786440 | tf_op jit(solution)/shard_map/ppermute | solution.py:281
  31.6 1.0 select_select_fusion.4
  32.6 1.3 collective-permute-start.11
  33.9 1.0 select_select_fusion.3
  35.2 1.6 %collective-permute-done.10 = bf16[256,512]{1,0:T(8,128)(2,1)S(1)} collective-permute-done((bf16[256,512]{1,0:T(8,128)(2,1)S(1)}, bf16[256,512]{1,0:T(8,128)(2,1)S(1)}, u32[]{:S(2)}, u32[]{:S(2)}) %collective-permute-start.10) | collective-permute-done | bytes 262176 | tf_op jit(solution)/shard_map/ppermute | solution.py:281
  37.6 1.3 collective-permute-start.16
  38.9 1.0 select_select_fusion.2
  39.9 1.3 collective-permute-start.14
  42.2 4.5 %shard_map.50.refs_6_ = f32[256,896]{1,0:T(8,128)S(1)} custom-call(s32[2]{0:T(128)S(1)} %pad_add_fusion.1.place_ref, bf16[4096,7168]{1,0:T(8,128)(2,1)} %refs_3_.11, f32[4096,128]{1,0:T(8,128)S(1)} %pad.4.refs_1_.refs_4_, bf16[256,1024]{1,0:T(8,128)(2,1)S(1)} %pad_maximum_fusion.1.refs_2_, bf16[4096,7168]{1,0:T(8,128)(2,1)} %refs_3_.11, ...), custom_call_target="tpu_custom_call" | custom-call | flops 58720256 | bytes 917504 | tf_op jit(solution)/shard_map/pallas_call | solution.py:102
  46.9 4.5 %shard_map.51.refs_6_ = f32[256,896]{1,0:T(8,128)S(1)} custom-call(s32[2]{0:T(128)S(1)} %pad_add_fusion.2.place_ref, bf16[4096,7168]{1,0:T(8,128)(2,1)} %refs_3_.11, f32[4096,128]{1,0:T(8,128)S(1)} %pad.4.refs_1_.refs_4_, bf16[256,1024]{1,0:T(8,128)(2,1)S(1)} %pad_maximum_fusion.1.refs_2_, bf16[4096,7168]{1,0:T(8,128)(2,1)} %refs_3_.11, ...), custom_call_target="tpu_custom_call" | custom-call | flops 58720256 | bytes 917504 | tf_op jit(solution)/shard_map/pallas_call | solution.py:102
  52.3 1.6 %collective-permute-done.15 = bf16[256,512]{1,0:T(8,128)(2,1)S(1)} collective-permute-done((bf16[256,512]{1,0:T(8,128)(2,1)S(1)}, bf16[256,512]{1,0:T(8,128)(2,1)S(1)}, u32[]{:S(2)}, u32[]{:S(2)}) %collective-permute-start.15) | collective-permute-done | bytes 262176 | tf_op jit(solution)/shard_map/ppermute | solution.py:277
  54.8 7.0 %collective-permute-start.17 = (f32[256,256]{1,0:T(8,128)S(1)}, f32[256,256]{1,0:T(8,128)S(1)}, u32[]{:S(2)}, u32[]{:S(2)}) collective-permute-start(f32[256,256]{1,0:T(8,128)S(1)} %convolution_add_fusion), channel_id=1, source_target_pairs={{0,8},{8,0},{16,24},{24,16},{1,9},{9,1},{17,25},{25,17},{2,10},{10... | collective-permute-start | bytes 786440 | tf_op jit(solution)/shard_map/ppermute | solution.py:277
  61.9 1.1 collective-permute-done.17
  63.1 5.4 %shard_map.52 = f32[256,896]{1,0:T(8,128)} custom-call(s32[2]{0:T(128)S(1)} %pad_add_fusion.3.place_ref, bf16[4096,7168]{1,0:T(8,128)(2,1)} %refs_3_.11, f32[4096,128]{1,0:T(8,128)S(1)} %pad.4.refs_1_.refs_4_, bf16[256,1024]{1,0:T(8,128)(2,1)S(1)} %pad_maximum_fusion.2.refs_2_, bf16[4096,7168]{1,0:T(8,128)(2,1)} %refs_3_.11, ...), custom_call_target="tpu_custom_call" | custom-call | flops 58720256 | bytes 917504 | tf_op jit(solution)/shard_map/pallas_call | solution.py:102
  68.9 1.2 collective-permute-start.19
  70.1 4.5 %collective-permute-start.20 = (bf16[1024,256]{1,0:T(8,128)(2,1)}, bf16[1024,256]{1,0:T(8,128)(2,1)}, u32[]{:S(2)}, u32[]{:S(2)}) collective-permute-start(bf16[1024,256]{1,0:T(8,128)(2,1)} %copy-done.17), channel_id=1, source_target_pairs={{2,4},{3,5},{10,12},{11,13},{18,20},{19,21},{26,28},{27,29}} | collective-permute-start | bytes 1572872 | tf_op jit(solution)/shard_map/ppermute | solution.py:281
  74.7 1.2 copy-done.1
  75.9 8.2 %shard_map.53 = f32[256,896]{1,0:T(8,128)} custom-call(s32[2]{0:T(128)S(1)} %pad_add_fusion.4.place_ref, bf16[4096,7168]{1,0:T(8,128)(2,1)} %refs_3_.11, f32[4096,128]{1,0:T(8,128)S(1)} %pad.4.refs_1_.refs_4_, bf16[256,2048]{1,0:T(8,128)(2,1)S(1)} %pad_maximum_fusion.refs_2_, bf16[4096,7168]{1,0:T(8,128)(2,1)} %refs_3_.11, ...), custom_call_target="tpu_custom_call" | custom-call | flops 58720256 | bytes 917504 | tf_op jit(solution)/shard_map/pallas_call | solution.py:102
  84.9 1.0 add.61.head_ref
  86.0 5.7 %shard_map.54 = f32[256,896]{1,0:T(8,128)} custom-call(s32[2]{0:T(128)S(1)} %pad_add_fusion.5.place_ref, bf16[4096,7168]{1,0:T(8,128)(2,1)} %refs_3_.11, f32[4096,128]{1,0:T(8,128)S(1)} %pad.4.refs_1_.refs_4_, bf16[256,1024]{1,0:T(8,128)(2,1)S(1)} %copy-done.6, bf16[4096,7168]{1,0:T(8,128)(2,1)} %refs_3_.11, f32[4096,128]{1,0:T(8,128)S(1)} %pad.4.refs_1_.refs_4_, ...), custom_call_target="tpu_custom_call" | custom-call | flops 58720256 | bytes 917504 | tf_op jit(solution)/shard_map/pallas_call | solution.py:102
  92.0 1.5 collective-permute-start.21
  93.5 1.2 copy-done.2
  94.7 7.3 %shard_map.55.first_ref = f32[256,896]{1,0:T(8,128)S(1)} custom-call(s32[2]{0:T(128)S(1)} %pad_add_fusion.6.place_ref, bf16[4096,7168]{1,0:T(8,128)(2,1)} %refs_3_.11, f32[4096,128]{1,0:T(8,128)S(1)} %pad.4.refs_1_.refs_4_, bf16[256,2048]{1,0:T(8,128)(2,1)S(1)} %pad_maximum_fusion.refs_2_, bf16[4096,7168]{1,0:T(8,128)(2,1)} %refs_3_.11, ...), custom_call_target="tpu_custom_call" | custom-call | flops 58720256 | bytes 917504 | tf_op jit(solution)/shard_map/pallas_call | solution.py:102
  102.1 7.6 %shard_map.56.inverse_ref = f32[256,256]{1,0:T(8,128)S(1)} custom-call(f32[256,256]{1,0:T(8,128)S(1)} %add.61.head_ref), custom_call_target="tpu_custom_call" | custom-call | flops 33554432 | bytes 524288 | tf_op jit(solution)/shard_map/pallas_call | solution.py:151
  109.7 4.3 %collective-permute-done.23.third_ref = f32[256,896]{1,0:T(8,128)} collective-permute-done((f32[256,896]{1,0:T(8,128)}, f32[256,896]{1,0:T(8,128)}, u32[]{:S(2)}, u32[]{:S(2)}) %collective-permute-start.23) | collective-permute-done | bytes 917536 | tf_op jit(solution)/shard_map/ppermute | solution.py:277
  114.0 2.6 %shard_map.57 = (bf16[256,896]{1,0:T(8,128)(2,1)S(1)}, bf16[512,896]{1,0:T(8,128)(2,1)S(1)}) custom-call(s32[1]{0:T(128)} %bitcast.13.place_ref, f32[256,256]{1,0:T(8,128)S(1)} %shard_map.56.inverse_ref, f32[256,896]{1,0:T(8,128)S(1)} %shard_map.55.first_ref, f32[256,896]{1,0:T(8,128)} %collective-permute-done.22.second_ref, ...), custom_call_target="tpu_custom_call" | custom-call | flops 704643072 | bytes 3670016 | tf_op jit(solution)/shard_map/pallas_call | solution.py:177
  117.5 1.3 collective-permute-start.25
  120.5 6.7 %shard_map.58.refs_4_ = bf16[1024,7168]{1,0:T(8,128)(2,1)} custom-call(s32[2]{0:T(128)S(1)} %pad_add_fusion.7.place_ref, bf16[1024,256]{1,0:T(8,128)(2,1)S(1)} %select_select_fusion.error_ref, bf16[1024,7168]{1,0:T(8,128)(2,1)} %weights_ref.5, bf16[512,896]{1,0:T(8,128)(2,1)S(1)} %get-tuple-element.81.refs_0_, bf16[512,896]{1,0:T(8,128)(2,1)} %copy-done.16), custom_call_target="tpu_custom_call" | custom-call | flops 939524096 | bytes 7340032 | tf_op jit(solution)/shard_map/pallas_call | solution.py:259
  127.2 2.3 %collective-permute-done.25.refs_1_ = bf16[256,896]{1,0:T(8,128)(2,1)S(1)} collective-permute-done((bf16[256,896]{1,0:T(8,128)(2,1)S(1)}, bf16[256,896]{1,0:T(8,128)(2,1)S(1)}, u32[]{:S(2)}, u32[]{:S(2)}) %collective-permute-start.25) | collective-permute-done | bytes 458784 | tf_op jit(solution)/shard_map/ppermute | solution.py:277
  130.5 1.2 collective-permute-start.30
  133.8 8.0 %shard_map.59.refs_4_ = bf16[1024,7168]{1,0:T(8,128)(2,1)} custom-call(s32[4]{0:T(128)S(1)} %pad_add_fusion.8.place_ref, bf16[1024,256]{1,0:T(8,128)(2,1)} %copy-done.3, bf16[1024,7168]{1,0:T(8,128)(2,1)} %weights_ref.5, bf16[256,896]{1,0:T(8,128)(2,1)S(1)} %collective-permute-done.24.refs_0_, ...), custom_call_target="tpu_custom_call", output_to_operand_aliasing={{}: (7, {})} | custom-call | flops 1879048192 | bytes 14680064 | tf_op jit(solution)/shard_map/pallas_call | solution.py:259
  143.8 5.8 %shard_map.60 = bf16[1024,7168]{1,0:T(8,128)(2,1)} custom-call(s32[2]{0:T(128)S(1)} %pad_add_fusion.place_ref, bf16[1024,256]{1,0:T(8,128)(2,1)S(1)} %copy-done.4, bf16[1024,7168]{1,0:T(8,128)(2,1)} %weights_ref.5, bf16[128,896]{1,0:T(8,128)(2,1)S(1)} %collective-permute-done.27.refs_0_, ...), custom_call_target="tpu_custom_call", output_to_operand_aliasing={{}: (7, {})} | custom-call | flops 939524096 | bytes 7340032 | tf_op jit(solution)/shard_map/pallas_call | solution.py:259
  (106 shorter events, 16.0 us)
Async XLA Ops:
  3.0 9.2 %collective-permute-start = (bf16[256,512]{1,0:T(8,128)(2,1)S(1)}, bf16[256,512]{1,0:T(8,128)(2,1)}, u32[]{:S(2)}, u32[]{:S(2)}) collective-permute-start(bf16[256,512]{1,0:T(8,128)(2,1)S(1)} %shard_map.46), channel_id=1, source_target_pairs={{0,2},{1,3},{8,10},{9,11},{16,18},{17,19},{24,26},{25,27}} | collective-permute-start | bytes 786440 | tf_op jit(solution)/shard_map/ppermute | solution.py:281
  5.6 12.2 %collective-permute-start.2 = (bf16[256,512]{1,0:T(8,128)(2,1)S(1)}, bf16[256,512]{1,0:T(8,128)(2,1)}, u32[]{:S(2)}, u32[]{:S(2)}) collective-permute-start(bf16[256,512]{1,0:T(8,128)(2,1)S(1)} %shard_map.48), channel_id=1, source_target_pairs={{0,2},{1,3},{8,10},{9,11},{16,18},{17,19},{24,26},{25,27}} | collective-permute-start | bytes 786440 | tf_op jit(solution)/shard_map/ppermute | solution.py:281
  8.2 16.9 %collective-permute-start.6 = (bf16[256,512]{1,0:T(8,128)(2,1)S(1)}, bf16[256,512]{1,0:T(8,128)(2,1)}, u32[]{:S(2)}, u32[]{:S(2)}) collective-permute-start(bf16[256,512]{1,0:T(8,128)(2,1)S(1)} %shard_map.49), channel_id=1, source_target_pairs={{0,2},{1,3},{8,10},{9,11},{16,18},{17,19},{24,26},{25,27}} | collective-permute-start | bytes 786440 | tf_op jit(solution)/shard_map/ppermute | solution.py:281
  10.7 18.3 %collective-permute-start.4 = (bf16[256,512]{1,0:T(8,128)(2,1)S(1)}, bf16[256,512]{1,0:T(8,128)(2,1)S(1)}, u32[]{:S(2)}, u32[]{:S(2)}) collective-permute-start(bf16[256,512]{1,0:T(8,128)(2,1)S(1)} %shard_map.47), channel_id=1, source_target_pairs={{0,2},{1,3},{8,10},{9,11},{16,18},{17,19},{24,26},{25,27}} | collective-permute-start | bytes 786440 | tf_op jit(solution)/shard_map/ppermute | solution.py:281
  12.2 12.0 %collective-permute-start.1 = (bf16[256,512]{1,0:T(8,128)(2,1)}, bf16[256,512]{1,0:T(8,128)(2,1)}, u32[]{:S(2)}, u32[]{:S(2)}) collective-permute-start(bf16[256,512]{1,0:T(8,128)(2,1)} %collective-permute-done), channel_id=1, source_target_pairs={{2,4},{3,5},{10,12},{11,13},{18,20},{19,21},{26,28},{27,29}} | collective-permute-start | bytes 786440 | tf_op jit(solution)/shard_map/ppermute | solution.py:281
  17.8 8.6 %collective-permute-start.5 = (bf16[256,512]{1,0:T(8,128)(2,1)}, bf16[256,512]{1,0:T(8,128)(2,1)}, u32[]{:S(2)}, u32[]{:S(2)}) collective-permute-start(bf16[256,512]{1,0:T(8,128)(2,1)} %collective-permute-done.2), channel_id=1, source_target_pairs={{2,4},{3,5},{10,12},{11,13},{18,20},{19,21},{26,28},{27,29}} | collective-permute-start | bytes 786440 | tf_op jit(solution)/shard_map/ppermute | solution.py:281
  24.1 6.6 %slice-start = ((bf16[1024,7168]{1,0:T(8,128)(2,1)}), bf16[1024,256]{1,0:T(8,128)(2,1)S(1)}, s32[]{:S(2)}) async-start(bf16[1024,7168]{1,0:T(8,128)(2,1)} %weights_ref.5), calls=%async_computation | async-start | bytes 1048576 | tf_op jit(solution)/shard_map/slice | solution.py:341
  24.1 6.6 %copy-start.15 = (s32[1024,256]{1,0:T(8,128)S(1)}, s32[1024,256]{1,0:T(8,128)}, u32[]{:S(2)}) copy-start(s32[1024,256]{1,0:T(8,128)} %param.7) | copy-start | bytes 3145732
  24.2 6.6 %collective-permute-start.3 = (bf16[256,512]{1,0:T(8,128)(2,1)}, bf16[256,512]{1,0:T(8,128)(2,1)S(1)}, u32[]{:S(2)}, u32[]{:S(2)}) collective-permute-start(bf16[256,512]{1,0:T(8,128)(2,1)} %collective-permute-done.1), channel_id=1, source_target_pairs={{4,6},{5,7},{12,14},{13,15},{20,22},{21,23},{28,30},{29,31}} | collective-permute-start | bytes 786440 | tf_op jit(solution)/shard_map/ppermute | solution.py:281
  25.1 5.8 %collective-permute-start.8 = (bf16[256,512]{1,0:T(8,128)(2,1)}, bf16[256,512]{1,0:T(8,128)(2,1)S(1)}, u32[]{:S(2)}, u32[]{:S(2)}) collective-permute-start(bf16[256,512]{1,0:T(8,128)(2,1)} %collective-permute-done.6), channel_id=1, source_target_pairs={{2,4},{3,5},{10,12},{11,13},{18,20},{19,21},{26,28},{27,29}} | collective-permute-start | bytes 786440 | tf_op jit(solution)/shard_map/ppermute | solution.py:281
  26.4 6.2 %collective-permute-start.7 = (bf16[256,512]{1,0:T(8,128)(2,1)}, bf16[256,512]{1,0:T(8,128)(2,1)S(1)}, u32[]{:S(2)}, u32[]{:S(2)}) collective-permute-start(bf16[256,512]{1,0:T(8,128)(2,1)} %collective-permute-done.5), channel_id=1, source_target_pairs={{4,6},{5,7},{12,14},{13,15},{20,22},{21,23},{28,30},{29,31}} | collective-permute-start | bytes 786440 | tf_op jit(solution)/shard_map/ppermute | solution.py:281
  29.0 7.9 %collective-permute-start.10 = (bf16[256,512]{1,0:T(8,128)(2,1)S(1)}, bf16[256,512]{1,0:T(8,128)(2,1)S(1)}, u32[]{:S(2)}, u32[]{:S(2)}) collective-permute-start(bf16[256,512]{1,0:T(8,128)(2,1)S(1)} %collective-permute-done.4), channel_id=1, source_target_pairs={{2,4},{3,5},{10,12},{11,13},{18,20},{19,21},{26,28},{27,29}} | collective-permute-start | bytes 786440 | tf_op jit(solution)/shard_map/ppermute | solution.py:281
  30.8 9.1 %copy-start.11 = (bf16[1024,256]{1,0:T(8,128)(2,1)}, bf16[1024,256]{1,0:T(8,128)(2,1)S(1)}, u32[]{:S(2)}) copy-start(bf16[1024,256]{1,0:T(8,128)(2,1)S(1)} %compare_select_fusion) | copy-start | bytes 1572868
  30.9 8.0 %collective-permute-start.9 = (bf16[256,512]{1,0:T(8,128)(2,1)S(1)}, bf16[256,512]{1,0:T(8,128)(2,1)S(1)}, u32[]{:S(2)}, u32[]{:S(2)}) collective-permute-start(bf16[256,512]{1,0:T(8,128)(2,1)S(1)} %collective-permute-done.8), channel_id=1, source_target_pairs={{4,6},{5,7},{12,14},{13,15},{20,22},{21,23},{28,30},{29,31}} | collective-permute-start | bytes 786440 | tf_op jit(solution)/shard_map/ppermute | solution.py:281
  32.6 6.3 %collective-permute-start.11 = (bf16[256,512]{1,0:T(8,128)(2,1)S(1)}, bf16[256,512]{1,0:T(8,128)(2,1)S(1)}, u32[]{:S(2)}, u32[]{:S(2)}) collective-permute-start(bf16[256,512]{1,0:T(8,128)(2,1)S(1)} %select_select_fusion.4), channel_id=1, source_target_pairs={{0,1},{1,0},{2,3},{3,2},{4,5},{5,4},{6,7},{7,6},{8,9},{9,8},{10,11... | collective-permute-start | bytes 786440 | tf_op jit(solution)/shard_map/ppermute | solution.py:277
  34.9 7.2 %collective-permute-start.13 = (bf16[256,512]{1,0:T(8,128)(2,1)S(1)}, bf16[256,512]{1,0:T(8,128)(2,1)S(1)}, u32[]{:S(2)}, u32[]{:S(2)}) collective-permute-start(bf16[256,512]{1,0:T(8,128)(2,1)S(1)} %select_select_fusion.3), channel_id=1, source_target_pairs={{0,1},{1,0},{2,3},{3,2},{4,5},{5,4},{6,7},{7,6},{8,9},{9,8},{10,11... | collective-permute-start | bytes 786440 | tf_op jit(solution)/shard_map/ppermute | solution.py:277
  36.8 4.4 %collective-permute-start.12 = (bf16[256,512]{1,0:T(8,128)(2,1)S(1)}, bf16[256,512]{1,0:T(8,128)(2,1)S(1)}, u32[]{:S(2)}, u32[]{:S(2)}) collective-permute-start(bf16[256,512]{1,0:T(8,128)(2,1)S(1)} %collective-permute-done.10), channel_id=1, source_target_pairs={{4,6},{5,7},{12,14},{13,15},{20,22},{21,23},{28,30},{29,31}} | collective-permute-start | bytes 786440 | tf_op jit(solution)/shard_map/ppermute | solution.py:281
  37.6 16.4 %collective-permute-start.16 = (bf16[1024,256]{1,0:T(8,128)(2,1)S(1)}, bf16[1024,256]{1,0:T(8,128)(2,1)S(1)}, u32[]{:S(2)}, u32[]{:S(2)}) collective-permute-start(bf16[1024,256]{1,0:T(8,128)(2,1)S(1)} %compare_select_fusion), channel_id=1, source_target_pairs={{0,2},{1,3},{8,10},{9,11},{16,18},{17,19},{24,26},{25,27}} | collective-permute-start | bytes 1572872 | tf_op jit(solution)/shard_map/ppermute | solution.py:281
  39.9 14.1 %collective-permute-start.14 = (bf16[256,512]{1,0:T(8,128)(2,1)S(1)}, bf16[256,512]{1,0:T(8,128)(2,1)S(1)}, u32[]{:S(2)}, u32[]{:S(2)}) collective-permute-start(bf16[256,512]{1,0:T(8,128)(2,1)S(1)} %select_select_fusion.2), channel_id=1, source_target_pairs={{0,1},{1,0},{2,3},{3,2},{4,5},{5,4},{6,7},{7,6},{8,9},{9,8},{10,11... | collective-permute-start | bytes 786440 | tf_op jit(solution)/shard_map/ppermute | solution.py:277
  41.3 12.7 %collective-permute-start.15 = (bf16[256,512]{1,0:T(8,128)(2,1)S(1)}, bf16[256,512]{1,0:T(8,128)(2,1)S(1)}, u32[]{:S(2)}, u32[]{:S(2)}) collective-permute-start(bf16[256,512]{1,0:T(8,128)(2,1)S(1)} %select_select_fusion.1), channel_id=1, source_target_pairs={{0,1},{1,0},{2,3},{3,2},{4,5},{5,4},{6,7},{7,6},{8,9},{9,8},{10,11... | collective-permute-start | bytes 786440 | tf_op jit(solution)/shard_map/ppermute | solution.py:277
  54.1 8.9 %copy-start = (bf16[256,2048]{1,0:T(8,128)(2,1)}, bf16[256,2048]{1,0:T(8,128)(2,1)S(1)}, u32[]{:S(2)}) copy-start(bf16[256,2048]{1,0:T(8,128)(2,1)S(1)} %get-tuple-element.92.refs_5_) | copy-start | bytes 3145732
  54.1 9.0 %copy-start.9 = (bf16[256,1024]{1,0:T(8,128)(2,1)}, bf16[256,1024]{1,0:T(8,128)(2,1)S(1)}, u32[]{:S(2)}) copy-start(bf16[256,1024]{1,0:T(8,128)(2,1)S(1)} %get-tuple-element.91.refs_5_) | copy-start | bytes 1572868
  54.8 8.2 %collective-permute-start.17 = (f32[256,256]{1,0:T(8,128)S(1)}, f32[256,256]{1,0:T(8,128)S(1)}, u32[]{:S(2)}, u32[]{:S(2)}) collective-permute-start(f32[256,256]{1,0:T(8,128)S(1)} %convolution_add_fusion), channel_id=1, source_target_pairs={{0,8},{8,0},{16,24},{24,16},{1,9},{9,1},{17,25},{25,17},{2,10},{10... | collective-permute-start | bytes 786440 | tf_op jit(solution)/shard_map/ppermute | solution.py:277
  61.9 6.7 %copy-start.5 = (bf16[256,1024]{1,0:T(8,128)(2,1)}, bf16[256,1024]{1,0:T(8,128)(2,1)S(1)}, u32[]{:S(2)}) copy-start(bf16[256,1024]{1,0:T(8,128)(2,1)S(1)} %pad_maximum_fusion.2.refs_2_) | copy-start | bytes 1572868
  63.0 5.9 %copy-start.13 = (f32[256,256]{1,0:T(8,128)}, f32[256,256]{1,0:T(8,128)S(1)}, u32[]{:S(2)}) copy-start(f32[256,256]{1,0:T(8,128)S(1)} %add.60) | copy-start | bytes 786436
  68.6 17.4 %collective-permute-start.18 = (f32[256,896]{1,0:T(8,128)}, f32[256,896]{1,0:T(8,128)}, u32[]{:S(2)}, u32[]{:S(2)}) collective-permute-start(f32[256,896]{1,0:T(8,128)} %shard_map.52), channel_id=1, source_target_pairs={{0,8},{8,0},{16,24},{24,16},{1,9},{9,1},{17,25},{25,17},{2,10},{10... | collective-permute-start | bytes 2752520 | tf_op jit(solution)/shard_map/ppermute | solution.py:277
  68.9 16.0 %collective-permute-start.19 = (f32[256,256]{1,0:T(8,128)S(1)}, f32[256,256]{1,0:T(8,128)}, u32[]{:S(2)}, u32[]{:S(2)}) collective-permute-start(f32[256,256]{1,0:T(8,128)S(1)} %add.60), channel_id=1, source_target_pairs={{0,16},{8,24},{16,0},{24,8},{1,17},{9,25},{17,1},{25,9},{2,18},{10... | collective-permute-start | bytes 786440 | tf_op jit(solution)/shard_map/ppermute | solution.py:277
  70.1 21.8 %collective-permute-start.20 = (bf16[1024,256]{1,0:T(8,128)(2,1)}, bf16[1024,256]{1,0:T(8,128)(2,1)}, u32[]{:S(2)}, u32[]{:S(2)}) collective-permute-start(bf16[1024,256]{1,0:T(8,128)(2,1)} %copy-done.17), channel_id=1, source_target_pairs={{2,4},{3,5},{10,12},{11,13},{18,20},{19,21},{26,28},{27,29}} | collective-permute-start | bytes 1572872 | tf_op jit(solution)/shard_map/ppermute | solution.py:281
  75.9 9.0 %copy-start.14 = (f32[256,256]{1,0:T(8,128)S(1)}, f32[256,256]{1,0:T(8,128)}, u32[]{:S(2)}) copy-start(f32[256,256]{1,0:T(8,128)} %copy-done.13) | copy-start | bytes 786436
  75.9 10.0 %copy-start.6 = (bf16[256,1024]{1,0:T(8,128)(2,1)S(1)}, bf16[256,1024]{1,0:T(8,128)(2,1)}, u32[]{:S(2)}) copy-start(bf16[256,1024]{1,0:T(8,128)(2,1)} %copy-done.5) | copy-start | bytes 1572868
  75.9 10.1 %copy-start.8 = (f32[256,896]{1,0:T(8,128)S(1)}, f32[256,896]{1,0:T(8,128)}, u32[]{:S(2)}) copy-start(f32[256,896]{1,0:T(8,128)} %copy-done.7) | copy-start | bytes 2752516
  75.9 10.1 %copy-start.10 = (bf16[256,1024]{1,0:T(8,128)(2,1)S(1)}, bf16[256,1024]{1,0:T(8,128)(2,1)}, u32[]{:S(2)}) copy-start(bf16[256,1024]{1,0:T(8,128)(2,1)} %copy-done.9) | copy-start | bytes 1572868
  84.2 25.6 %collective-permute-start.22 = (f32[256,896]{1,0:T(8,128)}, f32[256,896]{1,0:T(8,128)}, u32[]{:S(2)}, u32[]{:S(2)}) collective-permute-start(f32[256,896]{1,0:T(8,128)} %shard_map.53), channel_id=1, source_target_pairs={{0,8},{8,0},{16,24},{24,16},{1,9},{9,1},{17,25},{25,17},{2,10},{10... | collective-permute-start | bytes 2752520 | tf_op jit(solution)/shard_map/ppermute | solution.py:277
  91.7 22.3 %collective-permute-start.23 = (f32[256,896]{1,0:T(8,128)}, f32[256,896]{1,0:T(8,128)}, u32[]{:S(2)}, u32[]{:S(2)}) collective-permute-start(f32[256,896]{1,0:T(8,128)} %shard_map.54), channel_id=1, source_target_pairs={{0,16},{8,24},{16,0},{24,8},{1,17},{9,25},{17,1},{25,9},{2,18},{10... | collective-permute-start | bytes 2752520 | tf_op jit(solution)/shard_map/ppermute | solution.py:277
  92.0 17.7 %collective-permute-start.21 = (bf16[1024,256]{1,0:T(8,128)(2,1)}, bf16[1024,256]{1,0:T(8,128)(2,1)}, u32[]{:S(2)}, u32[]{:S(2)}) collective-permute-start(bf16[1024,256]{1,0:T(8,128)(2,1)} %collective-permute-done.20), channel_id=1, source_target_pairs={{4,6},{5,7},{12,14},{13,15},{20,22},{21,23},{28,30},{29,31}} | collective-permute-start | bytes 1572872 | tf_op jit(solution)/shard_map/ppermute | solution.py:281
  102.0 17.0 %copy-start.12 = (bf16[1024,256]{1,0:T(8,128)(2,1)S(1)}, bf16[1024,256]{1,0:T(8,128)(2,1)}, u32[]{:S(2)}) copy-start(bf16[1024,256]{1,0:T(8,128)(2,1)} %copy-done.11) | copy-start | bytes 1572868
  102.1 17.0 %copy-start.18 = (bf16[1024,256]{1,0:T(8,128)(2,1)S(1)}, bf16[1024,256]{1,0:T(8,128)(2,1)}, u32[]{:S(2)}) copy-start(bf16[1024,256]{1,0:T(8,128)(2,1)} %copy-done.17) | copy-start | bytes 1572868
  116.6 2.9 %collective-permute-start.26 = (bf16[512,896]{1,0:T(8,128)(2,1)S(1)}, bf16[512,896]{1,0:T(8,128)(2,1)S(1)}, u32[]{:S(2)}, u32[]{:S(2)}) collective-permute-start(bf16[512,896]{1,0:T(8,128)(2,1)S(1)} %get-tuple-element.81.refs_0_), channel_id=1, source_target_pairs={{0,8},{8,0},{16,24},{24,16},{1,9},{9,1},{17,25},{25,17},{2,10},{10... | collective-permute-start | bytes 2752520 | tf_op jit(solution)/shard_map/ppermute | solution.py:277
  117.5 12.1 %collective-permute-start.25 = (bf16[256,896]{1,0:T(8,128)(2,1)S(1)}, bf16[256,896]{1,0:T(8,128)(2,1)S(1)}, u32[]{:S(2)}, u32[]{:S(2)}) collective-permute-start(bf16[256,896]{1,0:T(8,128)(2,1)S(1)} %get-tuple-element.80), channel_id=1, source_target_pairs={{0,1},{1,0},{2,3},{3,2},{4,5},{5,4},{6,7},{7,6},{8,9},{9,8},{10,11... | collective-permute-start | bytes 1376264 | tf_op jit(solution)/shard_map/ppermute | solution.py:277
  118.8 11.8 %collective-permute-start.24 = (bf16[256,896]{1,0:T(8,128)(2,1)S(1)}, bf16[256,896]{1,0:T(8,128)(2,1)S(1)}, u32[]{:S(2)}, u32[]{:S(2)}) collective-permute-start(bf16[256,896]{1,0:T(8,128)(2,1)S(1)} %get-tuple-element.80), channel_id=1, source_target_pairs={{0,16},{8,24},{16,0},{24,8},{1,17},{9,25},{17,1},{25,9},{2,18},{10... | collective-permute-start | bytes 1376264 | tf_op jit(solution)/shard_map/ppermute | solution.py:277
  119.2 8.0 %copy-start.3 = (bf16[1024,256]{1,0:T(8,128)(2,1)}, bf16[1024,256]{1,0:T(8,128)(2,1)S(1)}, u32[]{:S(2)}) copy-start(bf16[1024,256]{1,0:T(8,128)(2,1)S(1)} %select_select_fusion.error_ref) | copy-start | bytes 1572868
  130.5 2.6 %collective-permute-start.30 = (bf16[256,896]{1,0:T(8,128)(2,1)S(1)}, bf16[256,896]{1,0:T(8,128)(2,1)S(1)}, u32[]{:S(2)}, u32[]{:S(2)}) collective-permute-start(bf16[256,896]{1,0:T(8,128)(2,1)S(1)} %collective-permute-done.25.refs_1_), channel_id=1, source_target_pairs={{0,8},{8,0},{16,24},{24,16},{1,9},{9,1},{17,25},{25,17},{2,10},{10... | collective-permute-start | bytes 1376264 | tf_op jit(solution)/shard_map/ppermute | solution.py:277
  131.7 2.1 %collective-permute-start.29 = (bf16[256,896]{1,0:T(8,128)(2,1)S(1)}, bf16[256,896]{1,0:T(8,128)(2,1)S(1)}, u32[]{:S(2)}, u32[]{:S(2)}) collective-permute-start(bf16[256,896]{1,0:T(8,128)(2,1)S(1)} %collective-permute-done.24.refs_0_), channel_id=1, source_target_pairs={{0,8},{8,0},{16,24},{24,16},{1,9},{9,1},{17,25},{25,17},{2,10},{10... | collective-permute-start | bytes 1376264 | tf_op jit(solution)/shard_map/ppermute | solution.py:277
  131.7 10.1 %collective-permute-start.27 = (bf16[128,896]{1,0:T(8,128)(2,1)S(1)}, bf16[128,896]{1,0:T(8,128)(2,1)S(1)}, u32[]{:S(2)}, u32[]{:S(2)}) collective-permute-start(bf16[128,896]{1,0:T(8,128)(2,1)S(1)} %slice.10), channel_id=1, source_target_pairs={{0,16},{8,24},{16,0},{24,8},{1,17},{9,25},{17,1},{25,9},{2,18},{10... | collective-permute-start | bytes 688136 | tf_op jit(solution)/shard_map/ppermute | solution.py:277
  132.0 9.8 %collective-permute-start.28 = (bf16[128,896]{1,0:T(8,128)(2,1)S(1)}, bf16[128,896]{1,0:T(8,128)(2,1)S(1)}, u32[]{:S(2)}, u32[]{:S(2)}) collective-permute-start(bf16[128,896]{1,0:T(8,128)(2,1)S(1)} %slice.11), channel_id=1, source_target_pairs={{0,1},{1,0},{2,3},{3,2},{4,5},{5,4},{6,7},{7,6},{8,9},{9,8},{10,11... | collective-permute-start | bytes 688136 | tf_op jit(solution)/shard_map/ppermute | solution.py:277
  132.4 11.4 %copy-start.4 = (bf16[1024,256]{1,0:T(8,128)(2,1)S(1)}, bf16[1024,256]{1,0:T(8,128)(2,1)}, u32[]{:S(2)}) copy-start(bf16[1024,256]{1,0:T(8,128)(2,1)} %copy-done.3) | copy-start | bytes 1572868
  141.8 1.6 %collective-permute-start.31 = (bf16[128,896]{1,0:T(8,128)(2,1)S(1)}, bf16[128,896]{1,0:T(8,128)(2,1)S(1)}, u32[]{:S(2)}, u32[]{:S(2)}) collective-permute-start(bf16[128,896]{1,0:T(8,128)(2,1)S(1)} %collective-permute-done.27.refs_0_), channel_id=1, source_target_pairs={{0,8},{8,0},{16,24},{24,16},{1,9},{9,1},{17,25},{25,17},{2,10},{10... | collective-permute-start | bytes 688136 | tf_op jit(solution)/shard_map/ppermute | solution.py:277
  142.3 1.5 collective-permute-start.32
  (5 other events, 5.1 us)
